TPU v7x, 512 devices: a whole 4x8x8 slice. The times are simulated.
512 devices in a mesh: row: 32 (over y, x_lo, core), col: 16 (over x_hi, z).
Axes of the slice: x: 4 (x_hi: 2, x_lo: 2; x = x_hi * 2 + x_lo), y: 8, z: 8, core: 2. Of those that a mesh axis runs over, the one named last changes fastest.
Arguments:
- cotangent: bfloat16 [196608, 128], P(('row', 'col')), may hold values from -6 to 6
- pre_act: bfloat16 [196608, 128], P(('row', 'col')), may hold values from -6 to 6
- aggregated: bfloat16 [196608, 128], P(('row', 'col')), may hold values from -6 to 6
- weight: bfloat16 [128, 128], replicated, may hold values from -0.5 to 0.5
- tile_values: bfloat16 [16384, 128, 128], P(('row', 'col')), may hold values from -0.15625 to 0.15625
- tile_in: int32 [16384], P(('row', 'col')), may hold values from 0 to 1535, as said below
- tile_out: int32 [16384], P(('row', 'col')), may hold values from 0 to 1535, as said below
- order: int32 [196608], P(('row', 'col')), may hold values from 0 to 196607, as said below
Outputs:
- node_grad: bfloat16 [196608, 128], P(('row', 'col'))
- weight_grad: float32 [128, 128], replicated
Inputs may be any that keep to these rules, and one draw needn't show every extreme that they name: `tile_in`: devices are numbered row-major over (row, col), each holding 32 tiles and 3 consecutive blocks. A tile of the device at (r, c) reads a block held by the device (r + d mod 32, c) with -8 <= d <= 8; on every device one tile has d = -8 and one d = 8. `tile_out`: A tile of the device at (r, c) writes a block held by some device of row r. `order`: maps the rows of each device onto the rows of the same device, each once.
All inputs are finite; a program needn't handle non-finite values.
Results may differ from a plain program's by a relative error of at most 0.0049.
Values may be sent and summed in bfloat16 or wider, within the bound.
No kernel may reach another device: no remote copies, remote signals or barrier semaphores. Data moves between devices by JAX's collectives and lax.ppermute only.
A program may use at most 64 MiB of HBM per device.

v0:
```python
import jax
import jax.numpy as jnp
from jax import lax
from jax.sharding import PartitionSpec as P


def from_behind(value, axis, steps):
    count = lax.axis_size(axis)
    pairs = [(source, (source + steps) % count) for source in range(count)]
    return lax.ppermute(value, axis, pairs)


def on_device(cotangent, pre_act, aggregated, weight, tile_values, tile_in, tile_out, order):
    row_count = lax.axis_size("row")
    col_count = lax.axis_size("col")
    row_pos = lax.axis_index("row")
    feat_width = weight.shape[0]
    tile_side = tile_values.shape[1]
    local_nodes = cotangent.shape[0]
    blocks_dev = local_nodes // tile_side
    band_reach = row_count // 4
    local_order = order % local_nodes
    grad_rows = jnp.take(cotangent, local_order, axis=0)
    grad_pre = jnp.where(pre_act > 0, grad_rows, jnp.zeros_like(grad_rows))
    weight_part = lax.dot_general(
        aggregated, grad_pre, (((0,), (0,)), ((), ())), preferred_element_type=jnp.float32
    )
    grad_agg = lax.dot_general(
        grad_pre, weight, (((1,), (1,)), ((), ())), preferred_element_type=jnp.float32
    )
    agg_blocks = grad_agg.astype(jnp.bfloat16).reshape(blocks_dev, tile_side, feat_width)
    source_device = tile_in // blocks_dev
    source_group = source_device // col_count
    source_local = tile_in % blocks_dev
    forward_gap = (source_group - row_pos) % row_count
    distance = jnp.where(forward_gap > row_count // 2, forward_gap - row_count, forward_gap)
    slots = 2 * band_reach + 1
    current = from_behind(agg_blocks, "row", -band_reach)
    received = jnp.zeros((slots,) + agg_blocks.shape, jnp.bfloat16)
    received = lax.dynamic_update_index_in_dim(received, current, 0, 0)

    def turn_step(turn, carry):
        moving, stored = carry
        moving = from_behind(moving, "row", 1)
        return (moving, lax.dynamic_update_index_in_dim(stored, moving, turn, 0))

    current, received = lax.fori_loop(1, slots, turn_step, (current, received))
    slot_index = band_reach - distance
    flat_blocks = received.reshape(slots * blocks_dev, tile_side, feat_width)
    source_index = slot_index * blocks_dev + source_local
    picked = jnp.take(flat_blocks, source_index, axis=0)
    products = jnp.einsum("tij,tjf->tif", tile_values, picked, preferred_element_type=jnp.float32)
    target_local = tile_out - row_pos * col_count * blocks_dev
    partial_value = (
        jnp.zeros((col_count * blocks_dev, tile_side, feat_width), jnp.float32)
        .at[target_local]
        .add(products)
    )
    own_rows = lax.psum_scatter(partial_value, "col", scatter_dimension=0, tiled=True)
    wgrad_total = lax.psum(weight_part, ("row", "col"))
    node_grad = own_rows.reshape(local_nodes, feat_width).astype(jnp.bfloat16)
    all_nodes = local_nodes * row_count * col_count
    weight_grad = wgrad_total * (1.0 / float(all_nodes) ** 0.5)
    return (node_grad, weight_grad)


def solution(mesh):
    return jax.shard_map(
        on_device,
        mesh=mesh,
        in_specs=(
            P(("row", "col"), None),
            P(("row", "col"), None),
            P(("row", "col"), None),
            P(),
            P(("row", "col"), None, None),
            P(("row", "col")),
            P(("row", "col")),
            P(("row", "col")),
        ),
        out_specs=(P(("row", "col"), None), P()),
        check_vma=False,
    )
```

profile of v0, /device:TPU:1, one launch (start us, length us, event | category | flops | bytes accessed | tf_op | source)
XLA Modules:
  0.0 396.0 jit_solution(14158637123219687710)
XLA Ops:
  8.0 0.0 copy-start
  8.0 0.0 all-reduce.3.cloned.1.call-start
  8.1 0.8 compare_and_fusion
  8.8 2.1 gather_fusion
  10.9 1.9 convolution_bitcast_fusion.1
  12.8 0.0 all-reduce.3.cloned.1.call-update
  12.8 0.0 reduce-scatter.2.cloned.1.call-start
  12.9 1.1 convolution_convert_fusion
  14.0 6.7 %collective-permute-start.1 = (bf16[3,128,128]{2,1,0:T(8,128)(2,1)S(1)}, bf16[3,128,128]{2,1,0:T(8,128)(2,1)S(1)}, u32[]{:S(2)}, u32[]{:S(2)}) collective-permute-start(bf16[3,128,128]{2,1,0:T(8,128)(2,1)S(1)} %bitcast.18), channel_id=1, source_target_pairs={{0,384},{16,400},{32,416},{48,432},{64,448},{80,464},{96,480},{112... | collective-permute-start | bytes 294920 | tf_op jit(solution)/shard_map/ppermute | solution.py:10
  20.8 0.7 compare_and_fusion.1
  21.5 0.7 compare_select_fusion.4
  22.1 3.2 collective-permute-done.1
  25.3 0.4 dynamic_update_slice.11
  25.7 127.4 %while.15 = (s32[]{:T(128)}, bf16[3,128,128]{2,1,0:T(8,128)(2,1)S(1)}, bf16[17,3,128,128]{3,2,1,0:T(8,128)(2,1)S(1)}, s32[]{:T(128)}, s32[]{:T(128)}, /*index=5*/s32[]{:T(128)}) while((s32[]{:T(128)}, bf16[3,128,128]{2,1,0:T(8,128)(2,1)S(1)}, bf16[17,3,128,128]{3,2,1,0:T(8,128)(2,1)S(1)}, s32[]{:T(128)}, s32[]{:T(128)}, ...), condition=%wide.region_1.2_spmd, body=%wide.region_0.1_spmd.sunk | while | flops 5 | bytes 786579 | solution.py:47
  25.7 3.6 collective-permute-start
  29.3 2.1 collective-permute-done
  31.4 3.8 collective-permute-start
  35.3 4.2 %collective-permute-done = bf16[3,128,128]{2,1,0:T(8,128)(2,1)S(1)} collective-permute-done((bf16[3,128,128]{2,1,0:T(8,128)(2,1)S(1)}, bf16[3,128,128]{2,1,0:T(8,128)(2,1)S(1)}, u32[]{:S(2)}, u32[]{:S(2)}) %collective-permute-start) | collective-permute-done | bytes 98336 | tf_op jit(solution)/shard_map/while/body/eval_jaxpr/ppermute | solution.py:10
  39.5 1.9 collective-permute-start
  41.5 6.1 %collective-permute-done = bf16[3,128,128]{2,1,0:T(8,128)(2,1)S(1)} collective-permute-done((bf16[3,128,128]{2,1,0:T(8,128)(2,1)S(1)}, bf16[3,128,128]{2,1,0:T(8,128)(2,1)S(1)}, u32[]{:S(2)}, u32[]{:S(2)}) %collective-permute-start) | collective-permute-done | bytes 98336 | tf_op jit(solution)/shard_map/while/body/eval_jaxpr/ppermute | solution.py:10
  47.6 1.9 collective-permute-start
  49.6 6.1 %collective-permute-done = bf16[3,128,128]{2,1,0:T(8,128)(2,1)S(1)} collective-permute-done((bf16[3,128,128]{2,1,0:T(8,128)(2,1)S(1)}, bf16[3,128,128]{2,1,0:T(8,128)(2,1)S(1)}, u32[]{:S(2)}, u32[]{:S(2)}) %collective-permute-start) | collective-permute-done | bytes 98336 | tf_op jit(solution)/shard_map/while/body/eval_jaxpr/ppermute | solution.py:10
  55.7 1.9 collective-permute-start
  57.7 6.1 %collective-permute-done = bf16[3,128,128]{2,1,0:T(8,128)(2,1)S(1)} collective-permute-done((bf16[3,128,128]{2,1,0:T(8,128)(2,1)S(1)}, bf16[3,128,128]{2,1,0:T(8,128)(2,1)S(1)}, u32[]{:S(2)}, u32[]{:S(2)}) %collective-permute-start) | collective-permute-done | bytes 98336 | tf_op jit(solution)/shard_map/while/body/eval_jaxpr/ppermute | solution.py:10
  63.9 1.9 collective-permute-start
  65.8 6.1 %collective-permute-done = bf16[3,128,128]{2,1,0:T(8,128)(2,1)S(1)} collective-permute-done((bf16[3,128,128]{2,1,0:T(8,128)(2,1)S(1)}, bf16[3,128,128]{2,1,0:T(8,128)(2,1)S(1)}, u32[]{:S(2)}, u32[]{:S(2)}) %collective-permute-start) | collective-permute-done | bytes 98336 | tf_op jit(solution)/shard_map/while/body/eval_jaxpr/ppermute | solution.py:10
  72.0 1.9 collective-permute-start
  73.9 6.1 %collective-permute-done = bf16[3,128,128]{2,1,0:T(8,128)(2,1)S(1)} collective-permute-done((bf16[3,128,128]{2,1,0:T(8,128)(2,1)S(1)}, bf16[3,128,128]{2,1,0:T(8,128)(2,1)S(1)}, u32[]{:S(2)}, u32[]{:S(2)}) %collective-permute-start) | collective-permute-done | bytes 98336 | tf_op jit(solution)/shard_map/while/body/eval_jaxpr/ppermute | solution.py:10
  80.1 1.9 collective-permute-start
  82.0 6.1 %collective-permute-done = bf16[3,128,128]{2,1,0:T(8,128)(2,1)S(1)} collective-permute-done((bf16[3,128,128]{2,1,0:T(8,128)(2,1)S(1)}, bf16[3,128,128]{2,1,0:T(8,128)(2,1)S(1)}, u32[]{:S(2)}, u32[]{:S(2)}) %collective-permute-start) | collective-permute-done | bytes 98336 | tf_op jit(solution)/shard_map/while/body/eval_jaxpr/ppermute | solution.py:10
  88.2 1.9 collective-permute-start
  90.1 6.1 %collective-permute-done = bf16[3,128,128]{2,1,0:T(8,128)(2,1)S(1)} collective-permute-done((bf16[3,128,128]{2,1,0:T(8,128)(2,1)S(1)}, bf16[3,128,128]{2,1,0:T(8,128)(2,1)S(1)}, u32[]{:S(2)}, u32[]{:S(2)}) %collective-permute-start) | collective-permute-done | bytes 98336 | tf_op jit(solution)/shard_map/while/body/eval_jaxpr/ppermute | solution.py:10
  96.3 1.9 collective-permute-start
  98.2 6.1 %collective-permute-done = bf16[3,128,128]{2,1,0:T(8,128)(2,1)S(1)} collective-permute-done((bf16[3,128,128]{2,1,0:T(8,128)(2,1)S(1)}, bf16[3,128,128]{2,1,0:T(8,128)(2,1)S(1)}, u32[]{:S(2)}, u32[]{:S(2)}) %collective-permute-start) | collective-permute-done | bytes 98336 | tf_op jit(solution)/shard_map/while/body/eval_jaxpr/ppermute | solution.py:10
  104.4 1.9 collective-permute-start
  106.3 6.2 %collective-permute-done = bf16[3,128,128]{2,1,0:T(8,128)(2,1)S(1)} collective-permute-done((bf16[3,128,128]{2,1,0:T(8,128)(2,1)S(1)}, bf16[3,128,128]{2,1,0:T(8,128)(2,1)S(1)}, u32[]{:S(2)}, u32[]{:S(2)}) %collective-permute-start) | collective-permute-done | bytes 98336 | tf_op jit(solution)/shard_map/while/body/eval_jaxpr/ppermute | solution.py:10
  112.5 1.9 collective-permute-start
  114.5 6.1 %collective-permute-done = bf16[3,128,128]{2,1,0:T(8,128)(2,1)S(1)} collective-permute-done((bf16[3,128,128]{2,1,0:T(8,128)(2,1)S(1)}, bf16[3,128,128]{2,1,0:T(8,128)(2,1)S(1)}, u32[]{:S(2)}, u32[]{:S(2)}) %collective-permute-start) | collective-permute-done | bytes 98336 | tf_op jit(solution)/shard_map/while/body/eval_jaxpr/ppermute | solution.py:10
  120.6 1.9 collective-permute-start
  122.6 6.1 %collective-permute-done = bf16[3,128,128]{2,1,0:T(8,128)(2,1)S(1)} collective-permute-done((bf16[3,128,128]{2,1,0:T(8,128)(2,1)S(1)}, bf16[3,128,128]{2,1,0:T(8,128)(2,1)S(1)}, u32[]{:S(2)}, u32[]{:S(2)}) %collective-permute-start) | collective-permute-done | bytes 98336 | tf_op jit(solution)/shard_map/while/body/eval_jaxpr/ppermute | solution.py:10
  128.7 1.9 collective-permute-start
  130.7 6.1 %collective-permute-done = bf16[3,128,128]{2,1,0:T(8,128)(2,1)S(1)} collective-permute-done((bf16[3,128,128]{2,1,0:T(8,128)(2,1)S(1)}, bf16[3,128,128]{2,1,0:T(8,128)(2,1)S(1)}, u32[]{:S(2)}, u32[]{:S(2)}) %collective-permute-start) | collective-permute-done | bytes 98336 | tf_op jit(solution)/shard_map/while/body/eval_jaxpr/ppermute | solution.py:10
  136.8 1.9 collective-permute-start
  138.8 6.2 %collective-permute-done = bf16[3,128,128]{2,1,0:T(8,128)(2,1)S(1)} collective-permute-done((bf16[3,128,128]{2,1,0:T(8,128)(2,1)S(1)}, bf16[3,128,128]{2,1,0:T(8,128)(2,1)S(1)}, u32[]{:S(2)}, u32[]{:S(2)}) %collective-permute-start) | collective-permute-done | bytes 98336 | tf_op jit(solution)/shard_map/while/body/eval_jaxpr/ppermute | solution.py:10
  145.0 1.9 collective-permute-start
  146.9 6.1 %collective-permute-done = bf16[3,128,128]{2,1,0:T(8,128)(2,1)S(1)} collective-permute-done((bf16[3,128,128]{2,1,0:T(8,128)(2,1)S(1)}, bf16[3,128,128]{2,1,0:T(8,128)(2,1)S(1)}, u32[]{:S(2)}, u32[]{:S(2)}) %collective-permute-start) | collective-permute-done | bytes 98336 | tf_op jit(solution)/shard_map/while/body/eval_jaxpr/ppermute | solution.py:10
  153.1 1.7 gather_fusion.1
  154.8 0.0 copy-done
  154.8 3.6 convolution_bitcast_fusion
  158.3 1.9 copy.13
  160.3 2.0 broadcast_in_dim.42
  162.3 6.2 %scatter_fusion = f32[48,128,128]{2,1,0:T(8,128)} fusion(f32[48,128,128]{2,1,0:T(8,128)} %broadcast_in_dim.42, s32[32]{0:T(128)S(1)} %compare_select_fusion.4, f32[32,128,128]{2,1,0:T(8,128)S(1)} %copy.13), kind=kCustom, calls=%fused_computation.2 | custom fusion | flops 524288 | bytes 6291584 | tf_op jit(solution)/shard_map/scatter-add | solution.py:57
  168.5 0.0 reduce-scatter.2.cloned.1.call-update
  168.5 113.5 %all-reduce.3.cloned.1.call-done = f32[128,128]{0,1:T(8,128)} async-done(((f32[128,128]{0,1:T(8,128)}), f32[128,128]{0,1:T(8,128)}) %all-reduce.3.cloned.1.call-update) | async-done | bytes 65552 | tf_op jit(solution)/shard_map/psum | solution.py:60
  282.0 0.8 broadcast_multiply_fusion
  282.9 0.7 copy.14
  283.6 103.4 %reduce-scatter.2.cloned.1.call-done = f32[3,128,128]{2,1,0:T(8,128)} async-done(((f32[48,128,128]{2,1,0:T(8,128)}), f32[3,128,128]{2,1,0:T(8,128)}) %reduce-scatter.2.cloned.1.call-update) | async-done | bytes 196624 | tf_op jit(solution)/shard_map/reduce_scatter | solution.py:59
  387.0 1.6 convert_element_type.10
  (34 shorter events, 0.4 us)
Async XLA Ops:
  8.0 146.8 %copy-start = (bf16[32,128,128]{2,1,0:T(8,128)(2,1)S(1)}, bf16[32,128,128]{2,1,0:T(8,128)(2,1)}, u32[]{:S(2)}) copy-start(bf16[32,128,128]{2,1,0:T(8,128)(2,1)} %param.14) | copy-start | bytes 3145732
  8.0 274.0 %all-reduce.3.cloned.1.call-start = ((), (), s32[]{:S(2)}) async-start(), calls=%async_computation.2 | async-start | bytes 131072 | tf_op jit(solution)/shard_map/psum | solution.py:60
  12.8 374.2 %reduce-scatter.2.cloned.1.call-start = ((), (), s32[]{:S(2)}) async-start(), calls=%async_computation.1 | async-start | bytes 3342336 | tf_op jit(solution)/shard_map/reduce_scatter | solution.py:59
  14.0 11.3 %collective-permute-start.1 = (bf16[3,128,128]{2,1,0:T(8,128)(2,1)S(1)}, bf16[3,128,128]{2,1,0:T(8,128)(2,1)S(1)}, u32[]{:S(2)}, u32[]{:S(2)}) collective-permute-start(bf16[3,128,128]{2,1,0:T(8,128)(2,1)S(1)} %bitcast.18), channel_id=1, source_target_pairs={{0,384},{16,400},{32,416},{48,432},{64,448},{80,464},{96,480},{112... | collective-permute-start | bytes 294920 | tf_op jit(solution)/shard_map/ppermute | solution.py:10
  25.7 5.7 %collective-permute-start = (bf16[3,128,128]{2,1,0:T(8,128)(2,1)S(1)}, bf16[3,128,128]{2,1,0:T(8,128)(2,1)S(1)}, u32[]{:S(2)}, u32[]{:S(2)}) collective-permute-start(bf16[3,128,128]{2,1,0:T(8,128)(2,1)S(1)} %get-tuple-element.107), channel_id=1, source_target_pairs={{0,16},{16,32},{32,48},{48,64},{64,80},{80,96},{96,112},{112,128},... | collective-permute-start | bytes 294920 | tf_op jit(solution)/shard_map/while/body/eval_jaxpr/ppermute | solution.py:10
  31.4 8.0 %collective-permute-start = (bf16[3,128,128]{2,1,0:T(8,128)(2,1)S(1)}, bf16[3,128,128]{2,1,0:T(8,128)(2,1)S(1)}, u32[]{:S(2)}, u32[]{:S(2)}) collective-permute-start(bf16[3,128,128]{2,1,0:T(8,128)(2,1)S(1)} %get-tuple-element.107), channel_id=1, source_target_pairs={{0,16},{16,32},{32,48},{48,64},{64,80},{80,96},{96,112},{112,128},... | collective-permute-start | bytes 294920 | tf_op jit(solution)/shard_map/while/body/eval_jaxpr/ppermute | solution.py:10
  39.5 8.1 %collective-permute-start = (bf16[3,128,128]{2,1,0:T(8,128)(2,1)S(1)}, bf16[3,128,128]{2,1,0:T(8,128)(2,1)S(1)}, u32[]{:S(2)}, u32[]{:S(2)}) collective-permute-start(bf16[3,128,128]{2,1,0:T(8,128)(2,1)S(1)} %get-tuple-element.107), channel_id=1, source_target_pairs={{0,16},{16,32},{32,48},{48,64},{64,80},{80,96},{96,112},{112,128},... | collective-permute-start | bytes 294920 | tf_op jit(solution)/shard_map/while/body/eval_jaxpr/ppermute | solution.py:10
  47.6 8.1 %collective-permute-start = (bf16[3,128,128]{2,1,0:T(8,128)(2,1)S(1)}, bf16[3,128,128]{2,1,0:T(8,128)(2,1)S(1)}, u32[]{:S(2)}, u32[]{:S(2)}) collective-permute-start(bf16[3,128,128]{2,1,0:T(8,128)(2,1)S(1)} %get-tuple-element.107), channel_id=1, source_target_pairs={{0,16},{16,32},{32,48},{48,64},{64,80},{80,96},{96,112},{112,128},... | collective-permute-start | bytes 294920 | tf_op jit(solution)/shard_map/while/body/eval_jaxpr/ppermute | solution.py:10
  55.7 8.1 %collective-permute-start = (bf16[3,128,128]{2,1,0:T(8,128)(2,1)S(1)}, bf16[3,128,128]{2,1,0:T(8,128)(2,1)S(1)}, u32[]{:S(2)}, u32[]{:S(2)}) collective-permute-start(bf16[3,128,128]{2,1,0:T(8,128)(2,1)S(1)} %get-tuple-element.107), channel_id=1, source_target_pairs={{0,16},{16,32},{32,48},{48,64},{64,80},{80,96},{96,112},{112,128},... | collective-permute-start | bytes 294920 | tf_op jit(solution)/shard_map/while/body/eval_jaxpr/ppermute | solution.py:10
  63.9 8.1 %collective-permute-start = (bf16[3,128,128]{2,1,0:T(8,128)(2,1)S(1)}, bf16[3,128,128]{2,1,0:T(8,128)(2,1)S(1)}, u32[]{:S(2)}, u32[]{:S(2)}) collective-permute-start(bf16[3,128,128]{2,1,0:T(8,128)(2,1)S(1)} %get-tuple-element.107), channel_id=1, source_target_pairs={{0,16},{16,32},{32,48},{48,64},{64,80},{80,96},{96,112},{112,128},... | collective-permute-start | bytes 294920 | tf_op jit(solution)/shard_map/while/body/eval_jaxpr/ppermute | solution.py:10
  72.0 8.1 %collective-permute-start = (bf16[3,128,128]{2,1,0:T(8,128)(2,1)S(1)}, bf16[3,128,128]{2,1,0:T(8,128)(2,1)S(1)}, u32[]{:S(2)}, u32[]{:S(2)}) collective-permute-start(bf16[3,128,128]{2,1,0:T(8,128)(2,1)S(1)} %get-tuple-element.107), channel_id=1, source_target_pairs={{0,16},{16,32},{32,48},{48,64},{64,80},{80,96},{96,112},{112,128},... | collective-permute-start | bytes 294920 | tf_op jit(solution)/shard_map/while/body/eval_jaxpr/ppermute | solution.py:10
  80.1 8.0 %collective-permute-start = (bf16[3,128,128]{2,1,0:T(8,128)(2,1)S(1)}, bf16[3,128,128]{2,1,0:T(8,128)(2,1)S(1)}, u32[]{:S(2)}, u32[]{:S(2)}) collective-permute-start(bf16[3,128,128]{2,1,0:T(8,128)(2,1)S(1)} %get-tuple-element.107), channel_id=1, source_target_pairs={{0,16},{16,32},{32,48},{48,64},{64,80},{80,96},{96,112},{112,128},... | collective-permute-start | bytes 294920 | tf_op jit(solution)/shard_map/while/body/eval_jaxpr/ppermute | solution.py:10
  88.2 8.0 %collective-permute-start = (bf16[3,128,128]{2,1,0:T(8,128)(2,1)S(1)}, bf16[3,128,128]{2,1,0:T(8,128)(2,1)S(1)}, u32[]{:S(2)}, u32[]{:S(2)}) collective-permute-start(bf16[3,128,128]{2,1,0:T(8,128)(2,1)S(1)} %get-tuple-element.107), channel_id=1, source_target_pairs={{0,16},{16,32},{32,48},{48,64},{64,80},{80,96},{96,112},{112,128},... | collective-permute-start | bytes 294920 | tf_op jit(solution)/shard_map/while/body/eval_jaxpr/ppermute | solution.py:10
  96.3 8.1 %collective-permute-start = (bf16[3,128,128]{2,1,0:T(8,128)(2,1)S(1)}, bf16[3,128,128]{2,1,0:T(8,128)(2,1)S(1)}, u32[]{:S(2)}, u32[]{:S(2)}) collective-permute-start(bf16[3,128,128]{2,1,0:T(8,128)(2,1)S(1)} %get-tuple-element.107), channel_id=1, source_target_pairs={{0,16},{16,32},{32,48},{48,64},{64,80},{80,96},{96,112},{112,128},... | collective-permute-start | bytes 294920 | tf_op jit(solution)/shard_map/while/body/eval_jaxpr/ppermute | solution.py:10
  104.4 8.1 %collective-permute-start = (bf16[3,128,128]{2,1,0:T(8,128)(2,1)S(1)}, bf16[3,128,128]{2,1,0:T(8,128)(2,1)S(1)}, u32[]{:S(2)}, u32[]{:S(2)}) collective-permute-start(bf16[3,128,128]{2,1,0:T(8,128)(2,1)S(1)} %get-tuple-element.107), channel_id=1, source_target_pairs={{0,16},{16,32},{32,48},{48,64},{64,80},{80,96},{96,112},{112,128},... | collective-permute-start | bytes 294920 | tf_op jit(solution)/shard_map/while/body/eval_jaxpr/ppermute | solution.py:10
  112.5 8.1 %collective-permute-start = (bf16[3,128,128]{2,1,0:T(8,128)(2,1)S(1)}, bf16[3,128,128]{2,1,0:T(8,128)(2,1)S(1)}, u32[]{:S(2)}, u32[]{:S(2)}) collective-permute-start(bf16[3,128,128]{2,1,0:T(8,128)(2,1)S(1)} %get-tuple-element.107), channel_id=1, source_target_pairs={{0,16},{16,32},{32,48},{48,64},{64,80},{80,96},{96,112},{112,128},... | collective-permute-start | bytes 294920 | tf_op jit(solution)/shard_map/while/body/eval_jaxpr/ppermute | solution.py:10
  120.6 8.0 %collective-permute-start = (bf16[3,128,128]{2,1,0:T(8,128)(2,1)S(1)}, bf16[3,128,128]{2,1,0:T(8,128)(2,1)S(1)}, u32[]{:S(2)}, u32[]{:S(2)}) collective-permute-start(bf16[3,128,128]{2,1,0:T(8,128)(2,1)S(1)} %get-tuple-element.107), channel_id=1, source_target_pairs={{0,16},{16,32},{32,48},{48,64},{64,80},{80,96},{96,112},{112,128},... | collective-permute-start | bytes 294920 | tf_op jit(solution)/shard_map/while/body/eval_jaxpr/ppermute | solution.py:10
  128.7 8.0 %collective-permute-start = (bf16[3,128,128]{2,1,0:T(8,128)(2,1)S(1)}, bf16[3,128,128]{2,1,0:T(8,128)(2,1)S(1)}, u32[]{:S(2)}, u32[]{:S(2)}) collective-permute-start(bf16[3,128,128]{2,1,0:T(8,128)(2,1)S(1)} %get-tuple-element.107), channel_id=1, source_target_pairs={{0,16},{16,32},{32,48},{48,64},{64,80},{80,96},{96,112},{112,128},... | collective-permute-start | bytes 294920 | tf_op jit(solution)/shard_map/while/body/eval_jaxpr/ppermute | solution.py:10
  136.8 8.1 %collective-permute-start = (bf16[3,128,128]{2,1,0:T(8,128)(2,1)S(1)}, bf16[3,128,128]{2,1,0:T(8,128)(2,1)S(1)}, u32[]{:S(2)}, u32[]{:S(2)}) collective-permute-start(bf16[3,128,128]{2,1,0:T(8,128)(2,1)S(1)} %get-tuple-element.107), channel_id=1, source_target_pairs={{0,16},{16,32},{32,48},{48,64},{64,80},{80,96},{96,112},{112,128},... | collective-permute-start | bytes 294920 | tf_op jit(solution)/shard_map/while/body/eval_jaxpr/ppermute | solution.py:10
  145.0 8.1 %collective-permute-start = (bf16[3,128,128]{2,1,0:T(8,128)(2,1)S(1)}, bf16[3,128,128]{2,1,0:T(8,128)(2,1)S(1)}, u32[]{:S(2)}, u32[]{:S(2)}) collective-permute-start(bf16[3,128,128]{2,1,0:T(8,128)(2,1)S(1)} %get-tuple-element.107), channel_id=1, source_target_pairs={{0,16},{16,32},{32,48},{48,64},{64,80},{80,96},{96,112},{112,128},... | collective-permute-start | bytes 294920 | tf_op jit(solution)/shard_map/while/body/eval_jaxpr/ppermute | solution.py:10
Sparse Core Ops, SparseCore 0:
  15.2 266.8 all-reduce.2
Sparse Core Ops, SparseCore 1:
  168.6 218.3 reduce-scatter.1
where the time goes:
time: 400 us; the launch traced here: 396 us
  waiting for transfers between devices  312 us (78%)
  starting transfers between devices  41.1 us (10%)
  between operations  15.5 us (4%)
  other arithmetic  10.8 us (3%)
  local copies, waits for them, and re-layouts  9.24 us (2%)
  matrix products  6.56 us (2%)
    psum x1, waiting for transfers between devices, on_device(): wgrad_total = lax.psum(weight_part, ('row', 'col'))  113 us
    reduce_scatter x1, waiting for transfers between devices, on_device(): lax.psum_scatter(partial_value, 'col', scatter_dimension=0, tiled=True)  103 us
    ppermute x17, waiting for transfers between devices, from_behind(): return lax.ppermute(value, axis, pairs)  95.3 us
    ppermute x17, starting transfers between devices, from_behind(): return lax.ppermute(value, axis, pairs)  41 us
  transfers between devices with their start and end apart: 19, of which 19 were waited for; matrix products, arithmetic and copies ran while one was open for 5% of the time, Pallas kernels for 0%

commit v1 on v0

v1 whole, which is shorter than its diff:
```python
import functools

import jax
import jax.numpy as jnp
from jax import lax
from jax.experimental import pallas as pl
from jax.experimental.pallas import tpu as pltpu
from jax.sharding import PartitionSpec as P

BF = jnp.bfloat16
F32 = jnp.float32
SIDE = 128
PLANE = 4


def dot(a, b, contract):
    return lax.dot_general(a, b, ((contract[:1], contract[1:]), ((), ())), preferred_element_type=F32)


def adjoint_kernel(base_ref, order_ref, cot_ref, pre_ref, agg_ref, w_ref, out_ref, wpart_ref):
    rows = cot_ref.shape[0]
    cot = cot_ref[...]
    row_id = lax.broadcasted_iota(jnp.int32, (rows, SIDE), 0)
    base = base_ref[0]
    total = jnp.zeros(wpart_ref.shape, F32)
    for b in range(rows // SIDE):
        span = slice(b * SIDE, (b + 1) * SIDE)
        local = order_ref[b : b + 1, :] - base
        pick = jnp.where(row_id == local, 1.0, 0.0).astype(BF)
        grad_rows = dot(pick, cot, (0, 0))
        grad_pre = jnp.where(pre_ref[span, :].astype(F32) > 0, grad_rows, 0.0).astype(BF)
        total += dot(agg_ref[span, :], grad_pre, (0, 0))
        out_ref[span, :] = dot(grad_pre, w_ref[...], (1, 1)).astype(BF)
    wpart_ref[...] = total


def tile_kernel(src_ref, dst_ref, tiles_ref, blocks_ref, wsum_ref, out_ref, acc_ref):
    cols, rows, _ = out_ref.shape
    share = wsum_ref.shape[0]
    blocks = (rows - 2 * share) // SIDE
    acc_ref[...] = jnp.zeros_like(acc_ref)

    def one(t, carry):
        at = pl.multiple_of(src_ref[t] * SIDE, SIDE)
        to = dst_ref[t]
        acc_ref[to] += dot(tiles_ref[t], blocks_ref[pl.ds(at, SIDE), :], (1, 0))
        return carry

    lax.fori_loop(0, tiles_ref.shape[0], one, 0, unroll=8)
    high = wsum_ref[...].astype(BF)
    low = (wsum_ref[...] - high.astype(F32)).astype(BF)
    both = jnp.concatenate([high, low], axis=0)
    for c in range(cols):
        for b in range(blocks):
            out_ref[c, b * SIDE : (b + 1) * SIDE, :] = acc_ref[c * blocks + b].astype(BF)
        out_ref[c, blocks * SIDE :, :] = both


def finish_kernel(scale, got_ref, out_ref, wgrad_ref):
    cols, rows, _ = got_ref.shape
    share = wgrad_ref.shape[0] // cols
    nodes = rows - 2 * share
    total = got_ref[0, :nodes, :].astype(F32)
    for c in range(1, cols):
        total += got_ref[c, :nodes, :].astype(F32)
    out_ref[...] = total.astype(BF)
    for c in range(cols):
        pair = got_ref[c, nodes:, :].astype(F32)
        wgrad_ref[c * share : (c + 1) * share, :] = (pair[:share] + pair[share:]) * scale


def vmem():
    return pl.BlockSpec(memory_space=pltpu.VMEM)


def smem():
    return pl.BlockSpec(memory_space=pltpu.SMEM)


def on_device(cotangent, pre_act, aggregated, weight, tile_values, tile_in, tile_out, order):
    row_count = lax.axis_size("row")
    col_count = lax.axis_size("col")
    row_pos = lax.axis_index("row")
    col_pos = lax.axis_index("col")
    nodes, feat = cotangent.shape
    blocks_dev = nodes // SIDE
    planes = row_count // PLANE
    params = pltpu.CompilerParams(vmem_limit_bytes=24 << 20)

    base = ((row_pos * col_count + col_pos) * nodes).astype(jnp.int32).reshape(1)
    adjoint, wpart = pl.pallas_call(
        adjoint_kernel,
        out_shape=(jax.ShapeDtypeStruct((nodes, feat), BF), jax.ShapeDtypeStruct((feat, feat), F32)),
        in_specs=[smem()] + [vmem()] * 5,
        out_specs=(vmem(), vmem()),
        compiler_params=params,
        name="adjoint",
    )(base, order.reshape(blocks_dev, SIDE), cotangent, pre_act, aggregated, weight)

    def swap(value, bit):
        return lax.ppermute(value, "row", [(i, i ^ bit) for i in range(row_count)])

    def to_plane(value, steps):
        pairs = [(i, (i + PLANE * (steps if i % 2 == 0 else -steps)) % row_count) for i in range(row_count)]
        return lax.ppermute(value, "row", pairs)

    chip = jnp.concatenate([adjoint, swap(adjoint, 1)])
    near = to_plane(chip, 1)
    far = to_plane(chip, 2)
    mine = jnp.concatenate([near, far])
    side = swap(jnp.concatenate([adjoint, mine]), 2)
    half = jnp.concatenate([mine, side])
    other = swap(half, 1)
    sources = jnp.concatenate([chip, half, other])

    share = feat // col_count
    chunk = lax.all_to_all(wpart.reshape(col_count, share, feat), "col", 0, 0).sum(0)
    wsum = lax.all_to_all(jnp.broadcast_to(chunk, (row_count, share, feat)), "row", 0, 0).sum(0)

    source_device = tile_in // blocks_dev
    group = source_device // col_count
    local = tile_in % blocks_dev
    plane_gap = (group // PLANE - row_pos // PLANE) % planes
    other_chip = ((group // 2) ^ (row_pos // 2)) & 1
    other_core = (group ^ row_pos) & 1
    core = row_pos & 1
    below = plane_gap > planes // 2
    steps = jnp.where(below, planes - plane_gap, plane_gap)
    holder = jnp.where(below, 0, 1)
    from_core = group & 1
    sent_by_other = from_core ^ holder
    in_half = jnp.where(
        other_chip == 0,
        (steps - 1) * 2 + sent_by_other,
        4 + jnp.where(plane_gap == 0, 0, 1 + (steps - 1) * 2 + sent_by_other),
    )
    half_slots = 9
    holder = jnp.where(plane_gap == 0, from_core, holder)
    slot = 2 + in_half + jnp.where(holder == core, 0, half_slots)
    slot = jnp.where((plane_gap == 0) & (other_chip == 0), other_core, slot)
    src_index = slot * blocks_dev + local
    dst_index = tile_out - row_pos * col_count * blocks_dev

    rows_out = nodes + 2 * share
    tiles = tile_values.shape[0]
    sends = pl.pallas_call(
        tile_kernel,
        out_shape=jax.ShapeDtypeStruct((col_count, rows_out, feat), BF),
        in_specs=[smem(), smem(), vmem(), vmem(), vmem()],
        out_specs=vmem(),
        scratch_shapes=[pltpu.VMEM((col_count * blocks_dev, SIDE, feat), F32)],
        compiler_params=params,
        cost_estimate=pl.CostEstimate(
            flops=2 * tiles * SIDE * SIDE * feat, bytes_accessed=6 << 20, transcendentals=0
        ),
        name="tiles",
    )(src_index, dst_index, tile_values, sources, wsum)

    got = lax.all_to_all(sends, "col", 0, 0)
    scale = 1.0 / float(nodes * row_count * col_count) ** 0.5
    node_grad, weight_grad = pl.pallas_call(
        functools.partial(finish_kernel, scale),
        out_shape=(jax.ShapeDtypeStruct((nodes, feat), BF), jax.ShapeDtypeStruct((feat, feat), F32)),
        in_specs=[vmem()],
        out_specs=(vmem(), vmem()),
        compiler_params=params,
        name="finish",
    )(got)
    return (node_grad, weight_grad)


def solution(mesh):
    split = P(("row", "col"))
    return jax.shard_map(
        on_device,
        mesh=mesh,
        in_specs=(split, split, split, P(), split, split, split, split),
        out_specs=(split, P()),
        check_vma=False,
    )
```

time: 400 us -> 131 us (0.33)
  waiting for transfers between devices: 312 us -> 32.8 us
  blocking collectives: 0 us -> 43.9 us
  between operations: 15.5 us -> 0.8 us
  other arithmetic: 10.8 us -> 2.02 us
  matrix products: 6.56 us -> 0 us
  Pallas kernels: 0 us -> 4.01 us
    psum x1 -> x0, waiting for transfers between devices: 113 us -> none  [on_device(): wgrad_total = lax.psum(weight_part, ('row', 'col'))]
    reduce_scatter x1 -> x0, waiting for transfers between devices: 103 us -> none  [on_device(): lax.psum_scatter(partial_value, 'col', scatter_dimension=0, tiled=True)]
    ppermute x17 -> x5, waiting for transfers between devices: 95.3 us -> 16.5 us  [the longest x3 10.7 us: swap(): return lax.ppermute(value, 'row', [(i, i ^ bit) for i in range(row_count)])]
    all_to_all x0 -> x1, blocking collectives: none -> 43.9 us  [on_device(): got = lax.all_to_all(sends, 'col', 0, 0)]
    ppermute x17 -> x5, starting transfers between devices: 41 us -> 20.4 us  [the longest x3 16.5 us: swap(): return lax.ppermute(value, 'row', [(i, i ^ bit) for i in range(row_count)])]
    all_to_all x0 -> x2, starting transfers between devices: none -> 17.3 us  [the longest x1 10.3 us: on_device(): lax.all_to_all(wpart.reshape(col_count, share, feat), 'col', 0, 0).sum(0)]
    all_to_all x0 -> x2, waiting for transfers between devices: none -> 16.3 us  [the longest x1 8.96 us: on_device(): lax.all_to_all(wpart.reshape(col_count, share, feat), 'col', 0, 0).sum(0)]
    dot_general x3 -> x0, matrix products: 6.56 us -> none  [the longest x1 3.56 us: on_device(): jnp.einsum('tij,tjf->tif', tile_values, picked, preferred_element_type=jn...]
  transfers between devices with their start and end apart: 19 -> 7, of which waited for: 19 -> 6; matrix products, arithmetic and copies ran while one was open for 5% -> 3% of each run, Pallas kernels for 0% -> 0%
where the time goes in v1:
time: 131 us; the launch traced here: 129 us
  blocking collectives  43.9 us (34%)
  starting transfers between devices  37.7 us (29%)
  waiting for transfers between devices  32.8 us (25%)
  local copies, waits for them, and re-layouts  8.08 us (6%)
  Pallas kernels  4.01 us (3%)
  other arithmetic  2.02 us (2%)
    all_to_all x1, blocking collectives, on_device(): got = lax.all_to_all(sends, 'col', 0, 0)  43.9 us
    ppermute x3, starting transfers between devices, swap(): return lax.ppermute(value, 'row', [(i, i ^ bit) for i in range(row_count)])  16.5 us
    ppermute x3, waiting for transfers between devices, swap(): return lax.ppermute(value, 'row', [(i, i ^ bit) for i in range(row_count)])  10.7 us
    all_to_all x1, starting transfers between devices, on_device(): lax.all_to_all(wpart.reshape(col_count, share, feat), 'col', 0, 0).sum(0)  10.3 us
    all_to_all x1, waiting for transfers between devices, on_device(): lax.all_to_all(wpart.reshape(col_count, share, feat), 'col', 0, 0).sum(0)  8.96 us
    all_to_all x1, waiting for transfers between devices, on_device(): lax.all_to_all(jnp.broadcast_to(chunk, (row_count, share, feat)), 'row',...  7.32 us
    all_to_all x1, starting transfers between devices, on_device(): lax.all_to_all(jnp.broadcast_to(chunk, (row_count, share, feat)), 'row',...  7.02 us
    unnamed x24, local copies, waits for them, and re-layouts  6.11 us
  transfers between devices with their start and end apart: 7, of which 6 were waited for; matrix products, arithmetic and copies ran while one was open for 3% of the time, Pallas kernels for 0%

profile of v1, /device:TPU:1, one launch (start us, length us, event | category | flops | bytes accessed | tf_op | source)
XLA Modules:
  0.0 129.3 jit_solution(6678965822158421220)
XLA Ops:
  0.6 0.0 copy-start.1
  0.6 0.9 copy-done.1
  1.5 0.0 copy-start.2
  1.5 0.9 copy-done.2
  2.4 0.0 copy-start.3
  2.4 0.9 copy-done.3
  3.3 0.0 copy-start.4
  3.3 0.8 copy-done.4
  4.1 0.0 copy-start.5
  4.1 0.7 copy-done.5
  4.8 1.3 %adjoint.1 = (bf16[384,128]{1,0:T(8,128)(2,1)S(1)}, f32[128,128]{1,0:T(8,128)}) custom-call(s32[1]{0:T(128)} %bitcast.base_ref, s32[3,128]{1,0:T(4,128)S(1)} %bitcast.3, bf16[384,128]{1,0:T(8,128)(2,1)S(1)} %copy-done.1, bf16[384,128]{1,0:T(8,128)(2,1)S(1)} %copy-done.2, bf16[384,128]{1,0:T(8,128)(2,1)S(1)} %copy-done.3, bf16[128,128]{1,0:T(8,128)(2,1)S(1)} %copy-done.4), custom_call_target="tpu_custom_call" | custom-call | tf_op jit(solution)/shard_map/adjoint/pallas_call | solution.py:91
  6.1 0.0 copy-start.8
  6.1 0.0 copy-start.9
  6.1 8.9 %collective-permute-start = (bf16[384,128]{1,0:T(8,128)(2,1)S(1)}, bf16[384,128]{1,0:T(8,128)(2,1)S(1)}, u32[]{:S(2)}, u32[]{:S(2)}) collective-permute-start(bf16[384,128]{1,0:T(8,128)(2,1)S(1)} %get-tuple-element.4), channel_id=1, source_target_pairs={{0,16},{16,0},{32,48},{48,32},{64,80},{80,64},{96,112},{112,96},{1... | collective-permute-start | bytes 294920 | tf_op jit(solution)/shard_map/ppermute | solution.py:101
  15.0 0.9 collective-permute-done
  15.9 1.9 %collective-permute-start.2 = (bf16[768,128]{1,0:T(8,128)(2,1)S(1)}, bf16[768,128]{1,0:T(8,128)(2,1)S(1)}, u32[]{:S(2)}, u32[]{:S(2)}) collective-permute-start(bf16[768,128]{1,0:T(8,128)(2,1)S(1)} %get-tuple-element.6), channel_id=1, source_target_pairs={{0,128},{16,400},{32,160},{48,432},{64,192},{80,464},{96,224},{112... | collective-permute-start | bytes 589832 | tf_op jit(solution)/shard_map/ppermute | solution.py:105
  17.9 1.9 %collective-permute-start.1 = (bf16[768,128]{1,0:T(8,128)(2,1)S(1)}, bf16[768,128]{1,0:T(8,128)(2,1)S(1)}, u32[]{:S(2)}, u32[]{:S(2)}) collective-permute-start(bf16[768,128]{1,0:T(8,128)(2,1)S(1)} %get-tuple-element.6), channel_id=1, source_target_pairs={{0,64},{16,464},{32,96},{48,496},{64,128},{80,16},{96,160},{112,48... | collective-permute-start | bytes 589832 | tf_op jit(solution)/shard_map/ppermute | solution.py:105
  19.8 3.8 %collective-permute-done.2 = bf16[768,128]{1,0:T(8,128)(2,1)S(1)} collective-permute-done((bf16[768,128]{1,0:T(8,128)(2,1)S(1)}, bf16[768,128]{1,0:T(8,128)(2,1)S(1)}, u32[]{:S(2)}, u32[]{:S(2)}) %collective-permute-start.2) | collective-permute-done | bytes 196640 | tf_op jit(solution)/shard_map/ppermute | solution.py:105
  23.5 0.0 copy-start.6
  23.5 2.1 %collective-permute-done.1 = bf16[768,128]{1,0:T(8,128)(2,1)S(1)} collective-permute-done((bf16[768,128]{1,0:T(8,128)(2,1)S(1)}, bf16[768,128]{1,0:T(8,128)(2,1)S(1)}, u32[]{:S(2)}, u32[]{:S(2)}) %collective-permute-start.1) | collective-permute-done | bytes 196640 | tf_op jit(solution)/shard_map/ppermute | solution.py:105
  25.7 0.0 copy-start.7
  25.7 1.9 %collective-permute-start.3 = (bf16[1920,128]{1,0:T(8,128)(2,1)S(1)}, bf16[1920,128]{1,0:T(8,128)(2,1)S(1)}, u32[]{:S(2)}, u32[]{:S(2)}) collective-permute-start(bf16[1920,128]{1,0:T(8,128)(2,1)S(1)} %pad_maximum_fusion.1), channel_id=1, source_target_pairs={{0,32},{16,48},{32,0},{48,16},{64,96},{80,112},{96,64},{112,80},{1... | collective-permute-start | bytes 1474568 | tf_op jit(solution)/shard_map/ppermute | solution.py:101
  27.6 9.8 %collective-permute-done.3 = bf16[1920,128]{1,0:T(8,128)(2,1)S(1)} collective-permute-done((bf16[1920,128]{1,0:T(8,128)(2,1)S(1)}, bf16[1920,128]{1,0:T(8,128)(2,1)S(1)}, u32[]{:S(2)}, u32[]{:S(2)}) %collective-permute-start.3) | collective-permute-done | bytes 491552 | tf_op jit(solution)/shard_map/ppermute | solution.py:101
  37.4 0.0 copy-done.6
  37.4 1.0 pad_maximum_fusion
  38.4 0.0 copy-done.7
  38.4 5.7 %collective-permute-start.4 = (bf16[3456,128]{1,0:T(8,128)(2,1)}, bf16[3456,128]{1,0:T(8,128)(2,1)}, u32[]{:S(2)}, u32[]{:S(2)}) collective-permute-start(bf16[3456,128]{1,0:T(8,128)(2,1)} %pad_maximum_fusion), channel_id=1, source_target_pairs={{0,16},{16,0},{32,48},{48,32},{64,80},{80,64},{96,112},{112,96},{1... | collective-permute-start | bytes 2654216 | tf_op jit(solution)/shard_map/ppermute | solution.py:101
  44.1 10.3 %all-to-all-start = ((f32[16,8,128]{2,1,0:T(8,128)}), f32[16,8,128]{2,1,0:T(8,128)S(1)}, u32[]{:S(2)}, u32[]{:S(2)}) async-start(f32[16,8,128]{2,1,0:T(8,128)} %bitcast.2), calls=%async_computation | async-start | bytes 131072 | tf_op jit(solution)/shard_map/all_to_all | solution.py:117
  54.4 9.0 %all-to-all-done = f32[16,8,128]{2,1,0:T(8,128)S(1)} async-done(((f32[16,8,128]{2,1,0:T(8,128)}), f32[16,8,128]{2,1,0:T(8,128)S(1)}, u32[]{:S(2)}, u32[]{:S(2)}) %all-to-all-start) | async-done | bytes 65568 | tf_op jit(solution)/shard_map/all_to_all | solution.py:117
  63.4 0.7 broadcast_in_dim.14
  64.0 0.0 copy-start
  64.1 7.0 %all-to-all-start.1 = ((f32[32,8,128]{2,1,0:T(8,128)}), f32[32,8,128]{2,1,0:T(8,128)}, u32[]{:S(2)}, u32[]{:S(2)}) async-start(f32[32,8,128]{2,1,0:T(8,128)} %broadcast_in_dim.14), calls=%async_computation.1 | async-start | bytes 262144 | tf_op jit(solution)/shard_map/all_to_all | solution.py:118
  71.1 0.0 copy-done.8
  71.1 0.0 copy-done.9
  71.1 0.1 fusion
  71.2 1.0 constant_dynamic-update-slice_fusion.5
  72.1 1.0 constant_dynamic-update-slice_fusion.4
  73.1 7.3 %all-to-all-done.1 = f32[32,8,128]{2,1,0:T(8,128)} async-done(((f32[32,8,128]{2,1,0:T(8,128)}), f32[32,8,128]{2,1,0:T(8,128)}, u32[]{:S(2)}, u32[]{:S(2)}) %all-to-all-start.1) | async-done | bytes 131104 | tf_op jit(solution)/shard_map/all_to_all | solution.py:118
  80.4 0.9 reduce_sum.19.wsum_ref
  81.3 0.1 constant_dynamic-update-slice_fusion.3
  81.4 0.0 collective-permute-done.4
  81.4 1.3 constant_dynamic-update-slice_fusion.2.blocks_ref
  82.7 0.0 copy-done
  82.7 1.8 %tiles.1 = bf16[16,400,128]{2,1,0:T(8,128)(2,1)S(1)} custom-call(s32[32]{0:T(128)S(1)} %get-tuple-element.10.src_ref, s32[32]{0:T(128)S(1)} %get-tuple-element.11.dst_ref, bf16[32,128,128]{2,1,0:T(8,128)(2,1)S(1)} %copy-done, bf16[7680,128]{1,0:T(8,128)(2,1)S(1)} %constant_dynamic-update-slice_fusion.2.blocks_ref, f32[8,128]{1,0:T(8,128)S(1)} %reduce_sum.19.wsum_ref), custom_call_target="tpu_custom_call" | custom-call | flops 134217728 | bytes 6291456 | tf_op jit(solution)/shard_map/tiles/pallas_call | solution.py:146
  84.6 43.9 %all_to_all.15.got_ref = bf16[16,400,128]{2,1,0:T(8,128)(2,1)S(1)} all-to-all(bf16[16,400,128]{2,1,0:T(8,128)(2,1)S(1)} %tiles.1), channel_id=1, replica_groups=mesh['row'=32,'col'=16] {'col'}, dimensions={0} | all-to-all | bytes 3276800 | tf_op jit(solution)/shard_map/all_to_all | solution.py:159
  128.4 0.9 finish.1
  (4 shorter events, 0.1 us)
Async XLA Ops:
  0.6 0.9 copy-start.1
  1.5 0.9 copy-start.2
  2.4 0.9 copy-start.3
  3.3 0.8 copy-start.4
  4.1 0.7 copy-start.5
  6.1 65.0 %copy-start.8 = (s32[32]{0:T(128)S(1)}, s32[32]{0:T(128)}, u32[]{:S(2)}) copy-start(s32[32]{0:T(128)} %param.13) | copy-start | bytes 388
  6.1 65.0 %copy-start.9 = (s32[32]{0:T(128)S(1)}, s32[32]{0:T(128)}, u32[]{:S(2)}) copy-start(s32[32]{0:T(128)} %param.14) | copy-start | bytes 388
  6.1 9.8 %collective-permute-start = (bf16[384,128]{1,0:T(8,128)(2,1)S(1)}, bf16[384,128]{1,0:T(8,128)(2,1)S(1)}, u32[]{:S(2)}, u32[]{:S(2)}) collective-permute-start(bf16[384,128]{1,0:T(8,128)(2,1)S(1)} %get-tuple-element.4), channel_id=1, source_target_pairs={{0,16},{16,0},{32,48},{48,32},{64,80},{80,64},{96,112},{112,96},{1... | collective-permute-start | bytes 294920 | tf_op jit(solution)/shard_map/ppermute | solution.py:101
  15.9 7.6 %collective-permute-start.2 = (bf16[768,128]{1,0:T(8,128)(2,1)S(1)}, bf16[768,128]{1,0:T(8,128)(2,1)S(1)}, u32[]{:S(2)}, u32[]{:S(2)}) collective-permute-start(bf16[768,128]{1,0:T(8,128)(2,1)S(1)} %get-tuple-element.6), channel_id=1, source_target_pairs={{0,128},{16,400},{32,160},{48,432},{64,192},{80,464},{96,224},{112... | collective-permute-start | bytes 589832 | tf_op jit(solution)/shard_map/ppermute | solution.py:105
  17.9 7.8 %collective-permute-start.1 = (bf16[768,128]{1,0:T(8,128)(2,1)S(1)}, bf16[768,128]{1,0:T(8,128)(2,1)S(1)}, u32[]{:S(2)}, u32[]{:S(2)}) collective-permute-start(bf16[768,128]{1,0:T(8,128)(2,1)S(1)} %get-tuple-element.6), channel_id=1, source_target_pairs={{0,64},{16,464},{32,96},{48,496},{64,128},{80,16},{96,160},{112,48... | collective-permute-start | bytes 589832 | tf_op jit(solution)/shard_map/ppermute | solution.py:105
  23.5 13.9 %copy-start.6 = (bf16[768,128]{1,0:T(8,128)(2,1)}, bf16[768,128]{1,0:T(8,128)(2,1)S(1)}, u32[]{:S(2)}) copy-start(bf16[768,128]{1,0:T(8,128)(2,1)S(1)} %collective-permute-done.2) | copy-start | bytes 589828
  25.7 12.7 %copy-start.7 = (bf16[768,128]{1,0:T(8,128)(2,1)}, bf16[768,128]{1,0:T(8,128)(2,1)S(1)}, u32[]{:S(2)}) copy-start(bf16[768,128]{1,0:T(8,128)(2,1)S(1)} %collective-permute-done.1) | copy-start | bytes 589828
  25.7 11.7 %collective-permute-start.3 = (bf16[1920,128]{1,0:T(8,128)(2,1)S(1)}, bf16[1920,128]{1,0:T(8,128)(2,1)S(1)}, u32[]{:S(2)}, u32[]{:S(2)}) collective-permute-start(bf16[1920,128]{1,0:T(8,128)(2,1)S(1)} %pad_maximum_fusion.1), channel_id=1, source_target_pairs={{0,32},{16,48},{32,0},{48,16},{64,96},{80,112},{96,64},{112,80},{1... | collective-permute-start | bytes 1474568 | tf_op jit(solution)/shard_map/ppermute | solution.py:101
  38.4 43.0 %collective-permute-start.4 = (bf16[3456,128]{1,0:T(8,128)(2,1)}, bf16[3456,128]{1,0:T(8,128)(2,1)}, u32[]{:S(2)}, u32[]{:S(2)}) collective-permute-start(bf16[3456,128]{1,0:T(8,128)(2,1)} %pad_maximum_fusion), channel_id=1, source_target_pairs={{0,16},{16,0},{32,48},{48,32},{64,80},{80,64},{96,112},{112,96},{1... | collective-permute-start | bytes 2654216 | tf_op jit(solution)/shard_map/ppermute | solution.py:101
  44.1 19.3 %all-to-all-start = ((f32[16,8,128]{2,1,0:T(8,128)}), f32[16,8,128]{2,1,0:T(8,128)S(1)}, u32[]{:S(2)}, u32[]{:S(2)}) async-start(f32[16,8,128]{2,1,0:T(8,128)} %bitcast.2), calls=%async_computation | async-start | bytes 131072 | tf_op jit(solution)/shard_map/all_to_all | solution.py:117
  64.0 18.7 %copy-start = (bf16[32,128,128]{2,1,0:T(8,128)(2,1)S(1)}, bf16[32,128,128]{2,1,0:T(8,128)(2,1)}, u32[]{:S(2)}) copy-start(bf16[32,128,128]{2,1,0:T(8,128)(2,1)} %tiles_ref.1) | copy-start | bytes 3145732
  64.1 16.3 %all-to-all-start.1 = ((f32[32,8,128]{2,1,0:T(8,128)}), f32[32,8,128]{2,1,0:T(8,128)}, u32[]{:S(2)}, u32[]{:S(2)}) async-start(f32[32,8,128]{2,1,0:T(8,128)} %broadcast_in_dim.14), calls=%async_computation.1 | async-start | bytes 262144 | tf_op jit(solution)/shard_map/all_to_all | solution.py:118

commit v2 on v1

--- a/solution.py
+++ b/solution.py
@@ -17,7 +17,14 @@
     return lax.dot_general(a, b, ((contract[:1], contract[1:]), ((), ())), preferred_element_type=F32)
 
 
-def adjoint_kernel(base_ref, order_ref, cot_ref, pre_ref, agg_ref, w_ref, out_ref, wpart_ref):
+def adjoint_kernel(base_ref, order_in, cot_in, pre_in, agg_in, w_in, out_ref, wpart_ref, order_ref, cot_ref, pre_ref, agg_ref, w_ref, sems):
+    ins = (order_in, cot_in, pre_in, w_in, agg_in)
+    held = (order_ref, cot_ref, pre_ref, w_ref, agg_ref)
+    copies = [pltpu.make_async_copy(a, b, sems.at[i]) for i, (a, b) in enumerate(zip(ins, held))]
+    for copy in copies:
+        copy.start()
+    for copy in copies:
+        copy.wait()
     rows = cot_ref.shape[0]
     cot = cot_ref[...]
     row_id = lax.broadcasted_iota(jnp.int32, (rows, SIDE), 0)
@@ -34,9 +41,13 @@
     wpart_ref[...] = total
 
 
-def tile_kernel(src_ref, dst_ref, tiles_ref, blocks_ref, wsum_ref, out_ref, acc_ref):
+def tile_kernel(src_ref, dst_ref, tiles_ref, own, beside, near, far, side, other_near, other_side, wrow_ref, out_ref, blocks_ref, acc_ref):
     cols, rows, _ = out_ref.shape
-    share = wsum_ref.shape[0]
+    share = wrow_ref.shape[1]
+    at = 0
+    for piece in (own, beside, near, far, side, other_near, other_side):
+        blocks_ref[at : at + piece.shape[0], :] = piece[...]
+        at += piece.shape[0]
     blocks = (rows - 2 * share) // SIDE
     acc_ref[...] = jnp.zeros_like(acc_ref)
 
@@ -47,8 +58,11 @@
         return carry
 
     lax.fori_loop(0, tiles_ref.shape[0], one, 0, unroll=8)
-    high = wsum_ref[...].astype(BF)
-    low = (wsum_ref[...] - high.astype(F32)).astype(BF)
+    wsum = wrow_ref[0]
+    for r in range(1, wrow_ref.shape[0]):
+        wsum += wrow_ref[r]
+    high = wsum.astype(BF)
+    low = (wsum - high.astype(F32)).astype(BF)
     both = jnp.concatenate([high, low], axis=0)
     for c in range(cols):
         for b in range(blocks):
@@ -85,15 +99,23 @@
     nodes, feat = cotangent.shape
     blocks_dev = nodes // SIDE
     planes = row_count // PLANE
-    params = pltpu.CompilerParams(vmem_limit_bytes=24 << 20)
+    params = pltpu.CompilerParams(vmem_limit_bytes=12 << 20)
 
     base = ((row_pos * col_count + col_pos) * nodes).astype(jnp.int32).reshape(1)
     adjoint, wpart = pl.pallas_call(
         adjoint_kernel,
         out_shape=(jax.ShapeDtypeStruct((nodes, feat), BF), jax.ShapeDtypeStruct((feat, feat), F32)),
-        in_specs=[smem()] + [vmem()] * 5,
+        in_specs=[smem()] + [pl.BlockSpec(memory_space=pltpu.HBM)] * 5,
         out_specs=(vmem(), vmem()),
-        compiler_params=params,
+        scratch_shapes=[
+            pltpu.VMEM((blocks_dev, SIDE), jnp.int32),
+            pltpu.VMEM((nodes, feat), BF),
+            pltpu.VMEM((nodes, feat), BF),
+            pltpu.VMEM((nodes, feat), BF),
+            pltpu.VMEM((feat, feat), BF),
+            pltpu.SemaphoreType.DMA((5,)),
+        ],
+        compiler_params=pltpu.CompilerParams(vmem_limit_bytes=60 << 20),
         name="adjoint",
     )(base, order.reshape(blocks_dev, SIDE), cotangent, pre_act, aggregated, weight)
 
@@ -104,18 +126,20 @@
         pairs = [(i, (i + PLANE * (steps if i % 2 == 0 else -steps)) % row_count) for i in range(row_count)]
         return lax.ppermute(value, "row", pairs)
 
-    chip = jnp.concatenate([adjoint, swap(adjoint, 1)])
+    share = feat // col_count
+    chunk = lax.all_to_all(wpart.reshape(col_count, share, feat), "col", 0, 0).sum(0)
+    copies = jnp.broadcast_to(chunk, (row_count, share, feat))
+
+    beside = swap(adjoint, 1)
+    chip = jnp.concatenate([adjoint, beside])
     near = to_plane(chip, 1)
     far = to_plane(chip, 2)
-    mine = jnp.concatenate([near, far])
-    side = swap(jnp.concatenate([adjoint, mine]), 2)
-    half = jnp.concatenate([mine, side])
-    other = swap(half, 1)
-    sources = jnp.concatenate([chip, half, other])
-
-    share = feat // col_count
-    chunk = lax.all_to_all(wpart.reshape(col_count, share, feat), "col", 0, 0).sum(0)
-    wsum = lax.all_to_all(jnp.broadcast_to(chunk, (row_count, share, feat)), "row", 0, 0).sum(0)
+    across, copies = lax.optimization_barrier((jnp.concatenate([adjoint, near, far]), copies))
+    side = swap(across, 2)
+    wrow = lax.all_to_all(copies, "row", 0, 0)
+    other_near = swap(jnp.concatenate([near, far]), 1)
+    side, other_near, wrow = lax.optimization_barrier((side, other_near, wrow))
+    other_side = swap(side, 1)
 
     source_device = tile_in // blocks_dev
     group = source_device // col_count
@@ -146,15 +170,18 @@
     sends = pl.pallas_call(
         tile_kernel,
         out_shape=jax.ShapeDtypeStruct((col_count, rows_out, feat), BF),
-        in_specs=[smem(), smem(), vmem(), vmem(), vmem()],
+        in_specs=[smem(), smem()] + [vmem()] * 9,
         out_specs=vmem(),
-        scratch_shapes=[pltpu.VMEM((col_count * blocks_dev, SIDE, feat), F32)],
+        scratch_shapes=[
+            pltpu.VMEM((20 * nodes, feat), BF),
+            pltpu.VMEM((col_count * blocks_dev, SIDE, feat), F32),
+        ],
         compiler_params=params,
         cost_estimate=pl.CostEstimate(
             flops=2 * tiles * SIDE * SIDE * feat, bytes_accessed=6 << 20, transcendentals=0
         ),
         name="tiles",
-    )(src_index, dst_index, tile_values, sources, wsum)
+    )(src_index, dst_index, tile_values, adjoint, beside, near, far, side, other_near, other_side, wrow)
 
     got = lax.all_to_all(sends, "col", 0, 0)
     scale = 1.0 / float(nodes * row_count * col_count) ** 0.5

time: 131 us -> 112 us (0.85)
  blocking collectives: 43.9 us -> 79.9 us
  waiting for transfers between devices: 32.8 us -> 1.62 us
  starting transfers between devices: 37.7 us -> 20.7 us
  local copies, waits for them, and re-layouts: 8.08 us -> 0.95 us
  Pallas kernels: 4.01 us -> 5.32 us
    all_to_all x0 -> x2, blocking collectives: none -> 35.6 us  [the longest x1 21.1 us: on_device(): lax.all_to_all(wpart.reshape(col_count, share, feat), 'col', 0, 0).sum(0)]
    all_to_all x2 -> x0, starting transfers between devices: 17.3 us -> none  [the longest x1 10.3 us: on_device(): lax.all_to_all(wpart.reshape(col_count, share, feat), 'col', 0, 0).sum(0)]
    all_to_all x2 -> x0, waiting for transfers between devices: 16.3 us -> none  [the longest x1 8.96 us: on_device(): lax.all_to_all(wpart.reshape(col_count, share, feat), 'col', 0, 0).sum(0)]
    ppermute x3 -> x4, waiting for transfers between devices: 10.7 us -> 1.61 us  [swap(): return lax.ppermute(value, 'row', [(i, i ^ bit) for i in range(row_count)])]
    ppermute x2, waiting for transfers between devices: 5.86 us -> 0.01 us  [to_plane(): return lax.ppermute(value, 'row', pairs)]
    unnamed x24 -> x9, local copies, waits for them, and re-layouts: 6.11 us -> 0.92 us
    ppermute x3 -> x4, starting transfers between devices: 16.5 us -> 16.9 us  [swap(): return lax.ppermute(value, 'row', [(i, i ^ bit) for i in range(row_count)])]
  transfers between devices with their start and end apart: 7 -> 6, of which waited for: 6 -> 2; matrix products, arithmetic and copies ran while one was open for 3% -> 1% of each run, Pallas kernels for 0% -> 0%
where the time goes in v2:
time: 112 us; the launch traced here: 110 us
  blocking collectives  79.9 us (71%)
  starting transfers between devices  20.7 us (18%)
  Pallas kernels  5.32 us (5%)
  waiting for transfers between devices  1.62 us (1%)
    all_to_all x1, blocking collectives, on_device(): got = lax.all_to_all(sends, 'col', 0, 0)  44.3 us
    all_to_all x1, blocking collectives, on_device(): lax.all_to_all(wpart.reshape(col_count, share, feat), 'col', 0, 0).sum(0)  21.1 us
    ppermute x4, starting transfers between devices, swap(): return lax.ppermute(value, 'row', [(i, i ^ bit) for i in range(row_count)])  16.9 us
    all_to_all x1, blocking collectives, on_device(): wrow = lax.all_to_all(copies, 'row', 0, 0)  14.5 us
    ppermute x2, starting transfers between devices, to_plane(): return lax.ppermute(value, 'row', pairs)  3.84 us
    pallas_call x1, Pallas kernels, on_device(): pl.pallas_call(adjoint_kernel, out_shape=(jax.ShapeDtypeStruct((nodes, fe...  2.47 us
  transfers between devices with their start and end apart: 6, of which 2 were waited for; matrix products, arithmetic and copies ran while one was open for 1% of the time, Pallas kernels for 0%

profile of v2, /device:TPU:1, one launch (start us, length us, event | category | flops | bytes accessed | tf_op | source)
XLA Modules:
  0.0 110.3 jit_solution(9023820667180960804)
XLA Ops:
  0.6 0.0 copy-start.3
  0.6 0.0 copy-start.2
  0.7 0.0 copy-start
  0.7 2.5 %adjoint.1 = (bf16[384,128]{1,0:T(8,128)(2,1)}, f32[128,128]{1,0:T(8,128)}) custom-call(s32[1]{0:T(128)} %bitcast.base_ref, s32[3,128]{1,0:T(4,128)} %bitcast.4, bf16[384,128]{1,0:T(8,128)(2,1)} %cot_in.1, bf16[384,128]{1,0:T(8,128)(2,1)} %pre_in.1, bf16[384,128]{1,0:T(8,128)(2,1)} %agg_in.1, bf16[128,128]{1,0:T(8,128)(2,1)} %w_in.1), custom_call_target="tpu_custom_call" | custom-call | tf_op jit(solution)/shard_map/adjoint/pallas_call | solution.py:105
  3.1 0.0 copy-start.1
  3.2 8.9 %collective-permute-start = (bf16[384,128]{1,0:T(8,128)(2,1)}, bf16[384,128]{1,0:T(8,128)(2,1)S(1)}, u32[]{:S(2)}, u32[]{:S(2)}) collective-permute-start(bf16[384,128]{1,0:T(8,128)(2,1)} %get-tuple-element.9.own), channel_id=1, source_target_pairs={{0,16},{16,0},{32,48},{48,32},{64,80},{80,64},{96,112},{112,96},{1... | collective-permute-start | bytes 294920 | tf_op jit(solution)/shard_map/ppermute | solution.py:123
  12.1 0.9 constant_dynamic-update-slice_fusion.1
  13.0 0.2 collective-permute-done.beside
  13.2 1.9 %collective-permute-start.2 = (bf16[768,128]{1,0:T(8,128)(2,1)S(1)}, bf16[768,128]{1,0:T(8,128)(2,1)S(1)}, u32[]{:S(2)}, u32[]{:S(2)}) collective-permute-start(bf16[768,128]{1,0:T(8,128)(2,1)S(1)} %constant_dynamic-update-slice_fusion), channel_id=1, source_target_pairs={{0,128},{16,400},{32,160},{48,432},{64,192},{80,464},{96,224},{112... | collective-permute-start | bytes 589832 | tf_op jit(solution)/shard_map/ppermute | solution.py:127
  15.2 1.9 %collective-permute-start.1 = (bf16[768,128]{1,0:T(8,128)(2,1)S(1)}, bf16[768,128]{1,0:T(8,128)(2,1)S(1)}, u32[]{:S(2)}, u32[]{:S(2)}) collective-permute-start(bf16[768,128]{1,0:T(8,128)(2,1)S(1)} %constant_dynamic-update-slice_fusion), channel_id=1, source_target_pairs={{0,64},{16,464},{32,96},{48,496},{64,128},{80,16},{96,160},{112,48... | collective-permute-start | bytes 589832 | tf_op jit(solution)/shard_map/ppermute | solution.py:127
  17.1 21.1 %all_to_all.15 = f32[16,8,128]{2,1,0:T(8,128)S(1)} all-to-all(f32[16,8,128]{2,1,0:T(8,128)} %bitcast.3), channel_id=1, replica_groups=mesh['row'=32,'col'=16] {'col'}, dimensions={0} | all-to-all | bytes 131072 | tf_op jit(solution)/shard_map/all_to_all | solution.py:130
  38.2 0.0 collective-permute-done.2.far
  38.3 0.0 collective-permute-done.1.near
  38.3 0.9 pad_maximum_fusion
  39.2 2.2 %collective-permute-start.3 = (bf16[1920,128]{1,0:T(8,128)(2,1)S(1)}, bf16[1920,128]{1,0:T(8,128)(2,1)S(1)}, u32[]{:S(2)}, u32[]{:S(2)}) collective-permute-start(bf16[1920,128]{1,0:T(8,128)(2,1)S(1)} %pad_maximum_fusion), channel_id=1, source_target_pairs={{0,32},{16,48},{32,0},{48,16},{64,96},{80,112},{96,64},{112,80},{1... | collective-permute-start | bytes 1474568 | tf_op jit(solution)/shard_map/ppermute | solution.py:123
  41.5 3.3 %collective-permute-start.4 = (bf16[1536,128]{1,0:T(8,128)(2,1)S(1)}, bf16[1536,128]{1,0:T(8,128)(2,1)S(1)}, u32[]{:S(2)}, u32[]{:S(2)}) collective-permute-start(bf16[1536,128]{1,0:T(8,128)(2,1)S(1)} %pad_maximum_fusion.1), channel_id=1, source_target_pairs={{0,16},{16,0},{32,48},{48,32},{64,80},{80,64},{96,112},{112,96},{1... | collective-permute-start | bytes 1179656 | tf_op jit(solution)/shard_map/ppermute | solution.py:123
  44.7 14.5 %all_to_all.16.wrow_ref = f32[32,8,128]{2,1,0:T(8,128)S(1)} all-to-all(f32[32,8,128]{2,1,0:T(8,128)S(1)} %broadcast_in_dim.14), channel_id=1, replica_groups=mesh['row'=32,'col'=16] {'row'}, dimensions={0} | all-to-all | bytes 262144 | tf_op jit(solution)/shard_map/all_to_all | solution.py:139
  59.2 0.0 collective-permute-done.4.other_near
  59.2 0.0 collective-permute-done.3.side
  59.3 2.5 %collective-permute-start.5 = (bf16[1920,128]{1,0:T(8,128)(2,1)S(1)}, bf16[1920,128]{1,0:T(8,128)(2,1)S(1)}, u32[]{:S(2)}, u32[]{:S(2)}) collective-permute-start(bf16[1920,128]{1,0:T(8,128)(2,1)S(1)} %collective-permute-done.3.side), channel_id=1, source_target_pairs={{0,16},{16,0},{32,48},{48,32},{64,80},{80,64},{96,112},{112,96},{1... | collective-permute-start | bytes 1474568 | tf_op jit(solution)/shard_map/ppermute | solution.py:123
  61.8 0.0 copy-done.3
  61.8 0.0 copy-done.2
  61.8 0.1 fusion
  61.8 1.4 %collective-permute-done.5.other_side = bf16[1920,128]{1,0:T(8,128)(2,1)S(1)} collective-permute-done((bf16[1920,128]{1,0:T(8,128)(2,1)S(1)}, bf16[1920,128]{1,0:T(8,128)(2,1)S(1)}, u32[]{:S(2)}, u32[]{:S(2)}) %collective-permute-start.5) | collective-permute-done | bytes 491552 | tf_op jit(solution)/shard_map/ppermute | solution.py:123
  63.2 0.0 copy-done
  63.2 0.0 copy-done.1
  63.2 2.0 %tiles.1 = bf16[16,400,128]{2,1,0:T(8,128)(2,1)S(1)} custom-call(s32[32]{0:T(128)S(1)} %get-tuple-element.16.src_ref, s32[32]{0:T(128)S(1)} %get-tuple-element.17.dst_ref, bf16[32,128,128]{2,1,0:T(8,128)(2,1)S(1)} %copy-done, bf16[384,128]{1,0:T(8,128)(2,1)S(1)} %copy-done.1, bf16[384,128]{1,0:T(8,128)(2,1)S(1)} %collective-permute-done.beside, ...), custom_call_target="tpu_custom_call" | custom-call | flops 134217728 | bytes 6291456 | tf_op jit(solution)/shard_map/tiles/pallas_call | solution.py:170
  65.2 44.3 %all_to_all.17.got_ref = bf16[16,400,128]{2,1,0:T(8,128)(2,1)S(1)} all-to-all(bf16[16,400,128]{2,1,0:T(8,128)(2,1)S(1)} %tiles.1), channel_id=1, replica_groups=mesh['row'=32,'col'=16] {'col'}, dimensions={0} | all-to-all | bytes 3276800 | tf_op jit(solution)/shard_map/all_to_all | solution.py:186
  109.5 0.9 finish.1
  (4 shorter events, 0.1 us)
Async XLA Ops:
  0.6 61.1 %copy-start.3 = (s32[32]{0:T(128)S(1)}, s32[32]{0:T(128)}, u32[]{:S(2)}) copy-start(s32[32]{0:T(128)} %param.14) | copy-start | bytes 388
  0.6 61.1 %copy-start.2 = (s32[32]{0:T(128)S(1)}, s32[32]{0:T(128)}, u32[]{:S(2)}) copy-start(s32[32]{0:T(128)} %param.13) | copy-start | bytes 388
  0.7 62.6 %copy-start = (bf16[32,128,128]{2,1,0:T(8,128)(2,1)S(1)}, bf16[32,128,128]{2,1,0:T(8,128)(2,1)}, u32[]{:S(2)}) copy-start(bf16[32,128,128]{2,1,0:T(8,128)(2,1)} %tiles_ref.1) | copy-start | bytes 3145732
  3.1 60.1 %copy-start.1 = (bf16[384,128]{1,0:T(8,128)(2,1)S(1)}, bf16[384,128]{1,0:T(8,128)(2,1)}, u32[]{:S(2)}) copy-start(bf16[384,128]{1,0:T(8,128)(2,1)} %get-tuple-element.9.own) | copy-start | bytes 294916
  3.2 10.1 %collective-permute-start = (bf16[384,128]{1,0:T(8,128)(2,1)}, bf16[384,128]{1,0:T(8,128)(2,1)S(1)}, u32[]{:S(2)}, u32[]{:S(2)}) collective-permute-start(bf16[384,128]{1,0:T(8,128)(2,1)} %get-tuple-element.9.own), channel_id=1, source_target_pairs={{0,16},{16,0},{32,48},{48,32},{64,80},{80,64},{96,112},{112,96},{1... | collective-permute-start | bytes 294920 | tf_op jit(solution)/shard_map/ppermute | solution.py:123
  13.2 25.0 %collective-permute-start.2 = (bf16[768,128]{1,0:T(8,128)(2,1)S(1)}, bf16[768,128]{1,0:T(8,128)(2,1)S(1)}, u32[]{:S(2)}, u32[]{:S(2)}) collective-permute-start(bf16[768,128]{1,0:T(8,128)(2,1)S(1)} %constant_dynamic-update-slice_fusion), channel_id=1, source_target_pairs={{0,128},{16,400},{32,160},{48,432},{64,192},{80,464},{96,224},{112... | collective-permute-start | bytes 589832 | tf_op jit(solution)/shard_map/ppermute | solution.py:127
  15.2 23.1 %collective-permute-start.1 = (bf16[768,128]{1,0:T(8,128)(2,1)S(1)}, bf16[768,128]{1,0:T(8,128)(2,1)S(1)}, u32[]{:S(2)}, u32[]{:S(2)}) collective-permute-start(bf16[768,128]{1,0:T(8,128)(2,1)S(1)} %constant_dynamic-update-slice_fusion), channel_id=1, source_target_pairs={{0,64},{16,464},{32,96},{48,496},{64,128},{80,16},{96,160},{112,48... | collective-permute-start | bytes 589832 | tf_op jit(solution)/shard_map/ppermute | solution.py:127
  39.2 20.0 %collective-permute-start.3 = (bf16[1920,128]{1,0:T(8,128)(2,1)S(1)}, bf16[1920,128]{1,0:T(8,128)(2,1)S(1)}, u32[]{:S(2)}, u32[]{:S(2)}) collective-permute-start(bf16[1920,128]{1,0:T(8,128)(2,1)S(1)} %pad_maximum_fusion), channel_id=1, source_target_pairs={{0,32},{16,48},{32,0},{48,16},{64,96},{80,112},{96,64},{112,80},{1... | collective-permute-start | bytes 1474568 | tf_op jit(solution)/shard_map/ppermute | solution.py:123
  41.5 17.8 %collective-permute-start.4 = (bf16[1536,128]{1,0:T(8,128)(2,1)S(1)}, bf16[1536,128]{1,0:T(8,128)(2,1)S(1)}, u32[]{:S(2)}, u32[]{:S(2)}) collective-permute-start(bf16[1536,128]{1,0:T(8,128)(2,1)S(1)} %pad_maximum_fusion.1), channel_id=1, source_target_pairs={{0,16},{16,0},{32,48},{48,32},{64,80},{80,64},{96,112},{112,96},{1... | collective-permute-start | bytes 1179656 | tf_op jit(solution)/shard_map/ppermute | solution.py:123
  59.3 4.0 %collective-permute-start.5 = (bf16[1920,128]{1,0:T(8,128)(2,1)S(1)}, bf16[1920,128]{1,0:T(8,128)(2,1)S(1)}, u32[]{:S(2)}, u32[]{:S(2)}) collective-permute-start(bf16[1920,128]{1,0:T(8,128)(2,1)S(1)} %collective-permute-done.3.side), channel_id=1, source_target_pairs={{0,16},{16,0},{32,48},{48,32},{64,80},{80,64},{96,112},{112,96},{1... | collective-permute-start | bytes 1474568 | tf_op jit(solution)/shard_map/ppermute | solution.py:123

commit v3 on v2

--- a/solution.py
+++ b/solution.py
@@ -41,14 +41,13 @@
     wpart_ref[...] = total
 
 
-def tile_kernel(src_ref, dst_ref, tiles_ref, own, beside, near, far, side, other_near, other_side, wrow_ref, out_ref, blocks_ref, acc_ref):
+def tile_kernel(src_ref, dst_ref, tiles_ref, own, beside, near, far, side, other_near, other_side, out_ref, blocks_ref, acc_ref):
     cols, rows, _ = out_ref.shape
-    share = wrow_ref.shape[1]
     at = 0
     for piece in (own, beside, near, far, side, other_near, other_side):
         blocks_ref[at : at + piece.shape[0], :] = piece[...]
         at += piece.shape[0]
-    blocks = (rows - 2 * share) // SIDE
+    blocks = rows // SIDE
     acc_ref[...] = jnp.zeros_like(acc_ref)
 
     def one(t, carry):
@@ -58,29 +57,17 @@
         return carry
 
     lax.fori_loop(0, tiles_ref.shape[0], one, 0, unroll=8)
-    wsum = wrow_ref[0]
-    for r in range(1, wrow_ref.shape[0]):
-        wsum += wrow_ref[r]
-    high = wsum.astype(BF)
-    low = (wsum - high.astype(F32)).astype(BF)
-    both = jnp.concatenate([high, low], axis=0)
     for c in range(cols):
         for b in range(blocks):
             out_ref[c, b * SIDE : (b + 1) * SIDE, :] = acc_ref[c * blocks + b].astype(BF)
-        out_ref[c, blocks * SIDE :, :] = both
-
-
-def finish_kernel(scale, got_ref, out_ref, wgrad_ref):
-    cols, rows, _ = got_ref.shape
-    share = wgrad_ref.shape[0] // cols
-    nodes = rows - 2 * share
-    total = got_ref[0, :nodes, :].astype(F32)
-    for c in range(1, cols):
-        total += got_ref[c, :nodes, :].astype(F32)
+
+
+def finish_kernel(scale, got_ref, wsum_ref, out_ref, wgrad_ref):
+    total = got_ref[0].astype(F32)
+    for c in range(1, got_ref.shape[0]):
+        total += got_ref[c].astype(F32)
     out_ref[...] = total.astype(BF)
-    for c in range(cols):
-        pair = got_ref[c, nodes:, :].astype(F32)
-        wgrad_ref[c * share : (c + 1) * share, :] = (pair[:share] + pair[share:]) * scale
+    wgrad_ref[...] = wsum_ref[...] * scale
 
 
 def vmem():
@@ -126,19 +113,25 @@
         pairs = [(i, (i + PLANE * (steps if i % 2 == 0 else -steps)) % row_count) for i in range(row_count)]
         return lax.ppermute(value, "row", pairs)
 
-    share = feat // col_count
-    chunk = lax.all_to_all(wpart.reshape(col_count, share, feat), "col", 0, 0).sum(0)
-    copies = jnp.broadcast_to(chunk, (row_count, share, feat))
+    def with_partner(value, axis, bit):
+        pairs = [(i, i ^ bit) for i in range(lax.axis_size(axis))]
+        return value + lax.ppermute(value, axis, pairs)
 
     beside = swap(adjoint, 1)
     chip = jnp.concatenate([adjoint, beside])
     near = to_plane(chip, 1)
     far = to_plane(chip, 2)
-    across, copies = lax.optimization_barrier((jnp.concatenate([adjoint, near, far]), copies))
+    col_bits = [1 << k for k in reversed(range((col_count - 1).bit_length()))]
+    row_bits = [1 << k for k in range((row_count - 1).bit_length())]
+    wsum = wpart
+    for bit in col_bits[:1]:
+        wsum = with_partner(wsum, "col", bit)
+    across, wsum = lax.optimization_barrier((jnp.concatenate([adjoint, near, far]), wsum))
     side = swap(across, 2)
-    wrow = lax.all_to_all(copies, "row", 0, 0)
     other_near = swap(jnp.concatenate([near, far]), 1)
-    side, other_near, wrow = lax.optimization_barrier((side, other_near, wrow))
+    for bit in col_bits[1:2]:
+        wsum = with_partner(wsum, "col", bit)
+    side, other_near, wsum = lax.optimization_barrier((side, other_near, wsum))
     other_side = swap(side, 1)
 
     source_device = tile_in // blocks_dev
@@ -165,12 +158,11 @@
     src_index = slot * blocks_dev + local
     dst_index = tile_out - row_pos * col_count * blocks_dev
 
-    rows_out = nodes + 2 * share
     tiles = tile_values.shape[0]
     sends = pl.pallas_call(
         tile_kernel,
-        out_shape=jax.ShapeDtypeStruct((col_count, rows_out, feat), BF),
-        in_specs=[smem(), smem()] + [vmem()] * 9,
+        out_shape=jax.ShapeDtypeStruct((col_count, nodes, feat), BF),
+        in_specs=[smem(), smem()] + [vmem()] * 8,
         out_specs=vmem(),
         scratch_shapes=[
             pltpu.VMEM((20 * nodes, feat), BF),
@@ -181,18 +173,23 @@
             flops=2 * tiles * SIDE * SIDE * feat, bytes_accessed=6 << 20, transcendentals=0
         ),
         name="tiles",
-    )(src_index, dst_index, tile_values, adjoint, beside, near, far, side, other_near, other_side, wrow)
-
+    )(src_index, dst_index, tile_values, adjoint, beside, near, far, side, other_near, other_side)
+
+    sends, wsum = lax.optimization_barrier((sends, wsum))
     got = lax.all_to_all(sends, "col", 0, 0)
+    for bit in col_bits[2:]:
+        wsum = with_partner(wsum, "col", bit)
+    for bit in row_bits:
+        wsum = with_partner(wsum, "row", bit)
     scale = 1.0 / float(nodes * row_count * col_count) ** 0.5
     node_grad, weight_grad = pl.pallas_call(
         functools.partial(finish_kernel, scale),
         out_shape=(jax.ShapeDtypeStruct((nodes, feat), BF), jax.ShapeDtypeStruct((feat, feat), F32)),
-        in_specs=[vmem()],
+        in_specs=[vmem(), vmem()],
         out_specs=(vmem(), vmem()),
         compiler_params=params,
         name="finish",
-    )(got)
+    )(got, wsum)
     return (node_grad, weight_grad)
 
 

time: 112 us -> 143 us (1.28)
  the two profiles are of different devices: /device:TPU:1 before, /device:TPU:8 now
where the time goes in v3:
time: 143 us; the launch traced here: 142 us
  waiting for transfers between devices  69 us (48%)
  starting transfers between devices  62.7 us (44%)
  Pallas kernels  6.48 us (5%)
  other arithmetic  1.93 us (1%)
    ppermute x9, waiting for transfers between devices, with_partner(): return value + lax.ppermute(value, axis, pairs)  66.7 us
    ppermute x9, starting transfers between devices, with_partner(): return value + lax.ppermute(value, axis, pairs)  33.8 us
    all_to_all x1, starting transfers between devices, on_device(): got = lax.all_to_all(sends, 'col', 0, 0)  10.5 us
    ppermute x4, starting transfers between devices, swap(): return lax.ppermute(value, 'row', [(i, i ^ bit) for i in range(row_count)])  9.23 us
    ppermute x2, starting transfers between devices, to_plane(): return lax.ppermute(value, 'row', pairs)  9.19 us
    pallas_call x1, Pallas kernels, on_device(): pl.pallas_call(tile_kernel, out_shape=jax.ShapeDtypeStruct((col_count, no...  3.14 us
  transfers between devices with their start and end apart: 16, of which 11 were waited for; matrix products, arithmetic and copies ran while one was open for 1% of the time, Pallas kernels for 0%

profile of v3, /device:TPU:8, one launch (start us, length us, event | category | flops | bytes accessed | tf_op | source)
XLA Modules:
  0.0 142.0 jit_solution(5334068820490285886)
XLA Ops:
  0.6 0.0 copy-start.3
  0.6 0.0 copy-start.2
  0.7 0.0 copy-start
  0.7 2.5 %adjoint.1 = (bf16[384,128]{1,0:T(8,128)(2,1)}, f32[128,128]{1,0:T(8,128)}) custom-call(s32[1]{0:T(128)} %bitcast.base_ref, s32[3,128]{1,0:T(4,128)} %bitcast.2, bf16[384,128]{1,0:T(8,128)(2,1)} %cot_in.1, bf16[384,128]{1,0:T(8,128)(2,1)} %pre_in.1, bf16[384,128]{1,0:T(8,128)(2,1)} %agg_in.1, bf16[128,128]{1,0:T(8,128)(2,1)} %w_in.1), custom_call_target="tpu_custom_call" | custom-call | tf_op jit(solution)/shard_map/adjoint/pallas_call | solution.py:92
  3.2 0.0 copy-start.1
  3.2 2.1 %collective-permute-start = (bf16[384,128]{1,0:T(8,128)(2,1)}, bf16[384,128]{1,0:T(8,128)(2,1)S(1)}, u32[]{:S(2)}, u32[]{:S(2)}) collective-permute-start(bf16[384,128]{1,0:T(8,128)(2,1)} %get-tuple-element.11.own), channel_id=1, source_target_pairs={{0,16},{16,0},{32,48},{48,32},{64,80},{80,64},{96,112},{112,96},{1... | collective-permute-start | bytes 294920 | tf_op jit(solution)/shard_map/ppermute | solution.py:110
  5.2 0.9 constant_dynamic-update-slice_fusion.1
  6.1 0.6 collective-permute-done.beside
  6.7 4.5 %collective-permute-start.2 = (bf16[768,128]{1,0:T(8,128)(2,1)S(1)}, bf16[768,128]{1,0:T(8,128)(2,1)S(1)}, u32[]{:S(2)}, u32[]{:S(2)}) collective-permute-start(bf16[768,128]{1,0:T(8,128)(2,1)S(1)} %constant_dynamic-update-slice_fusion), channel_id=1, source_target_pairs={{0,128},{16,400},{32,160},{48,432},{64,192},{80,464},{96,224},{112... | collective-permute-start | bytes 589832 | tf_op jit(solution)/shard_map/ppermute | solution.py:114
  11.2 4.7 %collective-permute-start.1 = (bf16[768,128]{1,0:T(8,128)(2,1)S(1)}, bf16[768,128]{1,0:T(8,128)(2,1)S(1)}, u32[]{:S(2)}, u32[]{:S(2)}) collective-permute-start(bf16[768,128]{1,0:T(8,128)(2,1)S(1)} %constant_dynamic-update-slice_fusion), channel_id=1, source_target_pairs={{0,64},{16,464},{32,96},{48,496},{64,128},{80,16},{96,160},{112,48... | collective-permute-start | bytes 589832 | tf_op jit(solution)/shard_map/ppermute | solution.py:114
  15.9 4.9 %collective-permute-start.3 = (f32[128,128]{1,0:T(8,128)}, f32[128,128]{1,0:T(8,128)S(1)}, u32[]{:S(2)}, u32[]{:S(2)}) collective-permute-start(f32[128,128]{1,0:T(8,128)} %get-tuple-element.12), channel_id=1, source_target_pairs={{0,8},{1,9},{2,10},{3,11},{4,12},{5,13},{6,14},{7,15},{8,0},{9,1},... | collective-permute-start | bytes 196616 | tf_op jit(solution)/shard_map/ppermute | solution.py:118
  20.9 3.0 %collective-permute-done.3 = f32[128,128]{1,0:T(8,128)S(1)} collective-permute-done((f32[128,128]{1,0:T(8,128)}, f32[128,128]{1,0:T(8,128)S(1)}, u32[]{:S(2)}, u32[]{:S(2)}) %collective-permute-start.3) | collective-permute-done | bytes 65568 | tf_op jit(solution)/shard_map/ppermute | solution.py:118
  23.9 0.8 add.78
  24.7 0.0 collective-permute-done.2.far
  24.7 0.0 collective-permute-done.1.near
  24.7 0.9 pad_maximum_fusion
  25.7 3.3 %collective-permute-start.4 = (bf16[1920,128]{1,0:T(8,128)(2,1)S(1)}, bf16[1920,128]{1,0:T(8,128)(2,1)S(1)}, u32[]{:S(2)}, u32[]{:S(2)}) collective-permute-start(bf16[1920,128]{1,0:T(8,128)(2,1)S(1)} %pad_maximum_fusion), channel_id=1, source_target_pairs={{0,32},{16,48},{32,0},{48,16},{64,96},{80,112},{96,64},{112,80},{1... | collective-permute-start | bytes 1474568 | tf_op jit(solution)/shard_map/ppermute | solution.py:110
  29.0 1.9 %collective-permute-start.5 = (bf16[1536,128]{1,0:T(8,128)(2,1)S(1)}, bf16[1536,128]{1,0:T(8,128)(2,1)S(1)}, u32[]{:S(2)}, u32[]{:S(2)}) collective-permute-start(bf16[1536,128]{1,0:T(8,128)(2,1)S(1)} %pad_maximum_fusion.1), channel_id=1, source_target_pairs={{0,16},{16,0},{32,48},{48,32},{64,80},{80,64},{96,112},{112,96},{1... | collective-permute-start | bytes 1179656 | tf_op jit(solution)/shard_map/ppermute | solution.py:110
  31.0 10.9 %collective-permute-start.6 = (f32[128,128]{1,0:T(8,128)S(1)}, f32[128,128]{1,0:T(8,128)S(1)}, u32[]{:S(2)}, u32[]{:S(2)}) collective-permute-start(f32[128,128]{1,0:T(8,128)S(1)} %add.78), channel_id=1, source_target_pairs={{0,4},{1,5},{2,6},{3,7},{4,0},{5,1},{6,2},{7,3},{8,12},{9,13},{10,... | collective-permute-start | bytes 196616 | tf_op jit(solution)/shard_map/ppermute | solution.py:118
  41.9 2.8 %collective-permute-done.6 = f32[128,128]{1,0:T(8,128)S(1)} collective-permute-done((f32[128,128]{1,0:T(8,128)S(1)}, f32[128,128]{1,0:T(8,128)S(1)}, u32[]{:S(2)}, u32[]{:S(2)}) %collective-permute-start.6) | collective-permute-done | bytes 65568 | tf_op jit(solution)/shard_map/ppermute | solution.py:118
  44.7 0.0 collective-permute-done.5.other_near
  44.8 0.0 collective-permute-done.4.side
  44.8 1.9 %collective-permute-start.7 = (bf16[1920,128]{1,0:T(8,128)(2,1)S(1)}, bf16[1920,128]{1,0:T(8,128)(2,1)S(1)}, u32[]{:S(2)}, u32[]{:S(2)}) collective-permute-start(bf16[1920,128]{1,0:T(8,128)(2,1)S(1)} %collective-permute-done.4.side), channel_id=1, source_target_pairs={{0,16},{16,0},{32,48},{48,32},{64,80},{80,64},{96,112},{112,96},{1... | collective-permute-start | bytes 1474568 | tf_op jit(solution)/shard_map/ppermute | solution.py:110
  46.7 0.0 copy-done.3
  46.7 0.0 copy-done.2
  46.7 0.1 fusion
  46.8 1.7 %collective-permute-done.7.other_side = bf16[1920,128]{1,0:T(8,128)(2,1)S(1)} collective-permute-done((bf16[1920,128]{1,0:T(8,128)(2,1)S(1)}, bf16[1920,128]{1,0:T(8,128)(2,1)S(1)}, u32[]{:S(2)}, u32[]{:S(2)}) %collective-permute-start.7) | collective-permute-done | bytes 491552 | tf_op jit(solution)/shard_map/ppermute | solution.py:110
  48.5 0.0 copy-done
  48.5 0.0 copy-done.1
  48.5 3.1 %tiles.1 = bf16[16,384,128]{2,1,0:T(8,128)(2,1)} custom-call(s32[32]{0:T(128)S(1)} %get-tuple-element.20.src_ref, s32[32]{0:T(128)S(1)} %get-tuple-element.21.dst_ref, bf16[32,128,128]{2,1,0:T(8,128)(2,1)S(1)} %copy-done, bf16[384,128]{1,0:T(8,128)(2,1)S(1)} %copy-done.1, bf16[384,128]{1,0:T(8,128)(2,1)S(1)} %collective-permute-done.beside, ...), custom_call_target="tpu_custom_call" | custom-call | flops 134217728 | bytes 6291456 | tf_op jit(solution)/shard_map/tiles/pallas_call | solution.py:162
  51.7 10.5 %all-to-all-start = ((bf16[16,384,128]{2,1,0:T(8,128)(2,1)}), bf16[16,384,128]{2,1,0:T(8,128)(2,1)S(1)}, u32[]{:S(2)}, u32[]{:S(2)}) async-start(bf16[16,384,128]{2,1,0:T(8,128)(2,1)} %tiles.1), calls=%async_computation | async-start | bytes 3145728 | tf_op jit(solution)/shard_map/all_to_all | solution.py:179
  62.2 4.7 %collective-permute-start.8 = (f32[128,128]{1,0:T(8,128)S(1)}, f32[128,128]{1,0:T(8,128)S(1)}, u32[]{:S(2)}, u32[]{:S(2)}) collective-permute-start(f32[128,128]{1,0:T(8,128)S(1)} %add.79), channel_id=1, source_target_pairs={{0,2},{1,3},{2,0},{3,1},{4,6},{5,7},{6,4},{7,5},{8,10},{9,11},{10,... | collective-permute-start | bytes 196616 | tf_op jit(solution)/shard_map/ppermute | solution.py:118
  66.9 35.3 %collective-permute-done.8 = f32[128,128]{1,0:T(8,128)S(1)} collective-permute-done((f32[128,128]{1,0:T(8,128)S(1)}, f32[128,128]{1,0:T(8,128)S(1)}, u32[]{:S(2)}, u32[]{:S(2)}) %collective-permute-start.8) | collective-permute-done | bytes 65568 | tf_op jit(solution)/shard_map/ppermute | solution.py:118
  102.2 2.0 %collective-permute-start.9 = (f32[128,128]{1,0:T(8,128)S(1)}, f32[128,128]{1,0:T(8,128)S(1)}, u32[]{:S(2)}, u32[]{:S(2)}) collective-permute-start(f32[128,128]{1,0:T(8,128)S(1)} %add.80), channel_id=1, source_target_pairs={{0,1},{1,0},{2,3},{3,2},{4,5},{5,4},{6,7},{7,6},{8,9},{9,8},{10,11... | collective-permute-start | bytes 196616 | tf_op jit(solution)/shard_map/ppermute | solution.py:118
  104.3 4.1 %collective-permute-done.9 = f32[128,128]{1,0:T(8,128)S(1)} collective-permute-done((f32[128,128]{1,0:T(8,128)S(1)}, f32[128,128]{1,0:T(8,128)S(1)}, u32[]{:S(2)}, u32[]{:S(2)}) %collective-permute-start.9) | collective-permute-done | bytes 65568 | tf_op jit(solution)/shard_map/ppermute | solution.py:118
  108.4 1.9 %collective-permute-start.10 = (f32[128,128]{1,0:T(8,128)S(1)}, f32[128,128]{1,0:T(8,128)S(1)}, u32[]{:S(2)}, u32[]{:S(2)}) collective-permute-start(f32[128,128]{1,0:T(8,128)S(1)} %add.81), channel_id=1, source_target_pairs={{0,16},{16,0},{32,48},{48,32},{64,80},{80,64},{96,112},{112,96},{1... | collective-permute-start | bytes 196616 | tf_op jit(solution)/shard_map/ppermute | solution.py:118
  110.3 1.2 collective-permute-done.10
  111.6 2.1 %collective-permute-start.11 = (f32[128,128]{1,0:T(8,128)S(1)}, f32[128,128]{1,0:T(8,128)S(1)}, u32[]{:S(2)}, u32[]{:S(2)}) collective-permute-start(f32[128,128]{1,0:T(8,128)S(1)} %add.82), channel_id=1, source_target_pairs={{0,32},{16,48},{32,0},{48,16},{64,96},{80,112},{96,64},{112,80},{1... | collective-permute-start | bytes 196616 | tf_op jit(solution)/shard_map/ppermute | solution.py:118
  113.7 4.0 %collective-permute-done.11 = f32[128,128]{1,0:T(8,128)S(1)} collective-permute-done((f32[128,128]{1,0:T(8,128)S(1)}, f32[128,128]{1,0:T(8,128)S(1)}, u32[]{:S(2)}, u32[]{:S(2)}) %collective-permute-start.11) | collective-permute-done | bytes 65568 | tf_op jit(solution)/shard_map/ppermute | solution.py:118
  117.7 1.9 %collective-permute-start.12 = (f32[128,128]{1,0:T(8,128)S(1)}, f32[128,128]{1,0:T(8,128)S(1)}, u32[]{:S(2)}, u32[]{:S(2)}) collective-permute-start(f32[128,128]{1,0:T(8,128)S(1)} %add.83), channel_id=1, source_target_pairs={{0,64},{16,80},{32,96},{48,112},{64,0},{80,16},{96,32},{112,48},{1... | collective-permute-start | bytes 196616 | tf_op jit(solution)/shard_map/ppermute | solution.py:118
  119.7 4.2 %collective-permute-done.12 = f32[128,128]{1,0:T(8,128)S(1)} collective-permute-done((f32[128,128]{1,0:T(8,128)S(1)}, f32[128,128]{1,0:T(8,128)S(1)}, u32[]{:S(2)}, u32[]{:S(2)}) %collective-permute-start.12) | collective-permute-done | bytes 65568 | tf_op jit(solution)/shard_map/ppermute | solution.py:118
  123.9 2.7 %collective-permute-start.13 = (f32[128,128]{1,0:T(8,128)S(1)}, f32[128,128]{1,0:T(8,128)S(1)}, u32[]{:S(2)}, u32[]{:S(2)}) collective-permute-start(f32[128,128]{1,0:T(8,128)S(1)} %add.84), channel_id=1, source_target_pairs={{0,128},{16,144},{32,160},{48,176},{64,192},{80,208},{96,224},{112... | collective-permute-start | bytes 196616 | tf_op jit(solution)/shard_map/ppermute | solution.py:118
  126.6 4.3 %collective-permute-done.13 = f32[128,128]{1,0:T(8,128)S(1)} collective-permute-done((f32[128,128]{1,0:T(8,128)S(1)}, f32[128,128]{1,0:T(8,128)S(1)}, u32[]{:S(2)}, u32[]{:S(2)}) %collective-permute-start.13) | collective-permute-done | bytes 65568 | tf_op jit(solution)/shard_map/ppermute | solution.py:118
  131.0 2.5 %collective-permute-start.14 = (f32[128,128]{1,0:T(8,128)S(1)}, f32[128,128]{1,0:T(8,128)S(1)}, u32[]{:S(2)}, u32[]{:S(2)}) collective-permute-start(f32[128,128]{1,0:T(8,128)S(1)} %add.85), channel_id=1, source_target_pairs={{0,256},{16,272},{32,288},{48,304},{64,320},{80,336},{96,352},{112... | collective-permute-start | bytes 196616 | tf_op jit(solution)/shard_map/ppermute | solution.py:118
  133.5 7.6 %collective-permute-done.14 = f32[128,128]{1,0:T(8,128)S(1)} collective-permute-done((f32[128,128]{1,0:T(8,128)S(1)}, f32[128,128]{1,0:T(8,128)S(1)}, u32[]{:S(2)}, u32[]{:S(2)}) %collective-permute-start.14) | collective-permute-done | bytes 65568 | tf_op jit(solution)/shard_map/ppermute | solution.py:118
  141.1 0.0 all-to-all-done.got_ref
  141.1 0.9 finish.1
  (10 shorter events, 0.1 us)
Async XLA Ops:
  0.6 46.1 %copy-start.3 = (s32[32]{0:T(128)S(1)}, s32[32]{0:T(128)}, u32[]{:S(2)}) copy-start(s32[32]{0:T(128)} %param.14) | copy-start | bytes 388
  0.6 46.1 %copy-start.2 = (s32[32]{0:T(128)S(1)}, s32[32]{0:T(128)}, u32[]{:S(2)}) copy-start(s32[32]{0:T(128)} %param.13) | copy-start | bytes 388
  0.7 47.9 %copy-start = (bf16[32,128,128]{2,1,0:T(8,128)(2,1)S(1)}, bf16[32,128,128]{2,1,0:T(8,128)(2,1)}, u32[]{:S(2)}) copy-start(bf16[32,128,128]{2,1,0:T(8,128)(2,1)} %tiles_ref.1) | copy-start | bytes 3145732
  3.2 45.4 %copy-start.1 = (bf16[384,128]{1,0:T(8,128)(2,1)S(1)}, bf16[384,128]{1,0:T(8,128)(2,1)}, u32[]{:S(2)}) copy-start(bf16[384,128]{1,0:T(8,128)(2,1)} %get-tuple-element.11.own) | copy-start | bytes 294916
  3.2 3.5 %collective-permute-start = (bf16[384,128]{1,0:T(8,128)(2,1)}, bf16[384,128]{1,0:T(8,128)(2,1)S(1)}, u32[]{:S(2)}, u32[]{:S(2)}) collective-permute-start(bf16[384,128]{1,0:T(8,128)(2,1)} %get-tuple-element.11.own), channel_id=1, source_target_pairs={{0,16},{16,0},{32,48},{48,32},{64,80},{80,64},{96,112},{112,96},{1... | collective-permute-start | bytes 294920 | tf_op jit(solution)/shard_map/ppermute | solution.py:110
  6.7 18.0 %collective-permute-start.2 = (bf16[768,128]{1,0:T(8,128)(2,1)S(1)}, bf16[768,128]{1,0:T(8,128)(2,1)S(1)}, u32[]{:S(2)}, u32[]{:S(2)}) collective-permute-start(bf16[768,128]{1,0:T(8,128)(2,1)S(1)} %constant_dynamic-update-slice_fusion), channel_id=1, source_target_pairs={{0,128},{16,400},{32,160},{48,432},{64,192},{80,464},{96,224},{112... | collective-permute-start | bytes 589832 | tf_op jit(solution)/shard_map/ppermute | solution.py:114
  11.2 13.5 %collective-permute-start.1 = (bf16[768,128]{1,0:T(8,128)(2,1)S(1)}, bf16[768,128]{1,0:T(8,128)(2,1)S(1)}, u32[]{:S(2)}, u32[]{:S(2)}) collective-permute-start(bf16[768,128]{1,0:T(8,128)(2,1)S(1)} %constant_dynamic-update-slice_fusion), channel_id=1, source_target_pairs={{0,64},{16,464},{32,96},{48,496},{64,128},{80,16},{96,160},{112,48... | collective-permute-start | bytes 589832 | tf_op jit(solution)/shard_map/ppermute | solution.py:114
  15.9 7.9 %collective-permute-start.3 = (f32[128,128]{1,0:T(8,128)}, f32[128,128]{1,0:T(8,128)S(1)}, u32[]{:S(2)}, u32[]{:S(2)}) collective-permute-start(f32[128,128]{1,0:T(8,128)} %get-tuple-element.12), channel_id=1, source_target_pairs={{0,8},{1,9},{2,10},{3,11},{4,12},{5,13},{6,14},{7,15},{8,0},{9,1},... | collective-permute-start | bytes 196616 | tf_op jit(solution)/shard_map/ppermute | solution.py:118
  25.7 19.1 %collective-permute-start.4 = (bf16[1920,128]{1,0:T(8,128)(2,1)S(1)}, bf16[1920,128]{1,0:T(8,128)(2,1)S(1)}, u32[]{:S(2)}, u32[]{:S(2)}) collective-permute-start(bf16[1920,128]{1,0:T(8,128)(2,1)S(1)} %pad_maximum_fusion), channel_id=1, source_target_pairs={{0,32},{16,48},{32,0},{48,16},{64,96},{80,112},{96,64},{112,80},{1... | collective-permute-start | bytes 1474568 | tf_op jit(solution)/shard_map/ppermute | solution.py:110
  29.0 15.7 %collective-permute-start.5 = (bf16[1536,128]{1,0:T(8,128)(2,1)S(1)}, bf16[1536,128]{1,0:T(8,128)(2,1)S(1)}, u32[]{:S(2)}, u32[]{:S(2)}) collective-permute-start(bf16[1536,128]{1,0:T(8,128)(2,1)S(1)} %pad_maximum_fusion.1), channel_id=1, source_target_pairs={{0,16},{16,0},{32,48},{48,32},{64,80},{80,64},{96,112},{112,96},{1... | collective-permute-start | bytes 1179656 | tf_op jit(solution)/shard_map/ppermute | solution.py:110
  31.0 13.8 %collective-permute-start.6 = (f32[128,128]{1,0:T(8,128)S(1)}, f32[128,128]{1,0:T(8,128)S(1)}, u32[]{:S(2)}, u32[]{:S(2)}) collective-permute-start(f32[128,128]{1,0:T(8,128)S(1)} %add.78), channel_id=1, source_target_pairs={{0,4},{1,5},{2,6},{3,7},{4,0},{5,1},{6,2},{7,3},{8,12},{9,13},{10,... | collective-permute-start | bytes 196616 | tf_op jit(solution)/shard_map/ppermute | solution.py:118
  44.8 3.8 %collective-permute-start.7 = (bf16[1920,128]{1,0:T(8,128)(2,1)S(1)}, bf16[1920,128]{1,0:T(8,128)(2,1)S(1)}, u32[]{:S(2)}, u32[]{:S(2)}) collective-permute-start(bf16[1920,128]{1,0:T(8,128)(2,1)S(1)} %collective-permute-done.4.side), channel_id=1, source_target_pairs={{0,16},{16,0},{32,48},{48,32},{64,80},{80,64},{96,112},{112,96},{1... | collective-permute-start | bytes 1474568 | tf_op jit(solution)/shard_map/ppermute | solution.py:110
  51.7 89.4 %all-to-all-start = ((bf16[16,384,128]{2,1,0:T(8,128)(2,1)}), bf16[16,384,128]{2,1,0:T(8,128)(2,1)S(1)}, u32[]{:S(2)}, u32[]{:S(2)}) async-start(bf16[16,384,128]{2,1,0:T(8,128)(2,1)} %tiles.1), calls=%async_computation | async-start | bytes 3145728 | tf_op jit(solution)/shard_map/all_to_all | solution.py:179
  62.2 40.0 %collective-permute-start.8 = (f32[128,128]{1,0:T(8,128)S(1)}, f32[128,128]{1,0:T(8,128)S(1)}, u32[]{:S(2)}, u32[]{:S(2)}) collective-permute-start(f32[128,128]{1,0:T(8,128)S(1)} %add.79), channel_id=1, source_target_pairs={{0,2},{1,3},{2,0},{3,1},{4,6},{5,7},{6,4},{7,5},{8,10},{9,11},{10,... | collective-permute-start | bytes 196616 | tf_op jit(solution)/shard_map/ppermute | solution.py:118
  102.2 6.2 %collective-permute-start.9 = (f32[128,128]{1,0:T(8,128)S(1)}, f32[128,128]{1,0:T(8,128)S(1)}, u32[]{:S(2)}, u32[]{:S(2)}) collective-permute-start(f32[128,128]{1,0:T(8,128)S(1)} %add.80), channel_id=1, source_target_pairs={{0,1},{1,0},{2,3},{3,2},{4,5},{5,4},{6,7},{7,6},{8,9},{9,8},{10,11... | collective-permute-start | bytes 196616 | tf_op jit(solution)/shard_map/ppermute | solution.py:118
  108.4 3.1 %collective-permute-start.10 = (f32[128,128]{1,0:T(8,128)S(1)}, f32[128,128]{1,0:T(8,128)S(1)}, u32[]{:S(2)}, u32[]{:S(2)}) collective-permute-start(f32[128,128]{1,0:T(8,128)S(1)} %add.81), channel_id=1, source_target_pairs={{0,16},{16,0},{32,48},{48,32},{64,80},{80,64},{96,112},{112,96},{1... | collective-permute-start | bytes 196616 | tf_op jit(solution)/shard_map/ppermute | solution.py:118
  111.6 6.2 %collective-permute-start.11 = (f32[128,128]{1,0:T(8,128)S(1)}, f32[128,128]{1,0:T(8,128)S(1)}, u32[]{:S(2)}, u32[]{:S(2)}) collective-permute-start(f32[128,128]{1,0:T(8,128)S(1)} %add.82), channel_id=1, source_target_pairs={{0,32},{16,48},{32,0},{48,16},{64,96},{80,112},{96,64},{112,80},{1... | collective-permute-start | bytes 196616 | tf_op jit(solution)/shard_map/ppermute | solution.py:118
  117.7 6.2 %collective-permute-start.12 = (f32[128,128]{1,0:T(8,128)S(1)}, f32[128,128]{1,0:T(8,128)S(1)}, u32[]{:S(2)}, u32[]{:S(2)}) collective-permute-start(f32[128,128]{1,0:T(8,128)S(1)} %add.83), channel_id=1, source_target_pairs={{0,64},{16,80},{32,96},{48,112},{64,0},{80,16},{96,32},{112,48},{1... | collective-permute-start | bytes 196616 | tf_op jit(solution)/shard_map/ppermute | solution.py:118
  123.9 7.1 %collective-permute-start.13 = (f32[128,128]{1,0:T(8,128)S(1)}, f32[128,128]{1,0:T(8,128)S(1)}, u32[]{:S(2)}, u32[]{:S(2)}) collective-permute-start(f32[128,128]{1,0:T(8,128)S(1)} %add.84), channel_id=1, source_target_pairs={{0,128},{16,144},{32,160},{48,176},{64,192},{80,208},{96,224},{112... | collective-permute-start | bytes 196616 | tf_op jit(solution)/shard_map/ppermute | solution.py:118
  131.0 10.1 %collective-permute-start.14 = (f32[128,128]{1,0:T(8,128)S(1)}, f32[128,128]{1,0:T(8,128)S(1)}, u32[]{:S(2)}, u32[]{:S(2)}) collective-permute-start(f32[128,128]{1,0:T(8,128)S(1)} %add.85), channel_id=1, source_target_pairs={{0,256},{16,272},{32,288},{48,304},{64,320},{80,336},{96,352},{112... | collective-permute-start | bytes 196616 | tf_op jit(solution)/shard_map/ppermute | solution.py:118

commit v4 on v3

v4 whole, which is shorter than its diff:
```python
import functools

import jax
import jax.numpy as jnp
from jax import lax
from jax.experimental import pallas as pl
from jax.experimental.pallas import tpu as pltpu
from jax.sharding import PartitionSpec as P

BF = jnp.bfloat16
F32 = jnp.float32
SIDE = 128
PLANE = 4


def dot(a, b, contract):
    return lax.dot_general(a, b, ((contract[:1], contract[1:]), ((), ())), preferred_element_type=F32)


def adjoint_kernel(order_in, cot_in, pre_in, agg_in, w_in, out_ref, order_ref, cot_ref, pre_ref, agg_ref, w_ref, sems):
    ins = (order_in, cot_in, pre_in, w_in, agg_in)
    held = (order_ref, cot_ref, pre_ref, w_ref, agg_ref)
    copies = [pltpu.make_async_copy(a, b, sems.at[i]) for i, (a, b) in enumerate(zip(ins, held))]
    for copy in copies:
        copy.start()
    for copy in copies:
        copy.wait()
    rows = cot_ref.shape[0]
    cot = cot_ref[...]
    row_id = lax.broadcasted_iota(jnp.int32, (rows, SIDE), 0)
    base = (lax.axis_index("row") * lax.axis_size("col") + lax.axis_index("col")) * rows
    total = jnp.zeros(w_ref.shape, F32)
    for b in range(rows // SIDE):
        span = slice(b * SIDE, (b + 1) * SIDE)
        local = order_ref[b : b + 1, :] - base
        pick = jnp.where(row_id == local, 1.0, 0.0).astype(BF)
        grad_rows = dot(pick, cot, (0, 0))
        grad_pre = jnp.where(pre_ref[span, :].astype(F32) > 0, grad_rows, 0.0).astype(BF)
        total += dot(agg_ref[span, :], grad_pre, (0, 0))
        out_ref[span, :] = dot(grad_pre, w_ref[...], (1, 1)).astype(BF)
    high = total.astype(BF)
    out_ref[rows : rows + total.shape[0], :] = high
    out_ref[rows + total.shape[0] :, :] = (total - high.astype(F32)).astype(BF)


def whole(pair):
    feat = pair.shape[0] // 2
    return pair[:feat].astype(F32) + pair[feat:].astype(F32)


def chip_kernel(own, beside, out_ref, weight_ref):
    nodes = out_ref.shape[0] // 2 - SIDE // 2
    out_ref[:nodes, :] = own[:nodes, :]
    out_ref[nodes : 2 * nodes, :] = beside[:nodes, :]
    weight = (whole(own[nodes:, :]) + whole(beside[nodes:, :])).astype(BF)
    out_ref[2 * nodes :, :] = weight
    weight_ref[...] = weight


def across_kernel(beside, near, far, third, fourth, out_ref, weights_ref):
    nodes = out_ref.shape[0] // 5
    out_ref[:nodes, :] = beside[:nodes, :]
    out_ref[nodes : 3 * nodes, :] = near[: 2 * nodes, :]
    out_ref[3 * nodes :, :] = far[: 2 * nodes, :]
    feat = third.shape[0]
    weights_ref[:feat, :] = near[2 * nodes :, :]
    weights_ref[feat : 2 * feat, :] = far[2 * nodes :, :]
    weights_ref[2 * feat : 3 * feat, :] = third[...]
    weights_ref[3 * feat :, :] = fourth[...]


def plane_kernel(weight, weights, other, out_ref, held):
    planes = held.shape[0]
    row = lax.axis_index("row")
    at, way = lax.div(row, PLANE), 2 * lax.rem(row, 2) - 1
    feat = weight.shape[0]

    def put(steps, value):
        held[lax.rem(at + steps + planes, planes)] = value

    put(0, weight[...])
    put(4, weights[3 * feat :, :])
    for steps in (1, 2, 3):
        span = slice((steps - 1) * feat, steps * feat)
        put(steps * way, weights[span, :])
        put(-steps * way, other[span, :])
    total = held[0].astype(F32)
    for p in range(1, planes):
        total += held[p].astype(F32)
    out_ref[...] = total


def block_place(block, row, planes, cols, blocks):
    device = lax.div(block, blocks)
    group = lax.div(device, cols)
    gap = lax.rem(lax.div(group, PLANE) - lax.div(row, PLANE) + planes, planes)
    core = lax.rem(group, 2)
    same_core = core == lax.rem(row, 2)
    same_chip = lax.rem(lax.div(group, 2), 2) == lax.rem(lax.div(row, 2), 2)
    below = gap > planes // 2
    steps = jnp.where(below, planes - gap, gap)
    receiver = jnp.where(gap == 0, 1 - core, jnp.where(below, 0, 1))
    place = (steps - 1) * 2 + jnp.where(core == receiver, 0, 1)
    place = jnp.where(same_chip, place, jnp.where(gap == 0, 4, 5 + place))
    slot = 2 + place + jnp.where(receiver == lax.rem(row, 2), 0, 9)
    slot = jnp.where((gap == 0) & same_chip, jnp.where(same_core, 0, 1), slot)
    return slot * blocks + lax.rem(block, blocks)


def tile_kernel(
    in_ref, to_ref, tiles_ref, own, beside, near, far, side, other, other_side, wsum, wacross,
    direct_ref, keep_ref, give_ref, blocks_ref, acc_ref,
):
    cols = direct_ref.shape[0]
    half = cols // 2
    share = direct_ref.shape[1] - SIDE
    blocks = acc_ref.shape[0] // cols
    nodes = blocks * SIDE
    rows = near.shape[0]
    at = 0
    for piece in (
        own[:nodes, :],
        beside[:nodes, :],
        near[: 2 * nodes, :],
        far[: 2 * nodes, :],
        side[...],
        other[: 2 * nodes, :],
        other[rows : rows + 2 * nodes, :],
        other_side[...],
    ):
        blocks_ref[at : at + piece.shape[0], :] = piece
        at += piece.shape[0]
    acc_ref[...] = jnp.zeros_like(acc_ref)
    row, col = lax.axis_index("row"), lax.axis_index("col")
    planes = lax.axis_size("row") // PLANE

    def one(t, carry):
        at = pl.multiple_of(block_place(in_ref[t], row, planes, cols, blocks) * SIDE, SIDE)
        to = to_ref[t] - row * cols * blocks
        acc_ref[to] += dot(tiles_ref[t], blocks_ref[pl.ds(at, SIDE), :], (1, 0))
        return carry

    lax.fori_loop(0, tiles_ref.shape[0], one, 0, unroll=8)
    weight = (wsum[...] + wacross[...]).astype(BF)
    for c in range(cols):
        direct_ref[c, :SIDE, :] = acc_ref[c * blocks].astype(BF)
        z = c % half
        direct_ref[c, SIDE:, :] = weight[z * share : (z + 1) * share, :]
    mine = lax.div(col, half) * half
    theirs = half - mine
    for z in range(half):
        for b in range(1, blocks):
            span = slice((b - 1) * SIDE, b * SIDE)
            keep_ref[z, span, :] = acc_ref[(mine + z) * blocks + b]
            give_ref[z, span, :] = acc_ref[(theirs + z) * blocks + b].astype(BF)


def first_kernel(direct_ref, out_ref, weight_ref):
    share = direct_ref.shape[1] - SIDE
    total = direct_ref[0].astype(F32)
    for c in range(1, direct_ref.shape[0]):
        total += direct_ref[c].astype(F32)
    out_ref[...] = total[:SIDE].astype(BF)
    high = total[SIDE:].astype(BF)
    weight_ref[:share, :] = high
    weight_ref[share:, :] = (total[SIDE:] - high.astype(F32)).astype(BF)


def pair_kernel(keep_ref, got_ref, weight_ref, out_ref):
    rows = keep_ref.shape[1]
    for z in range(keep_ref.shape[0]):
        out_ref[z, :rows, :] = (keep_ref[z] + got_ref[z].astype(F32)).astype(BF)
        out_ref[z, rows:, :] = weight_ref[...]


def finish_kernel(scale, first_ref, got_ref, out_ref, wgrad_ref):
    half = got_ref.shape[0]
    rows = out_ref.shape[0] - SIDE
    share = wgrad_ref.shape[0] // half
    out_ref[:SIDE, :] = first_ref[...]
    total = got_ref[0, :rows, :].astype(F32)
    for z in range(1, half):
        total += got_ref[z, :rows, :].astype(F32)
    out_ref[SIDE:, :] = total.astype(BF)
    for z in range(half):
        wgrad_ref[z * share : (z + 1) * share, :] = whole(got_ref[z, rows:, :]) * scale


def vmem():
    return pl.BlockSpec(memory_space=pltpu.VMEM)


def smem():
    return pl.BlockSpec(memory_space=pltpu.SMEM)


def on_device(cotangent, pre_act, aggregated, weight, tile_values, tile_in, tile_out, order):
    row_count = lax.axis_size("row")
    col_count = lax.axis_size("col")
    nodes, feat = cotangent.shape
    blocks_dev = nodes // SIDE
    planes = row_count // PLANE
    params = pltpu.CompilerParams(vmem_limit_bytes=12 << 20)
    small = pltpu.CompilerParams(vmem_limit_bytes=4 << 20)

    adjoint = pl.pallas_call(
        adjoint_kernel,
        out_shape=jax.ShapeDtypeStruct((nodes + 2 * feat, feat), BF),
        in_specs=[pl.BlockSpec(memory_space=pltpu.HBM)] * 5,
        out_specs=vmem(),
        scratch_shapes=[
            pltpu.VMEM((blocks_dev, SIDE), jnp.int32),
            pltpu.VMEM((nodes, feat), BF),
            pltpu.VMEM((nodes, feat), BF),
            pltpu.VMEM((nodes, feat), BF),
            pltpu.VMEM((feat, feat), BF),
            pltpu.SemaphoreType.DMA((5,)),
        ],
        compiler_params=pltpu.CompilerParams(vmem_limit_bytes=60 << 20),
        name="adjoint",
    )(order.reshape(blocks_dev, SIDE), cotangent, pre_act, aggregated, weight)

    def swap(value, bit):
        return lax.ppermute(value, "row", [(i, i ^ bit) for i in range(row_count)])

    def to_plane(value, steps):
        pairs = [(i, (i + PLANE * (steps if i % 2 == 0 else -steps)) % row_count) for i in range(row_count)]
        return lax.ppermute(value, "row", pairs)

    beside = swap(adjoint, 1)
    chip, weight_sum = pl.pallas_call(
        chip_kernel,
        out_shape=(jax.ShapeDtypeStruct((2 * nodes + feat, feat), BF), jax.ShapeDtypeStruct((feat, feat), BF)),
        in_specs=[vmem()] * 2,
        out_specs=(vmem(), vmem()),
        compiler_params=small,
        name="chip",
    )(adjoint, beside)
    near = to_plane(chip, 1)
    far = to_plane(chip, 2)
    third = to_plane(weight_sum, 3)
    fourth = to_plane(weight_sum, 4)
    across, weight_sums = pl.pallas_call(
        across_kernel,
        out_shape=(jax.ShapeDtypeStruct((5 * nodes, feat), BF), jax.ShapeDtypeStruct((4 * feat, feat), BF)),
        in_specs=[vmem()] * 5,
        out_specs=(vmem(), vmem()),
        compiler_params=small,
        name="across",
    )(beside, near, far, third, fourth)
    side = swap(across, 2)
    other = swap(jnp.concatenate([near, far]), 1)
    other_weight = swap(weight_sums, 1)
    wsum = pl.pallas_call(
        plane_kernel,
        out_shape=jax.ShapeDtypeStruct((feat, feat), F32),
        in_specs=[vmem()] * 3,
        out_specs=vmem(),
        scratch_shapes=[pltpu.VMEM((planes, feat, feat), BF)],
        compiler_params=small,
        cost_estimate=pl.CostEstimate(flops=1000, bytes_accessed=1000, transcendentals=0),
        name="planes",
    )(weight_sum, weight_sums, other_weight)
    wacross = swap(wsum, 2)
    side, other, wacross = lax.optimization_barrier((side, other, wacross))
    other_side = swap(side, 1)

    tiles = tile_values.shape[0]
    half = col_count // 2
    share = feat // half
    rest = nodes - SIDE
    direct, keep, give = pl.pallas_call(
        tile_kernel,
        out_shape=(
            jax.ShapeDtypeStruct((col_count, SIDE + share, feat), BF),
            jax.ShapeDtypeStruct((half, rest, feat), F32),
            jax.ShapeDtypeStruct((half, rest, feat), BF),
        ),
        in_specs=[smem()] * 2 + [vmem()] * 10,
        out_specs=(vmem(),) * 3,
        scratch_shapes=[
            pltpu.VMEM((20 * nodes, feat), BF),
            pltpu.VMEM((col_count * blocks_dev, SIDE, feat), F32),
        ],
        compiler_params=params,
        cost_estimate=pl.CostEstimate(
            flops=2 * tiles * SIDE * SIDE * feat, bytes_accessed=6 << 20, transcendentals=0
        ),
        name="tiles",
    )(tile_in, tile_out, tile_values, adjoint, beside, near, far, side, other, other_side, wsum, wacross)

    got = lax.ppermute(give, "col", [(i, (i + half) % col_count) for i in range(col_count)])
    direct = lax.all_to_all(direct, "col", 0, 0)
    first, weight_share = pl.pallas_call(
        first_kernel,
        out_shape=(jax.ShapeDtypeStruct((SIDE, feat), BF), jax.ShapeDtypeStruct((2 * share, feat), BF)),
        in_specs=[vmem()],
        out_specs=(vmem(), vmem()),
        compiler_params=small,
        name="first",
    )(direct)
    pair = pl.pallas_call(
        pair_kernel,
        out_shape=jax.ShapeDtypeStruct((half, rest + 2 * share, feat), BF),
        in_specs=[vmem()] * 3,
        out_specs=vmem(),
        compiler_params=small,
        name="pair",
    )(keep, got, weight_share)
    groups = [list(range(half)), list(range(half, col_count))]
    summed = lax.all_to_all(pair, "col", 0, 0, axis_index_groups=groups)
    scale = 1.0 / float(nodes * row_count * col_count) ** 0.5
    node_grad, weight_grad = pl.pallas_call(
        functools.partial(finish_kernel, scale),
        out_shape=(jax.ShapeDtypeStruct((nodes, feat), BF), jax.ShapeDtypeStruct((feat, feat), F32)),
        in_specs=[vmem()] * 2,
        out_specs=(vmem(), vmem()),
        compiler_params=small,
        name="finish",
    )(first, summed)
    return (node_grad, weight_grad)


def solution(mesh):
    split = P(("row", "col"))
    return jax.shard_map(
        on_device,
        mesh=mesh,
        in_specs=(split, split, split, P(), split, split, split, split),
        out_specs=(split, P()),
        check_vma=False,
    )
```

time: 143 us -> 112 us (0.78)
  the two profiles are of different devices: /device:TPU:8 before, /device:TPU:1 now
where the time goes in v4:
time: 112 us; the launch traced here: 111 us
  starting transfers between devices  54.2 us (48%)
  waiting for transfers between devices  26 us (23%)
  blocking collectives  22.1 us (20%)
  Pallas kernels  6.75 us (6%)
    ppermute x6, starting transfers between devices, swap(): return lax.ppermute(value, 'row', [(i, i ^ bit) for i in range(row_count)])  23.7 us
    all_to_all x1, blocking collectives, on_device(): summed = lax.all_to_all(pair, 'col', 0, 0, axis_index_groups=groups)  22.1 us
    ppermute x4, starting transfers between devices, to_plane(): return lax.ppermute(value, 'row', pairs)  13.4 us
    all_to_all x1, waiting for transfers between devices, on_device(): direct = lax.all_to_all(direct, 'col', 0, 0)  12.5 us
    all_to_all x1, starting transfers between devices, on_device(): direct = lax.all_to_all(direct, 'col', 0, 0)  12.3 us
    ppermute x6, waiting for transfers between devices, swap(): return lax.ppermute(value, 'row', [(i, i ^ bit) for i in range(row_count)])  7.34 us
    ppermute x1, waiting for transfers between devices, on_device(): lax.ppermute(give, 'col', [(i, (i + half) % col_count) for i in range(col...  5.19 us
    ppermute x1, starting transfers between devices, on_device(): lax.ppermute(give, 'col', [(i, (i + half) % col_count) for i in range(col...  4.77 us
  transfers between devices with their start and end apart: 12, of which 7 were waited for; matrix products, arithmetic and copies ran while one was open for 0% of the time, Pallas kernels for 0%

profile of v4, /device:TPU:1, one launch (start us, length us, event | category | flops | bytes accessed | tf_op | source)
XLA Modules:
  0.0 110.9 jit_solution(1420344123185089472)
XLA Ops:
  0.6 2.4 %adjoint.1.own = bf16[640,128]{1,0:T(8,128)(2,1)} custom-call(s32[3,128]{1,0:T(4,128)} %bitcast.1, bf16[384,128]{1,0:T(8,128)(2,1)} %cot_in.1, bf16[384,128]{1,0:T(8,128)(2,1)} %pre_in.1, bf16[384,128]{1,0:T(8,128)(2,1)} %agg_in.1, bf16[128,128]{1,0:T(8,128)(2,1)} %w_in.1), custom_call_target="tpu_custom_call" | custom-call | tf_op jit(solution)/shard_map/adjoint/pallas_call | solution.py:206
  3.0 8.8 %collective-permute-start = (bf16[640,128]{1,0:T(8,128)(2,1)}, bf16[640,128]{1,0:T(8,128)(2,1)S(1)}, u32[]{:S(2)}, u32[]{:S(2)}) collective-permute-start(bf16[640,128]{1,0:T(8,128)(2,1)} %adjoint.1.own), channel_id=1, source_target_pairs={{0,16},{16,0},{32,48},{48,32},{64,80},{80,64},{96,112},{112,96},{1... | collective-permute-start | bytes 491528 | tf_op jit(solution)/shard_map/ppermute | solution.py:224
  11.8 1.2 %collective-permute-done.beside = bf16[640,128]{1,0:T(8,128)(2,1)S(1)} collective-permute-done((bf16[640,128]{1,0:T(8,128)(2,1)}, bf16[640,128]{1,0:T(8,128)(2,1)S(1)}, u32[]{:S(2)}, u32[]{:S(2)}) %collective-permute-start) | collective-permute-done | bytes 163872 | tf_op jit(solution)/shard_map/ppermute | solution.py:224
  13.1 0.0 copy-start
  13.1 0.9 copy-done
  14.0 0.0 copy-start.2
  14.0 2.1 %collective-permute-start.2 = (bf16[896,128]{1,0:T(8,128)(2,1)S(1)}, bf16[896,128]{1,0:T(8,128)(2,1)S(1)}, u32[]{:S(2)}, u32[]{:S(2)}) collective-permute-start(bf16[896,128]{1,0:T(8,128)(2,1)S(1)} %get-tuple-element.14), channel_id=1, source_target_pairs={{0,128},{16,400},{32,160},{48,432},{64,192},{80,464},{96,224},{112... | collective-permute-start | bytes 688136 | tf_op jit(solution)/shard_map/ppermute | solution.py:228
  16.1 1.9 %collective-permute-start.1 = (bf16[896,128]{1,0:T(8,128)(2,1)S(1)}, bf16[896,128]{1,0:T(8,128)(2,1)S(1)}, u32[]{:S(2)}, u32[]{:S(2)}) collective-permute-start(bf16[896,128]{1,0:T(8,128)(2,1)S(1)} %get-tuple-element.14), channel_id=1, source_target_pairs={{0,64},{16,464},{32,96},{48,496},{64,128},{80,16},{96,160},{112,48... | collective-permute-start | bytes 688136 | tf_op jit(solution)/shard_map/ppermute | solution.py:228
  18.0 2.3 %collective-permute-start.4 = (bf16[128,128]{1,0:T(8,128)(2,1)S(1)}, bf16[128,128]{1,0:T(8,128)(2,1)S(1)}, u32[]{:S(2)}, u32[]{:S(2)}) collective-permute-start(bf16[128,128]{1,0:T(8,128)(2,1)S(1)} %get-tuple-element.15.weight), channel_id=1, source_target_pairs={{0,256},{16,272},{32,288},{48,304},{64,320},{80,336},{96,352},{112... | collective-permute-start | bytes 98312 | tf_op jit(solution)/shard_map/ppermute | solution.py:228
  20.3 7.2 %collective-permute-start.3 = (bf16[128,128]{1,0:T(8,128)(2,1)S(1)}, bf16[128,128]{1,0:T(8,128)(2,1)S(1)}, u32[]{:S(2)}, u32[]{:S(2)}) collective-permute-start(bf16[128,128]{1,0:T(8,128)(2,1)S(1)} %get-tuple-element.15.weight), channel_id=1, source_target_pairs={{0,192},{16,336},{32,224},{48,368},{64,256},{80,400},{96,288},{112... | collective-permute-start | bytes 98312 | tf_op jit(solution)/shard_map/ppermute | solution.py:228
  27.5 0.0 collective-permute-done.4.fourth
  27.5 1.0 collective-permute-done.3.third
  28.5 0.0 collective-permute-done.2.far
  28.5 0.0 collective-permute-done.1.near
  28.5 1.9 %collective-permute-start.5 = (bf16[1920,128]{1,0:T(8,128)(2,1)S(1)}, bf16[1920,128]{1,0:T(8,128)(2,1)S(1)}, u32[]{:S(2)}, u32[]{:S(2)}) collective-permute-start(bf16[1920,128]{1,0:T(8,128)(2,1)S(1)} %get-tuple-element.16), channel_id=1, source_target_pairs={{0,32},{16,48},{32,0},{48,16},{64,96},{80,112},{96,64},{112,80},{1... | collective-permute-start | bytes 1474568 | tf_op jit(solution)/shard_map/ppermute | solution.py:224
  30.5 6.0 %collective-permute-start.6 = (bf16[1792,128]{1,0:T(8,128)(2,1)S(1)}, bf16[1792,128]{1,0:T(8,128)(2,1)S(1)}, u32[]{:S(2)}, u32[]{:S(2)}) collective-permute-start(bf16[1792,128]{1,0:T(8,128)(2,1)S(1)} %pad_maximum_fusion), channel_id=1, source_target_pairs={{0,16},{16,0},{32,48},{48,32},{64,80},{80,64},{96,112},{112,96},{1... | collective-permute-start | bytes 1376264 | tf_op jit(solution)/shard_map/ppermute | solution.py:224
  36.5 0.0 copy-start.1
  36.5 0.0 copy-start.3
  36.5 0.0 copy-start.4
  36.5 2.1 %collective-permute-start.7 = (bf16[512,128]{1,0:T(8,128)(2,1)S(1)}, bf16[512,128]{1,0:T(8,128)(2,1)S(1)}, u32[]{:S(2)}, u32[]{:S(2)}) collective-permute-start(bf16[512,128]{1,0:T(8,128)(2,1)S(1)} %get-tuple-element.17.weights), channel_id=1, source_target_pairs={{0,16},{16,0},{32,48},{48,32},{64,80},{80,64},{96,112},{112,96},{1... | collective-permute-start | bytes 393224 | tf_op jit(solution)/shard_map/ppermute | solution.py:224
  38.6 1.3 %collective-permute-done.7.other = bf16[512,128]{1,0:T(8,128)(2,1)S(1)} collective-permute-done((bf16[512,128]{1,0:T(8,128)(2,1)S(1)}, bf16[512,128]{1,0:T(8,128)(2,1)S(1)}, u32[]{:S(2)}, u32[]{:S(2)}) %collective-permute-start.7) | collective-permute-done | bytes 131104 | tf_op jit(solution)/shard_map/ppermute | solution.py:224
  39.9 0.1 planes.1.wsum
  40.0 2.1 %collective-permute-start.8 = (f32[128,128]{1,0:T(8,128)S(1)}, f32[128,128]{1,0:T(8,128)S(1)}, u32[]{:S(2)}, u32[]{:S(2)}) collective-permute-start(f32[128,128]{1,0:T(8,128)S(1)} %planes.1.wsum), channel_id=1, source_target_pairs={{0,32},{16,48},{32,0},{48,16},{64,96},{80,112},{96,64},{112,80},{1... | collective-permute-start | bytes 196616 | tf_op jit(solution)/shard_map/ppermute | solution.py:224
  42.1 3.3 %collective-permute-done.8.wacross = f32[128,128]{1,0:T(8,128)S(1)} collective-permute-done((f32[128,128]{1,0:T(8,128)S(1)}, f32[128,128]{1,0:T(8,128)S(1)}, u32[]{:S(2)}, u32[]{:S(2)}) %collective-permute-start.8) | collective-permute-done | bytes 65568 | tf_op jit(solution)/shard_map/ppermute | solution.py:224
  45.4 0.0 collective-permute-done.6.other
  45.4 0.0 collective-permute-done.5.side
  45.4 2.9 %collective-permute-start.9 = (bf16[1920,128]{1,0:T(8,128)(2,1)S(1)}, bf16[1920,128]{1,0:T(8,128)(2,1)S(1)}, u32[]{:S(2)}, u32[]{:S(2)}) collective-permute-start(bf16[1920,128]{1,0:T(8,128)(2,1)S(1)} %collective-permute-done.5.side), channel_id=1, source_target_pairs={{0,16},{16,0},{32,48},{48,32},{64,80},{80,64},{96,112},{112,96},{1... | collective-permute-start | bytes 1474568 | tf_op jit(solution)/shard_map/ppermute | solution.py:224
  48.3 1.5 %collective-permute-done.9.other_side = bf16[1920,128]{1,0:T(8,128)(2,1)S(1)} collective-permute-done((bf16[1920,128]{1,0:T(8,128)(2,1)S(1)}, bf16[1920,128]{1,0:T(8,128)(2,1)S(1)}, u32[]{:S(2)}, u32[]{:S(2)}) %collective-permute-start.9) | collective-permute-done | bytes 491552 | tf_op jit(solution)/shard_map/ppermute | solution.py:224
  49.8 0.0 copy-done.2
  49.8 0.0 copy-done.1
  49.8 0.0 copy-done.3
  49.8 0.0 copy-done.4
  49.8 3.3 %tiles.1 = (bf16[16,144,128]{2,1,0:T(8,128)(2,1)}, f32[8,256,128]{2,1,0:T(8,128)S(1)}, bf16[8,256,128]{2,1,0:T(8,128)(2,1)S(1)}) custom-call(s32[32]{0:T(128)S(1)} %copy-done.3, s32[32]{0:T(128)S(1)} %copy-done.4, bf16[32,128,128]{2,1,0:T(8,128)(2,1)S(1)} %copy-done.2, bf16[640,128]{1,0:T(8,128)(2,1)S(1)} %copy-done.1, ...), custom_call_target="tpu_custom_call" | custom-call | flops 134217728 | bytes 6291456 | tf_op jit(solution)/shard_map/tiles/pallas_call | solution.py:272
  53.1 12.3 %all-to-all-start = ((bf16[16,144,128]{2,1,0:T(8,128)(2,1)}), bf16[16,144,128]{2,1,0:T(8,128)(2,1)S(1)}, u32[]{:S(2)}, u32[]{:S(2)}) async-start(bf16[16,144,128]{2,1,0:T(8,128)(2,1)} %get-tuple-element.21), calls=%async_computation | async-start | bytes 1179648 | tf_op jit(solution)/shard_map/all_to_all | solution.py:293
  65.4 4.8 %collective-permute-start.10 = (bf16[8,256,128]{2,1,0:T(8,128)(2,1)S(1)}, bf16[8,256,128]{2,1,0:T(8,128)(2,1)S(1)}, u32[]{:S(2)}, u32[]{:S(2)}) collective-permute-start(bf16[8,256,128]{2,1,0:T(8,128)(2,1)S(1)} %get-tuple-element.24), channel_id=1, source_target_pairs={{0,8},{1,9},{2,10},{3,11},{4,12},{5,13},{6,14},{7,15},{8,0},{9,1},... | collective-permute-start | bytes 1572872 | tf_op jit(solution)/shard_map/ppermute | solution.py:292
  70.2 12.5 %all-to-all-done.direct_ref = bf16[16,144,128]{2,1,0:T(8,128)(2,1)S(1)} async-done(((bf16[16,144,128]{2,1,0:T(8,128)(2,1)}), bf16[16,144,128]{2,1,0:T(8,128)(2,1)S(1)}, u32[]{:S(2)}, u32[]{:S(2)}) %all-to-all-start) | async-done | bytes 589856 | tf_op jit(solution)/shard_map/all_to_all | solution.py:293
  82.6 0.1 first.1
  82.7 5.2 %collective-permute-done.10.got_ref = bf16[8,256,128]{2,1,0:T(8,128)(2,1)S(1)} collective-permute-done((bf16[8,256,128]{2,1,0:T(8,128)(2,1)S(1)}, bf16[8,256,128]{2,1,0:T(8,128)(2,1)S(1)}, u32[]{:S(2)}, u32[]{:S(2)}) %collective-permute-start.10) | collective-permute-done | bytes 524320 | tf_op jit(solution)/shard_map/ppermute | solution.py:292
  87.9 0.1 pair.1
  88.0 22.1 %all_to_all.10.got_ref = bf16[8,288,128]{2,1,0:T(8,128)(2,1)S(1)} all-to-all(bf16[8,288,128]{2,1,0:T(8,128)(2,1)S(1)} %pair.1), channel_id=1, replica_groups={{0,1,2,3,4,5,6,7},{8,9,10,11,12,13,14,15},{16,17,18,19,20,21,22,23},{24..., dimensions={0} | all-to-all | bytes 1179648 | tf_op jit(solution)/shard_map/all_to_all | solution.py:311
  110.1 0.7 finish.1
  (3 shorter events, 0.1 us)
Async XLA Ops:
  3.0 10.0 %collective-permute-start = (bf16[640,128]{1,0:T(8,128)(2,1)}, bf16[640,128]{1,0:T(8,128)(2,1)S(1)}, u32[]{:S(2)}, u32[]{:S(2)}) collective-permute-start(bf16[640,128]{1,0:T(8,128)(2,1)} %adjoint.1.own), channel_id=1, source_target_pairs={{0,16},{16,0},{32,48},{48,32},{64,80},{80,64},{96,112},{112,96},{1... | collective-permute-start | bytes 491528 | tf_op jit(solution)/shard_map/ppermute | solution.py:224
  13.1 0.9 copy-start
  14.0 35.8 %copy-start.2 = (bf16[32,128,128]{2,1,0:T(8,128)(2,1)S(1)}, bf16[32,128,128]{2,1,0:T(8,128)(2,1)}, u32[]{:S(2)}) copy-start(bf16[32,128,128]{2,1,0:T(8,128)(2,1)} %tiles_ref.1) | copy-start | bytes 3145732
  14.0 14.5 %collective-permute-start.2 = (bf16[896,128]{1,0:T(8,128)(2,1)S(1)}, bf16[896,128]{1,0:T(8,128)(2,1)S(1)}, u32[]{:S(2)}, u32[]{:S(2)}) collective-permute-start(bf16[896,128]{1,0:T(8,128)(2,1)S(1)} %get-tuple-element.14), channel_id=1, source_target_pairs={{0,128},{16,400},{32,160},{48,432},{64,192},{80,464},{96,224},{112... | collective-permute-start | bytes 688136 | tf_op jit(solution)/shard_map/ppermute | solution.py:228
  16.1 12.4 %collective-permute-start.1 = (bf16[896,128]{1,0:T(8,128)(2,1)S(1)}, bf16[896,128]{1,0:T(8,128)(2,1)S(1)}, u32[]{:S(2)}, u32[]{:S(2)}) collective-permute-start(bf16[896,128]{1,0:T(8,128)(2,1)S(1)} %get-tuple-element.14), channel_id=1, source_target_pairs={{0,64},{16,464},{32,96},{48,496},{64,128},{80,16},{96,160},{112,48... | collective-permute-start | bytes 688136 | tf_op jit(solution)/shard_map/ppermute | solution.py:228
  18.0 9.5 %collective-permute-start.4 = (bf16[128,128]{1,0:T(8,128)(2,1)S(1)}, bf16[128,128]{1,0:T(8,128)(2,1)S(1)}, u32[]{:S(2)}, u32[]{:S(2)}) collective-permute-start(bf16[128,128]{1,0:T(8,128)(2,1)S(1)} %get-tuple-element.15.weight), channel_id=1, source_target_pairs={{0,256},{16,272},{32,288},{48,304},{64,320},{80,336},{96,352},{112... | collective-permute-start | bytes 98312 | tf_op jit(solution)/shard_map/ppermute | solution.py:228
  20.3 8.2 %collective-permute-start.3 = (bf16[128,128]{1,0:T(8,128)(2,1)S(1)}, bf16[128,128]{1,0:T(8,128)(2,1)S(1)}, u32[]{:S(2)}, u32[]{:S(2)}) collective-permute-start(bf16[128,128]{1,0:T(8,128)(2,1)S(1)} %get-tuple-element.15.weight), channel_id=1, source_target_pairs={{0,192},{16,336},{32,224},{48,368},{64,256},{80,400},{96,288},{112... | collective-permute-start | bytes 98312 | tf_op jit(solution)/shard_map/ppermute | solution.py:228
  28.5 16.9 %collective-permute-start.5 = (bf16[1920,128]{1,0:T(8,128)(2,1)S(1)}, bf16[1920,128]{1,0:T(8,128)(2,1)S(1)}, u32[]{:S(2)}, u32[]{:S(2)}) collective-permute-start(bf16[1920,128]{1,0:T(8,128)(2,1)S(1)} %get-tuple-element.16), channel_id=1, source_target_pairs={{0,32},{16,48},{32,0},{48,16},{64,96},{80,112},{96,64},{112,80},{1... | collective-permute-start | bytes 1474568 | tf_op jit(solution)/shard_map/ppermute | solution.py:224
  30.5 14.9 %collective-permute-start.6 = (bf16[1792,128]{1,0:T(8,128)(2,1)S(1)}, bf16[1792,128]{1,0:T(8,128)(2,1)S(1)}, u32[]{:S(2)}, u32[]{:S(2)}) collective-permute-start(bf16[1792,128]{1,0:T(8,128)(2,1)S(1)} %pad_maximum_fusion), channel_id=1, source_target_pairs={{0,16},{16,0},{32,48},{48,32},{64,80},{80,64},{96,112},{112,96},{1... | collective-permute-start | bytes 1376264 | tf_op jit(solution)/shard_map/ppermute | solution.py:224
  36.5 13.3 %copy-start.1 = (bf16[640,128]{1,0:T(8,128)(2,1)S(1)}, bf16[640,128]{1,0:T(8,128)(2,1)}, u32[]{:S(2)}) copy-start(bf16[640,128]{1,0:T(8,128)(2,1)} %adjoint.1.own) | copy-start | bytes 491524
  36.5 13.3 %copy-start.3 = (s32[32]{0:T(128)S(1)}, s32[32]{0:T(128)}, u32[]{:S(2)}) copy-start(s32[32]{0:T(128)} %in_ref.1) | copy-start | bytes 388
  36.5 13.3 %copy-start.4 = (s32[32]{0:T(128)S(1)}, s32[32]{0:T(128)}, u32[]{:S(2)}) copy-start(s32[32]{0:T(128)} %to_ref.1) | copy-start | bytes 388
  36.5 3.4 %collective-permute-start.7 = (bf16[512,128]{1,0:T(8,128)(2,1)S(1)}, bf16[512,128]{1,0:T(8,128)(2,1)S(1)}, u32[]{:S(2)}, u32[]{:S(2)}) collective-permute-start(bf16[512,128]{1,0:T(8,128)(2,1)S(1)} %get-tuple-element.17.weights), channel_id=1, source_target_pairs={{0,16},{16,0},{32,48},{48,32},{64,80},{80,64},{96,112},{112,96},{1... | collective-permute-start | bytes 393224 | tf_op jit(solution)/shard_map/ppermute | solution.py:224
  40.0 5.4 %collective-permute-start.8 = (f32[128,128]{1,0:T(8,128)S(1)}, f32[128,128]{1,0:T(8,128)S(1)}, u32[]{:S(2)}, u32[]{:S(2)}) collective-permute-start(f32[128,128]{1,0:T(8,128)S(1)} %planes.1.wsum), channel_id=1, source_target_pairs={{0,32},{16,48},{32,0},{48,16},{64,96},{80,112},{96,64},{112,80},{1... | collective-permute-start | bytes 196616 | tf_op jit(solution)/shard_map/ppermute | solution.py:224
  45.4 4.3 %collective-permute-start.9 = (bf16[1920,128]{1,0:T(8,128)(2,1)S(1)}, bf16[1920,128]{1,0:T(8,128)(2,1)S(1)}, u32[]{:S(2)}, u32[]{:S(2)}) collective-permute-start(bf16[1920,128]{1,0:T(8,128)(2,1)S(1)} %collective-permute-done.5.side), channel_id=1, source_target_pairs={{0,16},{16,0},{32,48},{48,32},{64,80},{80,64},{96,112},{112,96},{1... | collective-permute-start | bytes 1474568 | tf_op jit(solution)/shard_map/ppermute | solution.py:224
  53.1 29.6 %all-to-all-start = ((bf16[16,144,128]{2,1,0:T(8,128)(2,1)}), bf16[16,144,128]{2,1,0:T(8,128)(2,1)S(1)}, u32[]{:S(2)}, u32[]{:S(2)}) async-start(bf16[16,144,128]{2,1,0:T(8,128)(2,1)} %get-tuple-element.21), calls=%async_computation | async-start | bytes 1179648 | tf_op jit(solution)/shard_map/all_to_all | solution.py:293
  65.4 22.5 %collective-permute-start.10 = (bf16[8,256,128]{2,1,0:T(8,128)(2,1)S(1)}, bf16[8,256,128]{2,1,0:T(8,128)(2,1)S(1)}, u32[]{:S(2)}, u32[]{:S(2)}) collective-permute-start(bf16[8,256,128]{2,1,0:T(8,128)(2,1)S(1)} %get-tuple-element.24), channel_id=1, source_target_pairs={{0,8},{1,9},{2,10},{3,11},{4,12},{5,13},{6,14},{7,15},{8,0},{9,1},... | collective-permute-start | bytes 1572872 | tf_op jit(solution)/shard_map/ppermute | solution.py:292

commit v5 on v3

v5 whole, which is shorter than its diff:
```python
import functools

import jax
import jax.numpy as jnp
from jax import lax
from jax.experimental import pallas as pl
from jax.experimental.pallas import tpu as pltpu
from jax.sharding import PartitionSpec as P

BF = jnp.bfloat16
F32 = jnp.float32
SIDE = 128
PLANE = 4


def dot(a, b, contract):
    return lax.dot_general(a, b, ((contract[:1], contract[1:]), ((), ())), preferred_element_type=F32)


def adjoint_kernel(order_in, cot_in, pre_in, agg_in, w_in, out_ref, wpart_ref, order_ref, cot_ref, pre_ref, agg_ref, w_ref, sems):
    ins = (order_in, cot_in, pre_in, w_in, agg_in)
    held = (order_ref, cot_ref, pre_ref, w_ref, agg_ref)
    copies = [pltpu.make_async_copy(a, b, sems.at[i]) for i, (a, b) in enumerate(zip(ins, held))]
    for copy in copies:
        copy.start()
    for copy in copies:
        copy.wait()
    rows = cot_ref.shape[0]
    cot = cot_ref[...]
    row_id = lax.broadcasted_iota(jnp.int32, (rows, SIDE), 0)
    base = (lax.axis_index("row") * lax.axis_size("col") + lax.axis_index("col")) * rows
    total = jnp.zeros(wpart_ref.shape, F32)
    for b in range(rows // SIDE):
        span = slice(b * SIDE, (b + 1) * SIDE)
        local = order_ref[b : b + 1, :] - base
        pick = jnp.where(row_id == local, 1.0, 0.0).astype(BF)
        grad_rows = dot(pick, cot, (0, 0))
        grad_pre = jnp.where(pre_ref[span, :].astype(F32) > 0, grad_rows, 0.0).astype(BF)
        total += dot(agg_ref[span, :], grad_pre, (0, 0))
        out_ref[span, :] = dot(grad_pre, w_ref[...], (1, 1)).astype(BF)
    wpart_ref[...] = total


def block_place(block, row, planes, cols, blocks):
    device = lax.div(block, blocks)
    group = lax.div(device, cols)
    gap = lax.rem(lax.div(group, PLANE) - lax.div(row, PLANE) + planes, planes)
    core = lax.rem(group, 2)
    same_core = core == lax.rem(row, 2)
    same_chip = lax.rem(lax.div(group, 2), 2) == lax.rem(lax.div(row, 2), 2)
    below = gap > planes // 2
    steps = jnp.where(below, planes - gap, gap)
    receiver = jnp.where(gap == 0, 1 - core, jnp.where(below, 0, 1))
    place = (steps - 1) * 2 + jnp.where(core == receiver, 0, 1)
    place = jnp.where(same_chip, place, jnp.where(gap == 0, 4, 5 + place))
    slot = 2 + place + jnp.where(receiver == lax.rem(row, 2), 0, 9)
    slot = jnp.where((gap == 0) & same_chip, jnp.where(same_core, 0, 1), slot)
    return slot * blocks + lax.rem(block, blocks)


def tile_kernel(in_ref, to_ref, tiles_ref, own, beside, near, far, side, other_near, other_side, out_ref, blocks_ref, acc_ref):
    cols, rows, _ = out_ref.shape
    blocks = rows // SIDE
    at = 0
    for piece in (own, beside, near, far, side, other_near, other_side):
        blocks_ref[at : at + piece.shape[0], :] = piece[...]
        at += piece.shape[0]
    acc_ref[...] = jnp.zeros_like(acc_ref)
    row = lax.axis_index("row")
    planes = lax.axis_size("row") // PLANE

    def one(t, carry):
        at = pl.multiple_of(block_place(in_ref[t], row, planes, cols, blocks) * SIDE, SIDE)
        to = to_ref[t] - row * cols * blocks
        acc_ref[to] += dot(tiles_ref[t], blocks_ref[pl.ds(at, SIDE), :], (1, 0))
        return carry

    lax.fori_loop(0, tiles_ref.shape[0], one, 0, unroll=8)
    for c in range(cols):
        for b in range(blocks):
            out_ref[c, b * SIDE : (b + 1) * SIDE, :] = acc_ref[c * blocks + b].astype(BF)


def finish_kernel(scale, got_ref, wsum_ref, out_ref, wgrad_ref):
    total = got_ref[0].astype(F32)
    for c in range(1, got_ref.shape[0]):
        total += got_ref[c].astype(F32)
    out_ref[...] = total.astype(BF)
    wgrad_ref[...] = wsum_ref[...] * scale


def vmem():
    return pl.BlockSpec(memory_space=pltpu.VMEM)


def smem():
    return pl.BlockSpec(memory_space=pltpu.SMEM)


def on_device(cotangent, pre_act, aggregated, weight, tile_values, tile_in, tile_out, order):
    row_count = lax.axis_size("row")
    col_count = lax.axis_size("col")
    nodes, feat = cotangent.shape
    blocks_dev = nodes // SIDE
    params = pltpu.CompilerParams(vmem_limit_bytes=12 << 20)
    small = pltpu.CompilerParams(vmem_limit_bytes=4 << 20)

    adjoint, wpart = pl.pallas_call(
        adjoint_kernel,
        out_shape=(jax.ShapeDtypeStruct((nodes, feat), BF), jax.ShapeDtypeStruct((feat, feat), F32)),
        in_specs=[pl.BlockSpec(memory_space=pltpu.HBM)] * 5,
        out_specs=(vmem(), vmem()),
        scratch_shapes=[
            pltpu.VMEM((blocks_dev, SIDE), jnp.int32),
            pltpu.VMEM((nodes, feat), BF),
            pltpu.VMEM((nodes, feat), BF),
            pltpu.VMEM((nodes, feat), BF),
            pltpu.VMEM((feat, feat), BF),
            pltpu.SemaphoreType.DMA((5,)),
        ],
        compiler_params=pltpu.CompilerParams(vmem_limit_bytes=60 << 20),
        name="adjoint",
    )(order.reshape(blocks_dev, SIDE), cotangent, pre_act, aggregated, weight)

    def swap(value, bit):
        return lax.ppermute(value, "row", [(i, i ^ bit) for i in range(row_count)])

    def to_plane(value, steps):
        pairs = [(i, (i + PLANE * (steps if i % 2 == 0 else -steps)) % row_count) for i in range(row_count)]
        return lax.ppermute(value, "row", pairs)

    def partner(value, axis, bit):
        return lax.ppermute(value, axis, [(i, i ^ bit) for i in range(lax.axis_size(axis))])

    beside = swap(adjoint, 1)
    chip = jnp.concatenate([adjoint, beside])
    near = to_plane(chip, 1)
    far = to_plane(chip, 2)
    z_bits = [1 << k for k in reversed(range((col_count // 2 - 1).bit_length()))]
    late_bits = [("row", 1 << k) for k in range((row_count - 1).bit_length())] + [("col", col_count // 2)]
    wsum = wpart
    for bit in z_bits[:-2]:
        wsum = wsum + partner(wsum, "col", bit)
    across, wsum = lax.optimization_barrier((jnp.concatenate([beside, near, far]), wsum))
    side = swap(across, 2)
    other_near = swap(jnp.concatenate([near, far]), 1)
    for bit in z_bits[-2:-1]:
        wsum = wsum + partner(wsum, "col", bit)
    side, other_near, wsum = lax.optimization_barrier((side, other_near, wsum))
    wnext = [partner(wsum, "col", bit) for bit in z_bits[-1:]]
    other_side = swap(side, 1)

    tiles = tile_values.shape[0]
    sends = pl.pallas_call(
        tile_kernel,
        out_shape=jax.ShapeDtypeStruct((col_count, nodes, feat), BF),
        in_specs=[smem(), smem()] + [vmem()] * 8,
        out_specs=vmem(),
        scratch_shapes=[
            pltpu.VMEM((20 * nodes, feat), BF),
            pltpu.VMEM((col_count * blocks_dev, SIDE, feat), F32),
        ],
        compiler_params=params,
        cost_estimate=pl.CostEstimate(
            flops=2 * tiles * SIDE * SIDE * feat, bytes_accessed=6 << 20, transcendentals=0
        ),
        name="tiles",
    )(tile_in, tile_out, tile_values, adjoint, beside, near, far, side, other_near, other_side)

    sends, wsum, wnext = lax.optimization_barrier((sends, wsum, wnext))
    got = lax.all_to_all(sends, "col", 0, 0)
    for value in wnext:
        wsum = wsum + value
    for axis, bit in late_bits:
        wsum = wsum + partner(wsum, axis, bit)
    scale = 1.0 / float(nodes * row_count * col_count) ** 0.5
    node_grad, weight_grad = pl.pallas_call(
        functools.partial(finish_kernel, scale),
        out_shape=(jax.ShapeDtypeStruct((nodes, feat), BF), jax.ShapeDtypeStruct((feat, feat), F32)),
        in_specs=[vmem(), vmem()],
        out_specs=(vmem(), vmem()),
        compiler_params=small,
        name="finish",
    )(got, wsum)
    return (node_grad, weight_grad)


def solution(mesh):
    split = P(("row", "col"))
    return jax.shard_map(
        on_device,
        mesh=mesh,
        in_specs=(split, split, split, P(), split, split, split, split),
        out_specs=(split, P()),
        check_vma=False,
    )
```

time: 143 us -> 109 us (0.76)
  the two profiles are of different devices: /device:TPU:8 before, /device:TPU:6 now
where the time goes in v5:
time: 109 us; the launch traced here: 108 us
  starting transfers between devices  62.5 us (57%)
  waiting for transfers between devices  35.8 us (33%)
  Pallas kernels  6.95 us (6%)
    ppermute x9, waiting for transfers between devices, partner(): lax.ppermute(value, axis, [(i, i ^ bit) for i in range(lax.axis_size(axis...  33.8 us
    ppermute x9, starting transfers between devices, partner(): lax.ppermute(value, axis, [(i, i ^ bit) for i in range(lax.axis_size(axis...  33.5 us
    all_to_all x1, starting transfers between devices, on_device(): got = lax.all_to_all(sends, 'col', 0, 0)  11.1 us
    ppermute x4, starting transfers between devices, swap(): return lax.ppermute(value, 'row', [(i, i ^ bit) for i in range(row_count)])  9.85 us
    ppermute x2, starting transfers between devices, to_plane(): return lax.ppermute(value, 'row', pairs)  7.98 us
    pallas_call x1, Pallas kernels, on_device(): pl.pallas_call(tile_kernel, out_shape=jax.ShapeDtypeStruct((col_count, no...  3.61 us
    pallas_call x1, Pallas kernels, on_device(): pl.pallas_call(adjoint_kernel, out_shape=(jax.ShapeDtypeStruct((nodes, fe...  2.48 us
  transfers between devices with their start and end apart: 16, of which 10 were waited for; matrix products, arithmetic and copies ran while one was open for 2% of the time, Pallas kernels for 3%

profile of v5, /device:TPU:6, one launch (start us, length us, event | category | flops | bytes accessed | tf_op | source)
XLA Modules:
  0.0 108.1 jit_solution(5970713731779294884)
XLA Ops:
  0.6 0.0 copy-start
  0.6 0.0 copy-start.2
  0.7 0.0 copy-start.3
  0.7 2.5 %adjoint.1 = (bf16[384,128]{1,0:T(8,128)(2,1)}, f32[128,128]{1,0:T(8,128)}) custom-call(s32[3,128]{1,0:T(4,128)} %bitcast.1, bf16[384,128]{1,0:T(8,128)(2,1)} %cot_in.1, bf16[384,128]{1,0:T(8,128)(2,1)} %pre_in.1, bf16[384,128]{1,0:T(8,128)(2,1)} %agg_in.1, bf16[128,128]{1,0:T(8,128)(2,1)} %w_in.1), custom_call_target="tpu_custom_call" | custom-call | tf_op jit(solution)/shard_map/adjoint/pallas_call | solution.py:108
  3.1 0.0 copy-start.1
  3.2 2.1 %collective-permute-start = (bf16[384,128]{1,0:T(8,128)(2,1)}, bf16[384,128]{1,0:T(8,128)(2,1)S(1)}, u32[]{:S(2)}, u32[]{:S(2)}) collective-permute-start(bf16[384,128]{1,0:T(8,128)(2,1)} %get-tuple-element.12.own), channel_id=1, source_target_pairs={{0,16},{16,0},{32,48},{48,32},{64,80},{80,64},{96,112},{112,96},{1... | collective-permute-start | bytes 294920 | tf_op jit(solution)/shard_map/ppermute | solution.py:126
  5.2 0.9 constant_dynamic-update-slice_fusion.1
  6.1 0.6 collective-permute-done.beside
  6.7 3.5 %collective-permute-start.1 = (bf16[768,128]{1,0:T(8,128)(2,1)S(1)}, bf16[768,128]{1,0:T(8,128)(2,1)S(1)}, u32[]{:S(2)}, u32[]{:S(2)}) collective-permute-start(bf16[768,128]{1,0:T(8,128)(2,1)S(1)} %constant_dynamic-update-slice_fusion), channel_id=1, source_target_pairs={{0,64},{16,464},{32,96},{48,496},{64,128},{80,16},{96,160},{112,48... | collective-permute-start | bytes 589832 | tf_op jit(solution)/shard_map/ppermute | solution.py:130
  10.2 4.5 %collective-permute-start.2 = (bf16[768,128]{1,0:T(8,128)(2,1)S(1)}, bf16[768,128]{1,0:T(8,128)(2,1)S(1)}, u32[]{:S(2)}, u32[]{:S(2)}) collective-permute-start(bf16[768,128]{1,0:T(8,128)(2,1)S(1)} %constant_dynamic-update-slice_fusion), channel_id=1, source_target_pairs={{0,128},{16,400},{32,160},{48,432},{64,192},{80,464},{96,224},{112... | collective-permute-start | bytes 589832 | tf_op jit(solution)/shard_map/ppermute | solution.py:130
  14.7 10.9 %collective-permute-start.3 = (f32[128,128]{1,0:T(8,128)}, f32[128,128]{1,0:T(8,128)S(1)}, u32[]{:S(2)}, u32[]{:S(2)}) collective-permute-start(f32[128,128]{1,0:T(8,128)} %get-tuple-element.13), channel_id=1, source_target_pairs={{0,4},{1,5},{2,6},{3,7},{4,0},{5,1},{6,2},{7,3},{8,12},{9,13},{10,... | collective-permute-start | bytes 196616 | tf_op jit(solution)/shard_map/ppermute | solution.py:133
  25.6 2.9 %collective-permute-done.3 = f32[128,128]{1,0:T(8,128)S(1)} collective-permute-done((f32[128,128]{1,0:T(8,128)}, f32[128,128]{1,0:T(8,128)S(1)}, u32[]{:S(2)}, u32[]{:S(2)}) %collective-permute-start.3) | collective-permute-done | bytes 65568 | tf_op jit(solution)/shard_map/ppermute | solution.py:133
  28.5 0.8 add.27
  29.4 0.0 collective-permute-done.1.near
  29.4 0.0 collective-permute-done.2.far
  29.4 2.7 %collective-permute-start.4 = (bf16[1920,128]{1,0:T(8,128)(2,1)S(1)}, bf16[1920,128]{1,0:T(8,128)(2,1)S(1)}, u32[]{:S(2)}, u32[]{:S(2)}) collective-permute-start(bf16[1920,128]{1,0:T(8,128)(2,1)S(1)} %pad_maximum_fusion), channel_id=1, source_target_pairs={{0,32},{16,48},{32,0},{48,16},{64,96},{80,112},{96,64},{112,80},{1... | collective-permute-start | bytes 1474568 | tf_op jit(solution)/shard_map/ppermute | solution.py:126
  32.2 3.0 %collective-permute-start.5 = (bf16[1536,128]{1,0:T(8,128)(2,1)S(1)}, bf16[1536,128]{1,0:T(8,128)(2,1)S(1)}, u32[]{:S(2)}, u32[]{:S(2)}) collective-permute-start(bf16[1536,128]{1,0:T(8,128)(2,1)S(1)} %pad_maximum_fusion.1), channel_id=1, source_target_pairs={{0,16},{16,0},{32,48},{48,32},{64,80},{80,64},{96,112},{112,96},{1... | collective-permute-start | bytes 1179656 | tf_op jit(solution)/shard_map/ppermute | solution.py:126
  35.2 4.9 %collective-permute-start.6 = (f32[128,128]{1,0:T(8,128)S(1)}, f32[128,128]{1,0:T(8,128)S(1)}, u32[]{:S(2)}, u32[]{:S(2)}) collective-permute-start(f32[128,128]{1,0:T(8,128)S(1)} %add.27), channel_id=1, source_target_pairs={{0,2},{1,3},{2,0},{3,1},{4,6},{5,7},{6,4},{7,5},{8,10},{9,11},{10,... | collective-permute-start | bytes 196616 | tf_op jit(solution)/shard_map/ppermute | solution.py:133
  40.1 3.5 %collective-permute-done.6 = f32[128,128]{1,0:T(8,128)S(1)} collective-permute-done((f32[128,128]{1,0:T(8,128)S(1)}, f32[128,128]{1,0:T(8,128)S(1)}, u32[]{:S(2)}, u32[]{:S(2)}) %collective-permute-start.6) | collective-permute-done | bytes 65568 | tf_op jit(solution)/shard_map/ppermute | solution.py:133
  43.7 0.0 collective-permute-done.5.other_near
  43.7 1.4 %collective-permute-done.4.side = bf16[1920,128]{1,0:T(8,128)(2,1)S(1)} collective-permute-done((bf16[1920,128]{1,0:T(8,128)(2,1)S(1)}, bf16[1920,128]{1,0:T(8,128)(2,1)S(1)}, u32[]{:S(2)}, u32[]{:S(2)}) %collective-permute-start.4) | collective-permute-done | bytes 491552 | tf_op jit(solution)/shard_map/ppermute | solution.py:126
  45.1 2.1 %collective-permute-start.7 = (bf16[1920,128]{1,0:T(8,128)(2,1)S(1)}, bf16[1920,128]{1,0:T(8,128)(2,1)S(1)}, u32[]{:S(2)}, u32[]{:S(2)}) collective-permute-start(bf16[1920,128]{1,0:T(8,128)(2,1)S(1)} %collective-permute-done.4.side), channel_id=1, source_target_pairs={{0,16},{16,0},{32,48},{48,32},{64,80},{80,64},{96,112},{112,96},{1... | collective-permute-start | bytes 1474568 | tf_op jit(solution)/shard_map/ppermute | solution.py:126
  47.2 2.7 %collective-permute-start.8 = (f32[128,128]{1,0:T(8,128)S(1)}, f32[128,128]{1,0:T(8,128)S(1)}, u32[]{:S(2)}, u32[]{:S(2)}) collective-permute-start(f32[128,128]{1,0:T(8,128)S(1)} %add.28), channel_id=1, source_target_pairs={{0,1},{1,0},{2,3},{3,2},{4,5},{5,4},{6,7},{7,6},{8,9},{9,8},{10,11... | collective-permute-start | bytes 196616 | tf_op jit(solution)/shard_map/ppermute | solution.py:133
  49.8 0.0 collective-permute-done.7.other_side
  49.8 0.0 copy-done
  49.9 0.0 copy-done.2
  49.9 0.0 copy-done.3
  49.9 0.0 copy-done.1
  49.9 3.6 %tiles.1 = bf16[16,384,128]{2,1,0:T(8,128)(2,1)} custom-call(s32[32]{0:T(128)S(1)} %copy-done.2, s32[32]{0:T(128)S(1)} %copy-done.3, bf16[32,128,128]{2,1,0:T(8,128)(2,1)S(1)} %copy-done, bf16[384,128]{1,0:T(8,128)(2,1)S(1)} %copy-done.1, bf16[384,128]{1,0:T(8,128)(2,1)S(1)} %collective-permute-done.beside, ...), custom_call_target="tpu_custom_call" | custom-call | flops 134217728 | bytes 6291456 | tf_op jit(solution)/shard_map/tiles/pallas_call | solution.py:154
  53.5 0.0 collective-permute-done.8
  53.5 11.1 %all-to-all-start = ((bf16[16,384,128]{2,1,0:T(8,128)(2,1)}), bf16[16,384,128]{2,1,0:T(8,128)(2,1)S(1)}, u32[]{:S(2)}, u32[]{:S(2)}) async-start(bf16[16,384,128]{2,1,0:T(8,128)(2,1)} %tiles.1), calls=%async_computation | async-start | bytes 3145728 | tf_op jit(solution)/shard_map/all_to_all | solution.py:171
  64.6 1.9 %collective-permute-start.9 = (f32[128,128]{1,0:T(8,128)S(1)}, f32[128,128]{1,0:T(8,128)S(1)}, u32[]{:S(2)}, u32[]{:S(2)}) collective-permute-start(f32[128,128]{1,0:T(8,128)S(1)} %add.29), channel_id=1, source_target_pairs={{0,16},{16,0},{32,48},{48,32},{64,80},{80,64},{96,112},{112,96},{1... | collective-permute-start | bytes 196616 | tf_op jit(solution)/shard_map/ppermute | solution.py:133
  66.5 1.2 %collective-permute-done.9 = f32[128,128]{1,0:T(8,128)S(1)} collective-permute-done((f32[128,128]{1,0:T(8,128)S(1)}, f32[128,128]{1,0:T(8,128)S(1)}, u32[]{:S(2)}, u32[]{:S(2)}) %collective-permute-start.9) | collective-permute-done | bytes 65568 | tf_op jit(solution)/shard_map/ppermute | solution.py:133
  67.8 2.7 %collective-permute-start.10 = (f32[128,128]{1,0:T(8,128)S(1)}, f32[128,128]{1,0:T(8,128)S(1)}, u32[]{:S(2)}, u32[]{:S(2)}) collective-permute-start(f32[128,128]{1,0:T(8,128)S(1)} %add.30), channel_id=1, source_target_pairs={{0,32},{16,48},{32,0},{48,16},{64,96},{80,112},{96,64},{112,80},{1... | collective-permute-start | bytes 196616 | tf_op jit(solution)/shard_map/ppermute | solution.py:133
  70.5 4.3 %collective-permute-done.10 = f32[128,128]{1,0:T(8,128)S(1)} collective-permute-done((f32[128,128]{1,0:T(8,128)S(1)}, f32[128,128]{1,0:T(8,128)S(1)}, u32[]{:S(2)}, u32[]{:S(2)}) %collective-permute-start.10) | collective-permute-done | bytes 65568 | tf_op jit(solution)/shard_map/ppermute | solution.py:133
  74.8 2.5 %collective-permute-start.11 = (f32[128,128]{1,0:T(8,128)S(1)}, f32[128,128]{1,0:T(8,128)S(1)}, u32[]{:S(2)}, u32[]{:S(2)}) collective-permute-start(f32[128,128]{1,0:T(8,128)S(1)} %add.31), channel_id=1, source_target_pairs={{0,64},{16,80},{32,96},{48,112},{64,0},{80,16},{96,32},{112,48},{1... | collective-permute-start | bytes 196616 | tf_op jit(solution)/shard_map/ppermute | solution.py:133
  77.4 3.6 %collective-permute-done.11 = f32[128,128]{1,0:T(8,128)S(1)} collective-permute-done((f32[128,128]{1,0:T(8,128)S(1)}, f32[128,128]{1,0:T(8,128)S(1)}, u32[]{:S(2)}, u32[]{:S(2)}) %collective-permute-start.11) | collective-permute-done | bytes 65568 | tf_op jit(solution)/shard_map/ppermute | solution.py:133
  81.0 2.6 %collective-permute-start.12 = (f32[128,128]{1,0:T(8,128)S(1)}, f32[128,128]{1,0:T(8,128)S(1)}, u32[]{:S(2)}, u32[]{:S(2)}) collective-permute-start(f32[128,128]{1,0:T(8,128)S(1)} %add.32), channel_id=1, source_target_pairs={{0,128},{16,144},{32,160},{48,176},{64,192},{80,208},{96,224},{112... | collective-permute-start | bytes 196616 | tf_op jit(solution)/shard_map/ppermute | solution.py:133
  83.6 5.1 %collective-permute-done.12 = f32[128,128]{1,0:T(8,128)S(1)} collective-permute-done((f32[128,128]{1,0:T(8,128)S(1)}, f32[128,128]{1,0:T(8,128)S(1)}, u32[]{:S(2)}, u32[]{:S(2)}) %collective-permute-start.12) | collective-permute-done | bytes 65568 | tf_op jit(solution)/shard_map/ppermute | solution.py:133
  88.8 2.2 %collective-permute-start.13 = (f32[128,128]{1,0:T(8,128)S(1)}, f32[128,128]{1,0:T(8,128)S(1)}, u32[]{:S(2)}, u32[]{:S(2)}) collective-permute-start(f32[128,128]{1,0:T(8,128)S(1)} %add.33), channel_id=1, source_target_pairs={{0,256},{16,272},{32,288},{48,304},{64,320},{80,336},{96,352},{112... | collective-permute-start | bytes 196616 | tf_op jit(solution)/shard_map/ppermute | solution.py:133
  90.9 8.6 %collective-permute-done.13 = f32[128,128]{1,0:T(8,128)S(1)} collective-permute-done((f32[128,128]{1,0:T(8,128)S(1)}, f32[128,128]{1,0:T(8,128)S(1)}, u32[]{:S(2)}, u32[]{:S(2)}) %collective-permute-start.13) | collective-permute-done | bytes 65568 | tf_op jit(solution)/shard_map/ppermute | solution.py:133
  99.6 3.1 %collective-permute-start.14 = (f32[128,128]{1,0:T(8,128)S(1)}, f32[128,128]{1,0:T(8,128)S(1)}, u32[]{:S(2)}, u32[]{:S(2)}) collective-permute-start(f32[128,128]{1,0:T(8,128)S(1)} %add.34), channel_id=1, source_target_pairs={{0,8},{1,9},{2,10},{3,11},{4,12},{5,13},{6,14},{7,15},{8,0},{9,1},... | collective-permute-start | bytes 196616 | tf_op jit(solution)/shard_map/ppermute | solution.py:133
  102.7 4.5 %collective-permute-done.14 = f32[128,128]{1,0:T(8,128)S(1)} collective-permute-done((f32[128,128]{1,0:T(8,128)S(1)}, f32[128,128]{1,0:T(8,128)S(1)}, u32[]{:S(2)}, u32[]{:S(2)}) %collective-permute-start.14) | collective-permute-done | bytes 65568 | tf_op jit(solution)/shard_map/ppermute | solution.py:133
  107.2 0.0 all-to-all-done.got_ref
  107.2 0.9 finish.1
  (11 shorter events, 0.1 us)
Async XLA Ops:
  0.6 49.2 %copy-start = (bf16[32,128,128]{2,1,0:T(8,128)(2,1)S(1)}, bf16[32,128,128]{2,1,0:T(8,128)(2,1)}, u32[]{:S(2)}) copy-start(bf16[32,128,128]{2,1,0:T(8,128)(2,1)} %tiles_ref.1) | copy-start | bytes 3145732
  0.6 49.2 %copy-start.2 = (s32[32]{0:T(128)S(1)}, s32[32]{0:T(128)}, u32[]{:S(2)}) copy-start(s32[32]{0:T(128)} %in_ref.1) | copy-start | bytes 388
  0.7 49.2 %copy-start.3 = (s32[32]{0:T(128)S(1)}, s32[32]{0:T(128)}, u32[]{:S(2)}) copy-start(s32[32]{0:T(128)} %to_ref.1) | copy-start | bytes 388
  3.1 46.7 %copy-start.1 = (bf16[384,128]{1,0:T(8,128)(2,1)S(1)}, bf16[384,128]{1,0:T(8,128)(2,1)}, u32[]{:S(2)}) copy-start(bf16[384,128]{1,0:T(8,128)(2,1)} %get-tuple-element.12.own) | copy-start | bytes 294916
  3.2 3.5 %collective-permute-start = (bf16[384,128]{1,0:T(8,128)(2,1)}, bf16[384,128]{1,0:T(8,128)(2,1)S(1)}, u32[]{:S(2)}, u32[]{:S(2)}) collective-permute-start(bf16[384,128]{1,0:T(8,128)(2,1)} %get-tuple-element.12.own), channel_id=1, source_target_pairs={{0,16},{16,0},{32,48},{48,32},{64,80},{80,64},{96,112},{112,96},{1... | collective-permute-start | bytes 294920 | tf_op jit(solution)/shard_map/ppermute | solution.py:126
  6.7 22.7 %collective-permute-start.1 = (bf16[768,128]{1,0:T(8,128)(2,1)S(1)}, bf16[768,128]{1,0:T(8,128)(2,1)S(1)}, u32[]{:S(2)}, u32[]{:S(2)}) collective-permute-start(bf16[768,128]{1,0:T(8,128)(2,1)S(1)} %constant_dynamic-update-slice_fusion), channel_id=1, source_target_pairs={{0,64},{16,464},{32,96},{48,496},{64,128},{80,16},{96,160},{112,48... | collective-permute-start | bytes 589832 | tf_op jit(solution)/shard_map/ppermute | solution.py:130
  10.2 19.2 %collective-permute-start.2 = (bf16[768,128]{1,0:T(8,128)(2,1)S(1)}, bf16[768,128]{1,0:T(8,128)(2,1)S(1)}, u32[]{:S(2)}, u32[]{:S(2)}) collective-permute-start(bf16[768,128]{1,0:T(8,128)(2,1)S(1)} %constant_dynamic-update-slice_fusion), channel_id=1, source_target_pairs={{0,128},{16,400},{32,160},{48,432},{64,192},{80,464},{96,224},{112... | collective-permute-start | bytes 589832 | tf_op jit(solution)/shard_map/ppermute | solution.py:130
  14.7 13.8 %collective-permute-start.3 = (f32[128,128]{1,0:T(8,128)}, f32[128,128]{1,0:T(8,128)S(1)}, u32[]{:S(2)}, u32[]{:S(2)}) collective-permute-start(f32[128,128]{1,0:T(8,128)} %get-tuple-element.13), channel_id=1, source_target_pairs={{0,4},{1,5},{2,6},{3,7},{4,0},{5,1},{6,2},{7,3},{8,12},{9,13},{10,... | collective-permute-start | bytes 196616 | tf_op jit(solution)/shard_map/ppermute | solution.py:133
  29.4 15.7 %collective-permute-start.4 = (bf16[1920,128]{1,0:T(8,128)(2,1)S(1)}, bf16[1920,128]{1,0:T(8,128)(2,1)S(1)}, u32[]{:S(2)}, u32[]{:S(2)}) collective-permute-start(bf16[1920,128]{1,0:T(8,128)(2,1)S(1)} %pad_maximum_fusion), channel_id=1, source_target_pairs={{0,32},{16,48},{32,0},{48,16},{64,96},{80,112},{96,64},{112,80},{1... | collective-permute-start | bytes 1474568 | tf_op jit(solution)/shard_map/ppermute | solution.py:126
  32.2 11.4 %collective-permute-start.5 = (bf16[1536,128]{1,0:T(8,128)(2,1)S(1)}, bf16[1536,128]{1,0:T(8,128)(2,1)S(1)}, u32[]{:S(2)}, u32[]{:S(2)}) collective-permute-start(bf16[1536,128]{1,0:T(8,128)(2,1)S(1)} %pad_maximum_fusion.1), channel_id=1, source_target_pairs={{0,16},{16,0},{32,48},{48,32},{64,80},{80,64},{96,112},{112,96},{1... | collective-permute-start | bytes 1179656 | tf_op jit(solution)/shard_map/ppermute | solution.py:126
  35.2 8.4 %collective-permute-start.6 = (f32[128,128]{1,0:T(8,128)S(1)}, f32[128,128]{1,0:T(8,128)S(1)}, u32[]{:S(2)}, u32[]{:S(2)}) collective-permute-start(f32[128,128]{1,0:T(8,128)S(1)} %add.27), channel_id=1, source_target_pairs={{0,2},{1,3},{2,0},{3,1},{4,6},{5,7},{6,4},{7,5},{8,10},{9,11},{10,... | collective-permute-start | bytes 196616 | tf_op jit(solution)/shard_map/ppermute | solution.py:133
  45.1 4.7 %collective-permute-start.7 = (bf16[1920,128]{1,0:T(8,128)(2,1)S(1)}, bf16[1920,128]{1,0:T(8,128)(2,1)S(1)}, u32[]{:S(2)}, u32[]{:S(2)}) collective-permute-start(bf16[1920,128]{1,0:T(8,128)(2,1)S(1)} %collective-permute-done.4.side), channel_id=1, source_target_pairs={{0,16},{16,0},{32,48},{48,32},{64,80},{80,64},{96,112},{112,96},{1... | collective-permute-start | bytes 1474568 | tf_op jit(solution)/shard_map/ppermute | solution.py:126
  47.2 6.3 %collective-permute-start.8 = (f32[128,128]{1,0:T(8,128)S(1)}, f32[128,128]{1,0:T(8,128)S(1)}, u32[]{:S(2)}, u32[]{:S(2)}) collective-permute-start(f32[128,128]{1,0:T(8,128)S(1)} %add.28), channel_id=1, source_target_pairs={{0,1},{1,0},{2,3},{3,2},{4,5},{5,4},{6,7},{7,6},{8,9},{9,8},{10,11... | collective-permute-start | bytes 196616 | tf_op jit(solution)/shard_map/ppermute | solution.py:133
  53.5 53.7 %all-to-all-start = ((bf16[16,384,128]{2,1,0:T(8,128)(2,1)}), bf16[16,384,128]{2,1,0:T(8,128)(2,1)S(1)}, u32[]{:S(2)}, u32[]{:S(2)}) async-start(bf16[16,384,128]{2,1,0:T(8,128)(2,1)} %tiles.1), calls=%async_computation | async-start | bytes 3145728 | tf_op jit(solution)/shard_map/all_to_all | solution.py:171
  64.6 3.1 %collective-permute-start.9 = (f32[128,128]{1,0:T(8,128)S(1)}, f32[128,128]{1,0:T(8,128)S(1)}, u32[]{:S(2)}, u32[]{:S(2)}) collective-permute-start(f32[128,128]{1,0:T(8,128)S(1)} %add.29), channel_id=1, source_target_pairs={{0,16},{16,0},{32,48},{48,32},{64,80},{80,64},{96,112},{112,96},{1... | collective-permute-start | bytes 196616 | tf_op jit(solution)/shard_map/ppermute | solution.py:133
  67.8 7.0 %collective-permute-start.10 = (f32[128,128]{1,0:T(8,128)S(1)}, f32[128,128]{1,0:T(8,128)S(1)}, u32[]{:S(2)}, u32[]{:S(2)}) collective-permute-start(f32[128,128]{1,0:T(8,128)S(1)} %add.30), channel_id=1, source_target_pairs={{0,32},{16,48},{32,0},{48,16},{64,96},{80,112},{96,64},{112,80},{1... | collective-permute-start | bytes 196616 | tf_op jit(solution)/shard_map/ppermute | solution.py:133
  74.8 6.2 %collective-permute-start.11 = (f32[128,128]{1,0:T(8,128)S(1)}, f32[128,128]{1,0:T(8,128)S(1)}, u32[]{:S(2)}, u32[]{:S(2)}) collective-permute-start(f32[128,128]{1,0:T(8,128)S(1)} %add.31), channel_id=1, source_target_pairs={{0,64},{16,80},{32,96},{48,112},{64,0},{80,16},{96,32},{112,48},{1... | collective-permute-start | bytes 196616 | tf_op jit(solution)/shard_map/ppermute | solution.py:133
  81.0 7.8 %collective-permute-start.12 = (f32[128,128]{1,0:T(8,128)S(1)}, f32[128,128]{1,0:T(8,128)S(1)}, u32[]{:S(2)}, u32[]{:S(2)}) collective-permute-start(f32[128,128]{1,0:T(8,128)S(1)} %add.32), channel_id=1, source_target_pairs={{0,128},{16,144},{32,160},{48,176},{64,192},{80,208},{96,224},{112... | collective-permute-start | bytes 196616 | tf_op jit(solution)/shard_map/ppermute | solution.py:133
  88.8 10.8 %collective-permute-start.13 = (f32[128,128]{1,0:T(8,128)S(1)}, f32[128,128]{1,0:T(8,128)S(1)}, u32[]{:S(2)}, u32[]{:S(2)}) collective-permute-start(f32[128,128]{1,0:T(8,128)S(1)} %add.33), channel_id=1, source_target_pairs={{0,256},{16,272},{32,288},{48,304},{64,320},{80,336},{96,352},{112... | collective-permute-start | bytes 196616 | tf_op jit(solution)/shard_map/ppermute | solution.py:133
  99.6 7.7 %collective-permute-start.14 = (f32[128,128]{1,0:T(8,128)S(1)}, f32[128,128]{1,0:T(8,128)S(1)}, u32[]{:S(2)}, u32[]{:S(2)}) collective-permute-start(f32[128,128]{1,0:T(8,128)S(1)} %add.34), channel_id=1, source_target_pairs={{0,8},{1,9},{2,10},{3,11},{4,12},{5,13},{6,14},{7,15},{8,0},{9,1},... | collective-permute-start | bytes 196616 | tf_op jit(solution)/shard_map/ppermute | solution.py:133

commit v6 on v5

--- a/solution.py
+++ b/solution.py
@@ -29,7 +29,7 @@
     cot = cot_ref[...]
     row_id = lax.broadcasted_iota(jnp.int32, (rows, SIDE), 0)
     base = (lax.axis_index("row") * lax.axis_size("col") + lax.axis_index("col")) * rows
-    total = jnp.zeros(wpart_ref.shape, F32)
+    total = jnp.zeros(w_ref.shape, F32)
     for b in range(rows // SIDE):
         span = slice(b * SIDE, (b + 1) * SIDE)
         local = order_ref[b : b + 1, :] - base
@@ -38,7 +38,8 @@
         grad_pre = jnp.where(pre_ref[span, :].astype(F32) > 0, grad_rows, 0.0).astype(BF)
         total += dot(agg_ref[span, :], grad_pre, (0, 0))
         out_ref[span, :] = dot(grad_pre, w_ref[...], (1, 1)).astype(BF)
-    wpart_ref[...] = total
+    for z in range(wpart_ref.shape[0]):
+        wpart_ref[z] = total.astype(BF)
 
 
 def block_place(block, row, planes, cols, blocks):
@@ -50,7 +51,7 @@
     same_chip = lax.rem(lax.div(group, 2), 2) == lax.rem(lax.div(row, 2), 2)
     below = gap > planes // 2
     steps = jnp.where(below, planes - gap, gap)
-    receiver = jnp.where(gap == 0, 1 - core, jnp.where(below, 0, 1))
+    receiver = jnp.where(gap == 0, core, jnp.where(below, 0, 1))
     place = (steps - 1) * 2 + jnp.where(core == receiver, 0, 1)
     place = jnp.where(same_chip, place, jnp.where(gap == 0, 4, 5 + place))
     slot = 2 + place + jnp.where(receiver == lax.rem(row, 2), 0, 9)
@@ -58,27 +59,43 @@
     return slot * blocks + lax.rem(block, blocks)
 
 
-def tile_kernel(in_ref, to_ref, tiles_ref, own, beside, near, far, side, other_near, other_side, out_ref, blocks_ref, acc_ref):
+def place_kernel(blocks, in_ref, out_ref, from_ref, to_ref):
+    row, cols = lax.axis_index("row"), lax.axis_size("col")
+    planes = lax.axis_size("row") // PLANE
+
+    def one(t, carry):
+        from_ref[t] = block_place(in_ref[t], row, planes, cols, blocks) * SIDE
+        to_ref[t] = out_ref[t] - row * cols * blocks
+        return carry
+
+    lax.fori_loop(0, in_ref.shape[0], one, 0)
+
+
+def tile_kernel(
+    from_ref, to_ref, tiles_ref, own, beside, near, far, across, across_near, across_far, other,
+    out_ref, blocks_ref, acc_ref, sent_ref, sems,
+):
     cols, rows, _ = out_ref.shape
     blocks = rows // SIDE
     at = 0
-    for piece in (own, beside, near, far, side, other_near, other_side):
+    for piece in (own, beside, near, far, across, across_near, across_far, other):
         blocks_ref[at : at + piece.shape[0], :] = piece[...]
         at += piece.shape[0]
     acc_ref[...] = jnp.zeros_like(acc_ref)
-    row = lax.axis_index("row")
-    planes = lax.axis_size("row") // PLANE
 
     def one(t, carry):
-        at = pl.multiple_of(block_place(in_ref[t], row, planes, cols, blocks) * SIDE, SIDE)
-        to = to_ref[t] - row * cols * blocks
-        acc_ref[to] += dot(tiles_ref[t], blocks_ref[pl.ds(at, SIDE), :], (1, 0))
+        at = pl.multiple_of(from_ref[t], SIDE)
+        acc_ref[to_ref[t]] += dot(tiles_ref[t], blocks_ref[pl.ds(at, SIDE), :], (1, 0))
         return carry
 
     lax.fori_loop(0, tiles_ref.shape[0], one, 0, unroll=8)
+    copies = [pltpu.make_async_copy(sent_ref.at[c], out_ref.at[c], sems.at[c]) for c in range(cols)]
     for c in range(cols):
         for b in range(blocks):
-            out_ref[c, b * SIDE : (b + 1) * SIDE, :] = acc_ref[c * blocks + b].astype(BF)
+            sent_ref[c, b * SIDE : (b + 1) * SIDE, :] = acc_ref[c * blocks + b].astype(BF)
+        copies[c].start()
+    for c in range(cols):
+        copies[c].wait()
 
 
 def finish_kernel(scale, got_ref, wsum_ref, out_ref, wgrad_ref):
@@ -102,12 +119,13 @@
     col_count = lax.axis_size("col")
     nodes, feat = cotangent.shape
     blocks_dev = nodes // SIDE
+    half = col_count // 2
     params = pltpu.CompilerParams(vmem_limit_bytes=12 << 20)
     small = pltpu.CompilerParams(vmem_limit_bytes=4 << 20)
 
     adjoint, wpart = pl.pallas_call(
         adjoint_kernel,
-        out_shape=(jax.ShapeDtypeStruct((nodes, feat), BF), jax.ShapeDtypeStruct((feat, feat), F32)),
+        out_shape=(jax.ShapeDtypeStruct((nodes, feat), BF), jax.ShapeDtypeStruct((half, feat, feat), BF)),
         in_specs=[pl.BlockSpec(memory_space=pltpu.HBM)] * 5,
         out_specs=(vmem(), vmem()),
         scratch_shapes=[
@@ -125,54 +143,63 @@
     def swap(value, bit):
         return lax.ppermute(value, "row", [(i, i ^ bit) for i in range(row_count)])
 
-    def to_plane(value, steps):
-        pairs = [(i, (i + PLANE * (steps if i % 2 == 0 else -steps)) % row_count) for i in range(row_count)]
-        return lax.ppermute(value, "row", pairs)
+    def to_plane(value, steps, chip_bit, wanted):
+        pairs = [(i, ((i ^ chip_bit) + PLANE * (steps if i % 2 == 0 else -steps)) % row_count) for i in range(row_count)]
+        return lax.ppermute(value, "row", [pair for pair in pairs if pair[0] % PLANE in wanted])
+
+    beside = swap(adjoint, 1)
+    across = swap(adjoint, 2)
+    chip = jnp.concatenate([adjoint, beside])
+    far = to_plane(chip, 2, 0, (0, 1, 2, 3))
+    across_far = to_plane(chip, 2, 2, (1, 2))
+    across_near = to_plane(chip, 1, 2, (0, 1, 2, 3))
+    near = to_plane(chip, 1, 0, (0, 1, 2, 3))
+
+    groups = [list(range(half)), list(range(half, col_count))]
+    wz = lax.all_to_all(wpart, "col", 0, 0, axis_index_groups=groups)
+    wsum = wz.astype(F32).sum(0)
 
     def partner(value, axis, bit):
         return lax.ppermute(value, axis, [(i, i ^ bit) for i in range(lax.axis_size(axis))])
 
-    beside = swap(adjoint, 1)
-    chip = jnp.concatenate([adjoint, beside])
-    near = to_plane(chip, 1)
-    far = to_plane(chip, 2)
-    z_bits = [1 << k for k in reversed(range((col_count // 2 - 1).bit_length()))]
-    late_bits = [("row", 1 << k) for k in range((row_count - 1).bit_length())] + [("col", col_count // 2)]
-    wsum = wpart
-    for bit in z_bits[:-2]:
-        wsum = wsum + partner(wsum, "col", bit)
-    across, wsum = lax.optimization_barrier((jnp.concatenate([beside, near, far]), wsum))
-    side = swap(across, 2)
-    other_near = swap(jnp.concatenate([near, far]), 1)
-    for bit in z_bits[-2:-1]:
-        wsum = wsum + partner(wsum, "col", bit)
-    side, other_near, wsum = lax.optimization_barrier((side, other_near, wsum))
-    wnext = [partner(wsum, "col", bit) for bit in z_bits[-1:]]
-    other_side = swap(side, 1)
-
+    received = jnp.concatenate([near, far, across, across_near, across_far])
+    received, wsum = lax.optimization_barrier((received, wsum))
+    other = swap(received, 1)
+    wnext = partner(wsum, "col", half)
+
+    scalars = jax.ShapeDtypeStruct(tile_in.shape, jnp.int32)
+    places, targets = pl.pallas_call(
+        functools.partial(place_kernel, blocks_dev),
+        out_shape=(scalars, scalars),
+        in_specs=[smem()] * 2,
+        out_specs=(smem(), smem()),
+        compiler_params=small,
+        name="places",
+    )(tile_in, tile_out)
     tiles = tile_values.shape[0]
     sends = pl.pallas_call(
         tile_kernel,
         out_shape=jax.ShapeDtypeStruct((col_count, nodes, feat), BF),
-        in_specs=[smem(), smem()] + [vmem()] * 8,
-        out_specs=vmem(),
+        in_specs=[smem(), smem()] + [vmem()] * 9,
+        out_specs=pl.BlockSpec(memory_space=pl.ANY),
         scratch_shapes=[
             pltpu.VMEM((20 * nodes, feat), BF),
             pltpu.VMEM((col_count * blocks_dev, SIDE, feat), F32),
+            pltpu.VMEM((col_count, nodes, feat), BF),
+            pltpu.SemaphoreType.DMA((col_count,)),
         ],
         compiler_params=params,
         cost_estimate=pl.CostEstimate(
             flops=2 * tiles * SIDE * SIDE * feat, bytes_accessed=6 << 20, transcendentals=0
         ),
         name="tiles",
-    )(tile_in, tile_out, tile_values, adjoint, beside, near, far, side, other_near, other_side)
+    )(places, targets, tile_values, adjoint, beside, near, far, across, across_near, across_far, other)
 
     sends, wsum, wnext = lax.optimization_barrier((sends, wsum, wnext))
     got = lax.all_to_all(sends, "col", 0, 0)
-    for value in wnext:
-        wsum = wsum + value
-    for axis, bit in late_bits:
-        wsum = wsum + partner(wsum, axis, bit)
+    wsum = wsum + wnext
+    for bit in [1 << k for k in range((row_count - 1).bit_length())]:
+        wsum = wsum + partner(wsum, "row", bit)
     scale = 1.0 / float(nodes * row_count * col_count) ** 0.5
     node_grad, weight_grad = pl.pallas_call(
         functools.partial(finish_kernel, scale),

time: 109 us -> 106 us (0.972)
  the two profiles are of different devices: /device:TPU:6 before, /device:TPU:1 now
where the time goes in v6:
time: 106 us; the launch traced here: 105 us
  starting transfers between devices  60 us (57%)
  waiting for transfers between devices  34.7 us (33%)
  Pallas kernels  8.65 us (8%)
    ppermute x6, waiting for transfers between devices, partner(): lax.ppermute(value, axis, [(i, i ^ bit) for i in range(lax.axis_size(axis...  20.6 us
    ppermute x3, starting transfers between devices, swap(): return lax.ppermute(value, 'row', [(i, i ^ bit) for i in range(row_count)])  18.4 us
    ppermute x6, starting transfers between devices, partner(): lax.ppermute(value, axis, [(i, i ^ bit) for i in range(lax.axis_size(axis...  14.8 us
    all_to_all x1, starting transfers between devices, on_device(): wz = lax.all_to_all(wpart, 'col', 0, 0, axis_index_groups=groups)  10 us
    ppermute x4, starting transfers between devices, to_plane(): lax.ppermute(value, 'row', [pair for pair in pairs if pair[0] % PLANE in...  9.67 us
    all_to_all x1, waiting for transfers between devices, on_device(): got = lax.all_to_all(sends, 'col', 0, 0)  7.49 us
    all_to_all x1, starting transfers between devices, on_device(): got = lax.all_to_all(sends, 'col', 0, 0)  7.04 us
    ppermute x4, waiting for transfers between devices, to_plane(): lax.ppermute(value, 'row', [pair for pair in pairs if pair[0] % PLANE in...  4.55 us
  transfers between devices with their start and end apart: 15, of which 10 were waited for; matrix products, arithmetic and copies ran while one was open for 1% of the time, Pallas kernels for 5%

profile of v6, /device:TPU:1, one launch (start us, length us, event | category | flops | bytes accessed | tf_op | source)
XLA Modules:
  0.0 105.4 jit_solution(14606888224846485545)
XLA Ops:
  0.6 2.5 %adjoint.1 = (bf16[384,128]{1,0:T(8,128)(2,1)}, bf16[8,128,128]{2,1,0:T(8,128)(2,1)}) custom-call(s32[3,128]{1,0:T(4,128)} %bitcast.1, bf16[384,128]{1,0:T(8,128)(2,1)} %cot_in.1, bf16[384,128]{1,0:T(8,128)(2,1)} %pre_in.1, bf16[384,128]{1,0:T(8,128)(2,1)} %agg_in.1, bf16[128,128]{1,0:T(8,128)(2,1)} %w_in.1), custom_call_target="tpu_custom_call" | custom-call | tf_op jit(solution)/shard_map/adjoint/pallas_call | solution.py:126
  3.1 0.0 copy-start.2
  3.1 0.0 copy-start.3
  3.1 0.0 copy-start
  3.1 0.0 copy-start.1
  3.1 8.9 %collective-permute-start = (bf16[384,128]{1,0:T(8,128)(2,1)}, bf16[384,128]{1,0:T(8,128)(2,1)S(1)}, u32[]{:S(2)}, u32[]{:S(2)}) collective-permute-start(bf16[384,128]{1,0:T(8,128)(2,1)} %get-tuple-element.13.own), channel_id=1, source_target_pairs={{0,16},{16,0},{32,48},{48,32},{64,80},{80,64},{96,112},{112,96},{1... | collective-permute-start | bytes 294920 | tf_op jit(solution)/shard_map/ppermute | solution.py:144
  12.1 0.9 constant_dynamic-update-slice_fusion.1
  13.0 0.2 collective-permute-done.beside
  13.2 1.9 %collective-permute-start.1 = (bf16[768,128]{1,0:T(8,128)(2,1)S(1)}, bf16[768,128]{1,0:T(8,128)(2,1)S(1)}, u32[]{:S(2)}, u32[]{:S(2)}) collective-permute-start(bf16[768,128]{1,0:T(8,128)(2,1)S(1)} %constant_dynamic-update-slice_fusion), channel_id=1, source_target_pairs={{0,64},{16,464},{32,96},{48,496},{64,128},{80,16},{96,160},{112,48... | collective-permute-start | bytes 589832 | tf_op jit(solution)/shard_map/ppermute | solution.py:148
  15.2 1.9 %collective-permute-start.2 = (bf16[768,128]{1,0:T(8,128)(2,1)S(1)}, bf16[768,128]{1,0:T(8,128)(2,1)S(1)}, u32[]{:S(2)}, u32[]{:S(2)}) collective-permute-start(bf16[768,128]{1,0:T(8,128)(2,1)S(1)} %constant_dynamic-update-slice_fusion), channel_id=1, source_target_pairs={{0,128},{16,400},{32,160},{48,432},{64,192},{80,464},{96,224},{112... | collective-permute-start | bytes 589832 | tf_op jit(solution)/shard_map/ppermute | solution.py:148
  17.1 2.8 %collective-permute-start.3 = (bf16[384,128]{1,0:T(8,128)(2,1)}, bf16[384,128]{1,0:T(8,128)(2,1)S(1)}, u32[]{:S(2)}, u32[]{:S(2)}) collective-permute-start(bf16[384,128]{1,0:T(8,128)(2,1)} %get-tuple-element.13.own), channel_id=1, source_target_pairs={{0,32},{16,48},{32,0},{48,16},{64,96},{80,112},{96,64},{112,80},{1... | collective-permute-start | bytes 294920 | tf_op jit(solution)/shard_map/ppermute | solution.py:144
  19.9 10.0 %all-to-all-start = ((bf16[8,128,128]{2,1,0:T(8,128)(2,1)}), bf16[8,128,128]{2,1,0:T(8,128)(2,1)S(1)}, u32[]{:S(2)}, u32[]{:S(2)}) async-start(bf16[8,128,128]{2,1,0:T(8,128)(2,1)} %get-tuple-element.14), calls=%async_computation | async-start | bytes 524288 | tf_op jit(solution)/shard_map/all_to_all | solution.py:159
  29.9 2.9 %collective-permute-start.4 = (bf16[768,128]{1,0:T(8,128)(2,1)S(1)}, bf16[768,128]{1,0:T(8,128)(2,1)S(1)}, u32[]{:S(2)}, u32[]{:S(2)}) collective-permute-start(bf16[768,128]{1,0:T(8,128)(2,1)S(1)} %constant_dynamic-update-slice_fusion), channel_id=1, source_target_pairs={{0,96},{16,496},{32,64},{48,464},{64,160},{80,48},{96,128},{112,16... | collective-permute-start | bytes 589832 | tf_op jit(solution)/shard_map/ppermute | solution.py:148
  32.8 2.9 %collective-permute-start.5 = (bf16[768,128]{1,0:T(8,128)(2,1)S(1)}, bf16[768,128]{1,0:T(8,128)(2,1)S(1)}, u32[]{:S(2)}, u32[]{:S(2)}) collective-permute-start(bf16[768,128]{1,0:T(8,128)(2,1)S(1)} %constant_dynamic-update-slice_fusion), channel_id=1, source_target_pairs={{16,432},{32,128},{80,496},{96,192},{144,48},{160,256},{208,112},{... | collective-permute-start | bytes 589832 | tf_op jit(solution)/shard_map/ppermute | solution.py:148
  35.8 0.0 collective-permute-done.1.near
  35.8 0.0 collective-permute-done.2.far
  35.8 0.0 collective-permute-done.3.across
  35.9 1.7 %collective-permute-done.4.across_near = bf16[768,128]{1,0:T(8,128)(2,1)S(1)} collective-permute-done((bf16[768,128]{1,0:T(8,128)(2,1)S(1)}, bf16[768,128]{1,0:T(8,128)(2,1)S(1)}, u32[]{:S(2)}, u32[]{:S(2)}) %collective-permute-start.4) | collective-permute-done | bytes 196640 | tf_op jit(solution)/shard_map/ppermute | solution.py:148
  37.6 2.8 %collective-permute-done.5.across_far = bf16[768,128]{1,0:T(8,128)(2,1)S(1)} collective-permute-done((bf16[768,128]{1,0:T(8,128)(2,1)S(1)}, bf16[768,128]{1,0:T(8,128)(2,1)S(1)}, u32[]{:S(2)}, u32[]{:S(2)}) %collective-permute-start.5) | collective-permute-done | bytes 196640 | tf_op jit(solution)/shard_map/ppermute | solution.py:148
  40.5 1.8 %all-to-all-done = bf16[8,128,128]{2,1,0:T(8,128)(2,1)S(1)} async-done(((bf16[8,128,128]{2,1,0:T(8,128)(2,1)}), bf16[8,128,128]{2,1,0:T(8,128)(2,1)S(1)}, u32[]{:S(2)}, u32[]{:S(2)}) %all-to-all-start) | async-done | bytes 262176 | tf_op jit(solution)/shard_map/all_to_all | solution.py:159
  42.3 6.7 %collective-permute-start.6 = (bf16[3456,128]{1,0:T(8,128)(2,1)S(1)}, bf16[3456,128]{1,0:T(8,128)(2,1)S(1)}, u32[]{:S(2)}, u32[]{:S(2)}) collective-permute-start(bf16[3456,128]{1,0:T(8,128)(2,1)S(1)} %constant_dynamic-update-slice_fusion.2), channel_id=1, source_target_pairs={{0,16},{16,0},{32,48},{48,32},{64,80},{80,64},{96,112},{112,96},{1... | collective-permute-start | bytes 2654216 | tf_op jit(solution)/shard_map/ppermute | solution.py:144
  49.0 4.7 %collective-permute-start.7 = (f32[128,128]{1,0:T(8,128)S(1)}, f32[128,128]{1,0:T(8,128)S(1)}, u32[]{:S(2)}, u32[]{:S(2)}) collective-permute-start(f32[128,128]{1,0:T(8,128)S(1)} %convert_reduce_fusion), channel_id=1, source_target_pairs={{0,8},{1,9},{2,10},{3,11},{4,12},{5,13},{6,14},{7,15},{8,0},{9,1},... | collective-permute-start | bytes 196616 | tf_op jit(solution)/shard_map/ppermute | solution.py:163
  53.7 0.0 copy-done.2
  53.7 0.0 copy-done.3
  53.7 2.2 %places.1 = (s32[32]{0:T(128)S(1)}, s32[32]{0:T(128)S(1)}) custom-call(s32[32]{0:T(128)S(1)} %copy-done.2, s32[32]{0:T(128)S(1)} %copy-done.3), custom_call_target="tpu_custom_call" | custom-call | tf_op jit(solution)/shard_map/places/pallas_call | solution.py:171
  55.9 0.0 collective-permute-done.6.other
  55.9 0.0 copy-done
  55.9 0.0 copy-done.1
  56.0 3.1 %tiles.1 = bf16[16,384,128]{2,1,0:T(8,128)(2,1)} custom-call(s32[32]{0:T(128)S(1)} %get-tuple-element.11.from_ref, s32[32]{0:T(128)S(1)} %get-tuple-element.12.to_ref, bf16[32,128,128]{2,1,0:T(8,128)(2,1)S(1)} %copy-done, bf16[384,128]{1,0:T(8,128)(2,1)S(1)} %copy-done.1, bf16[384,128]{1,0:T(8,128)(2,1)S(1)} %collective-permute-done.beside, ...), custom_call_target="tpu_custom_call" | custom-call | flops 134217728 | bytes 6291456 | tf_op jit(solution)/shard_map/tiles/pallas_call | solution.py:180
  59.1 0.0 collective-permute-done.7
  59.1 7.0 %all-to-all-start.1 = ((bf16[16,384,128]{2,1,0:T(8,128)(2,1)}), bf16[16,384,128]{2,1,0:T(8,128)(2,1)S(1)}, u32[]{:S(2)}, u32[]{:S(2)}) async-start(bf16[16,384,128]{2,1,0:T(8,128)(2,1)} %tiles.1), calls=%async_computation.1 | async-start | bytes 3145728 | tf_op jit(solution)/shard_map/all_to_all | solution.py:199
  66.2 2.5 %collective-permute-start.8 = (f32[128,128]{1,0:T(8,128)S(1)}, f32[128,128]{1,0:T(8,128)S(1)}, u32[]{:S(2)}, u32[]{:S(2)}) collective-permute-start(f32[128,128]{1,0:T(8,128)S(1)} %add.18), channel_id=1, source_target_pairs={{0,16},{16,0},{32,48},{48,32},{64,80},{80,64},{96,112},{112,96},{1... | collective-permute-start | bytes 196616 | tf_op jit(solution)/shard_map/ppermute | solution.py:163
  68.7 0.9 collective-permute-done.8
  69.6 1.9 %collective-permute-start.9 = (f32[128,128]{1,0:T(8,128)S(1)}, f32[128,128]{1,0:T(8,128)S(1)}, u32[]{:S(2)}, u32[]{:S(2)}) collective-permute-start(f32[128,128]{1,0:T(8,128)S(1)} %add.19), channel_id=1, source_target_pairs={{0,32},{16,48},{32,0},{48,16},{64,96},{80,112},{96,64},{112,80},{1... | collective-permute-start | bytes 196616 | tf_op jit(solution)/shard_map/ppermute | solution.py:163
  71.5 4.4 %collective-permute-done.9 = f32[128,128]{1,0:T(8,128)S(1)} collective-permute-done((f32[128,128]{1,0:T(8,128)S(1)}, f32[128,128]{1,0:T(8,128)S(1)}, u32[]{:S(2)}, u32[]{:S(2)}) %collective-permute-start.9) | collective-permute-done | bytes 65568 | tf_op jit(solution)/shard_map/ppermute | solution.py:163
  75.9 1.9 %collective-permute-start.10 = (f32[128,128]{1,0:T(8,128)S(1)}, f32[128,128]{1,0:T(8,128)S(1)}, u32[]{:S(2)}, u32[]{:S(2)}) collective-permute-start(f32[128,128]{1,0:T(8,128)S(1)} %add.20), channel_id=1, source_target_pairs={{0,64},{16,80},{32,96},{48,112},{64,0},{80,16},{96,32},{112,48},{1... | collective-permute-start | bytes 196616 | tf_op jit(solution)/shard_map/ppermute | solution.py:163
  77.9 3.4 %collective-permute-done.10 = f32[128,128]{1,0:T(8,128)S(1)} collective-permute-done((f32[128,128]{1,0:T(8,128)S(1)}, f32[128,128]{1,0:T(8,128)S(1)}, u32[]{:S(2)}, u32[]{:S(2)}) %collective-permute-start.10) | collective-permute-done | bytes 65568 | tf_op jit(solution)/shard_map/ppermute | solution.py:163
  81.3 1.9 %collective-permute-start.11 = (f32[128,128]{1,0:T(8,128)S(1)}, f32[128,128]{1,0:T(8,128)S(1)}, u32[]{:S(2)}, u32[]{:S(2)}) collective-permute-start(f32[128,128]{1,0:T(8,128)S(1)} %add.21), channel_id=1, source_target_pairs={{0,128},{16,144},{32,160},{48,176},{64,192},{80,208},{96,224},{112... | collective-permute-start | bytes 196616 | tf_op jit(solution)/shard_map/ppermute | solution.py:163
  83.2 4.7 %collective-permute-done.11 = f32[128,128]{1,0:T(8,128)S(1)} collective-permute-done((f32[128,128]{1,0:T(8,128)S(1)}, f32[128,128]{1,0:T(8,128)S(1)}, u32[]{:S(2)}, u32[]{:S(2)}) %collective-permute-start.11) | collective-permute-done | bytes 65568 | tf_op jit(solution)/shard_map/ppermute | solution.py:163
  87.9 1.9 %collective-permute-start.12 = (f32[128,128]{1,0:T(8,128)S(1)}, f32[128,128]{1,0:T(8,128)S(1)}, u32[]{:S(2)}, u32[]{:S(2)}) collective-permute-start(f32[128,128]{1,0:T(8,128)S(1)} %add.22), channel_id=1, source_target_pairs={{0,256},{16,272},{32,288},{48,304},{64,320},{80,336},{96,352},{112... | collective-permute-start | bytes 196616 | tf_op jit(solution)/shard_map/ppermute | solution.py:163
  89.8 7.2 %collective-permute-done.12 = f32[128,128]{1,0:T(8,128)S(1)} collective-permute-done((f32[128,128]{1,0:T(8,128)S(1)}, f32[128,128]{1,0:T(8,128)S(1)}, u32[]{:S(2)}, u32[]{:S(2)}) %collective-permute-start.12) | collective-permute-done | bytes 65568 | tf_op jit(solution)/shard_map/ppermute | solution.py:163
  97.1 7.5 %all-to-all-done.1.got_ref = bf16[16,384,128]{2,1,0:T(8,128)(2,1)S(1)} async-done(((bf16[16,384,128]{2,1,0:T(8,128)(2,1)}), bf16[16,384,128]{2,1,0:T(8,128)(2,1)S(1)}, u32[]{:S(2)}, u32[]{:S(2)}) %all-to-all-start.1) | async-done | bytes 1572896 | tf_op jit(solution)/shard_map/all_to_all | solution.py:199
  104.5 0.9 finish.1
  (13 shorter events, 0.2 us)
Async XLA Ops:
  3.1 50.6 %copy-start.2 = (s32[32]{0:T(128)S(1)}, s32[32]{0:T(128)}, u32[]{:S(2)}) copy-start(s32[32]{0:T(128)} %in_ref.1) | copy-start | bytes 388
  3.1 50.6 %copy-start.3 = (s32[32]{0:T(128)S(1)}, s32[32]{0:T(128)}, u32[]{:S(2)}) copy-start(s32[32]{0:T(128)} %out_ref.1) | copy-start | bytes 388
  3.1 52.8 %copy-start = (bf16[32,128,128]{2,1,0:T(8,128)(2,1)S(1)}, bf16[32,128,128]{2,1,0:T(8,128)(2,1)}, u32[]{:S(2)}) copy-start(bf16[32,128,128]{2,1,0:T(8,128)(2,1)} %tiles_ref.1) | copy-start | bytes 3145732
  3.1 52.8 %copy-start.1 = (bf16[384,128]{1,0:T(8,128)(2,1)S(1)}, bf16[384,128]{1,0:T(8,128)(2,1)}, u32[]{:S(2)}) copy-start(bf16[384,128]{1,0:T(8,128)(2,1)} %get-tuple-element.13.own) | copy-start | bytes 294916
  3.1 10.1 %collective-permute-start = (bf16[384,128]{1,0:T(8,128)(2,1)}, bf16[384,128]{1,0:T(8,128)(2,1)S(1)}, u32[]{:S(2)}, u32[]{:S(2)}) collective-permute-start(bf16[384,128]{1,0:T(8,128)(2,1)} %get-tuple-element.13.own), channel_id=1, source_target_pairs={{0,16},{16,0},{32,48},{48,32},{64,80},{80,64},{96,112},{112,96},{1... | collective-permute-start | bytes 294920 | tf_op jit(solution)/shard_map/ppermute | solution.py:144
  13.2 22.5 %collective-permute-start.1 = (bf16[768,128]{1,0:T(8,128)(2,1)S(1)}, bf16[768,128]{1,0:T(8,128)(2,1)S(1)}, u32[]{:S(2)}, u32[]{:S(2)}) collective-permute-start(bf16[768,128]{1,0:T(8,128)(2,1)S(1)} %constant_dynamic-update-slice_fusion), channel_id=1, source_target_pairs={{0,64},{16,464},{32,96},{48,496},{64,128},{80,16},{96,160},{112,48... | collective-permute-start | bytes 589832 | tf_op jit(solution)/shard_map/ppermute | solution.py:148
  15.2 20.6 %collective-permute-start.2 = (bf16[768,128]{1,0:T(8,128)(2,1)S(1)}, bf16[768,128]{1,0:T(8,128)(2,1)S(1)}, u32[]{:S(2)}, u32[]{:S(2)}) collective-permute-start(bf16[768,128]{1,0:T(8,128)(2,1)S(1)} %constant_dynamic-update-slice_fusion), channel_id=1, source_target_pairs={{0,128},{16,400},{32,160},{48,432},{64,192},{80,464},{96,224},{112... | collective-permute-start | bytes 589832 | tf_op jit(solution)/shard_map/ppermute | solution.py:148
  17.1 18.8 %collective-permute-start.3 = (bf16[384,128]{1,0:T(8,128)(2,1)}, bf16[384,128]{1,0:T(8,128)(2,1)S(1)}, u32[]{:S(2)}, u32[]{:S(2)}) collective-permute-start(bf16[384,128]{1,0:T(8,128)(2,1)} %get-tuple-element.13.own), channel_id=1, source_target_pairs={{0,32},{16,48},{32,0},{48,16},{64,96},{80,112},{96,64},{112,80},{1... | collective-permute-start | bytes 294920 | tf_op jit(solution)/shard_map/ppermute | solution.py:144
  19.9 22.4 %all-to-all-start = ((bf16[8,128,128]{2,1,0:T(8,128)(2,1)}), bf16[8,128,128]{2,1,0:T(8,128)(2,1)S(1)}, u32[]{:S(2)}, u32[]{:S(2)}) async-start(bf16[8,128,128]{2,1,0:T(8,128)(2,1)} %get-tuple-element.14), calls=%async_computation | async-start | bytes 524288 | tf_op jit(solution)/shard_map/all_to_all | solution.py:159
  29.9 7.7 %collective-permute-start.4 = (bf16[768,128]{1,0:T(8,128)(2,1)S(1)}, bf16[768,128]{1,0:T(8,128)(2,1)S(1)}, u32[]{:S(2)}, u32[]{:S(2)}) collective-permute-start(bf16[768,128]{1,0:T(8,128)(2,1)S(1)} %constant_dynamic-update-slice_fusion), channel_id=1, source_target_pairs={{0,96},{16,496},{32,64},{48,464},{64,160},{80,48},{96,128},{112,16... | collective-permute-start | bytes 589832 | tf_op jit(solution)/shard_map/ppermute | solution.py:148
  32.8 7.6 %collective-permute-start.5 = (bf16[768,128]{1,0:T(8,128)(2,1)S(1)}, bf16[768,128]{1,0:T(8,128)(2,1)S(1)}, u32[]{:S(2)}, u32[]{:S(2)}) collective-permute-start(bf16[768,128]{1,0:T(8,128)(2,1)S(1)} %constant_dynamic-update-slice_fusion), channel_id=1, source_target_pairs={{16,432},{32,128},{80,496},{96,192},{144,48},{160,256},{208,112},{... | collective-permute-start | bytes 589832 | tf_op jit(solution)/shard_map/ppermute | solution.py:148
  42.3 13.6 %collective-permute-start.6 = (bf16[3456,128]{1,0:T(8,128)(2,1)S(1)}, bf16[3456,128]{1,0:T(8,128)(2,1)S(1)}, u32[]{:S(2)}, u32[]{:S(2)}) collective-permute-start(bf16[3456,128]{1,0:T(8,128)(2,1)S(1)} %constant_dynamic-update-slice_fusion.2), channel_id=1, source_target_pairs={{0,16},{16,0},{32,48},{48,32},{64,80},{80,64},{96,112},{112,96},{1... | collective-permute-start | bytes 2654216 | tf_op jit(solution)/shard_map/ppermute | solution.py:144
  49.0 10.1 %collective-permute-start.7 = (f32[128,128]{1,0:T(8,128)S(1)}, f32[128,128]{1,0:T(8,128)S(1)}, u32[]{:S(2)}, u32[]{:S(2)}) collective-permute-start(f32[128,128]{1,0:T(8,128)S(1)} %convert_reduce_fusion), channel_id=1, source_target_pairs={{0,8},{1,9},{2,10},{3,11},{4,12},{5,13},{6,14},{7,15},{8,0},{9,1},... | collective-permute-start | bytes 196616 | tf_op jit(solution)/shard_map/ppermute | solution.py:163
  59.1 45.4 %all-to-all-start.1 = ((bf16[16,384,128]{2,1,0:T(8,128)(2,1)}), bf16[16,384,128]{2,1,0:T(8,128)(2,1)S(1)}, u32[]{:S(2)}, u32[]{:S(2)}) async-start(bf16[16,384,128]{2,1,0:T(8,128)(2,1)} %tiles.1), calls=%async_computation.1 | async-start | bytes 3145728 | tf_op jit(solution)/shard_map/all_to_all | solution.py:199
  66.2 3.4 %collective-permute-start.8 = (f32[128,128]{1,0:T(8,128)S(1)}, f32[128,128]{1,0:T(8,128)S(1)}, u32[]{:S(2)}, u32[]{:S(2)}) collective-permute-start(f32[128,128]{1,0:T(8,128)S(1)} %add.18), channel_id=1, source_target_pairs={{0,16},{16,0},{32,48},{48,32},{64,80},{80,64},{96,112},{112,96},{1... | collective-permute-start | bytes 196616 | tf_op jit(solution)/shard_map/ppermute | solution.py:163
  69.6 6.4 %collective-permute-start.9 = (f32[128,128]{1,0:T(8,128)S(1)}, f32[128,128]{1,0:T(8,128)S(1)}, u32[]{:S(2)}, u32[]{:S(2)}) collective-permute-start(f32[128,128]{1,0:T(8,128)S(1)} %add.19), channel_id=1, source_target_pairs={{0,32},{16,48},{32,0},{48,16},{64,96},{80,112},{96,64},{112,80},{1... | collective-permute-start | bytes 196616 | tf_op jit(solution)/shard_map/ppermute | solution.py:163
  75.9 5.3 %collective-permute-start.10 = (f32[128,128]{1,0:T(8,128)S(1)}, f32[128,128]{1,0:T(8,128)S(1)}, u32[]{:S(2)}, u32[]{:S(2)}) collective-permute-start(f32[128,128]{1,0:T(8,128)S(1)} %add.20), channel_id=1, source_target_pairs={{0,64},{16,80},{32,96},{48,112},{64,0},{80,16},{96,32},{112,48},{1... | collective-permute-start | bytes 196616 | tf_op jit(solution)/shard_map/ppermute | solution.py:163
  81.3 6.6 %collective-permute-start.11 = (f32[128,128]{1,0:T(8,128)S(1)}, f32[128,128]{1,0:T(8,128)S(1)}, u32[]{:S(2)}, u32[]{:S(2)}) collective-permute-start(f32[128,128]{1,0:T(8,128)S(1)} %add.21), channel_id=1, source_target_pairs={{0,128},{16,144},{32,160},{48,176},{64,192},{80,208},{96,224},{112... | collective-permute-start | bytes 196616 | tf_op jit(solution)/shard_map/ppermute | solution.py:163
  87.9 9.1 %collective-permute-start.12 = (f32[128,128]{1,0:T(8,128)S(1)}, f32[128,128]{1,0:T(8,128)S(1)}, u32[]{:S(2)}, u32[]{:S(2)}) collective-permute-start(f32[128,128]{1,0:T(8,128)S(1)} %add.22), channel_id=1, source_target_pairs={{0,256},{16,272},{32,288},{48,304},{64,320},{80,336},{96,352},{112... | collective-permute-start | bytes 196616 | tf_op jit(solution)/shard_map/ppermute | solution.py:163

commit v7 on v6

--- a/solution.py
+++ b/solution.py
@@ -17,15 +17,38 @@
     return lax.dot_general(a, b, ((contract[:1], contract[1:]), ((), ())), preferred_element_type=F32)
 
 
-def adjoint_kernel(order_in, cot_in, pre_in, agg_in, w_in, out_ref, wpart_ref, order_ref, cot_ref, pre_ref, agg_ref, w_ref, sems):
-    ins = (order_in, cot_in, pre_in, w_in, agg_in)
-    held = (order_ref, cot_ref, pre_ref, w_ref, agg_ref)
+def block_place(block, row, planes, cols, blocks):
+    device = lax.div(block, blocks)
+    group = lax.div(device, cols)
+    gap = lax.rem(lax.div(group, PLANE) - lax.div(row, PLANE) + planes, planes)
+    core = lax.rem(group, 2)
+    same_core = core == lax.rem(row, 2)
+    same_chip = lax.rem(lax.div(group, 2), 2) == lax.rem(lax.div(row, 2), 2)
+    below = gap > planes // 2
+    steps = jnp.where(below, planes - gap, gap)
+    receiver = jnp.where(gap == 0, core, jnp.where(below, 0, 1))
+    first = jnp.where(steps == 2, jnp.where(same_chip, 7, 1), jnp.where(same_chip, 3, 5))
+    place = jnp.where(gap == 0, 0, first + jnp.where(core == receiver, 0, 1))
+    slot = 2 + place + jnp.where(receiver == lax.rem(row, 2), 0, 9)
+    slot = jnp.where((gap == 0) & same_chip, jnp.where(same_core, 0, 1), slot)
+    return slot * blocks + lax.rem(block, blocks)
+
+
+def adjoint_kernel(
+    order_in, cot_in, pre_in, agg_in, w_in, in_in, to_in, out_ref, wpart_ref, place_ref, target_ref,
+    order_ref, cot_ref, pre_ref, agg_ref, w_ref, in_ref, to_ref, sems,
+):
+    ins = (order_in, cot_in, pre_in, w_in, agg_in, in_in, to_in)
+    held = (order_ref, cot_ref, pre_ref, w_ref, agg_ref, in_ref, to_ref)
     copies = [pltpu.make_async_copy(a, b, sems.at[i]) for i, (a, b) in enumerate(zip(ins, held))]
     for copy in copies:
         copy.start()
     for copy in copies:
         copy.wait()
     rows = cot_ref.shape[0]
+    row, cols, blocks = lax.axis_index("row"), lax.axis_size("col"), rows // SIDE
+    place_ref[...] = block_place(in_ref[...], row, lax.axis_size("row") // PLANE, cols, blocks) * SIDE
+    target_ref[...] = to_ref[...] - row * cols * blocks
     cot = cot_ref[...]
     row_id = lax.broadcasted_iota(jnp.int32, (rows, SIDE), 0)
     base = (lax.axis_index("row") * lax.axis_size("col") + lax.axis_index("col")) * rows
@@ -42,50 +65,21 @@
         wpart_ref[z] = total.astype(BF)
 
 
-def block_place(block, row, planes, cols, blocks):
-    device = lax.div(block, blocks)
-    group = lax.div(device, cols)
-    gap = lax.rem(lax.div(group, PLANE) - lax.div(row, PLANE) + planes, planes)
-    core = lax.rem(group, 2)
-    same_core = core == lax.rem(row, 2)
-    same_chip = lax.rem(lax.div(group, 2), 2) == lax.rem(lax.div(row, 2), 2)
-    below = gap > planes // 2
-    steps = jnp.where(below, planes - gap, gap)
-    receiver = jnp.where(gap == 0, core, jnp.where(below, 0, 1))
-    place = (steps - 1) * 2 + jnp.where(core == receiver, 0, 1)
-    place = jnp.where(same_chip, place, jnp.where(gap == 0, 4, 5 + place))
-    slot = 2 + place + jnp.where(receiver == lax.rem(row, 2), 0, 9)
-    slot = jnp.where((gap == 0) & same_chip, jnp.where(same_core, 0, 1), slot)
-    return slot * blocks + lax.rem(block, blocks)
-
-
-def place_kernel(blocks, in_ref, out_ref, from_ref, to_ref):
-    row, cols = lax.axis_index("row"), lax.axis_size("col")
-    planes = lax.axis_size("row") // PLANE
-
-    def one(t, carry):
-        from_ref[t] = block_place(in_ref[t], row, planes, cols, blocks) * SIDE
-        to_ref[t] = out_ref[t] - row * cols * blocks
-        return carry
-
-    lax.fori_loop(0, in_ref.shape[0], one, 0)
-
-
 def tile_kernel(
-    from_ref, to_ref, tiles_ref, own, beside, near, far, across, across_near, across_far, other,
+    from_ref, to_ref, tiles_ref, own, beside, received, other,
     out_ref, blocks_ref, acc_ref, sent_ref, sems,
 ):
     cols, rows, _ = out_ref.shape
     blocks = rows // SIDE
     at = 0
-    for piece in (own, beside, near, far, across, across_near, across_far, other):
+    for piece in (own, beside, received, other):
         blocks_ref[at : at + piece.shape[0], :] = piece[...]
         at += piece.shape[0]
     acc_ref[...] = jnp.zeros_like(acc_ref)
 
     def one(t, carry):
-        at = pl.multiple_of(from_ref[t], SIDE)
-        acc_ref[to_ref[t]] += dot(tiles_ref[t], blocks_ref[pl.ds(at, SIDE), :], (1, 0))
+        at = pl.multiple_of(from_ref[0, t], SIDE)
+        acc_ref[to_ref[0, t]] += dot(tiles_ref[t], blocks_ref[pl.ds(at, SIDE), :], (1, 0))
         return carry
 
     lax.fori_loop(0, tiles_ref.shape[0], one, 0, unroll=8)
@@ -123,22 +117,26 @@
     params = pltpu.CompilerParams(vmem_limit_bytes=12 << 20)
     small = pltpu.CompilerParams(vmem_limit_bytes=4 << 20)
 
-    adjoint, wpart = pl.pallas_call(
+    tiles = tile_values.shape[0]
+    scalars = jax.ShapeDtypeStruct((1, tiles), jnp.int32)
+    adjoint, wpart, places, targets = pl.pallas_call(
         adjoint_kernel,
-        out_shape=(jax.ShapeDtypeStruct((nodes, feat), BF), jax.ShapeDtypeStruct((half, feat, feat), BF)),
-        in_specs=[pl.BlockSpec(memory_space=pltpu.HBM)] * 5,
-        out_specs=(vmem(), vmem()),
+        out_shape=(jax.ShapeDtypeStruct((nodes, feat), BF), jax.ShapeDtypeStruct((half, feat, feat), BF), scalars, scalars),
+        in_specs=[pl.BlockSpec(memory_space=pltpu.HBM)] * 7,
+        out_specs=(vmem(),) * 4,
         scratch_shapes=[
             pltpu.VMEM((blocks_dev, SIDE), jnp.int32),
             pltpu.VMEM((nodes, feat), BF),
             pltpu.VMEM((nodes, feat), BF),
             pltpu.VMEM((nodes, feat), BF),
             pltpu.VMEM((feat, feat), BF),
-            pltpu.SemaphoreType.DMA((5,)),
+            pltpu.VMEM((1, tiles), jnp.int32),
+            pltpu.VMEM((1, tiles), jnp.int32),
+            pltpu.SemaphoreType.DMA((7,)),
         ],
         compiler_params=pltpu.CompilerParams(vmem_limit_bytes=60 << 20),
         name="adjoint",
-    )(order.reshape(blocks_dev, SIDE), cotangent, pre_act, aggregated, weight)
+    )(order.reshape(blocks_dev, SIDE), cotangent, pre_act, aggregated, weight, tile_in.reshape(1, tiles), tile_out.reshape(1, tiles))
 
     def swap(value, bit):
         return lax.ppermute(value, "row", [(i, i ^ bit) for i in range(row_count)])
@@ -162,25 +160,13 @@
     def partner(value, axis, bit):
         return lax.ppermute(value, axis, [(i, i ^ bit) for i in range(lax.axis_size(axis))])
 
-    received = jnp.concatenate([near, far, across, across_near, across_far])
+    received = jnp.concatenate([across, across_far, near, across_near, far])
     received, wsum = lax.optimization_barrier((received, wsum))
     other = swap(received, 1)
-    wnext = partner(wsum, "col", half)
-
-    scalars = jax.ShapeDtypeStruct(tile_in.shape, jnp.int32)
-    places, targets = pl.pallas_call(
-        functools.partial(place_kernel, blocks_dev),
-        out_shape=(scalars, scalars),
-        in_specs=[smem()] * 2,
-        out_specs=(smem(), smem()),
-        compiler_params=small,
-        name="places",
-    )(tile_in, tile_out)
-    tiles = tile_values.shape[0]
     sends = pl.pallas_call(
         tile_kernel,
         out_shape=jax.ShapeDtypeStruct((col_count, nodes, feat), BF),
-        in_specs=[smem(), smem()] + [vmem()] * 9,
+        in_specs=[smem(), smem()] + [vmem()] * 5,
         out_specs=pl.BlockSpec(memory_space=pl.ANY),
         scratch_shapes=[
             pltpu.VMEM((20 * nodes, feat), BF),
@@ -193,13 +179,13 @@
             flops=2 * tiles * SIDE * SIDE * feat, bytes_accessed=6 << 20, transcendentals=0
         ),
         name="tiles",
-    )(places, targets, tile_values, adjoint, beside, near, far, across, across_near, across_far, other)
-
-    sends, wsum, wnext = lax.optimization_barrier((sends, wsum, wnext))
+    )(places, targets, tile_values, adjoint, beside, received, other)
+
+    sends, wsum = lax.optimization_barrier((sends, wsum))
     got = lax.all_to_all(sends, "col", 0, 0)
-    wsum = wsum + wnext
     for bit in [1 << k for k in range((row_count - 1).bit_length())]:
         wsum = wsum + partner(wsum, "row", bit)
+    wsum = wsum + partner(wsum, "col", half)
     scale = 1.0 / float(nodes * row_count * col_count) ** 0.5
     node_grad, weight_grad = pl.pallas_call(
         functools.partial(finish_kernel, scale),

time: 106 us -> 104 us (0.981)
  the two profiles are of different devices: /device:TPU:1 before, /device:TPU:6 now
where the time goes in v7:
time: 104 us
  starting transfers between devices  58.2 us (56%)
  waiting for transfers between devices  37 us (36%)
  Pallas kernels  6.49 us (6%)
  local copies, waits for them, and re-layouts  1.06 us (1%)
    ppermute x6, waiting for transfers between devices, partner(): lax.ppermute(value, axis, [(i, i ^ bit) for i in range(lax.axis_size(axis...  27.9 us
    ppermute x6, starting transfers between devices, partner(): lax.ppermute(value, axis, [(i, i ^ bit) for i in range(lax.axis_size(axis...  15.6 us
    ppermute x4, starting transfers between devices, to_plane(): lax.ppermute(value, 'row', [pair for pair in pairs if pair[0] % PLANE in...  15.3 us
    all_to_all x1, starting transfers between devices, on_device(): wz = lax.all_to_all(wpart, 'col', 0, 0, axis_index_groups=groups)  10.3 us
    all_to_all x1, starting transfers between devices, on_device(): got = lax.all_to_all(sends, 'col', 0, 0)  10.2 us
    ppermute x3, starting transfers between devices, swap(): return lax.ppermute(value, 'row', [(i, i ^ bit) for i in range(row_count)])  6.71 us
    ppermute x4, waiting for transfers between devices, to_plane(): lax.ppermute(value, 'row', [pair for pair in pairs if pair[0] % PLANE in...  6.12 us
    pallas_call x1, Pallas kernels, on_device(): pl.pallas_call(tile_kernel, out_shape=jax.ShapeDtypeStruct((col_count, no...  3.15 us
  transfers between devices with their start and end apart: 15, of which 9 were waited for; matrix products, arithmetic and copies ran while one was open for 1% of the time, Pallas kernels for 0%

profile of v7, /device:TPU:6, one launch (start us, length us, event | category | flops | bytes accessed | tf_op | source)
XLA Modules:
  0.0 103.7 jit_solution(2065663561039288872)
XLA Ops:
  0.6 2.5 %adjoint.1 = (bf16[384,128]{1,0:T(8,128)(2,1)}, bf16[8,128,128]{2,1,0:T(8,128)(2,1)}, s32[1,32]{1,0:T(1,128)}, s32[1,32]{1,0:T(1,128)}) custom-call(s32[3,128]{1,0:T(4,128)} %bitcast.3, bf16[384,128]{1,0:T(8,128)(2,1)} %cot_in.1, bf16[384,128]{1,0:T(8,128)(2,1)} %pre_in.1, bf16[384,128]{1,0:T(8,128)(2,1)} %agg_in.1, bf16[128,128]{1,0:T(8,128)(2,1)} %w_in.1, ...), custom_call_target="tpu_custom_call" | custom-call | tf_op jit(solution)/shard_map/adjoint/pallas_call | solution.py:122
  3.1 0.0 copy-start
  3.1 0.0 copy-start.1
  3.1 0.0 copy-start.2
  3.2 0.0 copy-start.3
  3.2 2.9 %collective-permute-start.1 = (bf16[384,128]{1,0:T(8,128)(2,1)}, bf16[384,128]{1,0:T(8,128)(2,1)S(1)}, u32[]{:S(2)}, u32[]{:S(2)}) collective-permute-start(bf16[384,128]{1,0:T(8,128)(2,1)} %get-tuple-element.12.own), channel_id=1, source_target_pairs={{0,32},{16,48},{32,0},{48,16},{64,96},{80,112},{96,64},{112,80},{1... | collective-permute-start | bytes 294920 | tf_op jit(solution)/shard_map/ppermute | solution.py:142
  6.0 1.9 %collective-permute-start = (bf16[384,128]{1,0:T(8,128)(2,1)}, bf16[384,128]{1,0:T(8,128)(2,1)S(1)}, u32[]{:S(2)}, u32[]{:S(2)}) collective-permute-start(bf16[384,128]{1,0:T(8,128)(2,1)} %get-tuple-element.12.own), channel_id=1, source_target_pairs={{0,16},{16,0},{32,48},{48,32},{64,80},{80,64},{96,112},{112,96},{1... | collective-permute-start | bytes 294920 | tf_op jit(solution)/shard_map/ppermute | solution.py:142
  8.0 0.9 constant_dynamic-update-slice_fusion.1
  8.9 0.6 collective-permute-done.beside
  9.5 5.1 %collective-permute-start.2 = (bf16[768,128]{1,0:T(8,128)(2,1)S(1)}, bf16[768,128]{1,0:T(8,128)(2,1)S(1)}, u32[]{:S(2)}, u32[]{:S(2)}) collective-permute-start(bf16[768,128]{1,0:T(8,128)(2,1)S(1)} %constant_dynamic-update-slice_fusion), channel_id=1, source_target_pairs={{16,432},{32,128},{80,496},{96,192},{144,48},{160,256},{208,112},{... | collective-permute-start | bytes 589832 | tf_op jit(solution)/shard_map/ppermute | solution.py:146
  14.6 10.3 %all-to-all-start = ((bf16[8,128,128]{2,1,0:T(8,128)(2,1)}), bf16[8,128,128]{2,1,0:T(8,128)(2,1)S(1)}, u32[]{:S(2)}, u32[]{:S(2)}) async-start(bf16[8,128,128]{2,1,0:T(8,128)(2,1)} %get-tuple-element.13), calls=%async_computation | async-start | bytes 524288 | tf_op jit(solution)/shard_map/all_to_all | solution.py:157
  24.9 5.7 %collective-permute-start.5 = (bf16[768,128]{1,0:T(8,128)(2,1)S(1)}, bf16[768,128]{1,0:T(8,128)(2,1)S(1)}, u32[]{:S(2)}, u32[]{:S(2)}) collective-permute-start(bf16[768,128]{1,0:T(8,128)(2,1)S(1)} %constant_dynamic-update-slice_fusion), channel_id=1, source_target_pairs={{0,128},{16,400},{32,160},{48,432},{64,192},{80,464},{96,224},{112... | collective-permute-start | bytes 589832 | tf_op jit(solution)/shard_map/ppermute | solution.py:146
  30.6 1.9 %collective-permute-start.4 = (bf16[768,128]{1,0:T(8,128)(2,1)S(1)}, bf16[768,128]{1,0:T(8,128)(2,1)S(1)}, u32[]{:S(2)}, u32[]{:S(2)}) collective-permute-start(bf16[768,128]{1,0:T(8,128)(2,1)S(1)} %constant_dynamic-update-slice_fusion), channel_id=1, source_target_pairs={{0,96},{16,496},{32,64},{48,464},{64,160},{80,48},{96,128},{112,16... | collective-permute-start | bytes 589832 | tf_op jit(solution)/shard_map/ppermute | solution.py:146
  32.6 2.6 %collective-permute-start.3 = (bf16[768,128]{1,0:T(8,128)(2,1)S(1)}, bf16[768,128]{1,0:T(8,128)(2,1)S(1)}, u32[]{:S(2)}, u32[]{:S(2)}) collective-permute-start(bf16[768,128]{1,0:T(8,128)(2,1)S(1)} %constant_dynamic-update-slice_fusion), channel_id=1, source_target_pairs={{0,64},{16,464},{32,96},{48,496},{64,128},{80,16},{96,160},{112,48... | collective-permute-start | bytes 589832 | tf_op jit(solution)/shard_map/ppermute | solution.py:146
  35.2 0.0 collective-permute-done.1
  35.2 0.0 collective-permute-done.2
  35.2 6.1 %collective-permute-done.3 = bf16[768,128]{1,0:T(8,128)(2,1)S(1)} collective-permute-done((bf16[768,128]{1,0:T(8,128)(2,1)S(1)}, bf16[768,128]{1,0:T(8,128)(2,1)S(1)}, u32[]{:S(2)}, u32[]{:S(2)}) %collective-permute-start.3) | collective-permute-done | bytes 196640 | tf_op jit(solution)/shard_map/ppermute | solution.py:146
  41.4 0.0 collective-permute-done.4
  41.4 0.0 collective-permute-done.5
  41.5 0.0 all-to-all-done
  41.5 1.9 %collective-permute-start.6 = (bf16[3456,128]{1,0:T(8,128)(2,1)S(1)}, bf16[3456,128]{1,0:T(8,128)(2,1)S(1)}, u32[]{:S(2)}, u32[]{:S(2)}) collective-permute-start(bf16[3456,128]{1,0:T(8,128)(2,1)S(1)} %constant_dynamic-update-slice_fusion.2.received), channel_id=1, source_target_pairs={{0,16},{16,0},{32,48},{48,32},{64,80},{80,64},{96,112},{112,96},{1... | collective-permute-start | bytes 2654216 | tf_op jit(solution)/shard_map/ppermute | solution.py:142
  43.5 2.4 %collective-permute-done.6.other = bf16[3456,128]{1,0:T(8,128)(2,1)S(1)} collective-permute-done((bf16[3456,128]{1,0:T(8,128)(2,1)S(1)}, bf16[3456,128]{1,0:T(8,128)(2,1)S(1)}, u32[]{:S(2)}, u32[]{:S(2)}) %collective-permute-start.6) | collective-permute-done | bytes 884768 | tf_op jit(solution)/shard_map/ppermute | solution.py:142
  45.8 0.0 copy-done
  45.8 0.0 copy-done.1
  45.8 0.0 copy-done.2
  45.9 0.0 copy-done.3
  45.9 3.1 %tiles.1 = bf16[16,384,128]{2,1,0:T(8,128)(2,1)} custom-call(s32[1,32]{1,0:T(1,128)S(1)} %copy-done.2, s32[1,32]{1,0:T(1,128)S(1)} %copy-done.3, bf16[32,128,128]{2,1,0:T(8,128)(2,1)S(1)} %copy-done, bf16[384,128]{1,0:T(8,128)(2,1)S(1)} %copy-done.1, bf16[384,128]{1,0:T(8,128)(2,1)S(1)} %collective-permute-done.beside, ...), custom_call_target="tpu_custom_call" | custom-call | flops 134217728 | bytes 6291456 | tf_op jit(solution)/shard_map/tiles/pallas_call | solution.py:166
  49.0 10.2 %all-to-all-start.1 = ((bf16[16,384,128]{2,1,0:T(8,128)(2,1)}), bf16[16,384,128]{2,1,0:T(8,128)(2,1)S(1)}, u32[]{:S(2)}, u32[]{:S(2)}) async-start(bf16[16,384,128]{2,1,0:T(8,128)(2,1)} %tiles.1), calls=%async_computation.1 | async-start | bytes 3145728 | tf_op jit(solution)/shard_map/all_to_all | solution.py:185
  59.2 1.9 %collective-permute-start.7 = (f32[128,128]{1,0:T(8,128)S(1)}, f32[128,128]{1,0:T(8,128)S(1)}, u32[]{:S(2)}, u32[]{:S(2)}) collective-permute-start(f32[128,128]{1,0:T(8,128)S(1)} %convert_reduce_fusion), channel_id=1, source_target_pairs={{0,16},{16,0},{32,48},{48,32},{64,80},{80,64},{96,112},{112,96},{1... | collective-permute-start | bytes 196616 | tf_op jit(solution)/shard_map/ppermute | solution.py:161
  61.1 1.2 %collective-permute-done.7 = f32[128,128]{1,0:T(8,128)S(1)} collective-permute-done((f32[128,128]{1,0:T(8,128)S(1)}, f32[128,128]{1,0:T(8,128)S(1)}, u32[]{:S(2)}, u32[]{:S(2)}) %collective-permute-start.7) | collective-permute-done | bytes 65568 | tf_op jit(solution)/shard_map/ppermute | solution.py:161
  62.4 4.0 %collective-permute-start.8 = (f32[128,128]{1,0:T(8,128)S(1)}, f32[128,128]{1,0:T(8,128)S(1)}, u32[]{:S(2)}, u32[]{:S(2)}) collective-permute-start(f32[128,128]{1,0:T(8,128)S(1)} %add.18), channel_id=1, source_target_pairs={{0,32},{16,48},{32,0},{48,16},{64,96},{80,112},{96,64},{112,80},{1... | collective-permute-start | bytes 196616 | tf_op jit(solution)/shard_map/ppermute | solution.py:161
  66.4 4.6 %collective-permute-done.8 = f32[128,128]{1,0:T(8,128)S(1)} collective-permute-done((f32[128,128]{1,0:T(8,128)S(1)}, f32[128,128]{1,0:T(8,128)S(1)}, u32[]{:S(2)}, u32[]{:S(2)}) %collective-permute-start.8) | collective-permute-done | bytes 65568 | tf_op jit(solution)/shard_map/ppermute | solution.py:161
  71.0 1.9 %collective-permute-start.9 = (f32[128,128]{1,0:T(8,128)S(1)}, f32[128,128]{1,0:T(8,128)S(1)}, u32[]{:S(2)}, u32[]{:S(2)}) collective-permute-start(f32[128,128]{1,0:T(8,128)S(1)} %add.19), channel_id=1, source_target_pairs={{0,64},{16,80},{32,96},{48,112},{64,0},{80,16},{96,32},{112,48},{1... | collective-permute-start | bytes 196616 | tf_op jit(solution)/shard_map/ppermute | solution.py:161
  73.0 4.2 %collective-permute-done.9 = f32[128,128]{1,0:T(8,128)S(1)} collective-permute-done((f32[128,128]{1,0:T(8,128)S(1)}, f32[128,128]{1,0:T(8,128)S(1)}, u32[]{:S(2)}, u32[]{:S(2)}) %collective-permute-start.9) | collective-permute-done | bytes 65568 | tf_op jit(solution)/shard_map/ppermute | solution.py:161
  77.2 1.9 %collective-permute-start.10 = (f32[128,128]{1,0:T(8,128)S(1)}, f32[128,128]{1,0:T(8,128)S(1)}, u32[]{:S(2)}, u32[]{:S(2)}) collective-permute-start(f32[128,128]{1,0:T(8,128)S(1)} %add.20), channel_id=1, source_target_pairs={{0,128},{16,144},{32,160},{48,176},{64,192},{80,208},{96,224},{112... | collective-permute-start | bytes 196616 | tf_op jit(solution)/shard_map/ppermute | solution.py:161
  79.1 5.4 %collective-permute-done.10 = f32[128,128]{1,0:T(8,128)S(1)} collective-permute-done((f32[128,128]{1,0:T(8,128)S(1)}, f32[128,128]{1,0:T(8,128)S(1)}, u32[]{:S(2)}, u32[]{:S(2)}) %collective-permute-start.10) | collective-permute-done | bytes 65568 | tf_op jit(solution)/shard_map/ppermute | solution.py:161
  84.5 2.7 %collective-permute-start.11 = (f32[128,128]{1,0:T(8,128)S(1)}, f32[128,128]{1,0:T(8,128)S(1)}, u32[]{:S(2)}, u32[]{:S(2)}) collective-permute-start(f32[128,128]{1,0:T(8,128)S(1)} %add.21), channel_id=1, source_target_pairs={{0,256},{16,272},{32,288},{48,304},{64,320},{80,336},{96,352},{112... | collective-permute-start | bytes 196616 | tf_op jit(solution)/shard_map/ppermute | solution.py:161
  87.2 7.9 %collective-permute-done.11 = f32[128,128]{1,0:T(8,128)S(1)} collective-permute-done((f32[128,128]{1,0:T(8,128)S(1)}, f32[128,128]{1,0:T(8,128)S(1)}, u32[]{:S(2)}, u32[]{:S(2)}) %collective-permute-start.11) | collective-permute-done | bytes 65568 | tf_op jit(solution)/shard_map/ppermute | solution.py:161
  95.2 3.1 %collective-permute-start.12 = (f32[128,128]{1,0:T(8,128)S(1)}, f32[128,128]{1,0:T(8,128)S(1)}, u32[]{:S(2)}, u32[]{:S(2)}) collective-permute-start(f32[128,128]{1,0:T(8,128)S(1)} %add.22), channel_id=1, source_target_pairs={{0,8},{1,9},{2,10},{3,11},{4,12},{5,13},{6,14},{7,15},{8,0},{9,1},... | collective-permute-start | bytes 196616 | tf_op jit(solution)/shard_map/ppermute | solution.py:161
  98.3 4.6 %collective-permute-done.12 = f32[128,128]{1,0:T(8,128)S(1)} collective-permute-done((f32[128,128]{1,0:T(8,128)S(1)}, f32[128,128]{1,0:T(8,128)S(1)}, u32[]{:S(2)}, u32[]{:S(2)}) %collective-permute-start.12) | collective-permute-done | bytes 65568 | tf_op jit(solution)/shard_map/ppermute | solution.py:161
  102.9 0.0 all-to-all-done.1.got_ref
  102.9 0.9 finish.1
  (13 shorter events, 0.2 us)
Async XLA Ops:
  3.1 42.7 %copy-start = (bf16[32,128,128]{2,1,0:T(8,128)(2,1)S(1)}, bf16[32,128,128]{2,1,0:T(8,128)(2,1)}, u32[]{:S(2)}) copy-start(bf16[32,128,128]{2,1,0:T(8,128)(2,1)} %tiles_ref.1) | copy-start | bytes 3145732
  3.1 42.7 %copy-start.1 = (bf16[384,128]{1,0:T(8,128)(2,1)S(1)}, bf16[384,128]{1,0:T(8,128)(2,1)}, u32[]{:S(2)}) copy-start(bf16[384,128]{1,0:T(8,128)(2,1)} %get-tuple-element.12.own) | copy-start | bytes 294916
  3.1 42.7 %copy-start.2 = (s32[1,32]{1,0:T(1,128)S(1)}, s32[1,32]{1,0:T(1,128)}, u32[]{:S(2)}) copy-start(s32[1,32]{1,0:T(1,128)} %get-tuple-element.10.from_ref) | copy-start | bytes 388
  3.2 42.7 %copy-start.3 = (s32[1,32]{1,0:T(1,128)S(1)}, s32[1,32]{1,0:T(1,128)}, u32[]{:S(2)}) copy-start(s32[1,32]{1,0:T(1,128)} %get-tuple-element.11.to_ref) | copy-start | bytes 388
  3.2 32.0 %collective-permute-start.1 = (bf16[384,128]{1,0:T(8,128)(2,1)}, bf16[384,128]{1,0:T(8,128)(2,1)S(1)}, u32[]{:S(2)}, u32[]{:S(2)}) collective-permute-start(bf16[384,128]{1,0:T(8,128)(2,1)} %get-tuple-element.12.own), channel_id=1, source_target_pairs={{0,32},{16,48},{32,0},{48,16},{64,96},{80,112},{96,64},{112,80},{1... | collective-permute-start | bytes 294920 | tf_op jit(solution)/shard_map/ppermute | solution.py:142
  6.0 3.4 %collective-permute-start = (bf16[384,128]{1,0:T(8,128)(2,1)}, bf16[384,128]{1,0:T(8,128)(2,1)S(1)}, u32[]{:S(2)}, u32[]{:S(2)}) collective-permute-start(bf16[384,128]{1,0:T(8,128)(2,1)} %get-tuple-element.12.own), channel_id=1, source_target_pairs={{0,16},{16,0},{32,48},{48,32},{64,80},{80,64},{96,112},{112,96},{1... | collective-permute-start | bytes 294920 | tf_op jit(solution)/shard_map/ppermute | solution.py:142
  9.5 25.7 %collective-permute-start.2 = (bf16[768,128]{1,0:T(8,128)(2,1)S(1)}, bf16[768,128]{1,0:T(8,128)(2,1)S(1)}, u32[]{:S(2)}, u32[]{:S(2)}) collective-permute-start(bf16[768,128]{1,0:T(8,128)(2,1)S(1)} %constant_dynamic-update-slice_fusion), channel_id=1, source_target_pairs={{16,432},{32,128},{80,496},{96,192},{144,48},{160,256},{208,112},{... | collective-permute-start | bytes 589832 | tf_op jit(solution)/shard_map/ppermute | solution.py:146
  14.6 26.9 %all-to-all-start = ((bf16[8,128,128]{2,1,0:T(8,128)(2,1)}), bf16[8,128,128]{2,1,0:T(8,128)(2,1)S(1)}, u32[]{:S(2)}, u32[]{:S(2)}) async-start(bf16[8,128,128]{2,1,0:T(8,128)(2,1)} %get-tuple-element.13), calls=%async_computation | async-start | bytes 524288 | tf_op jit(solution)/shard_map/all_to_all | solution.py:157
  24.9 16.5 %collective-permute-start.5 = (bf16[768,128]{1,0:T(8,128)(2,1)S(1)}, bf16[768,128]{1,0:T(8,128)(2,1)S(1)}, u32[]{:S(2)}, u32[]{:S(2)}) collective-permute-start(bf16[768,128]{1,0:T(8,128)(2,1)S(1)} %constant_dynamic-update-slice_fusion), channel_id=1, source_target_pairs={{0,128},{16,400},{32,160},{48,432},{64,192},{80,464},{96,224},{112... | collective-permute-start | bytes 589832 | tf_op jit(solution)/shard_map/ppermute | solution.py:146
  30.6 10.7 %collective-permute-start.4 = (bf16[768,128]{1,0:T(8,128)(2,1)S(1)}, bf16[768,128]{1,0:T(8,128)(2,1)S(1)}, u32[]{:S(2)}, u32[]{:S(2)}) collective-permute-start(bf16[768,128]{1,0:T(8,128)(2,1)S(1)} %constant_dynamic-update-slice_fusion), channel_id=1, source_target_pairs={{0,96},{16,496},{32,64},{48,464},{64,160},{80,48},{96,128},{112,16... | collective-permute-start | bytes 589832 | tf_op jit(solution)/shard_map/ppermute | solution.py:146
  32.6 8.8 %collective-permute-start.3 = (bf16[768,128]{1,0:T(8,128)(2,1)S(1)}, bf16[768,128]{1,0:T(8,128)(2,1)S(1)}, u32[]{:S(2)}, u32[]{:S(2)}) collective-permute-start(bf16[768,128]{1,0:T(8,128)(2,1)S(1)} %constant_dynamic-update-slice_fusion), channel_id=1, source_target_pairs={{0,64},{16,464},{32,96},{48,496},{64,128},{80,16},{96,160},{112,48... | collective-permute-start | bytes 589832 | tf_op jit(solution)/shard_map/ppermute | solution.py:146
  41.5 4.3 %collective-permute-start.6 = (bf16[3456,128]{1,0:T(8,128)(2,1)S(1)}, bf16[3456,128]{1,0:T(8,128)(2,1)S(1)}, u32[]{:S(2)}, u32[]{:S(2)}) collective-permute-start(bf16[3456,128]{1,0:T(8,128)(2,1)S(1)} %constant_dynamic-update-slice_fusion.2.received), channel_id=1, source_target_pairs={{0,16},{16,0},{32,48},{48,32},{64,80},{80,64},{96,112},{112,96},{1... | collective-permute-start | bytes 2654216 | tf_op jit(solution)/shard_map/ppermute | solution.py:142
  49.0 53.8 %all-to-all-start.1 = ((bf16[16,384,128]{2,1,0:T(8,128)(2,1)}), bf16[16,384,128]{2,1,0:T(8,128)(2,1)S(1)}, u32[]{:S(2)}, u32[]{:S(2)}) async-start(bf16[16,384,128]{2,1,0:T(8,128)(2,1)} %tiles.1), calls=%async_computation.1 | async-start | bytes 3145728 | tf_op jit(solution)/shard_map/all_to_all | solution.py:185
  59.2 3.1 %collective-permute-start.7 = (f32[128,128]{1,0:T(8,128)S(1)}, f32[128,128]{1,0:T(8,128)S(1)}, u32[]{:S(2)}, u32[]{:S(2)}) collective-permute-start(f32[128,128]{1,0:T(8,128)S(1)} %convert_reduce_fusion), channel_id=1, source_target_pairs={{0,16},{16,0},{32,48},{48,32},{64,80},{80,64},{96,112},{112,96},{1... | collective-permute-start | bytes 196616 | tf_op jit(solution)/shard_map/ppermute | solution.py:161
  62.4 8.7 %collective-permute-start.8 = (f32[128,128]{1,0:T(8,128)S(1)}, f32[128,128]{1,0:T(8,128)S(1)}, u32[]{:S(2)}, u32[]{:S(2)}) collective-permute-start(f32[128,128]{1,0:T(8,128)S(1)} %add.18), channel_id=1, source_target_pairs={{0,32},{16,48},{32,0},{48,16},{64,96},{80,112},{96,64},{112,80},{1... | collective-permute-start | bytes 196616 | tf_op jit(solution)/shard_map/ppermute | solution.py:161
  71.0 6.2 %collective-permute-start.9 = (f32[128,128]{1,0:T(8,128)S(1)}, f32[128,128]{1,0:T(8,128)S(1)}, u32[]{:S(2)}, u32[]{:S(2)}) collective-permute-start(f32[128,128]{1,0:T(8,128)S(1)} %add.19), channel_id=1, source_target_pairs={{0,64},{16,80},{32,96},{48,112},{64,0},{80,16},{96,32},{112,48},{1... | collective-permute-start | bytes 196616 | tf_op jit(solution)/shard_map/ppermute | solution.py:161
  77.2 7.3 %collective-permute-start.10 = (f32[128,128]{1,0:T(8,128)S(1)}, f32[128,128]{1,0:T(8,128)S(1)}, u32[]{:S(2)}, u32[]{:S(2)}) collective-permute-start(f32[128,128]{1,0:T(8,128)S(1)} %add.20), channel_id=1, source_target_pairs={{0,128},{16,144},{32,160},{48,176},{64,192},{80,208},{96,224},{112... | collective-permute-start | bytes 196616 | tf_op jit(solution)/shard_map/ppermute | solution.py:161
  84.5 10.7 %collective-permute-start.11 = (f32[128,128]{1,0:T(8,128)S(1)}, f32[128,128]{1,0:T(8,128)S(1)}, u32[]{:S(2)}, u32[]{:S(2)}) collective-permute-start(f32[128,128]{1,0:T(8,128)S(1)} %add.21), channel_id=1, source_target_pairs={{0,256},{16,272},{32,288},{48,304},{64,320},{80,336},{96,352},{112... | collective-permute-start | bytes 196616 | tf_op jit(solution)/shard_map/ppermute | solution.py:161
  95.2 7.7 %collective-permute-start.12 = (f32[128,128]{1,0:T(8,128)S(1)}, f32[128,128]{1,0:T(8,128)S(1)}, u32[]{:S(2)}, u32[]{:S(2)}) collective-permute-start(f32[128,128]{1,0:T(8,128)S(1)} %add.22), channel_id=1, source_target_pairs={{0,8},{1,9},{2,10},{3,11},{4,12},{5,13},{6,14},{7,15},{8,0},{9,1},... | collective-permute-start | bytes 196616 | tf_op jit(solution)/shard_map/ppermute | solution.py:161

commit v8 on v7

--- a/solution.py
+++ b/solution.py
@@ -27,8 +27,8 @@
     below = gap > planes // 2
     steps = jnp.where(below, planes - gap, gap)
     receiver = jnp.where(gap == 0, core, jnp.where(below, 0, 1))
-    first = jnp.where(steps == 2, jnp.where(same_chip, 7, 1), jnp.where(same_chip, 3, 5))
-    place = jnp.where(gap == 0, 0, first + jnp.where(core == receiver, 0, 1))
+    first = jnp.where(steps == 2, jnp.where(same_chip, 2, 0), jnp.where(same_chip, 5, 7))
+    place = jnp.where(gap == 0, 4, first + jnp.where(core == receiver, 0, 1))
     slot = 2 + place + jnp.where(receiver == lax.rem(row, 2), 0, 9)
     slot = jnp.where((gap == 0) & same_chip, jnp.where(same_core, 0, 1), slot)
     return slot * blocks + lax.rem(block, blocks)
@@ -114,6 +114,7 @@
     nodes, feat = cotangent.shape
     blocks_dev = nodes // SIDE
     half = col_count // 2
+    quad = half // 2
     params = pltpu.CompilerParams(vmem_limit_bytes=12 << 20)
     small = pltpu.CompilerParams(vmem_limit_bytes=4 << 20)
 
@@ -121,7 +122,7 @@
     scalars = jax.ShapeDtypeStruct((1, tiles), jnp.int32)
     adjoint, wpart, places, targets = pl.pallas_call(
         adjoint_kernel,
-        out_shape=(jax.ShapeDtypeStruct((nodes, feat), BF), jax.ShapeDtypeStruct((half, feat, feat), BF), scalars, scalars),
+        out_shape=(jax.ShapeDtypeStruct((nodes, feat), BF), jax.ShapeDtypeStruct((quad, feat, feat), BF), scalars, scalars),
         in_specs=[pl.BlockSpec(memory_space=pltpu.HBM)] * 7,
         out_specs=(vmem(),) * 4,
         scratch_shapes=[
@@ -153,16 +154,16 @@
     across_near = to_plane(chip, 1, 2, (0, 1, 2, 3))
     near = to_plane(chip, 1, 0, (0, 1, 2, 3))
 
-    groups = [list(range(half)), list(range(half, col_count))]
-    wz = lax.all_to_all(wpart, "col", 0, 0, axis_index_groups=groups)
-    wsum = wz.astype(F32).sum(0)
-
     def partner(value, axis, bit):
         return lax.ppermute(value, axis, [(i, i ^ bit) for i in range(lax.axis_size(axis))])
 
-    received = jnp.concatenate([across, across_far, near, across_near, far])
+    wpart, across = lax.optimization_barrier((wpart, across))
+    groups = [list(range(i, i + quad)) for i in range(0, col_count, quad)]
+    wsum = lax.all_to_all(wpart, "col", 0, 0, axis_index_groups=groups).astype(F32).sum(0)
+    received = jnp.concatenate([across_far, far, across, near, across_near])
     received, wsum = lax.optimization_barrier((received, wsum))
     other = swap(received, 1)
+    wnext = partner(wsum, "col", quad)
     sends = pl.pallas_call(
         tile_kernel,
         out_shape=jax.ShapeDtypeStruct((col_count, nodes, feat), BF),
@@ -181,10 +182,15 @@
         name="tiles",
     )(places, targets, tile_values, adjoint, beside, received, other)
 
-    sends, wsum = lax.optimization_barrier((sends, wsum))
+    sends, wnext = lax.optimization_barrier((sends, wnext))
     got = lax.all_to_all(sends, "col", 0, 0)
-    for bit in [1 << k for k in range((row_count - 1).bit_length())]:
+    wsum = wsum + wnext
+    for bit in (1, 2):
         wsum = wsum + partner(wsum, "row", bit)
+    planes = (PLANE, 2 * PLANE, 3 * PLANE)
+    one, two, three = [partner(wsum, "row", bits) for bits in planes]
+    wsum = (wsum + one) + (two + three)
+    wsum = wsum + partner(wsum, "row", 4 * PLANE)
     wsum = wsum + partner(wsum, "col", half)
     scale = 1.0 / float(nodes * row_count * col_count) ** 0.5
     node_grad, weight_grad = pl.pallas_call(

time: 104 us -> 106 us (1.019)
  the two profiles are of different devices: /device:TPU:6 before, /device:TPU:4 now
where the time goes in v8:
time: 106 us; the launch traced here: 105 us
  starting transfers between devices  72.8 us (69%)
  waiting for transfers between devices  24 us (23%)
  Pallas kernels  6.52 us (6%)
    ppermute x8, starting transfers between devices, partner(): lax.ppermute(value, axis, [(i, i ^ bit) for i in range(lax.axis_size(axis...  32.8 us
    ppermute x8, waiting for transfers between devices, partner(): lax.ppermute(value, axis, [(i, i ^ bit) for i in range(lax.axis_size(axis...  17.6 us
    ppermute x4, starting transfers between devices, to_plane(): lax.ppermute(value, 'row', [pair for pair in pairs if pair[0] % PLANE in...  11.6 us
    all_to_all x1, starting transfers between devices, on_device(): got = lax.all_to_all(sends, 'col', 0, 0)  10.6 us
    ppermute x3, starting transfers between devices, swap(): return lax.ppermute(value, 'row', [(i, i ^ bit) for i in range(row_count)])  10.6 us
    all_to_all x1, starting transfers between devices, on_device(): lax.all_to_all(wpart, 'col', 0, 0, axis_index_groups=groups).astype(F32)  7.27 us
    all_to_all x1, waiting for transfers between devices, on_device(): lax.all_to_all(wpart, 'col', 0, 0, axis_index_groups=groups).astype(F32)  5.78 us
    pallas_call x1, Pallas kernels, on_device(): pl.pallas_call(tile_kernel, out_shape=jax.ShapeDtypeStruct((col_count, no...  3.14 us
  transfers between devices with their start and end apart: 17, of which 8 were waited for; matrix products, arithmetic and copies ran while one was open for 1% of the time, Pallas kernels for 3%

profile of v8, /device:TPU:4, one launch (start us, length us, event | category | flops | bytes accessed | tf_op | source)
XLA Modules:
  0.0 105.5 jit_solution(2060246987634714009)
XLA Ops:
  0.6 0.0 copy-start
  0.6 2.5 %adjoint.1 = (bf16[384,128]{1,0:T(8,128)(2,1)}, bf16[4,128,128]{2,1,0:T(8,128)(2,1)}, s32[1,32]{1,0:T(1,128)}, s32[1,32]{1,0:T(1,128)}) custom-call(s32[3,128]{1,0:T(4,128)} %bitcast.3, bf16[384,128]{1,0:T(8,128)(2,1)} %cot_in.1, bf16[384,128]{1,0:T(8,128)(2,1)} %pre_in.1, bf16[384,128]{1,0:T(8,128)(2,1)} %agg_in.1, bf16[128,128]{1,0:T(8,128)(2,1)} %w_in.1, ...), custom_call_target="tpu_custom_call" | custom-call | tf_op jit(solution)/shard_map/adjoint/pallas_call | solution.py:123
  3.2 0.0 copy-start.1
  3.2 0.0 copy-start.2
  3.2 0.0 copy-start.3
  3.2 2.1 %collective-permute-start = (bf16[384,128]{1,0:T(8,128)(2,1)}, bf16[384,128]{1,0:T(8,128)(2,1)S(1)}, u32[]{:S(2)}, u32[]{:S(2)}) collective-permute-start(bf16[384,128]{1,0:T(8,128)(2,1)} %get-tuple-element.14.own), channel_id=1, source_target_pairs={{0,16},{16,0},{32,48},{48,32},{64,80},{80,64},{96,112},{112,96},{1... | collective-permute-start | bytes 294920 | tf_op jit(solution)/shard_map/ppermute | solution.py:143
  5.3 0.9 constant_dynamic-update-slice_fusion.1
  6.2 0.6 collective-permute-done.beside
  6.8 1.3 %collective-permute-start.1 = (bf16[768,128]{1,0:T(8,128)(2,1)S(1)}, bf16[768,128]{1,0:T(8,128)(2,1)S(1)}, u32[]{:S(2)}, u32[]{:S(2)}) collective-permute-start(bf16[768,128]{1,0:T(8,128)(2,1)S(1)} %constant_dynamic-update-slice_fusion), channel_id=1, source_target_pairs={{16,432},{32,128},{80,496},{96,192},{144,48},{160,256},{208,112},{... | collective-permute-start | bytes 589832 | tf_op jit(solution)/shard_map/ppermute | solution.py:147
  8.1 6.6 %collective-permute-start.3 = (bf16[384,128]{1,0:T(8,128)(2,1)}, bf16[384,128]{1,0:T(8,128)(2,1)S(1)}, u32[]{:S(2)}, u32[]{:S(2)}) collective-permute-start(bf16[384,128]{1,0:T(8,128)(2,1)} %get-tuple-element.14.own), channel_id=1, source_target_pairs={{0,32},{16,48},{32,0},{48,16},{64,96},{80,112},{96,64},{112,80},{1... | collective-permute-start | bytes 294920 | tf_op jit(solution)/shard_map/ppermute | solution.py:143
  14.6 5.7 %collective-permute-start.2 = (bf16[768,128]{1,0:T(8,128)(2,1)S(1)}, bf16[768,128]{1,0:T(8,128)(2,1)S(1)}, u32[]{:S(2)}, u32[]{:S(2)}) collective-permute-start(bf16[768,128]{1,0:T(8,128)(2,1)S(1)} %constant_dynamic-update-slice_fusion), channel_id=1, source_target_pairs={{0,128},{16,400},{32,160},{48,432},{64,192},{80,464},{96,224},{112... | collective-permute-start | bytes 589832 | tf_op jit(solution)/shard_map/ppermute | solution.py:147
  20.4 2.6 %collective-permute-start.4 = (bf16[768,128]{1,0:T(8,128)(2,1)S(1)}, bf16[768,128]{1,0:T(8,128)(2,1)S(1)}, u32[]{:S(2)}, u32[]{:S(2)}) collective-permute-start(bf16[768,128]{1,0:T(8,128)(2,1)S(1)} %constant_dynamic-update-slice_fusion), channel_id=1, source_target_pairs={{0,64},{16,464},{32,96},{48,496},{64,128},{80,16},{96,160},{112,48... | collective-permute-start | bytes 589832 | tf_op jit(solution)/shard_map/ppermute | solution.py:147
  23.0 2.0 %collective-permute-start.5 = (bf16[768,128]{1,0:T(8,128)(2,1)S(1)}, bf16[768,128]{1,0:T(8,128)(2,1)S(1)}, u32[]{:S(2)}, u32[]{:S(2)}) collective-permute-start(bf16[768,128]{1,0:T(8,128)(2,1)S(1)} %constant_dynamic-update-slice_fusion), channel_id=1, source_target_pairs={{0,96},{16,496},{32,64},{48,464},{64,160},{80,48},{96,128},{112,16... | collective-permute-start | bytes 589832 | tf_op jit(solution)/shard_map/ppermute | solution.py:147
  25.0 0.0 collective-permute-done.3
  25.0 7.3 %all-to-all-start = ((bf16[4,128,128]{2,1,0:T(8,128)(2,1)}), bf16[4,128,128]{2,1,0:T(8,128)(2,1)S(1)}, u32[]{:S(2)}, u32[]{:S(2)}) async-start(bf16[4,128,128]{2,1,0:T(8,128)(2,1)} %get-tuple-element.17), calls=%async_computation | async-start | bytes 262144 | tf_op jit(solution)/shard_map/all_to_all | solution.py:162
  32.3 0.0 collective-permute-done.1
  32.3 0.0 collective-permute-done.2
  32.4 0.0 collective-permute-done.4
  32.4 5.8 %all-to-all-done = bf16[4,128,128]{2,1,0:T(8,128)(2,1)S(1)} async-done(((bf16[4,128,128]{2,1,0:T(8,128)(2,1)}), bf16[4,128,128]{2,1,0:T(8,128)(2,1)S(1)}, u32[]{:S(2)}, u32[]{:S(2)}) %all-to-all-start) | async-done | bytes 131104 | tf_op jit(solution)/shard_map/all_to_all | solution.py:162
  38.2 0.0 collective-permute-done.5
  38.3 1.9 %collective-permute-start.6 = (bf16[3456,128]{1,0:T(8,128)(2,1)S(1)}, bf16[3456,128]{1,0:T(8,128)(2,1)S(1)}, u32[]{:S(2)}, u32[]{:S(2)}) collective-permute-start(bf16[3456,128]{1,0:T(8,128)(2,1)S(1)} %constant_dynamic-update-slice_fusion.2.received), channel_id=1, source_target_pairs={{0,16},{16,0},{32,48},{48,32},{64,80},{80,64},{96,112},{112,96},{1... | collective-permute-start | bytes 2654216 | tf_op jit(solution)/shard_map/ppermute | solution.py:143
  40.2 8.2 %collective-permute-start.7 = (f32[128,128]{1,0:T(8,128)S(1)}, f32[128,128]{1,0:T(8,128)S(1)}, u32[]{:S(2)}, u32[]{:S(2)}) collective-permute-start(f32[128,128]{1,0:T(8,128)S(1)} %convert_reduce_fusion), channel_id=1, source_target_pairs={{0,4},{1,5},{2,6},{3,7},{4,0},{5,1},{6,2},{7,3},{8,12},{9,13},{10,... | collective-permute-start | bytes 196616 | tf_op jit(solution)/shard_map/ppermute | solution.py:158
  48.4 0.0 collective-permute-done.6.other
  48.4 0.0 copy-done
  48.4 0.0 copy-done.1
  48.5 0.0 copy-done.2
  48.5 0.0 copy-done.3
  48.5 3.1 %tiles.1 = bf16[16,384,128]{2,1,0:T(8,128)(2,1)} custom-call(s32[1,32]{1,0:T(1,128)S(1)} %copy-done.2, s32[1,32]{1,0:T(1,128)S(1)} %copy-done.3, bf16[32,128,128]{2,1,0:T(8,128)(2,1)S(1)} %copy-done, bf16[384,128]{1,0:T(8,128)(2,1)S(1)} %copy-done.1, bf16[384,128]{1,0:T(8,128)(2,1)S(1)} %collective-permute-done.beside, ...), custom_call_target="tpu_custom_call" | custom-call | flops 134217728 | bytes 6291456 | tf_op jit(solution)/shard_map/tiles/pallas_call | solution.py:167
  51.6 0.0 collective-permute-done.7
  51.6 10.6 %all-to-all-start.1 = ((bf16[16,384,128]{2,1,0:T(8,128)(2,1)}), bf16[16,384,128]{2,1,0:T(8,128)(2,1)S(1)}, u32[]{:S(2)}, u32[]{:S(2)}) async-start(bf16[16,384,128]{2,1,0:T(8,128)(2,1)} %tiles.1), calls=%async_computation.1 | async-start | bytes 3145728 | tf_op jit(solution)/shard_map/all_to_all | solution.py:186
  62.2 1.9 %collective-permute-start.8 = (f32[128,128]{1,0:T(8,128)S(1)}, f32[128,128]{1,0:T(8,128)S(1)}, u32[]{:S(2)}, u32[]{:S(2)}) collective-permute-start(f32[128,128]{1,0:T(8,128)S(1)} %add.24), channel_id=1, source_target_pairs={{0,16},{16,0},{32,48},{48,32},{64,80},{80,64},{96,112},{112,96},{1... | collective-permute-start | bytes 196616 | tf_op jit(solution)/shard_map/ppermute | solution.py:158
  64.2 1.2 %collective-permute-done.8 = f32[128,128]{1,0:T(8,128)S(1)} collective-permute-done((f32[128,128]{1,0:T(8,128)S(1)}, f32[128,128]{1,0:T(8,128)S(1)}, u32[]{:S(2)}, u32[]{:S(2)}) %collective-permute-start.8) | collective-permute-done | bytes 65568 | tf_op jit(solution)/shard_map/ppermute | solution.py:158
  65.4 3.9 %collective-permute-start.9 = (f32[128,128]{1,0:T(8,128)S(1)}, f32[128,128]{1,0:T(8,128)S(1)}, u32[]{:S(2)}, u32[]{:S(2)}) collective-permute-start(f32[128,128]{1,0:T(8,128)S(1)} %add.25), channel_id=1, source_target_pairs={{0,32},{16,48},{32,0},{48,16},{64,96},{80,112},{96,64},{112,80},{1... | collective-permute-start | bytes 196616 | tf_op jit(solution)/shard_map/ppermute | solution.py:158
  69.3 4.1 %collective-permute-done.9 = f32[128,128]{1,0:T(8,128)S(1)} collective-permute-done((f32[128,128]{1,0:T(8,128)S(1)}, f32[128,128]{1,0:T(8,128)S(1)}, u32[]{:S(2)}, u32[]{:S(2)}) %collective-permute-start.9) | collective-permute-done | bytes 65568 | tf_op jit(solution)/shard_map/ppermute | solution.py:158
  73.5 2.6 %collective-permute-start.10 = (f32[128,128]{1,0:T(8,128)S(1)}, f32[128,128]{1,0:T(8,128)S(1)}, u32[]{:S(2)}, u32[]{:S(2)}) collective-permute-start(f32[128,128]{1,0:T(8,128)S(1)} %add.26), channel_id=1, source_target_pairs={{0,64},{16,80},{32,96},{48,112},{64,0},{80,16},{96,32},{112,48},{1... | collective-permute-start | bytes 196616 | tf_op jit(solution)/shard_map/ppermute | solution.py:158
  76.1 2.7 %collective-permute-start.11 = (f32[128,128]{1,0:T(8,128)S(1)}, f32[128,128]{1,0:T(8,128)S(1)}, u32[]{:S(2)}, u32[]{:S(2)}) collective-permute-start(f32[128,128]{1,0:T(8,128)S(1)} %add.26), channel_id=1, source_target_pairs={{0,128},{16,144},{32,160},{48,176},{64,192},{80,208},{96,224},{112... | collective-permute-start | bytes 196616 | tf_op jit(solution)/shard_map/ppermute | solution.py:158
  78.8 4.8 %collective-permute-start.12 = (f32[128,128]{1,0:T(8,128)S(1)}, f32[128,128]{1,0:T(8,128)S(1)}, u32[]{:S(2)}, u32[]{:S(2)}) collective-permute-start(f32[128,128]{1,0:T(8,128)S(1)} %add.26), channel_id=1, source_target_pairs={{0,192},{16,208},{32,224},{48,240},{64,128},{80,144},{96,160},{112... | collective-permute-start | bytes 196616 | tf_op jit(solution)/shard_map/ppermute | solution.py:158
  83.6 0.0 collective-permute-done.10
  83.6 1.5 %collective-permute-done.11 = f32[128,128]{1,0:T(8,128)S(1)} collective-permute-done((f32[128,128]{1,0:T(8,128)S(1)}, f32[128,128]{1,0:T(8,128)S(1)}, u32[]{:S(2)}, u32[]{:S(2)}) %collective-permute-start.11) | collective-permute-done | bytes 65568 | tf_op jit(solution)/shard_map/ppermute | solution.py:158
  85.1 1.7 %collective-permute-done.12 = f32[128,128]{1,0:T(8,128)S(1)} collective-permute-done((f32[128,128]{1,0:T(8,128)S(1)}, f32[128,128]{1,0:T(8,128)S(1)}, u32[]{:S(2)}, u32[]{:S(2)}) %collective-permute-start.12) | collective-permute-done | bytes 65568 | tf_op jit(solution)/shard_map/ppermute | solution.py:158
  86.8 6.7 %collective-permute-start.13 = (f32[128,128]{1,0:T(8,128)S(1)}, f32[128,128]{1,0:T(8,128)S(1)}, u32[]{:S(2)}, u32[]{:S(2)}) collective-permute-start(f32[128,128]{1,0:T(8,128)S(1)} %add_add_fusion), channel_id=1, source_target_pairs={{0,256},{16,272},{32,288},{48,304},{64,320},{80,336},{96,352},{112... | collective-permute-start | bytes 196616 | tf_op jit(solution)/shard_map/ppermute | solution.py:158
  93.6 3.3 %collective-permute-done.13 = f32[128,128]{1,0:T(8,128)S(1)} collective-permute-done((f32[128,128]{1,0:T(8,128)S(1)}, f32[128,128]{1,0:T(8,128)S(1)}, u32[]{:S(2)}, u32[]{:S(2)}) %collective-permute-start.13) | collective-permute-done | bytes 65568 | tf_op jit(solution)/shard_map/ppermute | solution.py:158
  96.9 1.9 %collective-permute-start.14 = (f32[128,128]{1,0:T(8,128)S(1)}, f32[128,128]{1,0:T(8,128)S(1)}, u32[]{:S(2)}, u32[]{:S(2)}) collective-permute-start(f32[128,128]{1,0:T(8,128)S(1)} %add.30), channel_id=1, source_target_pairs={{0,8},{1,9},{2,10},{3,11},{4,12},{5,13},{6,14},{7,15},{8,0},{9,1},... | collective-permute-start | bytes 196616 | tf_op jit(solution)/shard_map/ppermute | solution.py:158
  98.9 5.7 %collective-permute-done.14 = f32[128,128]{1,0:T(8,128)S(1)} collective-permute-done((f32[128,128]{1,0:T(8,128)S(1)}, f32[128,128]{1,0:T(8,128)S(1)}, u32[]{:S(2)}, u32[]{:S(2)}) %collective-permute-start.14) | collective-permute-done | bytes 65568 | tf_op jit(solution)/shard_map/ppermute | solution.py:158
  104.6 0.0 all-to-all-done.1.got_ref
  104.6 0.9 finish.1
  (13 shorter events, 0.2 us)
Async XLA Ops:
  0.6 47.8 %copy-start = (bf16[32,128,128]{2,1,0:T(8,128)(2,1)S(1)}, bf16[32,128,128]{2,1,0:T(8,128)(2,1)}, u32[]{:S(2)}) copy-start(bf16[32,128,128]{2,1,0:T(8,128)(2,1)} %tiles_ref.1) | copy-start | bytes 3145732
  3.2 45.3 %copy-start.1 = (bf16[384,128]{1,0:T(8,128)(2,1)S(1)}, bf16[384,128]{1,0:T(8,128)(2,1)}, u32[]{:S(2)}) copy-start(bf16[384,128]{1,0:T(8,128)(2,1)} %get-tuple-element.14.own) | copy-start | bytes 294916
  3.2 45.3 %copy-start.2 = (s32[1,32]{1,0:T(1,128)S(1)}, s32[1,32]{1,0:T(1,128)}, u32[]{:S(2)}) copy-start(s32[1,32]{1,0:T(1,128)} %get-tuple-element.12.from_ref) | copy-start | bytes 388
  3.2 45.3 %copy-start.3 = (s32[1,32]{1,0:T(1,128)S(1)}, s32[1,32]{1,0:T(1,128)}, u32[]{:S(2)}) copy-start(s32[1,32]{1,0:T(1,128)} %get-tuple-element.13.to_ref) | copy-start | bytes 388
  3.2 3.5 %collective-permute-start = (bf16[384,128]{1,0:T(8,128)(2,1)}, bf16[384,128]{1,0:T(8,128)(2,1)S(1)}, u32[]{:S(2)}, u32[]{:S(2)}) collective-permute-start(bf16[384,128]{1,0:T(8,128)(2,1)} %get-tuple-element.14.own), channel_id=1, source_target_pairs={{0,16},{16,0},{32,48},{48,32},{64,80},{80,64},{96,112},{112,96},{1... | collective-permute-start | bytes 294920 | tf_op jit(solution)/shard_map/ppermute | solution.py:143
  6.8 25.5 %collective-permute-start.1 = (bf16[768,128]{1,0:T(8,128)(2,1)S(1)}, bf16[768,128]{1,0:T(8,128)(2,1)S(1)}, u32[]{:S(2)}, u32[]{:S(2)}) collective-permute-start(bf16[768,128]{1,0:T(8,128)(2,1)S(1)} %constant_dynamic-update-slice_fusion), channel_id=1, source_target_pairs={{16,432},{32,128},{80,496},{96,192},{144,48},{160,256},{208,112},{... | collective-permute-start | bytes 589832 | tf_op jit(solution)/shard_map/ppermute | solution.py:147
  8.1 16.9 %collective-permute-start.3 = (bf16[384,128]{1,0:T(8,128)(2,1)}, bf16[384,128]{1,0:T(8,128)(2,1)S(1)}, u32[]{:S(2)}, u32[]{:S(2)}) collective-permute-start(bf16[384,128]{1,0:T(8,128)(2,1)} %get-tuple-element.14.own), channel_id=1, source_target_pairs={{0,32},{16,48},{32,0},{48,16},{64,96},{80,112},{96,64},{112,80},{1... | collective-permute-start | bytes 294920 | tf_op jit(solution)/shard_map/ppermute | solution.py:143
  14.6 17.7 %collective-permute-start.2 = (bf16[768,128]{1,0:T(8,128)(2,1)S(1)}, bf16[768,128]{1,0:T(8,128)(2,1)S(1)}, u32[]{:S(2)}, u32[]{:S(2)}) collective-permute-start(bf16[768,128]{1,0:T(8,128)(2,1)S(1)} %constant_dynamic-update-slice_fusion), channel_id=1, source_target_pairs={{0,128},{16,400},{32,160},{48,432},{64,192},{80,464},{96,224},{112... | collective-permute-start | bytes 589832 | tf_op jit(solution)/shard_map/ppermute | solution.py:147
  20.4 12.0 %collective-permute-start.4 = (bf16[768,128]{1,0:T(8,128)(2,1)S(1)}, bf16[768,128]{1,0:T(8,128)(2,1)S(1)}, u32[]{:S(2)}, u32[]{:S(2)}) collective-permute-start(bf16[768,128]{1,0:T(8,128)(2,1)S(1)} %constant_dynamic-update-slice_fusion), channel_id=1, source_target_pairs={{0,64},{16,464},{32,96},{48,496},{64,128},{80,16},{96,160},{112,48... | collective-permute-start | bytes 589832 | tf_op jit(solution)/shard_map/ppermute | solution.py:147
  23.0 15.3 %collective-permute-start.5 = (bf16[768,128]{1,0:T(8,128)(2,1)S(1)}, bf16[768,128]{1,0:T(8,128)(2,1)S(1)}, u32[]{:S(2)}, u32[]{:S(2)}) collective-permute-start(bf16[768,128]{1,0:T(8,128)(2,1)S(1)} %constant_dynamic-update-slice_fusion), channel_id=1, source_target_pairs={{0,96},{16,496},{32,64},{48,464},{64,160},{80,48},{96,128},{112,16... | collective-permute-start | bytes 589832 | tf_op jit(solution)/shard_map/ppermute | solution.py:147
  25.0 13.2 %all-to-all-start = ((bf16[4,128,128]{2,1,0:T(8,128)(2,1)}), bf16[4,128,128]{2,1,0:T(8,128)(2,1)S(1)}, u32[]{:S(2)}, u32[]{:S(2)}) async-start(bf16[4,128,128]{2,1,0:T(8,128)(2,1)} %get-tuple-element.17), calls=%async_computation | async-start | bytes 262144 | tf_op jit(solution)/shard_map/all_to_all | solution.py:162
  38.3 10.2 %collective-permute-start.6 = (bf16[3456,128]{1,0:T(8,128)(2,1)S(1)}, bf16[3456,128]{1,0:T(8,128)(2,1)S(1)}, u32[]{:S(2)}, u32[]{:S(2)}) collective-permute-start(bf16[3456,128]{1,0:T(8,128)(2,1)S(1)} %constant_dynamic-update-slice_fusion.2.received), channel_id=1, source_target_pairs={{0,16},{16,0},{32,48},{48,32},{64,80},{80,64},{96,112},{112,96},{1... | collective-permute-start | bytes 2654216 | tf_op jit(solution)/shard_map/ppermute | solution.py:143
  40.2 11.4 %collective-permute-start.7 = (f32[128,128]{1,0:T(8,128)S(1)}, f32[128,128]{1,0:T(8,128)S(1)}, u32[]{:S(2)}, u32[]{:S(2)}) collective-permute-start(f32[128,128]{1,0:T(8,128)S(1)} %convert_reduce_fusion), channel_id=1, source_target_pairs={{0,4},{1,5},{2,6},{3,7},{4,0},{5,1},{6,2},{7,3},{8,12},{9,13},{10,... | collective-permute-start | bytes 196616 | tf_op jit(solution)/shard_map/ppermute | solution.py:158
  51.6 53.0 %all-to-all-start.1 = ((bf16[16,384,128]{2,1,0:T(8,128)(2,1)}), bf16[16,384,128]{2,1,0:T(8,128)(2,1)S(1)}, u32[]{:S(2)}, u32[]{:S(2)}) async-start(bf16[16,384,128]{2,1,0:T(8,128)(2,1)} %tiles.1), calls=%async_computation.1 | async-start | bytes 3145728 | tf_op jit(solution)/shard_map/all_to_all | solution.py:186
  62.2 3.1 %collective-permute-start.8 = (f32[128,128]{1,0:T(8,128)S(1)}, f32[128,128]{1,0:T(8,128)S(1)}, u32[]{:S(2)}, u32[]{:S(2)}) collective-permute-start(f32[128,128]{1,0:T(8,128)S(1)} %add.24), channel_id=1, source_target_pairs={{0,16},{16,0},{32,48},{48,32},{64,80},{80,64},{96,112},{112,96},{1... | collective-permute-start | bytes 196616 | tf_op jit(solution)/shard_map/ppermute | solution.py:158
  65.4 8.1 %collective-permute-start.9 = (f32[128,128]{1,0:T(8,128)S(1)}, f32[128,128]{1,0:T(8,128)S(1)}, u32[]{:S(2)}, u32[]{:S(2)}) collective-permute-start(f32[128,128]{1,0:T(8,128)S(1)} %add.25), channel_id=1, source_target_pairs={{0,32},{16,48},{32,0},{48,16},{64,96},{80,112},{96,64},{112,80},{1... | collective-permute-start | bytes 196616 | tf_op jit(solution)/shard_map/ppermute | solution.py:158
  73.5 10.1 %collective-permute-start.10 = (f32[128,128]{1,0:T(8,128)S(1)}, f32[128,128]{1,0:T(8,128)S(1)}, u32[]{:S(2)}, u32[]{:S(2)}) collective-permute-start(f32[128,128]{1,0:T(8,128)S(1)} %add.26), channel_id=1, source_target_pairs={{0,64},{16,80},{32,96},{48,112},{64,0},{80,16},{96,32},{112,48},{1... | collective-permute-start | bytes 196616 | tf_op jit(solution)/shard_map/ppermute | solution.py:158
  76.1 9.1 %collective-permute-start.11 = (f32[128,128]{1,0:T(8,128)S(1)}, f32[128,128]{1,0:T(8,128)S(1)}, u32[]{:S(2)}, u32[]{:S(2)}) collective-permute-start(f32[128,128]{1,0:T(8,128)S(1)} %add.26), channel_id=1, source_target_pairs={{0,128},{16,144},{32,160},{48,176},{64,192},{80,208},{96,224},{112... | collective-permute-start | bytes 196616 | tf_op jit(solution)/shard_map/ppermute | solution.py:158
  78.8 8.1 %collective-permute-start.12 = (f32[128,128]{1,0:T(8,128)S(1)}, f32[128,128]{1,0:T(8,128)S(1)}, u32[]{:S(2)}, u32[]{:S(2)}) collective-permute-start(f32[128,128]{1,0:T(8,128)S(1)} %add.26), channel_id=1, source_target_pairs={{0,192},{16,208},{32,224},{48,240},{64,128},{80,144},{96,160},{112... | collective-permute-start | bytes 196616 | tf_op jit(solution)/shard_map/ppermute | solution.py:158
  86.8 10.1 %collective-permute-start.13 = (f32[128,128]{1,0:T(8,128)S(1)}, f32[128,128]{1,0:T(8,128)S(1)}, u32[]{:S(2)}, u32[]{:S(2)}) collective-permute-start(f32[128,128]{1,0:T(8,128)S(1)} %add_add_fusion), channel_id=1, source_target_pairs={{0,256},{16,272},{32,288},{48,304},{64,320},{80,336},{96,352},{112... | collective-permute-start | bytes 196616 | tf_op jit(solution)/shard_map/ppermute | solution.py:158
  96.9 7.7 %collective-permute-start.14 = (f32[128,128]{1,0:T(8,128)S(1)}, f32[128,128]{1,0:T(8,128)S(1)}, u32[]{:S(2)}, u32[]{:S(2)}) collective-permute-start(f32[128,128]{1,0:T(8,128)S(1)} %add.30), channel_id=1, source_target_pairs={{0,8},{1,9},{2,10},{3,11},{4,12},{5,13},{6,14},{7,15},{8,0},{9,1},... | collective-permute-start | bytes 196616 | tf_op jit(solution)/shard_map/ppermute | solution.py:158

commit v9 on v7

--- a/solution.py
+++ b/solution.py
@@ -65,15 +65,25 @@
         wpart_ref[z] = total.astype(BF)
 
 
+def halves_kernel(parts_ref, out_ref):
+    total = parts_ref[0].astype(F32)
+    for z in range(1, parts_ref.shape[0]):
+        total += parts_ref[z].astype(F32)
+    high = total.astype(BF)
+    out_ref[: total.shape[0], :] = high
+    out_ref[total.shape[0] :, :] = (total - high.astype(F32)).astype(BF)
+
+
 def tile_kernel(
-    from_ref, to_ref, tiles_ref, own, beside, received, other,
-    out_ref, blocks_ref, acc_ref, sent_ref, sems,
+    from_ref, to_ref, tiles_ref, own, beside, ours, theirs, out_ref, weight_ref, blocks_ref, acc_ref, sent_ref, sems
 ):
     cols, rows, _ = out_ref.shape
     blocks = rows // SIDE
+    feat = weight_ref.shape[0]
+    sets = ours.shape[0] - 2 * feat
     at = 0
-    for piece in (own, beside, received, other):
-        blocks_ref[at : at + piece.shape[0], :] = piece[...]
+    for piece in (own[...], beside[...], ours[:sets, :], theirs[:sets, :]):
+        blocks_ref[at : at + piece.shape[0], :] = piece
         at += piece.shape[0]
     acc_ref[...] = jnp.zeros_like(acc_ref)
 
@@ -88,6 +98,10 @@
         for b in range(blocks):
             sent_ref[c, b * SIDE : (b + 1) * SIDE, :] = acc_ref[c * blocks + b].astype(BF)
         copies[c].start()
+    mine, yours = [
+        pair[sets : sets + feat, :].astype(F32) + pair[sets + feat :, :].astype(F32) for pair in (ours, theirs)
+    ]
+    weight_ref[...] = mine + yours
     for c in range(cols):
         copies[c].wait()
 
@@ -155,19 +169,26 @@
 
     groups = [list(range(half)), list(range(half, col_count))]
     wz = lax.all_to_all(wpart, "col", 0, 0, axis_index_groups=groups)
-    wsum = wz.astype(F32).sum(0)
+    halves = pl.pallas_call(
+        halves_kernel,
+        out_shape=jax.ShapeDtypeStruct((2 * feat, feat), BF),
+        in_specs=[vmem()],
+        out_specs=vmem(),
+        compiler_params=small,
+        name="halves",
+    )(wz)
 
     def partner(value, axis, bit):
         return lax.ppermute(value, axis, [(i, i ^ bit) for i in range(lax.axis_size(axis))])
 
-    received = jnp.concatenate([across, across_far, near, across_near, far])
-    received, wsum = lax.optimization_barrier((received, wsum))
+    received = jnp.concatenate([across, across_far, near, across_near, far, halves])
     other = swap(received, 1)
-    sends = pl.pallas_call(
+
+    sends, wsum = pl.pallas_call(
         tile_kernel,
-        out_shape=jax.ShapeDtypeStruct((col_count, nodes, feat), BF),
+        out_shape=(jax.ShapeDtypeStruct((col_count, nodes, feat), BF), jax.ShapeDtypeStruct((feat, feat), F32)),
         in_specs=[smem(), smem()] + [vmem()] * 5,
-        out_specs=pl.BlockSpec(memory_space=pl.ANY),
+        out_specs=(pl.BlockSpec(memory_space=pl.ANY), vmem()),
         scratch_shapes=[
             pltpu.VMEM((20 * nodes, feat), BF),
             pltpu.VMEM((col_count * blocks_dev, SIDE, feat), F32),
@@ -181,9 +202,8 @@
         name="tiles",
     )(places, targets, tile_values, adjoint, beside, received, other)
 
-    sends, wsum = lax.optimization_barrier((sends, wsum))
     got = lax.all_to_all(sends, "col", 0, 0)
-    for bit in [1 << k for k in range((row_count - 1).bit_length())]:
+    for bit in [1 << k for k in range(1, (row_count - 1).bit_length())]:
         wsum = wsum + partner(wsum, "row", bit)
     wsum = wsum + partner(wsum, "col", half)
     scale = 1.0 / float(nodes * row_count * col_count) ** 0.5

time: 104 us -> 103 us (level)
  the two profiles are of different devices: /device:TPU:6 before, /device:TPU:134 now
where the time goes in v9:
time: 103 us
  starting transfers between devices  55.1 us (53%)
  waiting for transfers between devices  39.2 us (38%)
  Pallas kernels  6.53 us (6%)
  local copies, waits for them, and re-layouts  1.07 us (1%)
    ppermute x5, waiting for transfers between devices, partner(): lax.ppermute(value, axis, [(i, i ^ bit) for i in range(lax.axis_size(axis...  30 us
    ppermute x4, starting transfers between devices, to_plane(): lax.ppermute(value, 'row', [pair for pair in pairs if pair[0] % PLANE in...  15.3 us
    ppermute x5, starting transfers between devices, partner(): lax.ppermute(value, axis, [(i, i ^ bit) for i in range(lax.axis_size(axis...  14.3 us
    all_to_all x1, starting transfers between devices, on_device(): got = lax.all_to_all(sends, 'col', 0, 0)  9.64 us
    all_to_all x1, starting transfers between devices, on_device(): wz = lax.all_to_all(wpart, 'col', 0, 0, axis_index_groups=groups)  9.07 us
    ppermute x3, starting transfers between devices, swap(): return lax.ppermute(value, 'row', [(i, i ^ bit) for i in range(row_count)])  6.71 us
    ppermute x4, waiting for transfers between devices, to_plane(): lax.ppermute(value, 'row', [pair for pair in pairs if pair[0] % PLANE in...  6.12 us
    pallas_call x1, Pallas kernels, on_device(): pl.pallas_call(tile_kernel, out_shape=(jax.ShapeDtypeStruct((col_count, n...  3.14 us
  transfers between devices with their start and end apart: 14, of which 8 were waited for; matrix products, arithmetic and copies ran while one was open for 1% of the time, Pallas kernels for 0%

profile of v9, /device:TPU:134, one launch (start us, length us, event | category | flops | bytes accessed | tf_op | source)
XLA Modules:
  0.0 102.8 jit_solution(7127859332667015035)
XLA Ops:
  0.6 2.5 %adjoint.1 = (bf16[384,128]{1,0:T(8,128)(2,1)}, bf16[8,128,128]{2,1,0:T(8,128)(2,1)}, s32[1,32]{1,0:T(1,128)}, s32[1,32]{1,0:T(1,128)}) custom-call(s32[3,128]{1,0:T(4,128)} %bitcast.3, bf16[384,128]{1,0:T(8,128)(2,1)} %cot_in.1, bf16[384,128]{1,0:T(8,128)(2,1)} %pre_in.1, bf16[384,128]{1,0:T(8,128)(2,1)} %agg_in.1, bf16[128,128]{1,0:T(8,128)(2,1)} %w_in.1, ...), custom_call_target="tpu_custom_call" | custom-call | tf_op jit(solution)/shard_map/adjoint/pallas_call | solution.py:136
  3.1 0.0 copy-start
  3.1 0.0 copy-start.1
  3.1 0.0 copy-start.2
  3.2 0.0 copy-start.3
  3.2 2.9 %collective-permute-start.1 = (bf16[384,128]{1,0:T(8,128)(2,1)}, bf16[384,128]{1,0:T(8,128)(2,1)S(1)}, u32[]{:S(2)}, u32[]{:S(2)}) collective-permute-start(bf16[384,128]{1,0:T(8,128)(2,1)} %get-tuple-element.10.own), channel_id=1, source_target_pairs={{0,32},{16,48},{32,0},{48,16},{64,96},{80,112},{96,64},{112,80},{1... | collective-permute-start | bytes 294920 | tf_op jit(solution)/shard_map/ppermute | solution.py:156
  6.0 1.9 %collective-permute-start = (bf16[384,128]{1,0:T(8,128)(2,1)}, bf16[384,128]{1,0:T(8,128)(2,1)S(1)}, u32[]{:S(2)}, u32[]{:S(2)}) collective-permute-start(bf16[384,128]{1,0:T(8,128)(2,1)} %get-tuple-element.10.own), channel_id=1, source_target_pairs={{0,16},{16,0},{32,48},{48,32},{64,80},{80,64},{96,112},{112,96},{1... | collective-permute-start | bytes 294920 | tf_op jit(solution)/shard_map/ppermute | solution.py:156
  8.0 0.9 constant_dynamic-update-slice_fusion.1
  8.9 0.6 collective-permute-done.beside
  9.5 5.1 %collective-permute-start.2 = (bf16[768,128]{1,0:T(8,128)(2,1)S(1)}, bf16[768,128]{1,0:T(8,128)(2,1)S(1)}, u32[]{:S(2)}, u32[]{:S(2)}) collective-permute-start(bf16[768,128]{1,0:T(8,128)(2,1)S(1)} %constant_dynamic-update-slice_fusion), channel_id=1, source_target_pairs={{16,432},{32,128},{80,496},{96,192},{144,48},{160,256},{208,112},{... | collective-permute-start | bytes 589832 | tf_op jit(solution)/shard_map/ppermute | solution.py:160
  14.6 9.1 %all-to-all-start = ((bf16[8,128,128]{2,1,0:T(8,128)(2,1)}), bf16[8,128,128]{2,1,0:T(8,128)(2,1)S(1)}, u32[]{:S(2)}, u32[]{:S(2)}) async-start(bf16[8,128,128]{2,1,0:T(8,128)(2,1)} %get-tuple-element.11), calls=%async_computation | async-start | bytes 524288 | tf_op jit(solution)/shard_map/all_to_all | solution.py:171
  23.7 5.7 %collective-permute-start.5 = (bf16[768,128]{1,0:T(8,128)(2,1)S(1)}, bf16[768,128]{1,0:T(8,128)(2,1)S(1)}, u32[]{:S(2)}, u32[]{:S(2)}) collective-permute-start(bf16[768,128]{1,0:T(8,128)(2,1)S(1)} %constant_dynamic-update-slice_fusion), channel_id=1, source_target_pairs={{0,128},{16,400},{32,160},{48,432},{64,192},{80,464},{96,224},{112... | collective-permute-start | bytes 589832 | tf_op jit(solution)/shard_map/ppermute | solution.py:160
  29.4 1.9 %collective-permute-start.4 = (bf16[768,128]{1,0:T(8,128)(2,1)S(1)}, bf16[768,128]{1,0:T(8,128)(2,1)S(1)}, u32[]{:S(2)}, u32[]{:S(2)}) collective-permute-start(bf16[768,128]{1,0:T(8,128)(2,1)S(1)} %constant_dynamic-update-slice_fusion), channel_id=1, source_target_pairs={{0,96},{16,496},{32,64},{48,464},{64,160},{80,48},{96,128},{112,16... | collective-permute-start | bytes 589832 | tf_op jit(solution)/shard_map/ppermute | solution.py:160
  31.3 2.6 %collective-permute-start.3 = (bf16[768,128]{1,0:T(8,128)(2,1)S(1)}, bf16[768,128]{1,0:T(8,128)(2,1)S(1)}, u32[]{:S(2)}, u32[]{:S(2)}) collective-permute-start(bf16[768,128]{1,0:T(8,128)(2,1)S(1)} %constant_dynamic-update-slice_fusion), channel_id=1, source_target_pairs={{0,64},{16,464},{32,96},{48,496},{64,128},{80,16},{96,160},{112,48... | collective-permute-start | bytes 589832 | tf_op jit(solution)/shard_map/ppermute | solution.py:160
  33.9 0.0 collective-permute-done.1
  33.9 0.0 collective-permute-done.2
  34.0 6.1 %collective-permute-done.3 = bf16[768,128]{1,0:T(8,128)(2,1)S(1)} collective-permute-done((bf16[768,128]{1,0:T(8,128)(2,1)S(1)}, bf16[768,128]{1,0:T(8,128)(2,1)S(1)}, u32[]{:S(2)}, u32[]{:S(2)}) %collective-permute-start.3) | collective-permute-done | bytes 196640 | tf_op jit(solution)/shard_map/ppermute | solution.py:160
  40.1 0.0 collective-permute-done.4
  40.2 0.0 collective-permute-done.5
  40.2 0.0 all-to-all-done.parts_ref
  40.3 1.9 %collective-permute-start.6 = (bf16[3712,128]{1,0:T(8,128)(2,1)S(1)}, bf16[3712,128]{1,0:T(8,128)(2,1)S(1)}, u32[]{:S(2)}, u32[]{:S(2)}) collective-permute-start(bf16[3712,128]{1,0:T(8,128)(2,1)S(1)} %constant_dynamic-update-slice_fusion.2.ours), channel_id=1, source_target_pairs={{0,16},{16,0},{32,48},{48,32},{64,80},{80,64},{96,112},{112,96},{1... | collective-permute-start | bytes 2850824 | tf_op jit(solution)/shard_map/ppermute | solution.py:156
  42.2 2.5 %collective-permute-done.6.theirs = bf16[3712,128]{1,0:T(8,128)(2,1)S(1)} collective-permute-done((bf16[3712,128]{1,0:T(8,128)(2,1)S(1)}, bf16[3712,128]{1,0:T(8,128)(2,1)S(1)}, u32[]{:S(2)}, u32[]{:S(2)}) %collective-permute-start.6) | collective-permute-done | bytes 950304 | tf_op jit(solution)/shard_map/ppermute | solution.py:156
  44.7 0.0 copy-done
  44.7 0.0 copy-done.1
  44.7 0.0 copy-done.2
  44.7 0.0 copy-done.3
  44.7 3.1 %tiles.1 = (bf16[16,384,128]{2,1,0:T(8,128)(2,1)}, f32[128,128]{1,0:T(8,128)S(1)}) custom-call(s32[1,32]{1,0:T(1,128)S(1)} %copy-done.2, s32[1,32]{1,0:T(1,128)S(1)} %copy-done.3, bf16[32,128,128]{2,1,0:T(8,128)(2,1)S(1)} %copy-done, bf16[384,128]{1,0:T(8,128)(2,1)S(1)} %copy-done.1, bf16[384,128]{1,0:T(8,128)(2,1)S(1)} %collective-permute-done.beside, ...), custom_call_target="tpu_custom_call" | custom-call | flops 134217728 | bytes 6291456 | tf_op jit(solution)/shard_map/tiles/pallas_call | solution.py:187
  47.9 9.6 %all-to-all-start.1 = ((bf16[16,384,128]{2,1,0:T(8,128)(2,1)}), bf16[16,384,128]{2,1,0:T(8,128)(2,1)S(1)}, u32[]{:S(2)}, u32[]{:S(2)}) async-start(bf16[16,384,128]{2,1,0:T(8,128)(2,1)} %get-tuple-element.12), calls=%async_computation.1 | async-start | bytes 3145728 | tf_op jit(solution)/shard_map/all_to_all | solution.py:205
  57.5 4.0 %collective-permute-start.7 = (f32[128,128]{1,0:T(8,128)S(1)}, f32[128,128]{1,0:T(8,128)S(1)}, u32[]{:S(2)}, u32[]{:S(2)}) collective-permute-start(f32[128,128]{1,0:T(8,128)S(1)} %get-tuple-element.13), channel_id=1, source_target_pairs={{0,32},{16,48},{32,0},{48,16},{64,96},{80,112},{96,64},{112,80},{1... | collective-permute-start | bytes 196616 | tf_op jit(solution)/shard_map/ppermute | solution.py:182
  61.5 8.5 %collective-permute-done.7 = f32[128,128]{1,0:T(8,128)S(1)} collective-permute-done((f32[128,128]{1,0:T(8,128)S(1)}, f32[128,128]{1,0:T(8,128)S(1)}, u32[]{:S(2)}, u32[]{:S(2)}) %collective-permute-start.7) | collective-permute-done | bytes 65568 | tf_op jit(solution)/shard_map/ppermute | solution.py:182
  70.1 1.9 %collective-permute-start.8 = (f32[128,128]{1,0:T(8,128)S(1)}, f32[128,128]{1,0:T(8,128)S(1)}, u32[]{:S(2)}, u32[]{:S(2)}) collective-permute-start(f32[128,128]{1,0:T(8,128)S(1)} %add.15), channel_id=1, source_target_pairs={{0,64},{16,80},{32,96},{48,112},{64,0},{80,16},{96,32},{112,48},{1... | collective-permute-start | bytes 196616 | tf_op jit(solution)/shard_map/ppermute | solution.py:182
  72.0 4.2 %collective-permute-done.8 = f32[128,128]{1,0:T(8,128)S(1)} collective-permute-done((f32[128,128]{1,0:T(8,128)S(1)}, f32[128,128]{1,0:T(8,128)S(1)}, u32[]{:S(2)}, u32[]{:S(2)}) %collective-permute-start.8) | collective-permute-done | bytes 65568 | tf_op jit(solution)/shard_map/ppermute | solution.py:182
  76.3 1.9 %collective-permute-start.9 = (f32[128,128]{1,0:T(8,128)S(1)}, f32[128,128]{1,0:T(8,128)S(1)}, u32[]{:S(2)}, u32[]{:S(2)}) collective-permute-start(f32[128,128]{1,0:T(8,128)S(1)} %add.16), channel_id=1, source_target_pairs={{0,128},{16,144},{32,160},{48,176},{64,192},{80,208},{96,224},{112... | collective-permute-start | bytes 196616 | tf_op jit(solution)/shard_map/ppermute | solution.py:182
  78.2 5.3 %collective-permute-done.9 = f32[128,128]{1,0:T(8,128)S(1)} collective-permute-done((f32[128,128]{1,0:T(8,128)S(1)}, f32[128,128]{1,0:T(8,128)S(1)}, u32[]{:S(2)}, u32[]{:S(2)}) %collective-permute-start.9) | collective-permute-done | bytes 65568 | tf_op jit(solution)/shard_map/ppermute | solution.py:182
  83.5 3.8 %collective-permute-start.10 = (f32[128,128]{1,0:T(8,128)S(1)}, f32[128,128]{1,0:T(8,128)S(1)}, u32[]{:S(2)}, u32[]{:S(2)}) collective-permute-start(f32[128,128]{1,0:T(8,128)S(1)} %add.17), channel_id=1, source_target_pairs={{0,256},{16,272},{32,288},{48,304},{64,320},{80,336},{96,352},{112... | collective-permute-start | bytes 196616 | tf_op jit(solution)/shard_map/ppermute | solution.py:182
  87.3 7.0 %collective-permute-done.10 = f32[128,128]{1,0:T(8,128)S(1)} collective-permute-done((f32[128,128]{1,0:T(8,128)S(1)}, f32[128,128]{1,0:T(8,128)S(1)}, u32[]{:S(2)}, u32[]{:S(2)}) %collective-permute-start.10) | collective-permute-done | bytes 65568 | tf_op jit(solution)/shard_map/ppermute | solution.py:182
  94.3 2.7 %collective-permute-start.11 = (f32[128,128]{1,0:T(8,128)S(1)}, f32[128,128]{1,0:T(8,128)S(1)}, u32[]{:S(2)}, u32[]{:S(2)}) collective-permute-start(f32[128,128]{1,0:T(8,128)S(1)} %add.18), channel_id=1, source_target_pairs={{0,8},{1,9},{2,10},{3,11},{4,12},{5,13},{6,14},{7,15},{8,0},{9,1},... | collective-permute-start | bytes 196616 | tf_op jit(solution)/shard_map/ppermute | solution.py:182
  97.0 5.0 %collective-permute-done.11 = f32[128,128]{1,0:T(8,128)S(1)} collective-permute-done((f32[128,128]{1,0:T(8,128)S(1)}, f32[128,128]{1,0:T(8,128)S(1)}, u32[]{:S(2)}, u32[]{:S(2)}) %collective-permute-start.11) | collective-permute-done | bytes 65568 | tf_op jit(solution)/shard_map/ppermute | solution.py:182
  102.0 0.0 all-to-all-done.1.got_ref
  102.0 0.9 finish.1
  (13 shorter events, 0.2 us)
Async XLA Ops:
  3.1 41.6 %copy-start = (bf16[32,128,128]{2,1,0:T(8,128)(2,1)S(1)}, bf16[32,128,128]{2,1,0:T(8,128)(2,1)}, u32[]{:S(2)}) copy-start(bf16[32,128,128]{2,1,0:T(8,128)(2,1)} %tiles_ref.1) | copy-start | bytes 3145732
  3.1 41.6 %copy-start.1 = (bf16[384,128]{1,0:T(8,128)(2,1)S(1)}, bf16[384,128]{1,0:T(8,128)(2,1)}, u32[]{:S(2)}) copy-start(bf16[384,128]{1,0:T(8,128)(2,1)} %get-tuple-element.10.own) | copy-start | bytes 294916
  3.1 41.6 %copy-start.2 = (s32[1,32]{1,0:T(1,128)S(1)}, s32[1,32]{1,0:T(1,128)}, u32[]{:S(2)}) copy-start(s32[1,32]{1,0:T(1,128)} %get-tuple-element.8.from_ref) | copy-start | bytes 388
  3.2 41.6 %copy-start.3 = (s32[1,32]{1,0:T(1,128)S(1)}, s32[1,32]{1,0:T(1,128)}, u32[]{:S(2)}) copy-start(s32[1,32]{1,0:T(1,128)} %get-tuple-element.9.to_ref) | copy-start | bytes 388
  3.2 30.7 %collective-permute-start.1 = (bf16[384,128]{1,0:T(8,128)(2,1)}, bf16[384,128]{1,0:T(8,128)(2,1)S(1)}, u32[]{:S(2)}, u32[]{:S(2)}) collective-permute-start(bf16[384,128]{1,0:T(8,128)(2,1)} %get-tuple-element.10.own), channel_id=1, source_target_pairs={{0,32},{16,48},{32,0},{48,16},{64,96},{80,112},{96,64},{112,80},{1... | collective-permute-start | bytes 294920 | tf_op jit(solution)/shard_map/ppermute | solution.py:156
  6.0 3.4 %collective-permute-start = (bf16[384,128]{1,0:T(8,128)(2,1)}, bf16[384,128]{1,0:T(8,128)(2,1)S(1)}, u32[]{:S(2)}, u32[]{:S(2)}) collective-permute-start(bf16[384,128]{1,0:T(8,128)(2,1)} %get-tuple-element.10.own), channel_id=1, source_target_pairs={{0,16},{16,0},{32,48},{48,32},{64,80},{80,64},{96,112},{112,96},{1... | collective-permute-start | bytes 294920 | tf_op jit(solution)/shard_map/ppermute | solution.py:156
  9.5 24.5 %collective-permute-start.2 = (bf16[768,128]{1,0:T(8,128)(2,1)S(1)}, bf16[768,128]{1,0:T(8,128)(2,1)S(1)}, u32[]{:S(2)}, u32[]{:S(2)}) collective-permute-start(bf16[768,128]{1,0:T(8,128)(2,1)S(1)} %constant_dynamic-update-slice_fusion), channel_id=1, source_target_pairs={{16,432},{32,128},{80,496},{96,192},{144,48},{160,256},{208,112},{... | collective-permute-start | bytes 589832 | tf_op jit(solution)/shard_map/ppermute | solution.py:160
  14.6 25.6 %all-to-all-start = ((bf16[8,128,128]{2,1,0:T(8,128)(2,1)}), bf16[8,128,128]{2,1,0:T(8,128)(2,1)S(1)}, u32[]{:S(2)}, u32[]{:S(2)}) async-start(bf16[8,128,128]{2,1,0:T(8,128)(2,1)} %get-tuple-element.11), calls=%async_computation | async-start | bytes 524288 | tf_op jit(solution)/shard_map/all_to_all | solution.py:171
  23.7 16.5 %collective-permute-start.5 = (bf16[768,128]{1,0:T(8,128)(2,1)S(1)}, bf16[768,128]{1,0:T(8,128)(2,1)S(1)}, u32[]{:S(2)}, u32[]{:S(2)}) collective-permute-start(bf16[768,128]{1,0:T(8,128)(2,1)S(1)} %constant_dynamic-update-slice_fusion), channel_id=1, source_target_pairs={{0,128},{16,400},{32,160},{48,432},{64,192},{80,464},{96,224},{112... | collective-permute-start | bytes 589832 | tf_op jit(solution)/shard_map/ppermute | solution.py:160
  29.4 10.7 %collective-permute-start.4 = (bf16[768,128]{1,0:T(8,128)(2,1)S(1)}, bf16[768,128]{1,0:T(8,128)(2,1)S(1)}, u32[]{:S(2)}, u32[]{:S(2)}) collective-permute-start(bf16[768,128]{1,0:T(8,128)(2,1)S(1)} %constant_dynamic-update-slice_fusion), channel_id=1, source_target_pairs={{0,96},{16,496},{32,64},{48,464},{64,160},{80,48},{96,128},{112,16... | collective-permute-start | bytes 589832 | tf_op jit(solution)/shard_map/ppermute | solution.py:160
  31.3 8.8 %collective-permute-start.3 = (bf16[768,128]{1,0:T(8,128)(2,1)S(1)}, bf16[768,128]{1,0:T(8,128)(2,1)S(1)}, u32[]{:S(2)}, u32[]{:S(2)}) collective-permute-start(bf16[768,128]{1,0:T(8,128)(2,1)S(1)} %constant_dynamic-update-slice_fusion), channel_id=1, source_target_pairs={{0,64},{16,464},{32,96},{48,496},{64,128},{80,16},{96,160},{112,48... | collective-permute-start | bytes 589832 | tf_op jit(solution)/shard_map/ppermute | solution.py:160
  40.3 4.4 %collective-permute-start.6 = (bf16[3712,128]{1,0:T(8,128)(2,1)S(1)}, bf16[3712,128]{1,0:T(8,128)(2,1)S(1)}, u32[]{:S(2)}, u32[]{:S(2)}) collective-permute-start(bf16[3712,128]{1,0:T(8,128)(2,1)S(1)} %constant_dynamic-update-slice_fusion.2.ours), channel_id=1, source_target_pairs={{0,16},{16,0},{32,48},{48,32},{64,80},{80,64},{96,112},{112,96},{1... | collective-permute-start | bytes 2850824 | tf_op jit(solution)/shard_map/ppermute | solution.py:156
  47.9 54.1 %all-to-all-start.1 = ((bf16[16,384,128]{2,1,0:T(8,128)(2,1)}), bf16[16,384,128]{2,1,0:T(8,128)(2,1)S(1)}, u32[]{:S(2)}, u32[]{:S(2)}) async-start(bf16[16,384,128]{2,1,0:T(8,128)(2,1)} %get-tuple-element.12), calls=%async_computation.1 | async-start | bytes 3145728 | tf_op jit(solution)/shard_map/all_to_all | solution.py:205
  57.5 12.6 %collective-permute-start.7 = (f32[128,128]{1,0:T(8,128)S(1)}, f32[128,128]{1,0:T(8,128)S(1)}, u32[]{:S(2)}, u32[]{:S(2)}) collective-permute-start(f32[128,128]{1,0:T(8,128)S(1)} %get-tuple-element.13), channel_id=1, source_target_pairs={{0,32},{16,48},{32,0},{48,16},{64,96},{80,112},{96,64},{112,80},{1... | collective-permute-start | bytes 196616 | tf_op jit(solution)/shard_map/ppermute | solution.py:182
  70.1 6.2 %collective-permute-start.8 = (f32[128,128]{1,0:T(8,128)S(1)}, f32[128,128]{1,0:T(8,128)S(1)}, u32[]{:S(2)}, u32[]{:S(2)}) collective-permute-start(f32[128,128]{1,0:T(8,128)S(1)} %add.15), channel_id=1, source_target_pairs={{0,64},{16,80},{32,96},{48,112},{64,0},{80,16},{96,32},{112,48},{1... | collective-permute-start | bytes 196616 | tf_op jit(solution)/shard_map/ppermute | solution.py:182
  76.3 7.2 %collective-permute-start.9 = (f32[128,128]{1,0:T(8,128)S(1)}, f32[128,128]{1,0:T(8,128)S(1)}, u32[]{:S(2)}, u32[]{:S(2)}) collective-permute-start(f32[128,128]{1,0:T(8,128)S(1)} %add.16), channel_id=1, source_target_pairs={{0,128},{16,144},{32,160},{48,176},{64,192},{80,208},{96,224},{112... | collective-permute-start | bytes 196616 | tf_op jit(solution)/shard_map/ppermute | solution.py:182
  83.5 10.8 %collective-permute-start.10 = (f32[128,128]{1,0:T(8,128)S(1)}, f32[128,128]{1,0:T(8,128)S(1)}, u32[]{:S(2)}, u32[]{:S(2)}) collective-permute-start(f32[128,128]{1,0:T(8,128)S(1)} %add.17), channel_id=1, source_target_pairs={{0,256},{16,272},{32,288},{48,304},{64,320},{80,336},{96,352},{112... | collective-permute-start | bytes 196616 | tf_op jit(solution)/shard_map/ppermute | solution.py:182
  94.3 7.7 %collective-permute-start.11 = (f32[128,128]{1,0:T(8,128)S(1)}, f32[128,128]{1,0:T(8,128)S(1)}, u32[]{:S(2)}, u32[]{:S(2)}) collective-permute-start(f32[128,128]{1,0:T(8,128)S(1)} %add.18), channel_id=1, source_target_pairs={{0,8},{1,9},{2,10},{3,11},{4,12},{5,13},{6,14},{7,15},{8,0},{9,1},... | collective-permute-start | bytes 196616 | tf_op jit(solution)/shard_map/ppermute | solution.py:182

commit v10 on v9

--- a/solution.py
+++ b/solution.py
@@ -203,7 +203,7 @@
     )(places, targets, tile_values, adjoint, beside, received, other)
 
     got = lax.all_to_all(sends, "col", 0, 0)
-    for bit in [1 << k for k in range(1, (row_count - 1).bit_length())]:
+    for bit in [PLANE << k for k in range((row_count // PLANE - 1).bit_length())] + [2]:
         wsum = wsum + partner(wsum, "row", bit)
     wsum = wsum + partner(wsum, "col", half)
     scale = 1.0 / float(nodes * row_count * col_count) ** 0.5

time: 103 us -> 101 us (0.981)
  the two profiles are of different devices: /device:TPU:134 before, /device:TPU:1 now
where the time goes in v10:
time: 101 us; the launch traced here: 100 us
  starting transfers between devices  57.5 us (57%)
  waiting for transfers between devices  34 us (34%)
  Pallas kernels  6.53 us (6%)
  local copies, waits for them, and re-layouts  1.07 us (1%)
    ppermute x5, waiting for transfers between devices, partner(): lax.ppermute(value, axis, [(i, i ^ bit) for i in range(lax.axis_size(axis...  22.4 us
    ppermute x3, starting transfers between devices, swap(): return lax.ppermute(value, 'row', [(i, i ^ bit) for i in range(row_count)])  16.3 us
    ppermute x5, starting transfers between devices, partner(): lax.ppermute(value, axis, [(i, i ^ bit) for i in range(lax.axis_size(axis...  12.2 us
    all_to_all x1, starting transfers between devices, on_device(): wz = lax.all_to_all(wpart, 'col', 0, 0, axis_index_groups=groups)  10 us
    ppermute x4, starting transfers between devices, to_plane(): lax.ppermute(value, 'row', [pair for pair in pairs if pair[0] % PLANE in...  9.71 us
    all_to_all x1, starting transfers between devices, on_device(): got = lax.all_to_all(sends, 'col', 0, 0)  9.21 us
    ppermute x4, waiting for transfers between devices, to_plane(): lax.ppermute(value, 'row', [pair for pair in pairs if pair[0] % PLANE in...  5.84 us
    all_to_all x1, waiting for transfers between devices, on_device(): got = lax.all_to_all(sends, 'col', 0, 0)  3.4 us
  transfers between devices with their start and end apart: 14, of which 9 were waited for; matrix products, arithmetic and copies ran while one was open for 1% of the time, Pallas kernels for 0%

profile of v10, /device:TPU:1, one launch (start us, length us, event | category | flops | bytes accessed | tf_op | source)
XLA Modules:
  0.0 100.1 jit_solution(71385920796864424)
XLA Ops:
  0.6 2.5 %adjoint.1 = (bf16[384,128]{1,0:T(8,128)(2,1)}, bf16[8,128,128]{2,1,0:T(8,128)(2,1)}, s32[1,32]{1,0:T(1,128)}, s32[1,32]{1,0:T(1,128)}) custom-call(s32[3,128]{1,0:T(4,128)} %bitcast.3, bf16[384,128]{1,0:T(8,128)(2,1)} %cot_in.1, bf16[384,128]{1,0:T(8,128)(2,1)} %pre_in.1, bf16[384,128]{1,0:T(8,128)(2,1)} %agg_in.1, bf16[128,128]{1,0:T(8,128)(2,1)} %w_in.1, ...), custom_call_target="tpu_custom_call" | custom-call | tf_op jit(solution)/shard_map/adjoint/pallas_call | solution.py:136
  3.1 0.0 copy-start
  3.1 0.0 copy-start.1
  3.1 0.0 copy-start.2
  3.2 0.0 copy-start.3
  3.2 4.1 %collective-permute-start.1 = (bf16[384,128]{1,0:T(8,128)(2,1)}, bf16[384,128]{1,0:T(8,128)(2,1)S(1)}, u32[]{:S(2)}, u32[]{:S(2)}) collective-permute-start(bf16[384,128]{1,0:T(8,128)(2,1)} %get-tuple-element.10.own), channel_id=1, source_target_pairs={{0,32},{16,48},{32,0},{48,16},{64,96},{80,112},{96,64},{112,80},{1... | collective-permute-start | bytes 294920 | tf_op jit(solution)/shard_map/ppermute | solution.py:156
  7.3 6.8 %collective-permute-start = (bf16[384,128]{1,0:T(8,128)(2,1)}, bf16[384,128]{1,0:T(8,128)(2,1)S(1)}, u32[]{:S(2)}, u32[]{:S(2)}) collective-permute-start(bf16[384,128]{1,0:T(8,128)(2,1)} %get-tuple-element.10.own), channel_id=1, source_target_pairs={{0,16},{16,0},{32,48},{48,32},{64,80},{80,64},{96,112},{112,96},{1... | collective-permute-start | bytes 294920 | tf_op jit(solution)/shard_map/ppermute | solution.py:156
  14.0 0.9 constant_dynamic-update-slice_fusion.1
  14.9 0.2 collective-permute-done.beside
  15.2 2.0 %collective-permute-start.2 = (bf16[768,128]{1,0:T(8,128)(2,1)S(1)}, bf16[768,128]{1,0:T(8,128)(2,1)S(1)}, u32[]{:S(2)}, u32[]{:S(2)}) collective-permute-start(bf16[768,128]{1,0:T(8,128)(2,1)S(1)} %constant_dynamic-update-slice_fusion), channel_id=1, source_target_pairs={{16,432},{32,128},{80,496},{96,192},{144,48},{160,256},{208,112},{... | collective-permute-start | bytes 589832 | tf_op jit(solution)/shard_map/ppermute | solution.py:160
  17.1 10.0 %all-to-all-start = ((bf16[8,128,128]{2,1,0:T(8,128)(2,1)}), bf16[8,128,128]{2,1,0:T(8,128)(2,1)S(1)}, u32[]{:S(2)}, u32[]{:S(2)}) async-start(bf16[8,128,128]{2,1,0:T(8,128)(2,1)} %get-tuple-element.11), calls=%async_computation | async-start | bytes 524288 | tf_op jit(solution)/shard_map/all_to_all | solution.py:171
  27.2 3.8 %collective-permute-start.5 = (bf16[768,128]{1,0:T(8,128)(2,1)S(1)}, bf16[768,128]{1,0:T(8,128)(2,1)S(1)}, u32[]{:S(2)}, u32[]{:S(2)}) collective-permute-start(bf16[768,128]{1,0:T(8,128)(2,1)S(1)} %constant_dynamic-update-slice_fusion), channel_id=1, source_target_pairs={{0,128},{16,400},{32,160},{48,432},{64,192},{80,464},{96,224},{112... | collective-permute-start | bytes 589832 | tf_op jit(solution)/shard_map/ppermute | solution.py:160
  31.0 1.9 %collective-permute-start.4 = (bf16[768,128]{1,0:T(8,128)(2,1)S(1)}, bf16[768,128]{1,0:T(8,128)(2,1)S(1)}, u32[]{:S(2)}, u32[]{:S(2)}) collective-permute-start(bf16[768,128]{1,0:T(8,128)(2,1)S(1)} %constant_dynamic-update-slice_fusion), channel_id=1, source_target_pairs={{0,96},{16,496},{32,64},{48,464},{64,160},{80,48},{96,128},{112,16... | collective-permute-start | bytes 589832 | tf_op jit(solution)/shard_map/ppermute | solution.py:160
  32.9 2.1 %collective-permute-start.3 = (bf16[768,128]{1,0:T(8,128)(2,1)S(1)}, bf16[768,128]{1,0:T(8,128)(2,1)S(1)}, u32[]{:S(2)}, u32[]{:S(2)}) collective-permute-start(bf16[768,128]{1,0:T(8,128)(2,1)S(1)} %constant_dynamic-update-slice_fusion), channel_id=1, source_target_pairs={{0,64},{16,464},{32,96},{48,496},{64,128},{80,16},{96,160},{112,48... | collective-permute-start | bytes 589832 | tf_op jit(solution)/shard_map/ppermute | solution.py:160
  35.0 0.0 collective-permute-done.1
  35.0 0.0 collective-permute-done.2
  35.0 5.8 %collective-permute-done.3 = bf16[768,128]{1,0:T(8,128)(2,1)S(1)} collective-permute-done((bf16[768,128]{1,0:T(8,128)(2,1)S(1)}, bf16[768,128]{1,0:T(8,128)(2,1)S(1)}, u32[]{:S(2)}, u32[]{:S(2)}) %collective-permute-start.3) | collective-permute-done | bytes 196640 | tf_op jit(solution)/shard_map/ppermute | solution.py:160
  40.9 0.0 collective-permute-done.4
  40.9 0.0 collective-permute-done.5
  41.0 0.0 all-to-all-done.parts_ref
  41.1 5.5 %collective-permute-start.6 = (bf16[3712,128]{1,0:T(8,128)(2,1)S(1)}, bf16[3712,128]{1,0:T(8,128)(2,1)S(1)}, u32[]{:S(2)}, u32[]{:S(2)}) collective-permute-start(bf16[3712,128]{1,0:T(8,128)(2,1)S(1)} %constant_dynamic-update-slice_fusion.2.ours), channel_id=1, source_target_pairs={{0,16},{16,0},{32,48},{48,32},{64,80},{80,64},{96,112},{112,96},{1... | collective-permute-start | bytes 2850824 | tf_op jit(solution)/shard_map/ppermute | solution.py:156
  46.6 2.1 %collective-permute-done.6.theirs = bf16[3712,128]{1,0:T(8,128)(2,1)S(1)} collective-permute-done((bf16[3712,128]{1,0:T(8,128)(2,1)S(1)}, bf16[3712,128]{1,0:T(8,128)(2,1)S(1)}, u32[]{:S(2)}, u32[]{:S(2)}) %collective-permute-start.6) | collective-permute-done | bytes 950304 | tf_op jit(solution)/shard_map/ppermute | solution.py:156
  48.7 0.0 copy-done
  48.7 0.0 copy-done.1
  48.7 0.0 copy-done.2
  48.7 0.0 copy-done.3
  48.7 3.1 %tiles.1 = (bf16[16,384,128]{2,1,0:T(8,128)(2,1)}, f32[128,128]{1,0:T(8,128)S(1)}) custom-call(s32[1,32]{1,0:T(1,128)S(1)} %copy-done.2, s32[1,32]{1,0:T(1,128)S(1)} %copy-done.3, bf16[32,128,128]{2,1,0:T(8,128)(2,1)S(1)} %copy-done, bf16[384,128]{1,0:T(8,128)(2,1)S(1)} %copy-done.1, bf16[384,128]{1,0:T(8,128)(2,1)S(1)} %collective-permute-done.beside, ...), custom_call_target="tpu_custom_call" | custom-call | flops 134217728 | bytes 6291456 | tf_op jit(solution)/shard_map/tiles/pallas_call | solution.py:187
  51.8 9.2 %all-to-all-start.1 = ((bf16[16,384,128]{2,1,0:T(8,128)(2,1)}), bf16[16,384,128]{2,1,0:T(8,128)(2,1)S(1)}, u32[]{:S(2)}, u32[]{:S(2)}) async-start(bf16[16,384,128]{2,1,0:T(8,128)(2,1)} %get-tuple-element.12), calls=%async_computation.1 | async-start | bytes 3145728 | tf_op jit(solution)/shard_map/all_to_all | solution.py:205
  61.1 1.9 %collective-permute-start.7 = (f32[128,128]{1,0:T(8,128)S(1)}, f32[128,128]{1,0:T(8,128)S(1)}, u32[]{:S(2)}, u32[]{:S(2)}) collective-permute-start(f32[128,128]{1,0:T(8,128)S(1)} %get-tuple-element.13), channel_id=1, source_target_pairs={{0,64},{16,80},{32,96},{48,112},{64,0},{80,16},{96,32},{112,48},{1... | collective-permute-start | bytes 196616 | tf_op jit(solution)/shard_map/ppermute | solution.py:182
  63.0 3.1 %collective-permute-done.7 = f32[128,128]{1,0:T(8,128)S(1)} collective-permute-done((f32[128,128]{1,0:T(8,128)S(1)}, f32[128,128]{1,0:T(8,128)S(1)}, u32[]{:S(2)}, u32[]{:S(2)}) %collective-permute-start.7) | collective-permute-done | bytes 65568 | tf_op jit(solution)/shard_map/ppermute | solution.py:182
  66.1 1.9 %collective-permute-start.8 = (f32[128,128]{1,0:T(8,128)S(1)}, f32[128,128]{1,0:T(8,128)S(1)}, u32[]{:S(2)}, u32[]{:S(2)}) collective-permute-start(f32[128,128]{1,0:T(8,128)S(1)} %add.15), channel_id=1, source_target_pairs={{0,128},{16,144},{32,160},{48,176},{64,192},{80,208},{96,224},{112... | collective-permute-start | bytes 196616 | tf_op jit(solution)/shard_map/ppermute | solution.py:182
  68.0 5.0 %collective-permute-done.8 = f32[128,128]{1,0:T(8,128)S(1)} collective-permute-done((f32[128,128]{1,0:T(8,128)S(1)}, f32[128,128]{1,0:T(8,128)S(1)}, u32[]{:S(2)}, u32[]{:S(2)}) %collective-permute-start.8) | collective-permute-done | bytes 65568 | tf_op jit(solution)/shard_map/ppermute | solution.py:182
  73.0 2.0 %collective-permute-start.9 = (f32[128,128]{1,0:T(8,128)S(1)}, f32[128,128]{1,0:T(8,128)S(1)}, u32[]{:S(2)}, u32[]{:S(2)}) collective-permute-start(f32[128,128]{1,0:T(8,128)S(1)} %add.16), channel_id=1, source_target_pairs={{0,256},{16,272},{32,288},{48,304},{64,320},{80,336},{96,352},{112... | collective-permute-start | bytes 196616 | tf_op jit(solution)/shard_map/ppermute | solution.py:182
  75.0 7.9 %collective-permute-done.9 = f32[128,128]{1,0:T(8,128)S(1)} collective-permute-done((f32[128,128]{1,0:T(8,128)S(1)}, f32[128,128]{1,0:T(8,128)S(1)}, u32[]{:S(2)}, u32[]{:S(2)}) %collective-permute-start.9) | collective-permute-done | bytes 65568 | tf_op jit(solution)/shard_map/ppermute | solution.py:182
  82.9 1.9 %collective-permute-start.10 = (f32[128,128]{1,0:T(8,128)S(1)}, f32[128,128]{1,0:T(8,128)S(1)}, u32[]{:S(2)}, u32[]{:S(2)}) collective-permute-start(f32[128,128]{1,0:T(8,128)S(1)} %add.17), channel_id=1, source_target_pairs={{0,32},{16,48},{32,0},{48,16},{64,96},{80,112},{96,64},{112,80},{1... | collective-permute-start | bytes 196616 | tf_op jit(solution)/shard_map/ppermute | solution.py:182
  84.9 3.8 %collective-permute-done.10 = f32[128,128]{1,0:T(8,128)S(1)} collective-permute-done((f32[128,128]{1,0:T(8,128)S(1)}, f32[128,128]{1,0:T(8,128)S(1)}, u32[]{:S(2)}, u32[]{:S(2)}) %collective-permute-start.10) | collective-permute-done | bytes 65568 | tf_op jit(solution)/shard_map/ppermute | solution.py:182
  88.7 4.4 %collective-permute-start.11 = (f32[128,128]{1,0:T(8,128)S(1)}, f32[128,128]{1,0:T(8,128)S(1)}, u32[]{:S(2)}, u32[]{:S(2)}) collective-permute-start(f32[128,128]{1,0:T(8,128)S(1)} %add.18), channel_id=1, source_target_pairs={{0,8},{1,9},{2,10},{3,11},{4,12},{5,13},{6,14},{7,15},{8,0},{9,1},... | collective-permute-start | bytes 196616 | tf_op jit(solution)/shard_map/ppermute | solution.py:182
  93.1 2.7 %collective-permute-done.11 = f32[128,128]{1,0:T(8,128)S(1)} collective-permute-done((f32[128,128]{1,0:T(8,128)S(1)}, f32[128,128]{1,0:T(8,128)S(1)}, u32[]{:S(2)}, u32[]{:S(2)}) %collective-permute-start.11) | collective-permute-done | bytes 65568 | tf_op jit(solution)/shard_map/ppermute | solution.py:182
  95.8 3.4 %all-to-all-done.1.got_ref = bf16[16,384,128]{2,1,0:T(8,128)(2,1)S(1)} async-done(((bf16[16,384,128]{2,1,0:T(8,128)(2,1)}), bf16[16,384,128]{2,1,0:T(8,128)(2,1)S(1)}, u32[]{:S(2)}, u32[]{:S(2)}) %all-to-all-start.1) | async-done | bytes 1572896 | tf_op jit(solution)/shard_map/all_to_all | solution.py:205
  99.2 0.9 finish.1
  (13 shorter events, 0.2 us)
Async XLA Ops:
  3.1 45.6 %copy-start = (bf16[32,128,128]{2,1,0:T(8,128)(2,1)S(1)}, bf16[32,128,128]{2,1,0:T(8,128)(2,1)}, u32[]{:S(2)}) copy-start(bf16[32,128,128]{2,1,0:T(8,128)(2,1)} %tiles_ref.1) | copy-start | bytes 3145732
  3.1 45.6 %copy-start.1 = (bf16[384,128]{1,0:T(8,128)(2,1)S(1)}, bf16[384,128]{1,0:T(8,128)(2,1)}, u32[]{:S(2)}) copy-start(bf16[384,128]{1,0:T(8,128)(2,1)} %get-tuple-element.10.own) | copy-start | bytes 294916
  3.1 45.6 %copy-start.2 = (s32[1,32]{1,0:T(1,128)S(1)}, s32[1,32]{1,0:T(1,128)}, u32[]{:S(2)}) copy-start(s32[1,32]{1,0:T(1,128)} %get-tuple-element.8.from_ref) | copy-start | bytes 388
  3.2 45.5 %copy-start.3 = (s32[1,32]{1,0:T(1,128)S(1)}, s32[1,32]{1,0:T(1,128)}, u32[]{:S(2)}) copy-start(s32[1,32]{1,0:T(1,128)} %get-tuple-element.9.to_ref) | copy-start | bytes 388
  3.2 31.8 %collective-permute-start.1 = (bf16[384,128]{1,0:T(8,128)(2,1)}, bf16[384,128]{1,0:T(8,128)(2,1)S(1)}, u32[]{:S(2)}, u32[]{:S(2)}) collective-permute-start(bf16[384,128]{1,0:T(8,128)(2,1)} %get-tuple-element.10.own), channel_id=1, source_target_pairs={{0,32},{16,48},{32,0},{48,16},{64,96},{80,112},{96,64},{112,80},{1... | collective-permute-start | bytes 294920 | tf_op jit(solution)/shard_map/ppermute | solution.py:156
  7.3 7.9 %collective-permute-start = (bf16[384,128]{1,0:T(8,128)(2,1)}, bf16[384,128]{1,0:T(8,128)(2,1)S(1)}, u32[]{:S(2)}, u32[]{:S(2)}) collective-permute-start(bf16[384,128]{1,0:T(8,128)(2,1)} %get-tuple-element.10.own), channel_id=1, source_target_pairs={{0,16},{16,0},{32,48},{48,32},{64,80},{80,64},{96,112},{112,96},{1... | collective-permute-start | bytes 294920 | tf_op jit(solution)/shard_map/ppermute | solution.py:156
  15.2 19.8 %collective-permute-start.2 = (bf16[768,128]{1,0:T(8,128)(2,1)S(1)}, bf16[768,128]{1,0:T(8,128)(2,1)S(1)}, u32[]{:S(2)}, u32[]{:S(2)}) collective-permute-start(bf16[768,128]{1,0:T(8,128)(2,1)S(1)} %constant_dynamic-update-slice_fusion), channel_id=1, source_target_pairs={{16,432},{32,128},{80,496},{96,192},{144,48},{160,256},{208,112},{... | collective-permute-start | bytes 589832 | tf_op jit(solution)/shard_map/ppermute | solution.py:160
  17.1 23.8 %all-to-all-start = ((bf16[8,128,128]{2,1,0:T(8,128)(2,1)}), bf16[8,128,128]{2,1,0:T(8,128)(2,1)S(1)}, u32[]{:S(2)}, u32[]{:S(2)}) async-start(bf16[8,128,128]{2,1,0:T(8,128)(2,1)} %get-tuple-element.11), calls=%async_computation | async-start | bytes 524288 | tf_op jit(solution)/shard_map/all_to_all | solution.py:171
  27.2 13.8 %collective-permute-start.5 = (bf16[768,128]{1,0:T(8,128)(2,1)S(1)}, bf16[768,128]{1,0:T(8,128)(2,1)S(1)}, u32[]{:S(2)}, u32[]{:S(2)}) collective-permute-start(bf16[768,128]{1,0:T(8,128)(2,1)S(1)} %constant_dynamic-update-slice_fusion), channel_id=1, source_target_pairs={{0,128},{16,400},{32,160},{48,432},{64,192},{80,464},{96,224},{112... | collective-permute-start | bytes 589832 | tf_op jit(solution)/shard_map/ppermute | solution.py:160
  31.0 9.9 %collective-permute-start.4 = (bf16[768,128]{1,0:T(8,128)(2,1)S(1)}, bf16[768,128]{1,0:T(8,128)(2,1)S(1)}, u32[]{:S(2)}, u32[]{:S(2)}) collective-permute-start(bf16[768,128]{1,0:T(8,128)(2,1)S(1)} %constant_dynamic-update-slice_fusion), channel_id=1, source_target_pairs={{0,96},{16,496},{32,64},{48,464},{64,160},{80,48},{96,128},{112,16... | collective-permute-start | bytes 589832 | tf_op jit(solution)/shard_map/ppermute | solution.py:160
  32.9 8.0 %collective-permute-start.3 = (bf16[768,128]{1,0:T(8,128)(2,1)S(1)}, bf16[768,128]{1,0:T(8,128)(2,1)S(1)}, u32[]{:S(2)}, u32[]{:S(2)}) collective-permute-start(bf16[768,128]{1,0:T(8,128)(2,1)S(1)} %constant_dynamic-update-slice_fusion), channel_id=1, source_target_pairs={{0,64},{16,464},{32,96},{48,496},{64,128},{80,16},{96,160},{112,48... | collective-permute-start | bytes 589832 | tf_op jit(solution)/shard_map/ppermute | solution.py:160
  41.1 7.6 %collective-permute-start.6 = (bf16[3712,128]{1,0:T(8,128)(2,1)S(1)}, bf16[3712,128]{1,0:T(8,128)(2,1)S(1)}, u32[]{:S(2)}, u32[]{:S(2)}) collective-permute-start(bf16[3712,128]{1,0:T(8,128)(2,1)S(1)} %constant_dynamic-update-slice_fusion.2.ours), channel_id=1, source_target_pairs={{0,16},{16,0},{32,48},{48,32},{64,80},{80,64},{96,112},{112,96},{1... | collective-permute-start | bytes 2850824 | tf_op jit(solution)/shard_map/ppermute | solution.py:156
  51.8 47.3 %all-to-all-start.1 = ((bf16[16,384,128]{2,1,0:T(8,128)(2,1)}), bf16[16,384,128]{2,1,0:T(8,128)(2,1)S(1)}, u32[]{:S(2)}, u32[]{:S(2)}) async-start(bf16[16,384,128]{2,1,0:T(8,128)(2,1)} %get-tuple-element.12), calls=%async_computation.1 | async-start | bytes 3145728 | tf_op jit(solution)/shard_map/all_to_all | solution.py:205
  61.1 5.0 %collective-permute-start.7 = (f32[128,128]{1,0:T(8,128)S(1)}, f32[128,128]{1,0:T(8,128)S(1)}, u32[]{:S(2)}, u32[]{:S(2)}) collective-permute-start(f32[128,128]{1,0:T(8,128)S(1)} %get-tuple-element.13), channel_id=1, source_target_pairs={{0,64},{16,80},{32,96},{48,112},{64,0},{80,16},{96,32},{112,48},{1... | collective-permute-start | bytes 196616 | tf_op jit(solution)/shard_map/ppermute | solution.py:182
  66.1 6.9 %collective-permute-start.8 = (f32[128,128]{1,0:T(8,128)S(1)}, f32[128,128]{1,0:T(8,128)S(1)}, u32[]{:S(2)}, u32[]{:S(2)}) collective-permute-start(f32[128,128]{1,0:T(8,128)S(1)} %add.15), channel_id=1, source_target_pairs={{0,128},{16,144},{32,160},{48,176},{64,192},{80,208},{96,224},{112... | collective-permute-start | bytes 196616 | tf_op jit(solution)/shard_map/ppermute | solution.py:182
  73.0 9.9 %collective-permute-start.9 = (f32[128,128]{1,0:T(8,128)S(1)}, f32[128,128]{1,0:T(8,128)S(1)}, u32[]{:S(2)}, u32[]{:S(2)}) collective-permute-start(f32[128,128]{1,0:T(8,128)S(1)} %add.16), channel_id=1, source_target_pairs={{0,256},{16,272},{32,288},{48,304},{64,320},{80,336},{96,352},{112... | collective-permute-start | bytes 196616 | tf_op jit(solution)/shard_map/ppermute | solution.py:182
  82.9 5.7 %collective-permute-start.10 = (f32[128,128]{1,0:T(8,128)S(1)}, f32[128,128]{1,0:T(8,128)S(1)}, u32[]{:S(2)}, u32[]{:S(2)}) collective-permute-start(f32[128,128]{1,0:T(8,128)S(1)} %add.17), channel_id=1, source_target_pairs={{0,32},{16,48},{32,0},{48,16},{64,96},{80,112},{96,64},{112,80},{1... | collective-permute-start | bytes 196616 | tf_op jit(solution)/shard_map/ppermute | solution.py:182
  88.7 7.1 %collective-permute-start.11 = (f32[128,128]{1,0:T(8,128)S(1)}, f32[128,128]{1,0:T(8,128)S(1)}, u32[]{:S(2)}, u32[]{:S(2)}) collective-permute-start(f32[128,128]{1,0:T(8,128)S(1)} %add.18), channel_id=1, source_target_pairs={{0,8},{1,9},{2,10},{3,11},{4,12},{5,13},{6,14},{7,15},{8,0},{9,1},... | collective-permute-start | bytes 196616 | tf_op jit(solution)/shard_map/ppermute | solution.py:182

commit v11 on v10

--- a/solution.py
+++ b/solution.py
@@ -27,7 +27,7 @@
     below = gap > planes // 2
     steps = jnp.where(below, planes - gap, gap)
     receiver = jnp.where(gap == 0, core, jnp.where(below, 0, 1))
-    first = jnp.where(steps == 2, jnp.where(same_chip, 7, 1), jnp.where(same_chip, 3, 5))
+    first = jnp.where(steps == 2, jnp.where(same_chip, 5, 1), jnp.where(same_chip, 3, 7))
     place = jnp.where(gap == 0, 0, first + jnp.where(core == receiver, 0, 1))
     slot = 2 + place + jnp.where(receiver == lax.rem(row, 2), 0, 9)
     slot = jnp.where((gap == 0) & same_chip, jnp.where(same_core, 0, 1), slot)
@@ -165,10 +165,11 @@
     far = to_plane(chip, 2, 0, (0, 1, 2, 3))
     across_far = to_plane(chip, 2, 2, (1, 2))
     across_near = to_plane(chip, 1, 2, (0, 1, 2, 3))
-    near = to_plane(chip, 1, 0, (0, 1, 2, 3))
-
     groups = [list(range(half)), list(range(half, col_count))]
     wz = lax.all_to_all(wpart, "col", 0, 0, axis_index_groups=groups)
+    near_chip, wz = lax.optimization_barrier((chip, wz))
+    near = to_plane(near_chip, 1, 0, (0, 1, 2, 3))
+
     halves = pl.pallas_call(
         halves_kernel,
         out_shape=jax.ShapeDtypeStruct((2 * feat, feat), BF),
@@ -181,7 +182,7 @@
     def partner(value, axis, bit):
         return lax.ppermute(value, axis, [(i, i ^ bit) for i in range(lax.axis_size(axis))])
 
-    received = jnp.concatenate([across, across_far, near, across_near, far, halves])
+    received = jnp.concatenate([across, across_far, near, far, across_near, halves])
     other = swap(received, 1)
 
     sends, wsum = pl.pallas_call(

time: 101 us -> 101 us (level)
  starting transfers between devices: 57.5 us -> 61.1 us
  waiting for transfers between devices: 34 us -> 30.7 us
    ppermute x3, starting transfers between devices: 16.3 us -> 11.9 us  [swap(): return lax.ppermute(value, 'row', [(i, i ^ bit) for i in range(row_count)])]
    ppermute x4, starting transfers between devices: 9.71 us -> 13.6 us  [to_plane(): lax.ppermute(value, 'row', [pair for pair in pairs if pair[0] % PLANE in...]
    ppermute x5, waiting for transfers between devices: 22.4 us -> 19.1 us  [partner(): lax.ppermute(value, axis, [(i, i ^ bit) for i in range(lax.axis_size(axis...]
    ppermute x5, starting transfers between devices: 12.2 us -> 15.4 us  [partner(): lax.ppermute(value, axis, [(i, i ^ bit) for i in range(lax.axis_size(axis...]
where the time goes in v11:
time: 101 us; the launch traced here: 100 us
  starting transfers between devices  61.1 us (60%)
  waiting for transfers between devices  30.7 us (30%)
  Pallas kernels  6.53 us (6%)
  local copies, waits for them, and re-layouts  1.07 us (1%)
    ppermute x5, waiting for transfers between devices, partner(): lax.ppermute(value, axis, [(i, i ^ bit) for i in range(lax.axis_size(axis...  19.1 us
    ppermute x5, starting transfers between devices, partner(): lax.ppermute(value, axis, [(i, i ^ bit) for i in range(lax.axis_size(axis...  15.4 us
    ppermute x4, starting transfers between devices, to_plane(): lax.ppermute(value, 'row', [pair for pair in pairs if pair[0] % PLANE in...  13.6 us
    ppermute x3, starting transfers between devices, swap(): return lax.ppermute(value, 'row', [(i, i ^ bit) for i in range(row_count)])  11.9 us
    all_to_all x1, starting transfers between devices, on_device(): wz = lax.all_to_all(wpart, 'col', 0, 0, axis_index_groups=groups)  11 us
    all_to_all x1, starting transfers between devices, on_device(): got = lax.all_to_all(sends, 'col', 0, 0)  9.2 us
    ppermute x4, waiting for transfers between devices, to_plane(): lax.ppermute(value, 'row', [pair for pair in pairs if pair[0] % PLANE in...  5.73 us
    all_to_all x1, waiting for transfers between devices, on_device(): got = lax.all_to_all(sends, 'col', 0, 0)  3.44 us
  transfers between devices with their start and end apart: 14, of which 9 were waited for; matrix products, arithmetic and copies ran while one was open for 1% of the time, Pallas kernels for 0%

profile of v11, /device:TPU:1, one launch (start us, length us, event | category | flops | bytes accessed | tf_op | source)
XLA Modules:
  0.0 100.3 jit_solution(6331851921764802121)
XLA Ops:
  0.6 2.5 %adjoint.1 = (bf16[384,128]{1,0:T(8,128)(2,1)}, bf16[8,128,128]{2,1,0:T(8,128)(2,1)}, s32[1,32]{1,0:T(1,128)}, s32[1,32]{1,0:T(1,128)}) custom-call(s32[3,128]{1,0:T(4,128)} %bitcast.3, bf16[384,128]{1,0:T(8,128)(2,1)} %cot_in.1, bf16[384,128]{1,0:T(8,128)(2,1)} %pre_in.1, bf16[384,128]{1,0:T(8,128)(2,1)} %agg_in.1, bf16[128,128]{1,0:T(8,128)(2,1)} %w_in.1, ...), custom_call_target="tpu_custom_call" | custom-call | tf_op jit(solution)/shard_map/adjoint/pallas_call | solution.py:136
  3.1 0.0 copy-start
  3.1 0.0 copy-start.1
  3.1 0.0 copy-start.2
  3.2 0.0 copy-start.3
  3.2 11.0 %all-to-all-start = ((bf16[8,128,128]{2,1,0:T(8,128)(2,1)}), bf16[8,128,128]{2,1,0:T(8,128)(2,1)S(1)}, u32[]{:S(2)}, u32[]{:S(2)}) async-start(bf16[8,128,128]{2,1,0:T(8,128)(2,1)} %get-tuple-element.13), calls=%async_computation | async-start | bytes 524288 | tf_op jit(solution)/shard_map/all_to_all | solution.py:169
  14.2 3.1 %collective-permute-start.1 = (bf16[384,128]{1,0:T(8,128)(2,1)}, bf16[384,128]{1,0:T(8,128)(2,1)S(1)}, u32[]{:S(2)}, u32[]{:S(2)}) collective-permute-start(bf16[384,128]{1,0:T(8,128)(2,1)} %get-tuple-element.12.own), channel_id=1, source_target_pairs={{0,32},{16,48},{32,0},{48,16},{64,96},{80,112},{96,64},{112,80},{1... | collective-permute-start | bytes 294920 | tf_op jit(solution)/shard_map/ppermute | solution.py:156
  17.3 3.1 %collective-permute-start = (bf16[384,128]{1,0:T(8,128)(2,1)}, bf16[384,128]{1,0:T(8,128)(2,1)S(1)}, u32[]{:S(2)}, u32[]{:S(2)}) collective-permute-start(bf16[384,128]{1,0:T(8,128)(2,1)} %get-tuple-element.12.own), channel_id=1, source_target_pairs={{0,16},{16,0},{32,48},{48,32},{64,80},{80,64},{96,112},{112,96},{1... | collective-permute-start | bytes 294920 | tf_op jit(solution)/shard_map/ppermute | solution.py:156
  20.4 0.9 constant_dynamic-update-slice_fusion.1
  21.3 0.2 collective-permute-done.beside
  21.6 5.9 %collective-permute-start.2 = (bf16[768,128]{1,0:T(8,128)(2,1)S(1)}, bf16[768,128]{1,0:T(8,128)(2,1)S(1)}, u32[]{:S(2)}, u32[]{:S(2)}) collective-permute-start(bf16[768,128]{1,0:T(8,128)(2,1)S(1)} %constant_dynamic-update-slice_fusion), channel_id=1, source_target_pairs={{16,432},{32,128},{80,496},{96,192},{144,48},{160,256},{208,112},{... | collective-permute-start | bytes 589832 | tf_op jit(solution)/shard_map/ppermute | solution.py:160
  27.5 1.9 %collective-permute-start.5 = (bf16[768,128]{1,0:T(8,128)(2,1)S(1)}, bf16[768,128]{1,0:T(8,128)(2,1)S(1)}, u32[]{:S(2)}, u32[]{:S(2)}) collective-permute-start(bf16[768,128]{1,0:T(8,128)(2,1)S(1)} %constant_dynamic-update-slice_fusion), channel_id=1, source_target_pairs={{0,96},{16,496},{32,64},{48,464},{64,160},{80,48},{96,128},{112,16... | collective-permute-start | bytes 589832 | tf_op jit(solution)/shard_map/ppermute | solution.py:160
  29.4 3.8 %collective-permute-start.4 = (bf16[768,128]{1,0:T(8,128)(2,1)S(1)}, bf16[768,128]{1,0:T(8,128)(2,1)S(1)}, u32[]{:S(2)}, u32[]{:S(2)}) collective-permute-start(bf16[768,128]{1,0:T(8,128)(2,1)S(1)} %constant_dynamic-update-slice_fusion), channel_id=1, source_target_pairs={{0,128},{16,400},{32,160},{48,432},{64,192},{80,464},{96,224},{112... | collective-permute-start | bytes 589832 | tf_op jit(solution)/shard_map/ppermute | solution.py:160
  33.2 0.0 all-to-all-done.parts_ref
  33.2 2.1 %collective-permute-start.3 = (bf16[768,128]{1,0:T(8,128)(2,1)S(1)}, bf16[768,128]{1,0:T(8,128)(2,1)S(1)}, u32[]{:S(2)}, u32[]{:S(2)}) collective-permute-start(bf16[768,128]{1,0:T(8,128)(2,1)S(1)} %constant_dynamic-update-slice_fusion), channel_id=1, source_target_pairs={{0,64},{16,464},{32,96},{48,496},{64,128},{80,16},{96,160},{112,48... | collective-permute-start | bytes 589832 | tf_op jit(solution)/shard_map/ppermute | solution.py:160
  35.3 0.0 collective-permute-done.1
  35.3 0.0 collective-permute-done.2
  35.4 5.7 %collective-permute-done.3 = bf16[768,128]{1,0:T(8,128)(2,1)S(1)} collective-permute-done((bf16[768,128]{1,0:T(8,128)(2,1)S(1)}, bf16[768,128]{1,0:T(8,128)(2,1)S(1)}, u32[]{:S(2)}, u32[]{:S(2)}) %collective-permute-start.3) | collective-permute-done | bytes 196640 | tf_op jit(solution)/shard_map/ppermute | solution.py:160
  41.1 0.0 collective-permute-done.4
  41.2 0.0 collective-permute-done.5
  41.2 5.6 %collective-permute-start.6 = (bf16[3712,128]{1,0:T(8,128)(2,1)S(1)}, bf16[3712,128]{1,0:T(8,128)(2,1)S(1)}, u32[]{:S(2)}, u32[]{:S(2)}) collective-permute-start(bf16[3712,128]{1,0:T(8,128)(2,1)S(1)} %constant_dynamic-update-slice_fusion.2.ours), channel_id=1, source_target_pairs={{0,16},{16,0},{32,48},{48,32},{64,80},{80,64},{96,112},{112,96},{1... | collective-permute-start | bytes 2850824 | tf_op jit(solution)/shard_map/ppermute | solution.py:156
  46.9 2.1 %collective-permute-done.6.theirs = bf16[3712,128]{1,0:T(8,128)(2,1)S(1)} collective-permute-done((bf16[3712,128]{1,0:T(8,128)(2,1)S(1)}, bf16[3712,128]{1,0:T(8,128)(2,1)S(1)}, u32[]{:S(2)}, u32[]{:S(2)}) %collective-permute-start.6) | collective-permute-done | bytes 950304 | tf_op jit(solution)/shard_map/ppermute | solution.py:156
  49.0 0.0 copy-done
  49.0 0.0 copy-done.1
  49.0 0.0 copy-done.2
  49.0 0.0 copy-done.3
  49.0 3.1 %tiles.1 = (bf16[16,384,128]{2,1,0:T(8,128)(2,1)}, f32[128,128]{1,0:T(8,128)S(1)}) custom-call(s32[1,32]{1,0:T(1,128)S(1)} %copy-done.2, s32[1,32]{1,0:T(1,128)S(1)} %copy-done.3, bf16[32,128,128]{2,1,0:T(8,128)(2,1)S(1)} %copy-done, bf16[384,128]{1,0:T(8,128)(2,1)S(1)} %copy-done.1, bf16[384,128]{1,0:T(8,128)(2,1)S(1)} %collective-permute-done.beside, ...), custom_call_target="tpu_custom_call" | custom-call | flops 134217728 | bytes 6291456 | tf_op jit(solution)/shard_map/tiles/pallas_call | solution.py:188
  52.2 9.2 %all-to-all-start.1 = ((bf16[16,384,128]{2,1,0:T(8,128)(2,1)}), bf16[16,384,128]{2,1,0:T(8,128)(2,1)S(1)}, u32[]{:S(2)}, u32[]{:S(2)}) async-start(bf16[16,384,128]{2,1,0:T(8,128)(2,1)} %get-tuple-element.16), calls=%async_computation.1 | async-start | bytes 3145728 | tf_op jit(solution)/shard_map/all_to_all | solution.py:206
  61.4 2.4 %collective-permute-start.7 = (f32[128,128]{1,0:T(8,128)S(1)}, f32[128,128]{1,0:T(8,128)S(1)}, u32[]{:S(2)}, u32[]{:S(2)}) collective-permute-start(f32[128,128]{1,0:T(8,128)S(1)} %get-tuple-element.17), channel_id=1, source_target_pairs={{0,64},{16,80},{32,96},{48,112},{64,0},{80,16},{96,32},{112,48},{1... | collective-permute-start | bytes 196616 | tf_op jit(solution)/shard_map/ppermute | solution.py:183
  63.8 2.6 %collective-permute-done.7 = f32[128,128]{1,0:T(8,128)S(1)} collective-permute-done((f32[128,128]{1,0:T(8,128)S(1)}, f32[128,128]{1,0:T(8,128)S(1)}, u32[]{:S(2)}, u32[]{:S(2)}) %collective-permute-start.7) | collective-permute-done | bytes 65568 | tf_op jit(solution)/shard_map/ppermute | solution.py:183
  66.4 2.5 %collective-permute-start.8 = (f32[128,128]{1,0:T(8,128)S(1)}, f32[128,128]{1,0:T(8,128)S(1)}, u32[]{:S(2)}, u32[]{:S(2)}) collective-permute-start(f32[128,128]{1,0:T(8,128)S(1)} %add.15), channel_id=1, source_target_pairs={{0,128},{16,144},{32,160},{48,176},{64,192},{80,208},{96,224},{112... | collective-permute-start | bytes 196616 | tf_op jit(solution)/shard_map/ppermute | solution.py:183
  68.9 4.4 %collective-permute-done.8 = f32[128,128]{1,0:T(8,128)S(1)} collective-permute-done((f32[128,128]{1,0:T(8,128)S(1)}, f32[128,128]{1,0:T(8,128)S(1)}, u32[]{:S(2)}, u32[]{:S(2)}) %collective-permute-start.8) | collective-permute-done | bytes 65568 | tf_op jit(solution)/shard_map/ppermute | solution.py:183
  73.3 3.9 %collective-permute-start.9 = (f32[128,128]{1,0:T(8,128)S(1)}, f32[128,128]{1,0:T(8,128)S(1)}, u32[]{:S(2)}, u32[]{:S(2)}) collective-permute-start(f32[128,128]{1,0:T(8,128)S(1)} %add.16), channel_id=1, source_target_pairs={{0,256},{16,272},{32,288},{48,304},{64,320},{80,336},{96,352},{112... | collective-permute-start | bytes 196616 | tf_op jit(solution)/shard_map/ppermute | solution.py:183
  77.3 6.0 %collective-permute-done.9 = f32[128,128]{1,0:T(8,128)S(1)} collective-permute-done((f32[128,128]{1,0:T(8,128)S(1)}, f32[128,128]{1,0:T(8,128)S(1)}, u32[]{:S(2)}, u32[]{:S(2)}) %collective-permute-start.9) | collective-permute-done | bytes 65568 | tf_op jit(solution)/shard_map/ppermute | solution.py:183
  83.3 1.9 %collective-permute-start.10 = (f32[128,128]{1,0:T(8,128)S(1)}, f32[128,128]{1,0:T(8,128)S(1)}, u32[]{:S(2)}, u32[]{:S(2)}) collective-permute-start(f32[128,128]{1,0:T(8,128)S(1)} %add.17), channel_id=1, source_target_pairs={{0,32},{16,48},{32,0},{48,16},{64,96},{80,112},{96,64},{112,80},{1... | collective-permute-start | bytes 196616 | tf_op jit(solution)/shard_map/ppermute | solution.py:183
  85.2 3.7 %collective-permute-done.10 = f32[128,128]{1,0:T(8,128)S(1)} collective-permute-done((f32[128,128]{1,0:T(8,128)S(1)}, f32[128,128]{1,0:T(8,128)S(1)}, u32[]{:S(2)}, u32[]{:S(2)}) %collective-permute-start.10) | collective-permute-done | bytes 65568 | tf_op jit(solution)/shard_map/ppermute | solution.py:183
  88.9 4.6 %collective-permute-start.11 = (f32[128,128]{1,0:T(8,128)S(1)}, f32[128,128]{1,0:T(8,128)S(1)}, u32[]{:S(2)}, u32[]{:S(2)}) collective-permute-start(f32[128,128]{1,0:T(8,128)S(1)} %add.18), channel_id=1, source_target_pairs={{0,8},{1,9},{2,10},{3,11},{4,12},{5,13},{6,14},{7,15},{8,0},{9,1},... | collective-permute-start | bytes 196616 | tf_op jit(solution)/shard_map/ppermute | solution.py:183
  93.5 2.4 %collective-permute-done.11 = f32[128,128]{1,0:T(8,128)S(1)} collective-permute-done((f32[128,128]{1,0:T(8,128)S(1)}, f32[128,128]{1,0:T(8,128)S(1)}, u32[]{:S(2)}, u32[]{:S(2)}) %collective-permute-start.11) | collective-permute-done | bytes 65568 | tf_op jit(solution)/shard_map/ppermute | solution.py:183
  96.0 3.4 %all-to-all-done.1.got_ref = bf16[16,384,128]{2,1,0:T(8,128)(2,1)S(1)} async-done(((bf16[16,384,128]{2,1,0:T(8,128)(2,1)}), bf16[16,384,128]{2,1,0:T(8,128)(2,1)S(1)}, u32[]{:S(2)}, u32[]{:S(2)}) %all-to-all-start.1) | async-done | bytes 1572896 | tf_op jit(solution)/shard_map/all_to_all | solution.py:206
  99.4 0.9 finish.1
  (13 shorter events, 0.2 us)
Async XLA Ops:
  3.1 45.9 %copy-start = (bf16[32,128,128]{2,1,0:T(8,128)(2,1)S(1)}, bf16[32,128,128]{2,1,0:T(8,128)(2,1)}, u32[]{:S(2)}) copy-start(bf16[32,128,128]{2,1,0:T(8,128)(2,1)} %tiles_ref.1) | copy-start | bytes 3145732
  3.1 45.9 %copy-start.1 = (bf16[384,128]{1,0:T(8,128)(2,1)S(1)}, bf16[384,128]{1,0:T(8,128)(2,1)}, u32[]{:S(2)}) copy-start(bf16[384,128]{1,0:T(8,128)(2,1)} %get-tuple-element.12.own) | copy-start | bytes 294916
  3.1 45.9 %copy-start.2 = (s32[1,32]{1,0:T(1,128)S(1)}, s32[1,32]{1,0:T(1,128)}, u32[]{:S(2)}) copy-start(s32[1,32]{1,0:T(1,128)} %get-tuple-element.10.from_ref) | copy-start | bytes 388
  3.2 45.9 %copy-start.3 = (s32[1,32]{1,0:T(1,128)S(1)}, s32[1,32]{1,0:T(1,128)}, u32[]{:S(2)}) copy-start(s32[1,32]{1,0:T(1,128)} %get-tuple-element.11.to_ref) | copy-start | bytes 388
  3.2 30.0 %all-to-all-start = ((bf16[8,128,128]{2,1,0:T(8,128)(2,1)}), bf16[8,128,128]{2,1,0:T(8,128)(2,1)S(1)}, u32[]{:S(2)}, u32[]{:S(2)}) async-start(bf16[8,128,128]{2,1,0:T(8,128)(2,1)} %get-tuple-element.13), calls=%async_computation | async-start | bytes 524288 | tf_op jit(solution)/shard_map/all_to_all | solution.py:169
  14.2 21.1 %collective-permute-start.1 = (bf16[384,128]{1,0:T(8,128)(2,1)}, bf16[384,128]{1,0:T(8,128)(2,1)S(1)}, u32[]{:S(2)}, u32[]{:S(2)}) collective-permute-start(bf16[384,128]{1,0:T(8,128)(2,1)} %get-tuple-element.12.own), channel_id=1, source_target_pairs={{0,32},{16,48},{32,0},{48,16},{64,96},{80,112},{96,64},{112,80},{1... | collective-permute-start | bytes 294920 | tf_op jit(solution)/shard_map/ppermute | solution.py:156
  17.3 4.3 %collective-permute-start = (bf16[384,128]{1,0:T(8,128)(2,1)}, bf16[384,128]{1,0:T(8,128)(2,1)S(1)}, u32[]{:S(2)}, u32[]{:S(2)}) collective-permute-start(bf16[384,128]{1,0:T(8,128)(2,1)} %get-tuple-element.12.own), channel_id=1, source_target_pairs={{0,16},{16,0},{32,48},{48,32},{64,80},{80,64},{96,112},{112,96},{1... | collective-permute-start | bytes 294920 | tf_op jit(solution)/shard_map/ppermute | solution.py:156
  21.6 13.7 %collective-permute-start.2 = (bf16[768,128]{1,0:T(8,128)(2,1)S(1)}, bf16[768,128]{1,0:T(8,128)(2,1)S(1)}, u32[]{:S(2)}, u32[]{:S(2)}) collective-permute-start(bf16[768,128]{1,0:T(8,128)(2,1)S(1)} %constant_dynamic-update-slice_fusion), channel_id=1, source_target_pairs={{16,432},{32,128},{80,496},{96,192},{144,48},{160,256},{208,112},{... | collective-permute-start | bytes 589832 | tf_op jit(solution)/shard_map/ppermute | solution.py:160
  27.5 13.7 %collective-permute-start.5 = (bf16[768,128]{1,0:T(8,128)(2,1)S(1)}, bf16[768,128]{1,0:T(8,128)(2,1)S(1)}, u32[]{:S(2)}, u32[]{:S(2)}) collective-permute-start(bf16[768,128]{1,0:T(8,128)(2,1)S(1)} %constant_dynamic-update-slice_fusion), channel_id=1, source_target_pairs={{0,96},{16,496},{32,64},{48,464},{64,160},{80,48},{96,128},{112,16... | collective-permute-start | bytes 589832 | tf_op jit(solution)/shard_map/ppermute | solution.py:160
  29.4 11.7 %collective-permute-start.4 = (bf16[768,128]{1,0:T(8,128)(2,1)S(1)}, bf16[768,128]{1,0:T(8,128)(2,1)S(1)}, u32[]{:S(2)}, u32[]{:S(2)}) collective-permute-start(bf16[768,128]{1,0:T(8,128)(2,1)S(1)} %constant_dynamic-update-slice_fusion), channel_id=1, source_target_pairs={{0,128},{16,400},{32,160},{48,432},{64,192},{80,464},{96,224},{112... | collective-permute-start | bytes 589832 | tf_op jit(solution)/shard_map/ppermute | solution.py:160
  33.2 7.9 %collective-permute-start.3 = (bf16[768,128]{1,0:T(8,128)(2,1)S(1)}, bf16[768,128]{1,0:T(8,128)(2,1)S(1)}, u32[]{:S(2)}, u32[]{:S(2)}) collective-permute-start(bf16[768,128]{1,0:T(8,128)(2,1)S(1)} %constant_dynamic-update-slice_fusion), channel_id=1, source_target_pairs={{0,64},{16,464},{32,96},{48,496},{64,128},{80,16},{96,160},{112,48... | collective-permute-start | bytes 589832 | tf_op jit(solution)/shard_map/ppermute | solution.py:160
  41.2 7.8 %collective-permute-start.6 = (bf16[3712,128]{1,0:T(8,128)(2,1)S(1)}, bf16[3712,128]{1,0:T(8,128)(2,1)S(1)}, u32[]{:S(2)}, u32[]{:S(2)}) collective-permute-start(bf16[3712,128]{1,0:T(8,128)(2,1)S(1)} %constant_dynamic-update-slice_fusion.2.ours), channel_id=1, source_target_pairs={{0,16},{16,0},{32,48},{48,32},{64,80},{80,64},{96,112},{112,96},{1... | collective-permute-start | bytes 2850824 | tf_op jit(solution)/shard_map/ppermute | solution.py:156
  52.2 47.2 %all-to-all-start.1 = ((bf16[16,384,128]{2,1,0:T(8,128)(2,1)}), bf16[16,384,128]{2,1,0:T(8,128)(2,1)S(1)}, u32[]{:S(2)}, u32[]{:S(2)}) async-start(bf16[16,384,128]{2,1,0:T(8,128)(2,1)} %get-tuple-element.16), calls=%async_computation.1 | async-start | bytes 3145728 | tf_op jit(solution)/shard_map/all_to_all | solution.py:206
  61.4 5.0 %collective-permute-start.7 = (f32[128,128]{1,0:T(8,128)S(1)}, f32[128,128]{1,0:T(8,128)S(1)}, u32[]{:S(2)}, u32[]{:S(2)}) collective-permute-start(f32[128,128]{1,0:T(8,128)S(1)} %get-tuple-element.17), channel_id=1, source_target_pairs={{0,64},{16,80},{32,96},{48,112},{64,0},{80,16},{96,32},{112,48},{1... | collective-permute-start | bytes 196616 | tf_op jit(solution)/shard_map/ppermute | solution.py:183
  66.4 6.9 %collective-permute-start.8 = (f32[128,128]{1,0:T(8,128)S(1)}, f32[128,128]{1,0:T(8,128)S(1)}, u32[]{:S(2)}, u32[]{:S(2)}) collective-permute-start(f32[128,128]{1,0:T(8,128)S(1)} %add.15), channel_id=1, source_target_pairs={{0,128},{16,144},{32,160},{48,176},{64,192},{80,208},{96,224},{112... | collective-permute-start | bytes 196616 | tf_op jit(solution)/shard_map/ppermute | solution.py:183
  73.3 9.9 %collective-permute-start.9 = (f32[128,128]{1,0:T(8,128)S(1)}, f32[128,128]{1,0:T(8,128)S(1)}, u32[]{:S(2)}, u32[]{:S(2)}) collective-permute-start(f32[128,128]{1,0:T(8,128)S(1)} %add.16), channel_id=1, source_target_pairs={{0,256},{16,272},{32,288},{48,304},{64,320},{80,336},{96,352},{112... | collective-permute-start | bytes 196616 | tf_op jit(solution)/shard_map/ppermute | solution.py:183
  83.3 5.6 %collective-permute-start.10 = (f32[128,128]{1,0:T(8,128)S(1)}, f32[128,128]{1,0:T(8,128)S(1)}, u32[]{:S(2)}, u32[]{:S(2)}) collective-permute-start(f32[128,128]{1,0:T(8,128)S(1)} %add.17), channel_id=1, source_target_pairs={{0,32},{16,48},{32,0},{48,16},{64,96},{80,112},{96,64},{112,80},{1... | collective-permute-start | bytes 196616 | tf_op jit(solution)/shard_map/ppermute | solution.py:183
  88.9 7.1 %collective-permute-start.11 = (f32[128,128]{1,0:T(8,128)S(1)}, f32[128,128]{1,0:T(8,128)S(1)}, u32[]{:S(2)}, u32[]{:S(2)}) collective-permute-start(f32[128,128]{1,0:T(8,128)S(1)} %add.18), channel_id=1, source_target_pairs={{0,8},{1,9},{2,10},{3,11},{4,12},{5,13},{6,14},{7,15},{8,0},{9,1},... | collective-permute-start | bytes 196616 | tf_op jit(solution)/shard_map/ppermute | solution.py:183

commit v12 on v10

--- a/solution.py
+++ b/solution.py
@@ -27,7 +27,7 @@
     below = gap > planes // 2
     steps = jnp.where(below, planes - gap, gap)
     receiver = jnp.where(gap == 0, core, jnp.where(below, 0, 1))
-    first = jnp.where(steps == 2, jnp.where(same_chip, 7, 1), jnp.where(same_chip, 3, 5))
+    first = jnp.where(steps == 2, jnp.where(same_chip, 1, 7), jnp.where(same_chip, 3, 5))
     place = jnp.where(gap == 0, 0, first + jnp.where(core == receiver, 0, 1))
     slot = 2 + place + jnp.where(receiver == lax.rem(row, 2), 0, 9)
     slot = jnp.where((gap == 0) & same_chip, jnp.where(same_core, 0, 1), slot)
@@ -155,17 +155,18 @@
     def swap(value, bit):
         return lax.ppermute(value, "row", [(i, i ^ bit) for i in range(row_count)])
 
-    def to_plane(value, steps, chip_bit, wanted):
+    def to_plane(value, steps, chip_bit):
         pairs = [(i, ((i ^ chip_bit) + PLANE * (steps if i % 2 == 0 else -steps)) % row_count) for i in range(row_count)]
-        return lax.ppermute(value, "row", [pair for pair in pairs if pair[0] % PLANE in wanted])
+        return lax.ppermute(value, "row", pairs)
 
     beside = swap(adjoint, 1)
     across = swap(adjoint, 2)
     chip = jnp.concatenate([adjoint, beside])
-    far = to_plane(chip, 2, 0, (0, 1, 2, 3))
-    across_far = to_plane(chip, 2, 2, (1, 2))
-    across_near = to_plane(chip, 1, 2, (0, 1, 2, 3))
-    near = to_plane(chip, 1, 0, (0, 1, 2, 3))
+    far = to_plane(chip, 2, 0)
+    across_near = to_plane(chip, 1, 2)
+    near = to_plane(chip, 1, 0)
+    wanted = [(i, i ^ 2) for i in range(row_count) if i % PLANE in (1, 2)]
+    across_far = lax.ppermute(far, "row", wanted)
 
     groups = [list(range(half)), list(range(half, col_count))]
     wz = lax.all_to_all(wpart, "col", 0, 0, axis_index_groups=groups)
@@ -181,7 +182,7 @@
     def partner(value, axis, bit):
         return lax.ppermute(value, axis, [(i, i ^ bit) for i in range(lax.axis_size(axis))])
 
-    received = jnp.concatenate([across, across_far, near, across_near, far, halves])
+    received = jnp.concatenate([across, far, near, across_near, across_far, halves])
     other = swap(received, 1)
 
     sends, wsum = pl.pallas_call(

time: 101 us -> 98.7 us (0.977)
  waiting for transfers between devices: 34 us -> 29.8 us
  starting transfers between devices: 57.5 us -> 59.6 us
    ppermute x4, waiting for transfers between devices: 5.84 us -> 0.52 us  [the longest x3 0.52 us: to_plane(): return lax.ppermute(value, 'row', pairs)]
    all_to_all x1, waiting for transfers between devices: 0.01 us -> 2.39 us  [on_device(): wz = lax.all_to_all(wpart, 'col', 0, 0, axis_index_groups=groups)]
    ppermute x5, waiting for transfers between devices: 22.4 us -> 20.8 us  [partner(): lax.ppermute(value, axis, [(i, i ^ bit) for i in range(lax.axis_size(axis...]
    ppermute x4, starting transfers between devices: 9.71 us -> 11 us  [the longest x3 7.9 us: to_plane(): return lax.ppermute(value, 'row', pairs)]
    ppermute x5, starting transfers between devices: 12.2 us -> 13.5 us  [partner(): lax.ppermute(value, axis, [(i, i ^ bit) for i in range(lax.axis_size(axis...]
  transfers between devices with their start and end apart: 14 -> 14, of which waited for: 9 -> 10; matrix products, arithmetic and copies ran while one was open for 1% -> 1% of each run, Pallas kernels for 0% -> 0%
where the time goes in v12:
time: 98.7 us; the launch traced here: 97.9 us
  starting transfers between devices  59.6 us (60%)
  waiting for transfers between devices  29.8 us (30%)
  Pallas kernels  6.53 us (7%)
  local copies, waits for them, and re-layouts  1.07 us (1%)
    ppermute x5, waiting for transfers between devices, partner(): lax.ppermute(value, axis, [(i, i ^ bit) for i in range(lax.axis_size(axis...  20.8 us
    ppermute x3, starting transfers between devices, swap(): return lax.ppermute(value, 'row', [(i, i ^ bit) for i in range(row_count)])  15.6 us
    ppermute x5, starting transfers between devices, partner(): lax.ppermute(value, axis, [(i, i ^ bit) for i in range(lax.axis_size(axis...  13.5 us
    all_to_all x1, starting transfers between devices, on_device(): wz = lax.all_to_all(wpart, 'col', 0, 0, axis_index_groups=groups)  10 us
    all_to_all x1, starting transfers between devices, on_device(): got = lax.all_to_all(sends, 'col', 0, 0)  9.5 us
    ppermute x3, starting transfers between devices, to_plane(): return lax.ppermute(value, 'row', pairs)  7.9 us
    all_to_all x1, waiting for transfers between devices, on_device(): got = lax.all_to_all(sends, 'col', 0, 0)  3.68 us
    pallas_call x1, Pallas kernels, on_device(): pl.pallas_call(tile_kernel, out_shape=(jax.ShapeDtypeStruct((col_count, n...  3.14 us
  transfers between devices with their start and end apart: 14, of which 10 were waited for; matrix products, arithmetic and copies ran while one was open for 1% of the time, Pallas kernels for 0%

profile of v12, /device:TPU:1, one launch (start us, length us, event | category | flops | bytes accessed | tf_op | source)
XLA Modules:
  0.0 97.9 jit_solution(6542710706457309281)
XLA Ops:
  0.6 2.5 %adjoint.1 = (bf16[384,128]{1,0:T(8,128)(2,1)}, bf16[8,128,128]{2,1,0:T(8,128)(2,1)}, s32[1,32]{1,0:T(1,128)}, s32[1,32]{1,0:T(1,128)}) custom-call(s32[3,128]{1,0:T(4,128)} %bitcast.3, bf16[384,128]{1,0:T(8,128)(2,1)} %cot_in.1, bf16[384,128]{1,0:T(8,128)(2,1)} %pre_in.1, bf16[384,128]{1,0:T(8,128)(2,1)} %agg_in.1, bf16[128,128]{1,0:T(8,128)(2,1)} %w_in.1, ...), custom_call_target="tpu_custom_call" | custom-call | tf_op jit(solution)/shard_map/adjoint/pallas_call | solution.py:136
  3.1 0.0 copy-start
  3.1 0.0 copy-start.1
  3.1 0.0 copy-start.2
  3.2 0.0 copy-start.3
  3.2 4.1 %collective-permute-start.1 = (bf16[384,128]{1,0:T(8,128)(2,1)}, bf16[384,128]{1,0:T(8,128)(2,1)S(1)}, u32[]{:S(2)}, u32[]{:S(2)}) collective-permute-start(bf16[384,128]{1,0:T(8,128)(2,1)} %get-tuple-element.10.own), channel_id=1, source_target_pairs={{0,32},{16,48},{32,0},{48,16},{64,96},{80,112},{96,64},{112,80},{1... | collective-permute-start | bytes 294920 | tf_op jit(solution)/shard_map/ppermute | solution.py:156
  7.3 6.8 %collective-permute-start = (bf16[384,128]{1,0:T(8,128)(2,1)}, bf16[384,128]{1,0:T(8,128)(2,1)S(1)}, u32[]{:S(2)}, u32[]{:S(2)}) collective-permute-start(bf16[384,128]{1,0:T(8,128)(2,1)} %get-tuple-element.10.own), channel_id=1, source_target_pairs={{0,16},{16,0},{32,48},{48,32},{64,80},{80,64},{96,112},{112,96},{1... | collective-permute-start | bytes 294920 | tf_op jit(solution)/shard_map/ppermute | solution.py:156
  14.0 0.9 constant_dynamic-update-slice_fusion.1
  14.9 0.2 collective-permute-done.beside
  15.2 2.0 %collective-permute-start.2 = (bf16[768,128]{1,0:T(8,128)(2,1)S(1)}, bf16[768,128]{1,0:T(8,128)(2,1)S(1)}, u32[]{:S(2)}, u32[]{:S(2)}) collective-permute-start(bf16[768,128]{1,0:T(8,128)(2,1)S(1)} %constant_dynamic-update-slice_fusion), channel_id=1, source_target_pairs={{0,128},{16,400},{32,160},{48,432},{64,192},{80,464},{96,224},{112... | collective-permute-start | bytes 589832 | tf_op jit(solution)/shard_map/ppermute | solution.py:160
  17.2 10.0 %all-to-all-start = ((bf16[8,128,128]{2,1,0:T(8,128)(2,1)}), bf16[8,128,128]{2,1,0:T(8,128)(2,1)S(1)}, u32[]{:S(2)}, u32[]{:S(2)}) async-start(bf16[8,128,128]{2,1,0:T(8,128)(2,1)} %get-tuple-element.11), calls=%async_computation | async-start | bytes 524288 | tf_op jit(solution)/shard_map/all_to_all | solution.py:172
  27.2 2.9 %collective-permute-start.4 = (bf16[768,128]{1,0:T(8,128)(2,1)S(1)}, bf16[768,128]{1,0:T(8,128)(2,1)S(1)}, u32[]{:S(2)}, u32[]{:S(2)}) collective-permute-start(bf16[768,128]{1,0:T(8,128)(2,1)S(1)} %constant_dynamic-update-slice_fusion), channel_id=1, source_target_pairs={{0,96},{16,496},{32,64},{48,464},{64,160},{80,48},{96,128},{112,16... | collective-permute-start | bytes 589832 | tf_op jit(solution)/shard_map/ppermute | solution.py:160
  30.2 3.0 %collective-permute-start.3 = (bf16[768,128]{1,0:T(8,128)(2,1)S(1)}, bf16[768,128]{1,0:T(8,128)(2,1)S(1)}, u32[]{:S(2)}, u32[]{:S(2)}) collective-permute-start(bf16[768,128]{1,0:T(8,128)(2,1)S(1)} %constant_dynamic-update-slice_fusion), channel_id=1, source_target_pairs={{0,64},{16,464},{32,96},{48,496},{64,128},{80,16},{96,160},{112,48... | collective-permute-start | bytes 589832 | tf_op jit(solution)/shard_map/ppermute | solution.py:160
  33.1 0.0 collective-permute-done.1
  33.2 0.0 collective-permute-done.2
  33.2 3.1 %collective-permute-start.5 = (bf16[768,128]{1,0:T(8,128)(2,1)S(1)}, bf16[768,128]{1,0:T(8,128)(2,1)S(1)}, u32[]{:S(2)}, u32[]{:S(2)}) collective-permute-start(bf16[768,128]{1,0:T(8,128)(2,1)S(1)} %collective-permute-done.2), channel_id=1, source_target_pairs={{16,48},{32,0},{80,112},{96,64},{144,176},{160,128},{208,240},{224... | collective-permute-start | bytes 589832 | tf_op jit(solution)/shard_map/ppermute | solution.py:169
  36.4 0.5 collective-permute-done.3
  36.9 0.0 collective-permute-done.4
  36.9 2.4 %all-to-all-done.parts_ref = bf16[8,128,128]{2,1,0:T(8,128)(2,1)S(1)} async-done(((bf16[8,128,128]{2,1,0:T(8,128)(2,1)}), bf16[8,128,128]{2,1,0:T(8,128)(2,1)S(1)}, u32[]{:S(2)}, u32[]{:S(2)}) %all-to-all-start) | async-done | bytes 262176 | tf_op jit(solution)/shard_map/all_to_all | solution.py:172
  39.4 0.0 collective-permute-done.5
  39.4 4.7 %collective-permute-start.6 = (bf16[3712,128]{1,0:T(8,128)(2,1)S(1)}, bf16[3712,128]{1,0:T(8,128)(2,1)S(1)}, u32[]{:S(2)}, u32[]{:S(2)}) collective-permute-start(bf16[3712,128]{1,0:T(8,128)(2,1)S(1)} %constant_dynamic-update-slice_fusion.2.ours), channel_id=1, source_target_pairs={{0,16},{16,0},{32,48},{48,32},{64,80},{80,64},{96,112},{112,96},{1... | collective-permute-start | bytes 2850824 | tf_op jit(solution)/shard_map/ppermute | solution.py:156
  44.2 2.1 %collective-permute-done.6.theirs = bf16[3712,128]{1,0:T(8,128)(2,1)S(1)} collective-permute-done((bf16[3712,128]{1,0:T(8,128)(2,1)S(1)}, bf16[3712,128]{1,0:T(8,128)(2,1)S(1)}, u32[]{:S(2)}, u32[]{:S(2)}) %collective-permute-start.6) | collective-permute-done | bytes 950304 | tf_op jit(solution)/shard_map/ppermute | solution.py:156
  46.3 0.0 copy-done
  46.3 0.0 copy-done.1
  46.3 0.0 copy-done.2
  46.3 0.0 copy-done.3
  46.3 3.1 %tiles.1 = (bf16[16,384,128]{2,1,0:T(8,128)(2,1)}, f32[128,128]{1,0:T(8,128)S(1)}) custom-call(s32[1,32]{1,0:T(1,128)S(1)} %copy-done.2, s32[1,32]{1,0:T(1,128)S(1)} %copy-done.3, bf16[32,128,128]{2,1,0:T(8,128)(2,1)S(1)} %copy-done, bf16[384,128]{1,0:T(8,128)(2,1)S(1)} %copy-done.1, bf16[384,128]{1,0:T(8,128)(2,1)S(1)} %collective-permute-done.beside, ...), custom_call_target="tpu_custom_call" | custom-call | flops 134217728 | bytes 6291456 | tf_op jit(solution)/shard_map/tiles/pallas_call | solution.py:188
  49.5 9.5 %all-to-all-start.1 = ((bf16[16,384,128]{2,1,0:T(8,128)(2,1)}), bf16[16,384,128]{2,1,0:T(8,128)(2,1)S(1)}, u32[]{:S(2)}, u32[]{:S(2)}) async-start(bf16[16,384,128]{2,1,0:T(8,128)(2,1)} %get-tuple-element.12), calls=%async_computation.1 | async-start | bytes 3145728 | tf_op jit(solution)/shard_map/all_to_all | solution.py:206
  59.0 2.3 %collective-permute-start.7 = (f32[128,128]{1,0:T(8,128)S(1)}, f32[128,128]{1,0:T(8,128)S(1)}, u32[]{:S(2)}, u32[]{:S(2)}) collective-permute-start(f32[128,128]{1,0:T(8,128)S(1)} %get-tuple-element.13), channel_id=1, source_target_pairs={{0,64},{16,80},{32,96},{48,112},{64,0},{80,16},{96,32},{112,48},{1... | collective-permute-start | bytes 196616 | tf_op jit(solution)/shard_map/ppermute | solution.py:183
  61.3 2.7 %collective-permute-done.7 = f32[128,128]{1,0:T(8,128)S(1)} collective-permute-done((f32[128,128]{1,0:T(8,128)S(1)}, f32[128,128]{1,0:T(8,128)S(1)}, u32[]{:S(2)}, u32[]{:S(2)}) %collective-permute-start.7) | collective-permute-done | bytes 65568 | tf_op jit(solution)/shard_map/ppermute | solution.py:183
  64.0 2.4 %collective-permute-start.8 = (f32[128,128]{1,0:T(8,128)S(1)}, f32[128,128]{1,0:T(8,128)S(1)}, u32[]{:S(2)}, u32[]{:S(2)}) collective-permute-start(f32[128,128]{1,0:T(8,128)S(1)} %add.15), channel_id=1, source_target_pairs={{0,128},{16,144},{32,160},{48,176},{64,192},{80,208},{96,224},{112... | collective-permute-start | bytes 196616 | tf_op jit(solution)/shard_map/ppermute | solution.py:183
  66.4 4.5 %collective-permute-done.8 = f32[128,128]{1,0:T(8,128)S(1)} collective-permute-done((f32[128,128]{1,0:T(8,128)S(1)}, f32[128,128]{1,0:T(8,128)S(1)}, u32[]{:S(2)}, u32[]{:S(2)}) %collective-permute-start.8) | collective-permute-done | bytes 65568 | tf_op jit(solution)/shard_map/ppermute | solution.py:183
  70.9 1.9 %collective-permute-start.9 = (f32[128,128]{1,0:T(8,128)S(1)}, f32[128,128]{1,0:T(8,128)S(1)}, u32[]{:S(2)}, u32[]{:S(2)}) collective-permute-start(f32[128,128]{1,0:T(8,128)S(1)} %add.16), channel_id=1, source_target_pairs={{0,256},{16,272},{32,288},{48,304},{64,320},{80,336},{96,352},{112... | collective-permute-start | bytes 196616 | tf_op jit(solution)/shard_map/ppermute | solution.py:183
  72.9 7.3 %collective-permute-done.9 = f32[128,128]{1,0:T(8,128)S(1)} collective-permute-done((f32[128,128]{1,0:T(8,128)S(1)}, f32[128,128]{1,0:T(8,128)S(1)}, u32[]{:S(2)}, u32[]{:S(2)}) %collective-permute-start.9) | collective-permute-done | bytes 65568 | tf_op jit(solution)/shard_map/ppermute | solution.py:183
  80.1 1.9 %collective-permute-start.10 = (f32[128,128]{1,0:T(8,128)S(1)}, f32[128,128]{1,0:T(8,128)S(1)}, u32[]{:S(2)}, u32[]{:S(2)}) collective-permute-start(f32[128,128]{1,0:T(8,128)S(1)} %add.17), channel_id=1, source_target_pairs={{0,32},{16,48},{32,0},{48,16},{64,96},{80,112},{96,64},{112,80},{1... | collective-permute-start | bytes 196616 | tf_op jit(solution)/shard_map/ppermute | solution.py:183
  82.1 3.9 %collective-permute-done.10 = f32[128,128]{1,0:T(8,128)S(1)} collective-permute-done((f32[128,128]{1,0:T(8,128)S(1)}, f32[128,128]{1,0:T(8,128)S(1)}, u32[]{:S(2)}, u32[]{:S(2)}) %collective-permute-start.10) | collective-permute-done | bytes 65568 | tf_op jit(solution)/shard_map/ppermute | solution.py:183
  86.0 4.9 %collective-permute-start.11 = (f32[128,128]{1,0:T(8,128)S(1)}, f32[128,128]{1,0:T(8,128)S(1)}, u32[]{:S(2)}, u32[]{:S(2)}) collective-permute-start(f32[128,128]{1,0:T(8,128)S(1)} %add.18), channel_id=1, source_target_pairs={{0,8},{1,9},{2,10},{3,11},{4,12},{5,13},{6,14},{7,15},{8,0},{9,1},... | collective-permute-start | bytes 196616 | tf_op jit(solution)/shard_map/ppermute | solution.py:183
  90.9 2.5 %collective-permute-done.11 = f32[128,128]{1,0:T(8,128)S(1)} collective-permute-done((f32[128,128]{1,0:T(8,128)S(1)}, f32[128,128]{1,0:T(8,128)S(1)}, u32[]{:S(2)}, u32[]{:S(2)}) %collective-permute-start.11) | collective-permute-done | bytes 65568 | tf_op jit(solution)/shard_map/ppermute | solution.py:183
  93.4 3.7 %all-to-all-done.1.got_ref = bf16[16,384,128]{2,1,0:T(8,128)(2,1)S(1)} async-done(((bf16[16,384,128]{2,1,0:T(8,128)(2,1)}), bf16[16,384,128]{2,1,0:T(8,128)(2,1)S(1)}, u32[]{:S(2)}, u32[]{:S(2)}) %all-to-all-start.1) | async-done | bytes 1572896 | tf_op jit(solution)/shard_map/all_to_all | solution.py:206
  97.1 0.9 finish.1
  (13 shorter events, 0.2 us)
Async XLA Ops:
  3.1 43.2 %copy-start = (bf16[32,128,128]{2,1,0:T(8,128)(2,1)S(1)}, bf16[32,128,128]{2,1,0:T(8,128)(2,1)}, u32[]{:S(2)}) copy-start(bf16[32,128,128]{2,1,0:T(8,128)(2,1)} %tiles_ref.1) | copy-start | bytes 3145732
  3.1 43.2 %copy-start.1 = (bf16[384,128]{1,0:T(8,128)(2,1)S(1)}, bf16[384,128]{1,0:T(8,128)(2,1)}, u32[]{:S(2)}) copy-start(bf16[384,128]{1,0:T(8,128)(2,1)} %get-tuple-element.10.own) | copy-start | bytes 294916
  3.1 43.2 %copy-start.2 = (s32[1,32]{1,0:T(1,128)S(1)}, s32[1,32]{1,0:T(1,128)}, u32[]{:S(2)}) copy-start(s32[1,32]{1,0:T(1,128)} %get-tuple-element.8.from_ref) | copy-start | bytes 388
  3.2 43.2 %copy-start.3 = (s32[1,32]{1,0:T(1,128)S(1)}, s32[1,32]{1,0:T(1,128)}, u32[]{:S(2)}) copy-start(s32[1,32]{1,0:T(1,128)} %get-tuple-element.9.to_ref) | copy-start | bytes 388
  3.2 30.0 %collective-permute-start.1 = (bf16[384,128]{1,0:T(8,128)(2,1)}, bf16[384,128]{1,0:T(8,128)(2,1)S(1)}, u32[]{:S(2)}, u32[]{:S(2)}) collective-permute-start(bf16[384,128]{1,0:T(8,128)(2,1)} %get-tuple-element.10.own), channel_id=1, source_target_pairs={{0,32},{16,48},{32,0},{48,16},{64,96},{80,112},{96,64},{112,80},{1... | collective-permute-start | bytes 294920 | tf_op jit(solution)/shard_map/ppermute | solution.py:156
  7.3 7.9 %collective-permute-start = (bf16[384,128]{1,0:T(8,128)(2,1)}, bf16[384,128]{1,0:T(8,128)(2,1)S(1)}, u32[]{:S(2)}, u32[]{:S(2)}) collective-permute-start(bf16[384,128]{1,0:T(8,128)(2,1)} %get-tuple-element.10.own), channel_id=1, source_target_pairs={{0,16},{16,0},{32,48},{48,32},{64,80},{80,64},{96,112},{112,96},{1... | collective-permute-start | bytes 294920 | tf_op jit(solution)/shard_map/ppermute | solution.py:156
  15.2 18.0 %collective-permute-start.2 = (bf16[768,128]{1,0:T(8,128)(2,1)S(1)}, bf16[768,128]{1,0:T(8,128)(2,1)S(1)}, u32[]{:S(2)}, u32[]{:S(2)}) collective-permute-start(bf16[768,128]{1,0:T(8,128)(2,1)S(1)} %constant_dynamic-update-slice_fusion), channel_id=1, source_target_pairs={{0,128},{16,400},{32,160},{48,432},{64,192},{80,464},{96,224},{112... | collective-permute-start | bytes 589832 | tf_op jit(solution)/shard_map/ppermute | solution.py:160
  17.2 22.2 %all-to-all-start = ((bf16[8,128,128]{2,1,0:T(8,128)(2,1)}), bf16[8,128,128]{2,1,0:T(8,128)(2,1)S(1)}, u32[]{:S(2)}, u32[]{:S(2)}) async-start(bf16[8,128,128]{2,1,0:T(8,128)(2,1)} %get-tuple-element.11), calls=%async_computation | async-start | bytes 524288 | tf_op jit(solution)/shard_map/all_to_all | solution.py:172
  27.2 9.7 %collective-permute-start.4 = (bf16[768,128]{1,0:T(8,128)(2,1)S(1)}, bf16[768,128]{1,0:T(8,128)(2,1)S(1)}, u32[]{:S(2)}, u32[]{:S(2)}) collective-permute-start(bf16[768,128]{1,0:T(8,128)(2,1)S(1)} %constant_dynamic-update-slice_fusion), channel_id=1, source_target_pairs={{0,96},{16,496},{32,64},{48,464},{64,160},{80,48},{96,128},{112,16... | collective-permute-start | bytes 589832 | tf_op jit(solution)/shard_map/ppermute | solution.py:160
  30.2 6.7 %collective-permute-start.3 = (bf16[768,128]{1,0:T(8,128)(2,1)S(1)}, bf16[768,128]{1,0:T(8,128)(2,1)S(1)}, u32[]{:S(2)}, u32[]{:S(2)}) collective-permute-start(bf16[768,128]{1,0:T(8,128)(2,1)S(1)} %constant_dynamic-update-slice_fusion), channel_id=1, source_target_pairs={{0,64},{16,464},{32,96},{48,496},{64,128},{80,16},{96,160},{112,48... | collective-permute-start | bytes 589832 | tf_op jit(solution)/shard_map/ppermute | solution.py:160
  33.2 6.2 %collective-permute-start.5 = (bf16[768,128]{1,0:T(8,128)(2,1)S(1)}, bf16[768,128]{1,0:T(8,128)(2,1)S(1)}, u32[]{:S(2)}, u32[]{:S(2)}) collective-permute-start(bf16[768,128]{1,0:T(8,128)(2,1)S(1)} %collective-permute-done.2), channel_id=1, source_target_pairs={{16,48},{32,0},{80,112},{96,64},{144,176},{160,128},{208,240},{224... | collective-permute-start | bytes 589832 | tf_op jit(solution)/shard_map/ppermute | solution.py:169
  39.4 6.9 %collective-permute-start.6 = (bf16[3712,128]{1,0:T(8,128)(2,1)S(1)}, bf16[3712,128]{1,0:T(8,128)(2,1)S(1)}, u32[]{:S(2)}, u32[]{:S(2)}) collective-permute-start(bf16[3712,128]{1,0:T(8,128)(2,1)S(1)} %constant_dynamic-update-slice_fusion.2.ours), channel_id=1, source_target_pairs={{0,16},{16,0},{32,48},{48,32},{64,80},{80,64},{96,112},{112,96},{1... | collective-permute-start | bytes 2850824 | tf_op jit(solution)/shard_map/ppermute | solution.py:156
  49.5 47.6 %all-to-all-start.1 = ((bf16[16,384,128]{2,1,0:T(8,128)(2,1)}), bf16[16,384,128]{2,1,0:T(8,128)(2,1)S(1)}, u32[]{:S(2)}, u32[]{:S(2)}) async-start(bf16[16,384,128]{2,1,0:T(8,128)(2,1)} %get-tuple-element.12), calls=%async_computation.1 | async-start | bytes 3145728 | tf_op jit(solution)/shard_map/all_to_all | solution.py:206
  59.0 5.0 %collective-permute-start.7 = (f32[128,128]{1,0:T(8,128)S(1)}, f32[128,128]{1,0:T(8,128)S(1)}, u32[]{:S(2)}, u32[]{:S(2)}) collective-permute-start(f32[128,128]{1,0:T(8,128)S(1)} %get-tuple-element.13), channel_id=1, source_target_pairs={{0,64},{16,80},{32,96},{48,112},{64,0},{80,16},{96,32},{112,48},{1... | collective-permute-start | bytes 196616 | tf_op jit(solution)/shard_map/ppermute | solution.py:183
  64.0 6.9 %collective-permute-start.8 = (f32[128,128]{1,0:T(8,128)S(1)}, f32[128,128]{1,0:T(8,128)S(1)}, u32[]{:S(2)}, u32[]{:S(2)}) collective-permute-start(f32[128,128]{1,0:T(8,128)S(1)} %add.15), channel_id=1, source_target_pairs={{0,128},{16,144},{32,160},{48,176},{64,192},{80,208},{96,224},{112... | collective-permute-start | bytes 196616 | tf_op jit(solution)/shard_map/ppermute | solution.py:183
  70.9 9.2 %collective-permute-start.9 = (f32[128,128]{1,0:T(8,128)S(1)}, f32[128,128]{1,0:T(8,128)S(1)}, u32[]{:S(2)}, u32[]{:S(2)}) collective-permute-start(f32[128,128]{1,0:T(8,128)S(1)} %add.16), channel_id=1, source_target_pairs={{0,256},{16,272},{32,288},{48,304},{64,320},{80,336},{96,352},{112... | collective-permute-start | bytes 196616 | tf_op jit(solution)/shard_map/ppermute | solution.py:183
  80.1 5.8 %collective-permute-start.10 = (f32[128,128]{1,0:T(8,128)S(1)}, f32[128,128]{1,0:T(8,128)S(1)}, u32[]{:S(2)}, u32[]{:S(2)}) collective-permute-start(f32[128,128]{1,0:T(8,128)S(1)} %add.17), channel_id=1, source_target_pairs={{0,32},{16,48},{32,0},{48,16},{64,96},{80,112},{96,64},{112,80},{1... | collective-permute-start | bytes 196616 | tf_op jit(solution)/shard_map/ppermute | solution.py:183
  86.0 7.4 %collective-permute-start.11 = (f32[128,128]{1,0:T(8,128)S(1)}, f32[128,128]{1,0:T(8,128)S(1)}, u32[]{:S(2)}, u32[]{:S(2)}) collective-permute-start(f32[128,128]{1,0:T(8,128)S(1)} %add.18), channel_id=1, source_target_pairs={{0,8},{1,9},{2,10},{3,11},{4,12},{5,13},{6,14},{7,15},{8,0},{9,1},... | collective-permute-start | bytes 196616 | tf_op jit(solution)/shard_map/ppermute | solution.py:183

commit v13 on v12

--- a/solution.py
+++ b/solution.py
@@ -27,8 +27,8 @@
     below = gap > planes // 2
     steps = jnp.where(below, planes - gap, gap)
     receiver = jnp.where(gap == 0, core, jnp.where(below, 0, 1))
-    first = jnp.where(steps == 2, jnp.where(same_chip, 1, 7), jnp.where(same_chip, 3, 5))
-    place = jnp.where(gap == 0, 0, first + jnp.where(core == receiver, 0, 1))
+    first = jnp.where(steps == 2, jnp.where(same_chip, 0, 7), jnp.where(same_chip, 4, 2))
+    place = jnp.where(gap == 0, 6, first + jnp.where(core == receiver, 0, 1))
     slot = 2 + place + jnp.where(receiver == lax.rem(row, 2), 0, 9)
     slot = jnp.where((gap == 0) & same_chip, jnp.where(same_core, 0, 1), slot)
     return slot * blocks + lax.rem(block, blocks)
@@ -182,7 +182,7 @@
     def partner(value, axis, bit):
         return lax.ppermute(value, axis, [(i, i ^ bit) for i in range(lax.axis_size(axis))])
 
-    received = jnp.concatenate([across, far, near, across_near, across_far, halves])
+    received = jnp.concatenate([far, across_near, near, across, across_far, halves])
     other = swap(received, 1)
 
     sends, wsum = pl.pallas_call(

time: 98.7 us -> 98.7 us (level)
  starting transfers between devices: 59.6 us -> 56.4 us
  waiting for transfers between devices: 29.8 us -> 33 us
    all_to_all x1, waiting for transfers between devices: 2.39 us -> 5.63 us  [on_device(): wz = lax.all_to_all(wpart, 'col', 0, 0, axis_index_groups=groups)]
    ppermute x3, starting transfers between devices: 15.6 us -> 13.4 us  [swap(): return lax.ppermute(value, 'row', [(i, i ^ bit) for i in range(row_count)])]
where the time goes in v13:
time: 98.7 us; the launch traced here: 97.9 us
  starting transfers between devices  56.4 us (57%)
  waiting for transfers between devices  33 us (33%)
  Pallas kernels  6.53 us (7%)
  local copies, waits for them, and re-layouts  1.07 us (1%)
    ppermute x5, waiting for transfers between devices, partner(): lax.ppermute(value, axis, [(i, i ^ bit) for i in range(lax.axis_size(axis...  20.8 us
    ppermute x5, starting transfers between devices, partner(): lax.ppermute(value, axis, [(i, i ^ bit) for i in range(lax.axis_size(axis...  13.5 us
    ppermute x3, starting transfers between devices, swap(): return lax.ppermute(value, 'row', [(i, i ^ bit) for i in range(row_count)])  13.4 us
    all_to_all x1, starting transfers between devices, on_device(): wz = lax.all_to_all(wpart, 'col', 0, 0, axis_index_groups=groups)  10 us
    all_to_all x1, starting transfers between devices, on_device(): got = lax.all_to_all(sends, 'col', 0, 0)  8.91 us
    ppermute x3, starting transfers between devices, to_plane(): return lax.ppermute(value, 'row', pairs)  7.38 us
    all_to_all x1, waiting for transfers between devices, on_device(): wz = lax.all_to_all(wpart, 'col', 0, 0, axis_index_groups=groups)  5.63 us
    all_to_all x1, waiting for transfers between devices, on_device(): got = lax.all_to_all(sends, 'col', 0, 0)  3.7 us
  transfers between devices with their start and end apart: 14, of which 10 were waited for; matrix products, arithmetic and copies ran while one was open for 1% of the time, Pallas kernels for 0%

profile of v13, /device:TPU:1, one launch (start us, length us, event | category | flops | bytes accessed | tf_op | source)
XLA Modules:
  0.0 97.9 jit_solution(1128487621750026891)
XLA Ops:
  0.6 2.5 %adjoint.1 = (bf16[384,128]{1,0:T(8,128)(2,1)}, bf16[8,128,128]{2,1,0:T(8,128)(2,1)}, s32[1,32]{1,0:T(1,128)}, s32[1,32]{1,0:T(1,128)}) custom-call(s32[3,128]{1,0:T(4,128)} %bitcast.3, bf16[384,128]{1,0:T(8,128)(2,1)} %cot_in.1, bf16[384,128]{1,0:T(8,128)(2,1)} %pre_in.1, bf16[384,128]{1,0:T(8,128)(2,1)} %agg_in.1, bf16[128,128]{1,0:T(8,128)(2,1)} %w_in.1, ...), custom_call_target="tpu_custom_call" | custom-call | tf_op jit(solution)/shard_map/adjoint/pallas_call | solution.py:136
  3.1 0.0 copy-start
  3.1 0.0 copy-start.1
  3.1 0.0 copy-start.2
  3.2 0.0 copy-start.3
  3.2 8.9 %collective-permute-start = (bf16[384,128]{1,0:T(8,128)(2,1)}, bf16[384,128]{1,0:T(8,128)(2,1)S(1)}, u32[]{:S(2)}, u32[]{:S(2)}) collective-permute-start(bf16[384,128]{1,0:T(8,128)(2,1)} %get-tuple-element.10.own), channel_id=1, source_target_pairs={{0,16},{16,0},{32,48},{48,32},{64,80},{80,64},{96,112},{112,96},{1... | collective-permute-start | bytes 294920 | tf_op jit(solution)/shard_map/ppermute | solution.py:156
  12.1 0.9 constant_dynamic-update-slice_fusion.1
  13.0 0.2 collective-permute-done.beside
  13.2 1.9 %collective-permute-start.1 = (bf16[768,128]{1,0:T(8,128)(2,1)S(1)}, bf16[768,128]{1,0:T(8,128)(2,1)S(1)}, u32[]{:S(2)}, u32[]{:S(2)}) collective-permute-start(bf16[768,128]{1,0:T(8,128)(2,1)S(1)} %constant_dynamic-update-slice_fusion), channel_id=1, source_target_pairs={{0,128},{16,400},{32,160},{48,432},{64,192},{80,464},{96,224},{112... | collective-permute-start | bytes 589832 | tf_op jit(solution)/shard_map/ppermute | solution.py:160
  15.2 2.5 %collective-permute-start.2 = (bf16[768,128]{1,0:T(8,128)(2,1)S(1)}, bf16[768,128]{1,0:T(8,128)(2,1)S(1)}, u32[]{:S(2)}, u32[]{:S(2)}) collective-permute-start(bf16[768,128]{1,0:T(8,128)(2,1)S(1)} %constant_dynamic-update-slice_fusion), channel_id=1, source_target_pairs={{0,96},{16,496},{32,64},{48,464},{64,160},{80,48},{96,128},{112,16... | collective-permute-start | bytes 589832 | tf_op jit(solution)/shard_map/ppermute | solution.py:160
  17.7 2.2 %collective-permute-start.4 = (bf16[384,128]{1,0:T(8,128)(2,1)}, bf16[384,128]{1,0:T(8,128)(2,1)S(1)}, u32[]{:S(2)}, u32[]{:S(2)}) collective-permute-start(bf16[384,128]{1,0:T(8,128)(2,1)} %get-tuple-element.10.own), channel_id=1, source_target_pairs={{0,32},{16,48},{32,0},{48,16},{64,96},{80,112},{96,64},{112,80},{1... | collective-permute-start | bytes 294920 | tf_op jit(solution)/shard_map/ppermute | solution.py:156
  19.8 10.0 %all-to-all-start = ((bf16[8,128,128]{2,1,0:T(8,128)(2,1)}), bf16[8,128,128]{2,1,0:T(8,128)(2,1)S(1)}, u32[]{:S(2)}, u32[]{:S(2)}) async-start(bf16[8,128,128]{2,1,0:T(8,128)(2,1)} %get-tuple-element.11), calls=%async_computation | async-start | bytes 524288 | tf_op jit(solution)/shard_map/all_to_all | solution.py:172
  29.9 3.0 %collective-permute-start.3 = (bf16[768,128]{1,0:T(8,128)(2,1)S(1)}, bf16[768,128]{1,0:T(8,128)(2,1)S(1)}, u32[]{:S(2)}, u32[]{:S(2)}) collective-permute-start(bf16[768,128]{1,0:T(8,128)(2,1)S(1)} %constant_dynamic-update-slice_fusion), channel_id=1, source_target_pairs={{0,64},{16,464},{32,96},{48,496},{64,128},{80,16},{96,160},{112,48... | collective-permute-start | bytes 589832 | tf_op jit(solution)/shard_map/ppermute | solution.py:160
  32.9 0.0 collective-permute-done.1
  32.9 3.1 %collective-permute-start.5 = (bf16[768,128]{1,0:T(8,128)(2,1)S(1)}, bf16[768,128]{1,0:T(8,128)(2,1)S(1)}, u32[]{:S(2)}, u32[]{:S(2)}) collective-permute-start(bf16[768,128]{1,0:T(8,128)(2,1)S(1)} %collective-permute-done.1), channel_id=1, source_target_pairs={{16,48},{32,0},{80,112},{96,64},{144,176},{160,128},{208,240},{224... | collective-permute-start | bytes 589832 | tf_op jit(solution)/shard_map/ppermute | solution.py:169
  36.0 0.0 collective-permute-done.2
  36.1 0.5 collective-permute-done.3
  36.6 0.0 collective-permute-done.4
  36.7 5.6 %all-to-all-done.parts_ref = bf16[8,128,128]{2,1,0:T(8,128)(2,1)S(1)} async-done(((bf16[8,128,128]{2,1,0:T(8,128)(2,1)}), bf16[8,128,128]{2,1,0:T(8,128)(2,1)S(1)}, u32[]{:S(2)}, u32[]{:S(2)}) %all-to-all-start) | async-done | bytes 262176 | tf_op jit(solution)/shard_map/all_to_all | solution.py:172
  42.3 0.0 collective-permute-done.5
  42.4 2.4 %collective-permute-start.6 = (bf16[3712,128]{1,0:T(8,128)(2,1)S(1)}, bf16[3712,128]{1,0:T(8,128)(2,1)S(1)}, u32[]{:S(2)}, u32[]{:S(2)}) collective-permute-start(bf16[3712,128]{1,0:T(8,128)(2,1)S(1)} %constant_dynamic-update-slice_fusion.2.ours), channel_id=1, source_target_pairs={{0,16},{16,0},{32,48},{48,32},{64,80},{80,64},{96,112},{112,96},{1... | collective-permute-start | bytes 2850824 | tf_op jit(solution)/shard_map/ppermute | solution.py:156
  44.8 2.1 %collective-permute-done.6.theirs = bf16[3712,128]{1,0:T(8,128)(2,1)S(1)} collective-permute-done((bf16[3712,128]{1,0:T(8,128)(2,1)S(1)}, bf16[3712,128]{1,0:T(8,128)(2,1)S(1)}, u32[]{:S(2)}, u32[]{:S(2)}) %collective-permute-start.6) | collective-permute-done | bytes 950304 | tf_op jit(solution)/shard_map/ppermute | solution.py:156
  46.9 0.0 copy-done
  46.9 0.0 copy-done.1
  46.9 0.0 copy-done.2
  46.9 0.0 copy-done.3
  46.9 3.1 %tiles.1 = (bf16[16,384,128]{2,1,0:T(8,128)(2,1)}, f32[128,128]{1,0:T(8,128)S(1)}) custom-call(s32[1,32]{1,0:T(1,128)S(1)} %copy-done.2, s32[1,32]{1,0:T(1,128)S(1)} %copy-done.3, bf16[32,128,128]{2,1,0:T(8,128)(2,1)S(1)} %copy-done, bf16[384,128]{1,0:T(8,128)(2,1)S(1)} %copy-done.1, bf16[384,128]{1,0:T(8,128)(2,1)S(1)} %collective-permute-done.beside, ...), custom_call_target="tpu_custom_call" | custom-call | flops 134217728 | bytes 6291456 | tf_op jit(solution)/shard_map/tiles/pallas_call | solution.py:188
  50.0 8.9 %all-to-all-start.1 = ((bf16[16,384,128]{2,1,0:T(8,128)(2,1)}), bf16[16,384,128]{2,1,0:T(8,128)(2,1)S(1)}, u32[]{:S(2)}, u32[]{:S(2)}) async-start(bf16[16,384,128]{2,1,0:T(8,128)(2,1)} %get-tuple-element.12), calls=%async_computation.1 | async-start | bytes 3145728 | tf_op jit(solution)/shard_map/all_to_all | solution.py:206
  59.0 2.3 %collective-permute-start.7 = (f32[128,128]{1,0:T(8,128)S(1)}, f32[128,128]{1,0:T(8,128)S(1)}, u32[]{:S(2)}, u32[]{:S(2)}) collective-permute-start(f32[128,128]{1,0:T(8,128)S(1)} %get-tuple-element.13), channel_id=1, source_target_pairs={{0,64},{16,80},{32,96},{48,112},{64,0},{80,16},{96,32},{112,48},{1... | collective-permute-start | bytes 196616 | tf_op jit(solution)/shard_map/ppermute | solution.py:183
  61.3 2.7 %collective-permute-done.7 = f32[128,128]{1,0:T(8,128)S(1)} collective-permute-done((f32[128,128]{1,0:T(8,128)S(1)}, f32[128,128]{1,0:T(8,128)S(1)}, u32[]{:S(2)}, u32[]{:S(2)}) %collective-permute-start.7) | collective-permute-done | bytes 65568 | tf_op jit(solution)/shard_map/ppermute | solution.py:183
  64.0 2.4 %collective-permute-start.8 = (f32[128,128]{1,0:T(8,128)S(1)}, f32[128,128]{1,0:T(8,128)S(1)}, u32[]{:S(2)}, u32[]{:S(2)}) collective-permute-start(f32[128,128]{1,0:T(8,128)S(1)} %add.15), channel_id=1, source_target_pairs={{0,128},{16,144},{32,160},{48,176},{64,192},{80,208},{96,224},{112... | collective-permute-start | bytes 196616 | tf_op jit(solution)/shard_map/ppermute | solution.py:183
  66.4 4.5 %collective-permute-done.8 = f32[128,128]{1,0:T(8,128)S(1)} collective-permute-done((f32[128,128]{1,0:T(8,128)S(1)}, f32[128,128]{1,0:T(8,128)S(1)}, u32[]{:S(2)}, u32[]{:S(2)}) %collective-permute-start.8) | collective-permute-done | bytes 65568 | tf_op jit(solution)/shard_map/ppermute | solution.py:183
  70.9 1.9 %collective-permute-start.9 = (f32[128,128]{1,0:T(8,128)S(1)}, f32[128,128]{1,0:T(8,128)S(1)}, u32[]{:S(2)}, u32[]{:S(2)}) collective-permute-start(f32[128,128]{1,0:T(8,128)S(1)} %add.16), channel_id=1, source_target_pairs={{0,256},{16,272},{32,288},{48,304},{64,320},{80,336},{96,352},{112... | collective-permute-start | bytes 196616 | tf_op jit(solution)/shard_map/ppermute | solution.py:183
  72.8 7.3 %collective-permute-done.9 = f32[128,128]{1,0:T(8,128)S(1)} collective-permute-done((f32[128,128]{1,0:T(8,128)S(1)}, f32[128,128]{1,0:T(8,128)S(1)}, u32[]{:S(2)}, u32[]{:S(2)}) %collective-permute-start.9) | collective-permute-done | bytes 65568 | tf_op jit(solution)/shard_map/ppermute | solution.py:183
  80.1 1.9 %collective-permute-start.10 = (f32[128,128]{1,0:T(8,128)S(1)}, f32[128,128]{1,0:T(8,128)S(1)}, u32[]{:S(2)}, u32[]{:S(2)}) collective-permute-start(f32[128,128]{1,0:T(8,128)S(1)} %add.17), channel_id=1, source_target_pairs={{0,32},{16,48},{32,0},{48,16},{64,96},{80,112},{96,64},{112,80},{1... | collective-permute-start | bytes 196616 | tf_op jit(solution)/shard_map/ppermute | solution.py:183
  82.1 3.9 %collective-permute-done.10 = f32[128,128]{1,0:T(8,128)S(1)} collective-permute-done((f32[128,128]{1,0:T(8,128)S(1)}, f32[128,128]{1,0:T(8,128)S(1)}, u32[]{:S(2)}, u32[]{:S(2)}) %collective-permute-start.10) | collective-permute-done | bytes 65568 | tf_op jit(solution)/shard_map/ppermute | solution.py:183
  86.0 4.9 %collective-permute-start.11 = (f32[128,128]{1,0:T(8,128)S(1)}, f32[128,128]{1,0:T(8,128)S(1)}, u32[]{:S(2)}, u32[]{:S(2)}) collective-permute-start(f32[128,128]{1,0:T(8,128)S(1)} %add.18), channel_id=1, source_target_pairs={{0,8},{1,9},{2,10},{3,11},{4,12},{5,13},{6,14},{7,15},{8,0},{9,1},... | collective-permute-start | bytes 196616 | tf_op jit(solution)/shard_map/ppermute | solution.py:183
  90.9 2.5 %collective-permute-done.11 = f32[128,128]{1,0:T(8,128)S(1)} collective-permute-done((f32[128,128]{1,0:T(8,128)S(1)}, f32[128,128]{1,0:T(8,128)S(1)}, u32[]{:S(2)}, u32[]{:S(2)}) %collective-permute-start.11) | collective-permute-done | bytes 65568 | tf_op jit(solution)/shard_map/ppermute | solution.py:183
  93.4 3.7 %all-to-all-done.1.got_ref = bf16[16,384,128]{2,1,0:T(8,128)(2,1)S(1)} async-done(((bf16[16,384,128]{2,1,0:T(8,128)(2,1)}), bf16[16,384,128]{2,1,0:T(8,128)(2,1)S(1)}, u32[]{:S(2)}, u32[]{:S(2)}) %all-to-all-start.1) | async-done | bytes 1572896 | tf_op jit(solution)/shard_map/all_to_all | solution.py:206
  97.0 0.9 finish.1
  (13 shorter events, 0.2 us)
Async XLA Ops:
  3.1 43.8 %copy-start = (bf16[32,128,128]{2,1,0:T(8,128)(2,1)S(1)}, bf16[32,128,128]{2,1,0:T(8,128)(2,1)}, u32[]{:S(2)}) copy-start(bf16[32,128,128]{2,1,0:T(8,128)(2,1)} %tiles_ref.1) | copy-start | bytes 3145732
  3.1 43.7 %copy-start.1 = (bf16[384,128]{1,0:T(8,128)(2,1)S(1)}, bf16[384,128]{1,0:T(8,128)(2,1)}, u32[]{:S(2)}) copy-start(bf16[384,128]{1,0:T(8,128)(2,1)} %get-tuple-element.10.own) | copy-start | bytes 294916
  3.1 43.7 %copy-start.2 = (s32[1,32]{1,0:T(1,128)S(1)}, s32[1,32]{1,0:T(1,128)}, u32[]{:S(2)}) copy-start(s32[1,32]{1,0:T(1,128)} %get-tuple-element.8.from_ref) | copy-start | bytes 388
  3.2 43.7 %copy-start.3 = (s32[1,32]{1,0:T(1,128)S(1)}, s32[1,32]{1,0:T(1,128)}, u32[]{:S(2)}) copy-start(s32[1,32]{1,0:T(1,128)} %get-tuple-element.9.to_ref) | copy-start | bytes 388
  3.2 10.1 %collective-permute-start = (bf16[384,128]{1,0:T(8,128)(2,1)}, bf16[384,128]{1,0:T(8,128)(2,1)S(1)}, u32[]{:S(2)}, u32[]{:S(2)}) collective-permute-start(bf16[384,128]{1,0:T(8,128)(2,1)} %get-tuple-element.10.own), channel_id=1, source_target_pairs={{0,16},{16,0},{32,48},{48,32},{64,80},{80,64},{96,112},{112,96},{1... | collective-permute-start | bytes 294920 | tf_op jit(solution)/shard_map/ppermute | solution.py:156
  13.2 19.6 %collective-permute-start.1 = (bf16[768,128]{1,0:T(8,128)(2,1)S(1)}, bf16[768,128]{1,0:T(8,128)(2,1)S(1)}, u32[]{:S(2)}, u32[]{:S(2)}) collective-permute-start(bf16[768,128]{1,0:T(8,128)(2,1)S(1)} %constant_dynamic-update-slice_fusion), channel_id=1, source_target_pairs={{0,128},{16,400},{32,160},{48,432},{64,192},{80,464},{96,224},{112... | collective-permute-start | bytes 589832 | tf_op jit(solution)/shard_map/ppermute | solution.py:160
  15.2 20.9 %collective-permute-start.2 = (bf16[768,128]{1,0:T(8,128)(2,1)S(1)}, bf16[768,128]{1,0:T(8,128)(2,1)S(1)}, u32[]{:S(2)}, u32[]{:S(2)}) collective-permute-start(bf16[768,128]{1,0:T(8,128)(2,1)S(1)} %constant_dynamic-update-slice_fusion), channel_id=1, source_target_pairs={{0,96},{16,496},{32,64},{48,464},{64,160},{80,48},{96,128},{112,16... | collective-permute-start | bytes 589832 | tf_op jit(solution)/shard_map/ppermute | solution.py:160
  17.7 18.9 %collective-permute-start.4 = (bf16[384,128]{1,0:T(8,128)(2,1)}, bf16[384,128]{1,0:T(8,128)(2,1)S(1)}, u32[]{:S(2)}, u32[]{:S(2)}) collective-permute-start(bf16[384,128]{1,0:T(8,128)(2,1)} %get-tuple-element.10.own), channel_id=1, source_target_pairs={{0,32},{16,48},{32,0},{48,16},{64,96},{80,112},{96,64},{112,80},{1... | collective-permute-start | bytes 294920 | tf_op jit(solution)/shard_map/ppermute | solution.py:156
  19.8 22.4 %all-to-all-start = ((bf16[8,128,128]{2,1,0:T(8,128)(2,1)}), bf16[8,128,128]{2,1,0:T(8,128)(2,1)S(1)}, u32[]{:S(2)}, u32[]{:S(2)}) async-start(bf16[8,128,128]{2,1,0:T(8,128)(2,1)} %get-tuple-element.11), calls=%async_computation | async-start | bytes 524288 | tf_op jit(solution)/shard_map/all_to_all | solution.py:172
  29.9 6.7 %collective-permute-start.3 = (bf16[768,128]{1,0:T(8,128)(2,1)S(1)}, bf16[768,128]{1,0:T(8,128)(2,1)S(1)}, u32[]{:S(2)}, u32[]{:S(2)}) collective-permute-start(bf16[768,128]{1,0:T(8,128)(2,1)S(1)} %constant_dynamic-update-slice_fusion), channel_id=1, source_target_pairs={{0,64},{16,464},{32,96},{48,496},{64,128},{80,16},{96,160},{112,48... | collective-permute-start | bytes 589832 | tf_op jit(solution)/shard_map/ppermute | solution.py:160
  32.9 9.5 %collective-permute-start.5 = (bf16[768,128]{1,0:T(8,128)(2,1)S(1)}, bf16[768,128]{1,0:T(8,128)(2,1)S(1)}, u32[]{:S(2)}, u32[]{:S(2)}) collective-permute-start(bf16[768,128]{1,0:T(8,128)(2,1)S(1)} %collective-permute-done.1), channel_id=1, source_target_pairs={{16,48},{32,0},{80,112},{96,64},{144,176},{160,128},{208,240},{224... | collective-permute-start | bytes 589832 | tf_op jit(solution)/shard_map/ppermute | solution.py:169
  42.4 4.5 %collective-permute-start.6 = (bf16[3712,128]{1,0:T(8,128)(2,1)S(1)}, bf16[3712,128]{1,0:T(8,128)(2,1)S(1)}, u32[]{:S(2)}, u32[]{:S(2)}) collective-permute-start(bf16[3712,128]{1,0:T(8,128)(2,1)S(1)} %constant_dynamic-update-slice_fusion.2.ours), channel_id=1, source_target_pairs={{0,16},{16,0},{32,48},{48,32},{64,80},{80,64},{96,112},{112,96},{1... | collective-permute-start | bytes 2850824 | tf_op jit(solution)/shard_map/ppermute | solution.py:156
  50.0 47.0 %all-to-all-start.1 = ((bf16[16,384,128]{2,1,0:T(8,128)(2,1)}), bf16[16,384,128]{2,1,0:T(8,128)(2,1)S(1)}, u32[]{:S(2)}, u32[]{:S(2)}) async-start(bf16[16,384,128]{2,1,0:T(8,128)(2,1)} %get-tuple-element.12), calls=%async_computation.1 | async-start | bytes 3145728 | tf_op jit(solution)/shard_map/all_to_all | solution.py:206
  59.0 5.0 %collective-permute-start.7 = (f32[128,128]{1,0:T(8,128)S(1)}, f32[128,128]{1,0:T(8,128)S(1)}, u32[]{:S(2)}, u32[]{:S(2)}) collective-permute-start(f32[128,128]{1,0:T(8,128)S(1)} %get-tuple-element.13), channel_id=1, source_target_pairs={{0,64},{16,80},{32,96},{48,112},{64,0},{80,16},{96,32},{112,48},{1... | collective-permute-start | bytes 196616 | tf_op jit(solution)/shard_map/ppermute | solution.py:183
  64.0 6.9 %collective-permute-start.8 = (f32[128,128]{1,0:T(8,128)S(1)}, f32[128,128]{1,0:T(8,128)S(1)}, u32[]{:S(2)}, u32[]{:S(2)}) collective-permute-start(f32[128,128]{1,0:T(8,128)S(1)} %add.15), channel_id=1, source_target_pairs={{0,128},{16,144},{32,160},{48,176},{64,192},{80,208},{96,224},{112... | collective-permute-start | bytes 196616 | tf_op jit(solution)/shard_map/ppermute | solution.py:183
  70.9 9.2 %collective-permute-start.9 = (f32[128,128]{1,0:T(8,128)S(1)}, f32[128,128]{1,0:T(8,128)S(1)}, u32[]{:S(2)}, u32[]{:S(2)}) collective-permute-start(f32[128,128]{1,0:T(8,128)S(1)} %add.16), channel_id=1, source_target_pairs={{0,256},{16,272},{32,288},{48,304},{64,320},{80,336},{96,352},{112... | collective-permute-start | bytes 196616 | tf_op jit(solution)/shard_map/ppermute | solution.py:183
  80.1 5.8 %collective-permute-start.10 = (f32[128,128]{1,0:T(8,128)S(1)}, f32[128,128]{1,0:T(8,128)S(1)}, u32[]{:S(2)}, u32[]{:S(2)}) collective-permute-start(f32[128,128]{1,0:T(8,128)S(1)} %add.17), channel_id=1, source_target_pairs={{0,32},{16,48},{32,0},{48,16},{64,96},{80,112},{96,64},{112,80},{1... | collective-permute-start | bytes 196616 | tf_op jit(solution)/shard_map/ppermute | solution.py:183
  86.0 7.4 %collective-permute-start.11 = (f32[128,128]{1,0:T(8,128)S(1)}, f32[128,128]{1,0:T(8,128)S(1)}, u32[]{:S(2)}, u32[]{:S(2)}) collective-permute-start(f32[128,128]{1,0:T(8,128)S(1)} %add.18), channel_id=1, source_target_pairs={{0,8},{1,9},{2,10},{3,11},{4,12},{5,13},{6,14},{7,15},{8,0},{9,1},... | collective-permute-start | bytes 196616 | tf_op jit(solution)/shard_map/ppermute | solution.py:183

commit v14 on v13

--- a/solution.py
+++ b/solution.py
@@ -27,8 +27,8 @@
     below = gap > planes // 2
     steps = jnp.where(below, planes - gap, gap)
     receiver = jnp.where(gap == 0, core, jnp.where(below, 0, 1))
-    first = jnp.where(steps == 2, jnp.where(same_chip, 0, 7), jnp.where(same_chip, 4, 2))
-    place = jnp.where(gap == 0, 6, first + jnp.where(core == receiver, 0, 1))
+    first = jnp.where(steps == 2, jnp.where(same_chip, 0, 6), jnp.where(same_chip, 2, 4))
+    place = jnp.where(gap == 0, 8, first + jnp.where(core == receiver, 0, 1))
     slot = 2 + place + jnp.where(receiver == lax.rem(row, 2), 0, 9)
     slot = jnp.where((gap == 0) & same_chip, jnp.where(same_core, 0, 1), slot)
     return slot * blocks + lax.rem(block, blocks)
@@ -182,7 +182,7 @@
     def partner(value, axis, bit):
         return lax.ppermute(value, axis, [(i, i ^ bit) for i in range(lax.axis_size(axis))])
 
-    received = jnp.concatenate([far, across_near, near, across, across_far, halves])
+    received = jnp.concatenate([far, near, across_near, across_far, across, halves])
     other = swap(received, 1)
 
     sends, wsum = pl.pallas_call(

time: 98.7 us -> 98.9 us (level)
  starting transfers between devices: 56.4 us -> 61.4 us
  waiting for transfers between devices: 33 us -> 28 us
    all_to_all x1, waiting for transfers between devices: 5.63 us -> 0.01 us  [on_device(): wz = lax.all_to_all(wpart, 'col', 0, 0, axis_index_groups=groups)]
    ppermute x3, starting transfers between devices: 13.4 us -> 16.4 us  [swap(): return lax.ppermute(value, 'row', [(i, i ^ bit) for i in range(row_count)])]
    ppermute x5, starting transfers between devices: 13.5 us -> 15.9 us  [partner(): lax.ppermute(value, axis, [(i, i ^ bit) for i in range(lax.axis_size(axis...]
    ppermute x1, waiting for transfers between devices: 0.01 us -> 2.07 us  [on_device(): across_far = lax.ppermute(far, 'row', wanted)]
    ppermute x5, waiting for transfers between devices: 20.8 us -> 18.8 us  [partner(): lax.ppermute(value, axis, [(i, i ^ bit) for i in range(lax.axis_size(axis...]
    all_to_all x1, starting transfers between devices: 10 us -> 8.64 us  [on_device(): wz = lax.all_to_all(wpart, 'col', 0, 0, axis_index_groups=groups)]
    ppermute x3, waiting for transfers between devices: 0.52 us -> 1.54 us  [to_plane(): return lax.ppermute(value, 'row', pairs)]
where the time goes in v14:
time: 98.9 us; the launch traced here: 97.9 us
  starting transfers between devices  61.4 us (62%)
  waiting for transfers between devices  28 us (28%)
  Pallas kernels  6.53 us (7%)
  local copies, waits for them, and re-layouts  1.06 us (1%)
    ppermute x5, waiting for transfers between devices, partner(): lax.ppermute(value, axis, [(i, i ^ bit) for i in range(lax.axis_size(axis...  18.8 us
    ppermute x3, starting transfers between devices, swap(): return lax.ppermute(value, 'row', [(i, i ^ bit) for i in range(row_count)])  16.4 us
    ppermute x5, starting transfers between devices, partner(): lax.ppermute(value, axis, [(i, i ^ bit) for i in range(lax.axis_size(axis...  15.9 us
    all_to_all x1, starting transfers between devices, on_device(): got = lax.all_to_all(sends, 'col', 0, 0)  9.5 us
    all_to_all x1, starting transfers between devices, on_device(): wz = lax.all_to_all(wpart, 'col', 0, 0, axis_index_groups=groups)  8.64 us
    ppermute x3, starting transfers between devices, to_plane(): return lax.ppermute(value, 'row', pairs)  7.83 us
    all_to_all x1, waiting for transfers between devices, on_device(): got = lax.all_to_all(sends, 'col', 0, 0)  3.25 us
    pallas_call x1, Pallas kernels, on_device(): pl.pallas_call(tile_kernel, out_shape=(jax.ShapeDtypeStruct((col_count, n...  3.14 us
  transfers between devices with their start and end apart: 14, of which 10 were waited for; matrix products, arithmetic and copies ran while one was open for 1% of the time, Pallas kernels for 0%

profile of v14, /device:TPU:1, one launch (start us, length us, event | category | flops | bytes accessed | tf_op | source)
XLA Modules:
  0.0 97.9 jit_solution(7238805925849473307)
XLA Ops:
  0.6 2.5 %adjoint.1 = (bf16[384,128]{1,0:T(8,128)(2,1)}, bf16[8,128,128]{2,1,0:T(8,128)(2,1)}, s32[1,32]{1,0:T(1,128)}, s32[1,32]{1,0:T(1,128)}) custom-call(s32[3,128]{1,0:T(4,128)} %bitcast.3, bf16[384,128]{1,0:T(8,128)(2,1)} %cot_in.1, bf16[384,128]{1,0:T(8,128)(2,1)} %pre_in.1, bf16[384,128]{1,0:T(8,128)(2,1)} %agg_in.1, bf16[128,128]{1,0:T(8,128)(2,1)} %w_in.1, ...), custom_call_target="tpu_custom_call" | custom-call | tf_op jit(solution)/shard_map/adjoint/pallas_call | solution.py:136
  3.1 0.0 copy-start
  3.1 0.0 copy-start.1
  3.1 0.0 copy-start.2
  3.2 0.0 copy-start.3
  3.2 8.9 %collective-permute-start = (bf16[384,128]{1,0:T(8,128)(2,1)}, bf16[384,128]{1,0:T(8,128)(2,1)S(1)}, u32[]{:S(2)}, u32[]{:S(2)}) collective-permute-start(bf16[384,128]{1,0:T(8,128)(2,1)} %get-tuple-element.10.own), channel_id=1, source_target_pairs={{0,16},{16,0},{32,48},{48,32},{64,80},{80,64},{96,112},{112,96},{1... | collective-permute-start | bytes 294920 | tf_op jit(solution)/shard_map/ppermute | solution.py:156
  12.1 0.9 constant_dynamic-update-slice_fusion.1
  13.0 0.2 collective-permute-done.beside
  13.2 1.9 %collective-permute-start.1 = (bf16[768,128]{1,0:T(8,128)(2,1)S(1)}, bf16[768,128]{1,0:T(8,128)(2,1)S(1)}, u32[]{:S(2)}, u32[]{:S(2)}) collective-permute-start(bf16[768,128]{1,0:T(8,128)(2,1)S(1)} %constant_dynamic-update-slice_fusion), channel_id=1, source_target_pairs={{0,128},{16,400},{32,160},{48,432},{64,192},{80,464},{96,224},{112... | collective-permute-start | bytes 589832 | tf_op jit(solution)/shard_map/ppermute | solution.py:160
  15.2 8.6 %all-to-all-start = ((bf16[8,128,128]{2,1,0:T(8,128)(2,1)}), bf16[8,128,128]{2,1,0:T(8,128)(2,1)S(1)}, u32[]{:S(2)}, u32[]{:S(2)}) async-start(bf16[8,128,128]{2,1,0:T(8,128)(2,1)} %get-tuple-element.11), calls=%async_computation | async-start | bytes 524288 | tf_op jit(solution)/shard_map/all_to_all | solution.py:172
  23.8 3.0 %collective-permute-start.2 = (bf16[768,128]{1,0:T(8,128)(2,1)S(1)}, bf16[768,128]{1,0:T(8,128)(2,1)S(1)}, u32[]{:S(2)}, u32[]{:S(2)}) collective-permute-start(bf16[768,128]{1,0:T(8,128)(2,1)S(1)} %constant_dynamic-update-slice_fusion), channel_id=1, source_target_pairs={{0,64},{16,464},{32,96},{48,496},{64,128},{80,16},{96,160},{112,48... | collective-permute-start | bytes 589832 | tf_op jit(solution)/shard_map/ppermute | solution.py:160
  26.8 3.1 %collective-permute-start.5 = (bf16[384,128]{1,0:T(8,128)(2,1)}, bf16[384,128]{1,0:T(8,128)(2,1)S(1)}, u32[]{:S(2)}, u32[]{:S(2)}) collective-permute-start(bf16[384,128]{1,0:T(8,128)(2,1)} %get-tuple-element.10.own), channel_id=1, source_target_pairs={{0,32},{16,48},{32,0},{48,16},{64,96},{80,112},{96,64},{112,80},{1... | collective-permute-start | bytes 294920 | tf_op jit(solution)/shard_map/ppermute | solution.py:156
  29.9 2.9 %collective-permute-start.3 = (bf16[768,128]{1,0:T(8,128)(2,1)S(1)}, bf16[768,128]{1,0:T(8,128)(2,1)S(1)}, u32[]{:S(2)}, u32[]{:S(2)}) collective-permute-start(bf16[768,128]{1,0:T(8,128)(2,1)S(1)} %constant_dynamic-update-slice_fusion), channel_id=1, source_target_pairs={{0,96},{16,496},{32,64},{48,464},{64,160},{80,48},{96,128},{112,16... | collective-permute-start | bytes 589832 | tf_op jit(solution)/shard_map/ppermute | solution.py:160
  32.9 0.0 collective-permute-done.1
  32.9 3.1 %collective-permute-start.4 = (bf16[768,128]{1,0:T(8,128)(2,1)S(1)}, bf16[768,128]{1,0:T(8,128)(2,1)S(1)}, u32[]{:S(2)}, u32[]{:S(2)}) collective-permute-start(bf16[768,128]{1,0:T(8,128)(2,1)S(1)} %collective-permute-done.1), channel_id=1, source_target_pairs={{16,48},{32,0},{80,112},{96,64},{144,176},{160,128},{208,240},{224... | collective-permute-start | bytes 589832 | tf_op jit(solution)/shard_map/ppermute | solution.py:169
  36.0 0.0 collective-permute-done.2
  36.1 1.5 %collective-permute-done.3 = bf16[768,128]{1,0:T(8,128)(2,1)S(1)} collective-permute-done((bf16[768,128]{1,0:T(8,128)(2,1)S(1)}, bf16[768,128]{1,0:T(8,128)(2,1)S(1)}, u32[]{:S(2)}, u32[]{:S(2)}) %collective-permute-start.3) | collective-permute-done | bytes 196640 | tf_op jit(solution)/shard_map/ppermute | solution.py:160
  37.6 0.0 all-to-all-done.parts_ref
  37.7 2.1 %collective-permute-done.4 = bf16[768,128]{1,0:T(8,128)(2,1)S(1)} collective-permute-done((bf16[768,128]{1,0:T(8,128)(2,1)S(1)}, bf16[768,128]{1,0:T(8,128)(2,1)S(1)}, u32[]{:S(2)}, u32[]{:S(2)}) %collective-permute-start.4) | collective-permute-done | bytes 196640 | tf_op jit(solution)/shard_map/ppermute | solution.py:169
  39.8 0.0 collective-permute-done.5
  39.9 4.3 %collective-permute-start.6 = (bf16[3712,128]{1,0:T(8,128)(2,1)S(1)}, bf16[3712,128]{1,0:T(8,128)(2,1)S(1)}, u32[]{:S(2)}, u32[]{:S(2)}) collective-permute-start(bf16[3712,128]{1,0:T(8,128)(2,1)S(1)} %constant_dynamic-update-slice_fusion.2.ours), channel_id=1, source_target_pairs={{0,16},{16,0},{32,48},{48,32},{64,80},{80,64},{96,112},{112,96},{1... | collective-permute-start | bytes 2850824 | tf_op jit(solution)/shard_map/ppermute | solution.py:156
  44.2 2.1 %collective-permute-done.6.theirs = bf16[3712,128]{1,0:T(8,128)(2,1)S(1)} collective-permute-done((bf16[3712,128]{1,0:T(8,128)(2,1)S(1)}, bf16[3712,128]{1,0:T(8,128)(2,1)S(1)}, u32[]{:S(2)}, u32[]{:S(2)}) %collective-permute-start.6) | collective-permute-done | bytes 950304 | tf_op jit(solution)/shard_map/ppermute | solution.py:156
  46.3 0.0 copy-done
  46.3 0.0 copy-done.1
  46.3 0.0 copy-done.2
  46.3 0.0 copy-done.3
  46.3 3.1 %tiles.1 = (bf16[16,384,128]{2,1,0:T(8,128)(2,1)}, f32[128,128]{1,0:T(8,128)S(1)}) custom-call(s32[1,32]{1,0:T(1,128)S(1)} %copy-done.2, s32[1,32]{1,0:T(1,128)S(1)} %copy-done.3, bf16[32,128,128]{2,1,0:T(8,128)(2,1)S(1)} %copy-done, bf16[384,128]{1,0:T(8,128)(2,1)S(1)} %copy-done.1, bf16[384,128]{1,0:T(8,128)(2,1)S(1)} %collective-permute-done.beside, ...), custom_call_target="tpu_custom_call" | custom-call | flops 134217728 | bytes 6291456 | tf_op jit(solution)/shard_map/tiles/pallas_call | solution.py:188
  49.5 9.5 %all-to-all-start.1 = ((bf16[16,384,128]{2,1,0:T(8,128)(2,1)}), bf16[16,384,128]{2,1,0:T(8,128)(2,1)S(1)}, u32[]{:S(2)}, u32[]{:S(2)}) async-start(bf16[16,384,128]{2,1,0:T(8,128)(2,1)} %get-tuple-element.12), calls=%async_computation.1 | async-start | bytes 3145728 | tf_op jit(solution)/shard_map/all_to_all | solution.py:206
  59.0 2.5 %collective-permute-start.7 = (f32[128,128]{1,0:T(8,128)S(1)}, f32[128,128]{1,0:T(8,128)S(1)}, u32[]{:S(2)}, u32[]{:S(2)}) collective-permute-start(f32[128,128]{1,0:T(8,128)S(1)} %get-tuple-element.13), channel_id=1, source_target_pairs={{0,64},{16,80},{32,96},{48,112},{64,0},{80,16},{96,32},{112,48},{1... | collective-permute-start | bytes 196616 | tf_op jit(solution)/shard_map/ppermute | solution.py:183
  61.4 2.6 %collective-permute-done.7 = f32[128,128]{1,0:T(8,128)S(1)} collective-permute-done((f32[128,128]{1,0:T(8,128)S(1)}, f32[128,128]{1,0:T(8,128)S(1)}, u32[]{:S(2)}, u32[]{:S(2)}) %collective-permute-start.7) | collective-permute-done | bytes 65568 | tf_op jit(solution)/shard_map/ppermute | solution.py:183
  64.0 2.6 %collective-permute-start.8 = (f32[128,128]{1,0:T(8,128)S(1)}, f32[128,128]{1,0:T(8,128)S(1)}, u32[]{:S(2)}, u32[]{:S(2)}) collective-permute-start(f32[128,128]{1,0:T(8,128)S(1)} %add.15), channel_id=1, source_target_pairs={{0,128},{16,144},{32,160},{48,176},{64,192},{80,208},{96,224},{112... | collective-permute-start | bytes 196616 | tf_op jit(solution)/shard_map/ppermute | solution.py:183
  66.6 4.3 %collective-permute-done.8 = f32[128,128]{1,0:T(8,128)S(1)} collective-permute-done((f32[128,128]{1,0:T(8,128)S(1)}, f32[128,128]{1,0:T(8,128)S(1)}, u32[]{:S(2)}, u32[]{:S(2)}) %collective-permute-start.8) | collective-permute-done | bytes 65568 | tf_op jit(solution)/shard_map/ppermute | solution.py:183
  70.9 4.0 %collective-permute-start.9 = (f32[128,128]{1,0:T(8,128)S(1)}, f32[128,128]{1,0:T(8,128)S(1)}, u32[]{:S(2)}, u32[]{:S(2)}) collective-permute-start(f32[128,128]{1,0:T(8,128)S(1)} %add.16), channel_id=1, source_target_pairs={{0,256},{16,272},{32,288},{48,304},{64,320},{80,336},{96,352},{112... | collective-permute-start | bytes 196616 | tf_op jit(solution)/shard_map/ppermute | solution.py:183
  74.9 5.9 %collective-permute-done.9 = f32[128,128]{1,0:T(8,128)S(1)} collective-permute-done((f32[128,128]{1,0:T(8,128)S(1)}, f32[128,128]{1,0:T(8,128)S(1)}, u32[]{:S(2)}, u32[]{:S(2)}) %collective-permute-start.9) | collective-permute-done | bytes 65568 | tf_op jit(solution)/shard_map/ppermute | solution.py:183
  80.9 1.9 %collective-permute-start.10 = (f32[128,128]{1,0:T(8,128)S(1)}, f32[128,128]{1,0:T(8,128)S(1)}, u32[]{:S(2)}, u32[]{:S(2)}) collective-permute-start(f32[128,128]{1,0:T(8,128)S(1)} %add.17), channel_id=1, source_target_pairs={{0,32},{16,48},{32,0},{48,16},{64,96},{80,112},{96,64},{112,80},{1... | collective-permute-start | bytes 196616 | tf_op jit(solution)/shard_map/ppermute | solution.py:183
  82.8 3.9 %collective-permute-done.10 = f32[128,128]{1,0:T(8,128)S(1)} collective-permute-done((f32[128,128]{1,0:T(8,128)S(1)}, f32[128,128]{1,0:T(8,128)S(1)}, u32[]{:S(2)}, u32[]{:S(2)}) %collective-permute-start.10) | collective-permute-done | bytes 65568 | tf_op jit(solution)/shard_map/ppermute | solution.py:183
  86.7 5.0 %collective-permute-start.11 = (f32[128,128]{1,0:T(8,128)S(1)}, f32[128,128]{1,0:T(8,128)S(1)}, u32[]{:S(2)}, u32[]{:S(2)}) collective-permute-start(f32[128,128]{1,0:T(8,128)S(1)} %add.18), channel_id=1, source_target_pairs={{0,8},{1,9},{2,10},{3,11},{4,12},{5,13},{6,14},{7,15},{8,0},{9,1},... | collective-permute-start | bytes 196616 | tf_op jit(solution)/shard_map/ppermute | solution.py:183
  91.6 2.1 %collective-permute-done.11 = f32[128,128]{1,0:T(8,128)S(1)} collective-permute-done((f32[128,128]{1,0:T(8,128)S(1)}, f32[128,128]{1,0:T(8,128)S(1)}, u32[]{:S(2)}, u32[]{:S(2)}) %collective-permute-start.11) | collective-permute-done | bytes 65568 | tf_op jit(solution)/shard_map/ppermute | solution.py:183
  93.8 3.3 %all-to-all-done.1.got_ref = bf16[16,384,128]{2,1,0:T(8,128)(2,1)S(1)} async-done(((bf16[16,384,128]{2,1,0:T(8,128)(2,1)}), bf16[16,384,128]{2,1,0:T(8,128)(2,1)S(1)}, u32[]{:S(2)}, u32[]{:S(2)}) %all-to-all-start.1) | async-done | bytes 1572896 | tf_op jit(solution)/shard_map/all_to_all | solution.py:206
  97.0 0.9 finish.1
  (13 shorter events, 0.2 us)
Async XLA Ops:
  3.1 43.2 %copy-start = (bf16[32,128,128]{2,1,0:T(8,128)(2,1)S(1)}, bf16[32,128,128]{2,1,0:T(8,128)(2,1)}, u32[]{:S(2)}) copy-start(bf16[32,128,128]{2,1,0:T(8,128)(2,1)} %tiles_ref.1) | copy-start | bytes 3145732
  3.1 43.2 %copy-start.1 = (bf16[384,128]{1,0:T(8,128)(2,1)S(1)}, bf16[384,128]{1,0:T(8,128)(2,1)}, u32[]{:S(2)}) copy-start(bf16[384,128]{1,0:T(8,128)(2,1)} %get-tuple-element.10.own) | copy-start | bytes 294916
  3.1 43.2 %copy-start.2 = (s32[1,32]{1,0:T(1,128)S(1)}, s32[1,32]{1,0:T(1,128)}, u32[]{:S(2)}) copy-start(s32[1,32]{1,0:T(1,128)} %get-tuple-element.8.from_ref) | copy-start | bytes 388
  3.2 43.2 %copy-start.3 = (s32[1,32]{1,0:T(1,128)S(1)}, s32[1,32]{1,0:T(1,128)}, u32[]{:S(2)}) copy-start(s32[1,32]{1,0:T(1,128)} %get-tuple-element.9.to_ref) | copy-start | bytes 388
  3.2 10.1 %collective-permute-start = (bf16[384,128]{1,0:T(8,128)(2,1)}, bf16[384,128]{1,0:T(8,128)(2,1)S(1)}, u32[]{:S(2)}, u32[]{:S(2)}) collective-permute-start(bf16[384,128]{1,0:T(8,128)(2,1)} %get-tuple-element.10.own), channel_id=1, source_target_pairs={{0,16},{16,0},{32,48},{48,32},{64,80},{80,64},{96,112},{112,96},{1... | collective-permute-start | bytes 294920 | tf_op jit(solution)/shard_map/ppermute | solution.py:156
  13.2 19.6 %collective-permute-start.1 = (bf16[768,128]{1,0:T(8,128)(2,1)S(1)}, bf16[768,128]{1,0:T(8,128)(2,1)S(1)}, u32[]{:S(2)}, u32[]{:S(2)}) collective-permute-start(bf16[768,128]{1,0:T(8,128)(2,1)S(1)} %constant_dynamic-update-slice_fusion), channel_id=1, source_target_pairs={{0,128},{16,400},{32,160},{48,432},{64,192},{80,464},{96,224},{112... | collective-permute-start | bytes 589832 | tf_op jit(solution)/shard_map/ppermute | solution.py:160
  15.2 22.5 %all-to-all-start = ((bf16[8,128,128]{2,1,0:T(8,128)(2,1)}), bf16[8,128,128]{2,1,0:T(8,128)(2,1)S(1)}, u32[]{:S(2)}, u32[]{:S(2)}) async-start(bf16[8,128,128]{2,1,0:T(8,128)(2,1)} %get-tuple-element.11), calls=%async_computation | async-start | bytes 524288 | tf_op jit(solution)/shard_map/all_to_all | solution.py:172
  23.8 12.2 %collective-permute-start.2 = (bf16[768,128]{1,0:T(8,128)(2,1)S(1)}, bf16[768,128]{1,0:T(8,128)(2,1)S(1)}, u32[]{:S(2)}, u32[]{:S(2)}) collective-permute-start(bf16[768,128]{1,0:T(8,128)(2,1)S(1)} %constant_dynamic-update-slice_fusion), channel_id=1, source_target_pairs={{0,64},{16,464},{32,96},{48,496},{64,128},{80,16},{96,160},{112,48... | collective-permute-start | bytes 589832 | tf_op jit(solution)/shard_map/ppermute | solution.py:160
  26.8 13.0 %collective-permute-start.5 = (bf16[384,128]{1,0:T(8,128)(2,1)}, bf16[384,128]{1,0:T(8,128)(2,1)S(1)}, u32[]{:S(2)}, u32[]{:S(2)}) collective-permute-start(bf16[384,128]{1,0:T(8,128)(2,1)} %get-tuple-element.10.own), channel_id=1, source_target_pairs={{0,32},{16,48},{32,0},{48,16},{64,96},{80,112},{96,64},{112,80},{1... | collective-permute-start | bytes 294920 | tf_op jit(solution)/shard_map/ppermute | solution.py:156
  29.9 7.7 %collective-permute-start.3 = (bf16[768,128]{1,0:T(8,128)(2,1)S(1)}, bf16[768,128]{1,0:T(8,128)(2,1)S(1)}, u32[]{:S(2)}, u32[]{:S(2)}) collective-permute-start(bf16[768,128]{1,0:T(8,128)(2,1)S(1)} %constant_dynamic-update-slice_fusion), channel_id=1, source_target_pairs={{0,96},{16,496},{32,64},{48,464},{64,160},{80,48},{96,128},{112,16... | collective-permute-start | bytes 589832 | tf_op jit(solution)/shard_map/ppermute | solution.py:160
  32.9 6.9 %collective-permute-start.4 = (bf16[768,128]{1,0:T(8,128)(2,1)S(1)}, bf16[768,128]{1,0:T(8,128)(2,1)S(1)}, u32[]{:S(2)}, u32[]{:S(2)}) collective-permute-start(bf16[768,128]{1,0:T(8,128)(2,1)S(1)} %collective-permute-done.1), channel_id=1, source_target_pairs={{16,48},{32,0},{80,112},{96,64},{144,176},{160,128},{208,240},{224... | collective-permute-start | bytes 589832 | tf_op jit(solution)/shard_map/ppermute | solution.py:169
  39.9 6.5 %collective-permute-start.6 = (bf16[3712,128]{1,0:T(8,128)(2,1)S(1)}, bf16[3712,128]{1,0:T(8,128)(2,1)S(1)}, u32[]{:S(2)}, u32[]{:S(2)}) collective-permute-start(bf16[3712,128]{1,0:T(8,128)(2,1)S(1)} %constant_dynamic-update-slice_fusion.2.ours), channel_id=1, source_target_pairs={{0,16},{16,0},{32,48},{48,32},{64,80},{80,64},{96,112},{112,96},{1... | collective-permute-start | bytes 2850824 | tf_op jit(solution)/shard_map/ppermute | solution.py:156
  49.5 47.5 %all-to-all-start.1 = ((bf16[16,384,128]{2,1,0:T(8,128)(2,1)}), bf16[16,384,128]{2,1,0:T(8,128)(2,1)S(1)}, u32[]{:S(2)}, u32[]{:S(2)}) async-start(bf16[16,384,128]{2,1,0:T(8,128)(2,1)} %get-tuple-element.12), calls=%async_computation.1 | async-start | bytes 3145728 | tf_op jit(solution)/shard_map/all_to_all | solution.py:206
  59.0 5.0 %collective-permute-start.7 = (f32[128,128]{1,0:T(8,128)S(1)}, f32[128,128]{1,0:T(8,128)S(1)}, u32[]{:S(2)}, u32[]{:S(2)}) collective-permute-start(f32[128,128]{1,0:T(8,128)S(1)} %get-tuple-element.13), channel_id=1, source_target_pairs={{0,64},{16,80},{32,96},{48,112},{64,0},{80,16},{96,32},{112,48},{1... | collective-permute-start | bytes 196616 | tf_op jit(solution)/shard_map/ppermute | solution.py:183
  64.0 6.9 %collective-permute-start.8 = (f32[128,128]{1,0:T(8,128)S(1)}, f32[128,128]{1,0:T(8,128)S(1)}, u32[]{:S(2)}, u32[]{:S(2)}) collective-permute-start(f32[128,128]{1,0:T(8,128)S(1)} %add.15), channel_id=1, source_target_pairs={{0,128},{16,144},{32,160},{48,176},{64,192},{80,208},{96,224},{112... | collective-permute-start | bytes 196616 | tf_op jit(solution)/shard_map/ppermute | solution.py:183
  70.9 9.9 %collective-permute-start.9 = (f32[128,128]{1,0:T(8,128)S(1)}, f32[128,128]{1,0:T(8,128)S(1)}, u32[]{:S(2)}, u32[]{:S(2)}) collective-permute-start(f32[128,128]{1,0:T(8,128)S(1)} %add.16), channel_id=1, source_target_pairs={{0,256},{16,272},{32,288},{48,304},{64,320},{80,336},{96,352},{112... | collective-permute-start | bytes 196616 | tf_op jit(solution)/shard_map/ppermute | solution.py:183
  80.9 5.8 %collective-permute-start.10 = (f32[128,128]{1,0:T(8,128)S(1)}, f32[128,128]{1,0:T(8,128)S(1)}, u32[]{:S(2)}, u32[]{:S(2)}) collective-permute-start(f32[128,128]{1,0:T(8,128)S(1)} %add.17), channel_id=1, source_target_pairs={{0,32},{16,48},{32,0},{48,16},{64,96},{80,112},{96,64},{112,80},{1... | collective-permute-start | bytes 196616 | tf_op jit(solution)/shard_map/ppermute | solution.py:183
  86.7 7.1 %collective-permute-start.11 = (f32[128,128]{1,0:T(8,128)S(1)}, f32[128,128]{1,0:T(8,128)S(1)}, u32[]{:S(2)}, u32[]{:S(2)}) collective-permute-start(f32[128,128]{1,0:T(8,128)S(1)} %add.18), channel_id=1, source_target_pairs={{0,8},{1,9},{2,10},{3,11},{4,12},{5,13},{6,14},{7,15},{8,0},{9,1},... | collective-permute-start | bytes 196616 | tf_op jit(solution)/shard_map/ppermute | solution.py:183

commit v15 on v10

--- a/solution.py
+++ b/solution.py
@@ -26,9 +26,9 @@
     same_chip = lax.rem(lax.div(group, 2), 2) == lax.rem(lax.div(row, 2), 2)
     below = gap > planes // 2
     steps = jnp.where(below, planes - gap, gap)
-    receiver = jnp.where(gap == 0, core, jnp.where(below, 0, 1))
-    first = jnp.where(steps == 2, jnp.where(same_chip, 7, 1), jnp.where(same_chip, 3, 5))
-    place = jnp.where(gap == 0, 0, first + jnp.where(core == receiver, 0, 1))
+    receiver = jnp.where(gap == 0, 1 - core, jnp.where(below, 0, 1))
+    first = jnp.where(steps == 2, jnp.where(same_chip, 2, 4), jnp.where(same_chip, 0, 7))
+    place = jnp.where(gap == 0, 6, first + jnp.where(core == receiver, 0, 1))
     slot = 2 + place + jnp.where(receiver == lax.rem(row, 2), 0, 9)
     slot = jnp.where((gap == 0) & same_chip, jnp.where(same_core, 0, 1), slot)
     return slot * blocks + lax.rem(block, blocks)
@@ -160,12 +160,11 @@
         return lax.ppermute(value, "row", [pair for pair in pairs if pair[0] % PLANE in wanted])
 
     beside = swap(adjoint, 1)
-    across = swap(adjoint, 2)
     chip = jnp.concatenate([adjoint, beside])
+    near = to_plane(chip, 1, 0, (0, 1, 2, 3))
     far = to_plane(chip, 2, 0, (0, 1, 2, 3))
     across_far = to_plane(chip, 2, 2, (1, 2))
-    across_near = to_plane(chip, 1, 2, (0, 1, 2, 3))
-    near = to_plane(chip, 1, 0, (0, 1, 2, 3))
+    across = swap(jnp.concatenate([beside, near]), 2)
 
     groups = [list(range(half)), list(range(half, col_count))]
     wz = lax.all_to_all(wpart, "col", 0, 0, axis_index_groups=groups)
@@ -181,7 +180,7 @@
     def partner(value, axis, bit):
         return lax.ppermute(value, axis, [(i, i ^ bit) for i in range(lax.axis_size(axis))])
 
-    received = jnp.concatenate([across, across_far, near, across_near, far, halves])
+    received = jnp.concatenate([near, far, across_far, across, halves])
     other = swap(received, 1)
 
     sends, wsum = pl.pallas_call(

time: 101 us -> 98.7 us (0.977)
  waiting for transfers between devices: 34 us -> 29.9 us
  starting transfers between devices: 57.5 us -> 58.7 us
    ppermute x5, waiting for transfers between devices: 22.4 us -> 15.8 us  [partner(): lax.ppermute(value, axis, [(i, i ^ bit) for i in range(lax.axis_size(axis...]
    ppermute x5, starting transfers between devices: 12.2 us -> 18.6 us  [partner(): lax.ppermute(value, axis, [(i, i ^ bit) for i in range(lax.axis_size(axis...]
    ppermute x3, waiting for transfers between devices: 2.36 us -> 5.93 us  [swap(): return lax.ppermute(value, 'row', [(i, i ^ bit) for i in range(row_count)])]
    ppermute x3, starting transfers between devices: 16.3 us -> 13.7 us  [swap(): return lax.ppermute(value, 'row', [(i, i ^ bit) for i in range(row_count)])]
    all_to_all x1, starting transfers between devices: 10 us -> 7.98 us  [on_device(): wz = lax.all_to_all(wpart, 'col', 0, 0, axis_index_groups=groups)]
    ppermute x4 -> x3, waiting for transfers between devices: 5.84 us -> 4.61 us  [to_plane(): lax.ppermute(value, 'row', [pair for pair in pairs if pair[0] % PLANE in...]
    ppermute x4 -> x3, starting transfers between devices: 9.71 us -> 9.47 us  [to_plane(): lax.ppermute(value, 'row', [pair for pair in pairs if pair[0] % PLANE in...]
  transfers between devices with their start and end apart: 14 -> 13, of which waited for: 9 -> 10; matrix products, arithmetic and copies ran while one was open for 1% -> 1% of each run, Pallas kernels for 0% -> 0%
where the time goes in v15:
time: 98.7 us; the launch traced here: 97.1 us
  starting transfers between devices  58.7 us (59%)
  waiting for transfers between devices  29.9 us (30%)
  Pallas kernels  6.54 us (7%)
  local copies, waits for them, and re-layouts  1.06 us (1%)
    ppermute x5, starting transfers between devices, partner(): lax.ppermute(value, axis, [(i, i ^ bit) for i in range(lax.axis_size(axis...  18.6 us
    ppermute x5, waiting for transfers between devices, partner(): lax.ppermute(value, axis, [(i, i ^ bit) for i in range(lax.axis_size(axis...  15.8 us
    ppermute x3, starting transfers between devices, swap(): return lax.ppermute(value, 'row', [(i, i ^ bit) for i in range(row_count)])  13.7 us
    ppermute x3, starting transfers between devices, to_plane(): lax.ppermute(value, 'row', [pair for pair in pairs if pair[0] % PLANE in...  9.47 us
    all_to_all x1, starting transfers between devices, on_device(): got = lax.all_to_all(sends, 'col', 0, 0)  8.93 us
    all_to_all x1, starting transfers between devices, on_device(): wz = lax.all_to_all(wpart, 'col', 0, 0, axis_index_groups=groups)  7.98 us
    ppermute x3, waiting for transfers between devices, swap(): return lax.ppermute(value, 'row', [(i, i ^ bit) for i in range(row_count)])  5.93 us
    ppermute x3, waiting for transfers between devices, to_plane(): lax.ppermute(value, 'row', [pair for pair in pairs if pair[0] % PLANE in...  4.61 us
  transfers between devices with their start and end apart: 13, of which 10 were waited for; matrix products, arithmetic and copies ran while one was open for 1% of the time, Pallas kernels for 0%

profile of v15, /device:TPU:1, one launch (start us, length us, event | category | flops | bytes accessed | tf_op | source)
XLA Modules:
  0.0 97.1 jit_solution(9113358614557195666)
XLA Ops:
  0.6 2.5 %adjoint.1 = (bf16[384,128]{1,0:T(8,128)(2,1)}, bf16[8,128,128]{2,1,0:T(8,128)(2,1)}, s32[1,32]{1,0:T(1,128)}, s32[1,32]{1,0:T(1,128)}) custom-call(s32[3,128]{1,0:T(4,128)} %bitcast.3, bf16[384,128]{1,0:T(8,128)(2,1)} %cot_in.1, bf16[384,128]{1,0:T(8,128)(2,1)} %pre_in.1, bf16[384,128]{1,0:T(8,128)(2,1)} %agg_in.1, bf16[128,128]{1,0:T(8,128)(2,1)} %w_in.1, ...), custom_call_target="tpu_custom_call" | custom-call | tf_op jit(solution)/shard_map/adjoint/pallas_call | solution.py:136
  3.1 8.8 %collective-permute-start = (bf16[384,128]{1,0:T(8,128)(2,1)}, bf16[384,128]{1,0:T(8,128)(2,1)S(1)}, u32[]{:S(2)}, u32[]{:S(2)}) collective-permute-start(bf16[384,128]{1,0:T(8,128)(2,1)} %get-tuple-element.10.own), channel_id=1, source_target_pairs={{0,16},{16,0},{32,48},{48,32},{64,80},{80,64},{96,112},{112,96},{1... | collective-permute-start | bytes 294920 | tf_op jit(solution)/shard_map/ppermute | solution.py:156
  11.9 0.9 constant_dynamic-update-slice_fusion.1
  12.8 0.2 collective-permute-done.beside
  13.1 1.9 %collective-permute-start.1 = (bf16[768,128]{1,0:T(8,128)(2,1)S(1)}, bf16[768,128]{1,0:T(8,128)(2,1)S(1)}, u32[]{:S(2)}, u32[]{:S(2)}) collective-permute-start(bf16[768,128]{1,0:T(8,128)(2,1)S(1)} %constant_dynamic-update-slice_fusion), channel_id=1, source_target_pairs={{0,64},{16,464},{32,96},{48,496},{64,128},{80,16},{96,160},{112,48... | collective-permute-start | bytes 589832 | tf_op jit(solution)/shard_map/ppermute | solution.py:160
  15.0 0.0 copy-start
  15.0 0.0 copy-start.1
  15.0 0.0 copy-start.2
  15.0 0.0 copy-start.3
  15.0 8.0 %all-to-all-start = ((bf16[8,128,128]{2,1,0:T(8,128)(2,1)}), bf16[8,128,128]{2,1,0:T(8,128)(2,1)S(1)}, u32[]{:S(2)}, u32[]{:S(2)}) async-start(bf16[8,128,128]{2,1,0:T(8,128)(2,1)} %get-tuple-element.11), calls=%async_computation | async-start | bytes 524288 | tf_op jit(solution)/shard_map/all_to_all | solution.py:170
  23.0 4.7 %collective-permute-start.3 = (bf16[768,128]{1,0:T(8,128)(2,1)S(1)}, bf16[768,128]{1,0:T(8,128)(2,1)S(1)}, u32[]{:S(2)}, u32[]{:S(2)}) collective-permute-start(bf16[768,128]{1,0:T(8,128)(2,1)S(1)} %constant_dynamic-update-slice_fusion), channel_id=1, source_target_pairs={{16,432},{32,128},{80,496},{96,192},{144,48},{160,256},{208,112},{... | collective-permute-start | bytes 589832 | tf_op jit(solution)/shard_map/ppermute | solution.py:160
  27.7 2.9 %collective-permute-start.2 = (bf16[768,128]{1,0:T(8,128)(2,1)S(1)}, bf16[768,128]{1,0:T(8,128)(2,1)S(1)}, u32[]{:S(2)}, u32[]{:S(2)}) collective-permute-start(bf16[768,128]{1,0:T(8,128)(2,1)S(1)} %constant_dynamic-update-slice_fusion), channel_id=1, source_target_pairs={{0,128},{16,400},{32,160},{48,432},{64,192},{80,464},{96,224},{112... | collective-permute-start | bytes 589832 | tf_op jit(solution)/shard_map/ppermute | solution.py:160
  30.6 0.0 collective-permute-done.1
  30.6 1.9 %collective-permute-start.4 = (bf16[1152,128]{1,0:T(8,128)(2,1)S(1)}, bf16[1152,128]{1,0:T(8,128)(2,1)S(1)}, u32[]{:S(2)}, u32[]{:S(2)}) collective-permute-start(bf16[1152,128]{1,0:T(8,128)(2,1)S(1)} %pad_maximum_fusion), channel_id=1, source_target_pairs={{0,32},{16,48},{32,0},{48,16},{64,96},{80,112},{96,64},{112,80},{1... | collective-permute-start | bytes 884744 | tf_op jit(solution)/shard_map/ppermute | solution.py:156
  32.6 4.6 %collective-permute-done.2 = bf16[768,128]{1,0:T(8,128)(2,1)S(1)} collective-permute-done((bf16[768,128]{1,0:T(8,128)(2,1)S(1)}, bf16[768,128]{1,0:T(8,128)(2,1)S(1)}, u32[]{:S(2)}, u32[]{:S(2)}) %collective-permute-start.2) | collective-permute-done | bytes 196640 | tf_op jit(solution)/shard_map/ppermute | solution.py:160
  37.2 0.0 collective-permute-done.3
  37.3 0.0 all-to-all-done.parts_ref
  37.3 3.6 %collective-permute-done.4 = bf16[1152,128]{1,0:T(8,128)(2,1)S(1)} collective-permute-done((bf16[1152,128]{1,0:T(8,128)(2,1)S(1)}, bf16[1152,128]{1,0:T(8,128)(2,1)S(1)}, u32[]{:S(2)}, u32[]{:S(2)}) %collective-permute-start.4) | collective-permute-done | bytes 294944 | tf_op jit(solution)/shard_map/ppermute | solution.py:156
  41.0 3.0 %collective-permute-start.5 = (bf16[3712,128]{1,0:T(8,128)(2,1)S(1)}, bf16[3712,128]{1,0:T(8,128)(2,1)S(1)}, u32[]{:S(2)}, u32[]{:S(2)}) collective-permute-start(bf16[3712,128]{1,0:T(8,128)(2,1)S(1)} %constant_dynamic-update-slice_fusion.2.ours), channel_id=1, source_target_pairs={{0,16},{16,0},{32,48},{48,32},{64,80},{80,64},{96,112},{112,96},{1... | collective-permute-start | bytes 2850824 | tf_op jit(solution)/shard_map/ppermute | solution.py:156
  43.9 2.1 %collective-permute-done.5.theirs = bf16[3712,128]{1,0:T(8,128)(2,1)S(1)} collective-permute-done((bf16[3712,128]{1,0:T(8,128)(2,1)S(1)}, bf16[3712,128]{1,0:T(8,128)(2,1)S(1)}, u32[]{:S(2)}, u32[]{:S(2)}) %collective-permute-start.5) | collective-permute-done | bytes 950304 | tf_op jit(solution)/shard_map/ppermute | solution.py:156
  46.1 0.0 copy-done
  46.1 0.0 copy-done.1
  46.1 0.0 copy-done.2
  46.1 0.0 copy-done.3
  46.1 3.1 %tiles.1 = (bf16[16,384,128]{2,1,0:T(8,128)(2,1)}, f32[128,128]{1,0:T(8,128)S(1)}) custom-call(s32[1,32]{1,0:T(1,128)S(1)} %copy-done.2, s32[1,32]{1,0:T(1,128)S(1)} %copy-done.3, bf16[32,128,128]{2,1,0:T(8,128)(2,1)S(1)} %copy-done, bf16[384,128]{1,0:T(8,128)(2,1)S(1)} %copy-done.1, bf16[384,128]{1,0:T(8,128)(2,1)S(1)} %collective-permute-done.beside, ...), custom_call_target="tpu_custom_call" | custom-call | flops 134217728 | bytes 6291456 | tf_op jit(solution)/shard_map/tiles/pallas_call | solution.py:186
  49.2 8.9 %all-to-all-start.1 = ((bf16[16,384,128]{2,1,0:T(8,128)(2,1)}), bf16[16,384,128]{2,1,0:T(8,128)(2,1)S(1)}, u32[]{:S(2)}, u32[]{:S(2)}) async-start(bf16[16,384,128]{2,1,0:T(8,128)(2,1)} %get-tuple-element.12), calls=%async_computation.1 | async-start | bytes 3145728 | tf_op jit(solution)/shard_map/all_to_all | solution.py:204
  58.2 3.2 %collective-permute-start.6 = (f32[128,128]{1,0:T(8,128)S(1)}, f32[128,128]{1,0:T(8,128)S(1)}, u32[]{:S(2)}, u32[]{:S(2)}) collective-permute-start(f32[128,128]{1,0:T(8,128)S(1)} %get-tuple-element.13), channel_id=1, source_target_pairs={{0,64},{16,80},{32,96},{48,112},{64,0},{80,16},{96,32},{112,48},{1... | collective-permute-start | bytes 196616 | tf_op jit(solution)/shard_map/ppermute | solution.py:181
  61.4 1.8 %collective-permute-done.6 = f32[128,128]{1,0:T(8,128)S(1)} collective-permute-done((f32[128,128]{1,0:T(8,128)S(1)}, f32[128,128]{1,0:T(8,128)S(1)}, u32[]{:S(2)}, u32[]{:S(2)}) %collective-permute-start.6) | collective-permute-done | bytes 65568 | tf_op jit(solution)/shard_map/ppermute | solution.py:181
  63.2 3.3 %collective-permute-start.7 = (f32[128,128]{1,0:T(8,128)S(1)}, f32[128,128]{1,0:T(8,128)S(1)}, u32[]{:S(2)}, u32[]{:S(2)}) collective-permute-start(f32[128,128]{1,0:T(8,128)S(1)} %add.15), channel_id=1, source_target_pairs={{0,128},{16,144},{32,160},{48,176},{64,192},{80,208},{96,224},{112... | collective-permute-start | bytes 196616 | tf_op jit(solution)/shard_map/ppermute | solution.py:181
  66.5 2.9 %collective-permute-done.7 = f32[128,128]{1,0:T(8,128)S(1)} collective-permute-done((f32[128,128]{1,0:T(8,128)S(1)}, f32[128,128]{1,0:T(8,128)S(1)}, u32[]{:S(2)}, u32[]{:S(2)}) %collective-permute-start.7) | collective-permute-done | bytes 65568 | tf_op jit(solution)/shard_map/ppermute | solution.py:181
  69.4 5.5 %collective-permute-start.8 = (f32[128,128]{1,0:T(8,128)S(1)}, f32[128,128]{1,0:T(8,128)S(1)}, u32[]{:S(2)}, u32[]{:S(2)}) collective-permute-start(f32[128,128]{1,0:T(8,128)S(1)} %add.16), channel_id=1, source_target_pairs={{0,256},{16,272},{32,288},{48,304},{64,320},{80,336},{96,352},{112... | collective-permute-start | bytes 196616 | tf_op jit(solution)/shard_map/ppermute | solution.py:181
  74.9 3.7 %collective-permute-done.8 = f32[128,128]{1,0:T(8,128)S(1)} collective-permute-done((f32[128,128]{1,0:T(8,128)S(1)}, f32[128,128]{1,0:T(8,128)S(1)}, u32[]{:S(2)}, u32[]{:S(2)}) %collective-permute-start.8) | collective-permute-done | bytes 65568 | tf_op jit(solution)/shard_map/ppermute | solution.py:181
  78.6 1.9 %collective-permute-start.9 = (f32[128,128]{1,0:T(8,128)S(1)}, f32[128,128]{1,0:T(8,128)S(1)}, u32[]{:S(2)}, u32[]{:S(2)}) collective-permute-start(f32[128,128]{1,0:T(8,128)S(1)} %add.17), channel_id=1, source_target_pairs={{0,32},{16,48},{32,0},{48,16},{64,96},{80,112},{96,64},{112,80},{1... | collective-permute-start | bytes 196616 | tf_op jit(solution)/shard_map/ppermute | solution.py:181
  80.5 4.9 %collective-permute-done.9 = f32[128,128]{1,0:T(8,128)S(1)} collective-permute-done((f32[128,128]{1,0:T(8,128)S(1)}, f32[128,128]{1,0:T(8,128)S(1)}, u32[]{:S(2)}, u32[]{:S(2)}) %collective-permute-start.9) | collective-permute-done | bytes 65568 | tf_op jit(solution)/shard_map/ppermute | solution.py:181
  85.5 4.7 %collective-permute-start.10 = (f32[128,128]{1,0:T(8,128)S(1)}, f32[128,128]{1,0:T(8,128)S(1)}, u32[]{:S(2)}, u32[]{:S(2)}) collective-permute-start(f32[128,128]{1,0:T(8,128)S(1)} %add.18), channel_id=1, source_target_pairs={{0,8},{1,9},{2,10},{3,11},{4,12},{5,13},{6,14},{7,15},{8,0},{9,1},... | collective-permute-start | bytes 196616 | tf_op jit(solution)/shard_map/ppermute | solution.py:181
  90.1 2.5 %collective-permute-done.10 = f32[128,128]{1,0:T(8,128)S(1)} collective-permute-done((f32[128,128]{1,0:T(8,128)S(1)}, f32[128,128]{1,0:T(8,128)S(1)}, u32[]{:S(2)}, u32[]{:S(2)}) %collective-permute-start.10) | collective-permute-done | bytes 65568 | tf_op jit(solution)/shard_map/ppermute | solution.py:181
  92.7 3.6 %all-to-all-done.1.got_ref = bf16[16,384,128]{2,1,0:T(8,128)(2,1)S(1)} async-done(((bf16[16,384,128]{2,1,0:T(8,128)(2,1)}), bf16[16,384,128]{2,1,0:T(8,128)(2,1)S(1)}, u32[]{:S(2)}, u32[]{:S(2)}) %all-to-all-start.1) | async-done | bytes 1572896 | tf_op jit(solution)/shard_map/all_to_all | solution.py:204
  96.2 0.9 finish.1
  (13 shorter events, 0.2 us)
Async XLA Ops:
  3.1 9.9 %collective-permute-start = (bf16[384,128]{1,0:T(8,128)(2,1)}, bf16[384,128]{1,0:T(8,128)(2,1)S(1)}, u32[]{:S(2)}, u32[]{:S(2)}) collective-permute-start(bf16[384,128]{1,0:T(8,128)(2,1)} %get-tuple-element.10.own), channel_id=1, source_target_pairs={{0,16},{16,0},{32,48},{48,32},{64,80},{80,64},{96,112},{112,96},{1... | collective-permute-start | bytes 294920 | tf_op jit(solution)/shard_map/ppermute | solution.py:156
  13.1 17.5 %collective-permute-start.1 = (bf16[768,128]{1,0:T(8,128)(2,1)S(1)}, bf16[768,128]{1,0:T(8,128)(2,1)S(1)}, u32[]{:S(2)}, u32[]{:S(2)}) collective-permute-start(bf16[768,128]{1,0:T(8,128)(2,1)S(1)} %constant_dynamic-update-slice_fusion), channel_id=1, source_target_pairs={{0,64},{16,464},{32,96},{48,496},{64,128},{80,16},{96,160},{112,48... | collective-permute-start | bytes 589832 | tf_op jit(solution)/shard_map/ppermute | solution.py:160
  15.0 31.1 %copy-start = (bf16[32,128,128]{2,1,0:T(8,128)(2,1)S(1)}, bf16[32,128,128]{2,1,0:T(8,128)(2,1)}, u32[]{:S(2)}) copy-start(bf16[32,128,128]{2,1,0:T(8,128)(2,1)} %tiles_ref.1) | copy-start | bytes 3145732
  15.0 31.0 %copy-start.1 = (bf16[384,128]{1,0:T(8,128)(2,1)S(1)}, bf16[384,128]{1,0:T(8,128)(2,1)}, u32[]{:S(2)}) copy-start(bf16[384,128]{1,0:T(8,128)(2,1)} %get-tuple-element.10.own) | copy-start | bytes 294916
  15.0 31.0 %copy-start.2 = (s32[1,32]{1,0:T(1,128)S(1)}, s32[1,32]{1,0:T(1,128)}, u32[]{:S(2)}) copy-start(s32[1,32]{1,0:T(1,128)} %get-tuple-element.8.from_ref) | copy-start | bytes 388
  15.0 31.0 %copy-start.3 = (s32[1,32]{1,0:T(1,128)S(1)}, s32[1,32]{1,0:T(1,128)}, u32[]{:S(2)}) copy-start(s32[1,32]{1,0:T(1,128)} %get-tuple-element.9.to_ref) | copy-start | bytes 388
  15.0 22.2 %all-to-all-start = ((bf16[8,128,128]{2,1,0:T(8,128)(2,1)}), bf16[8,128,128]{2,1,0:T(8,128)(2,1)S(1)}, u32[]{:S(2)}, u32[]{:S(2)}) async-start(bf16[8,128,128]{2,1,0:T(8,128)(2,1)} %get-tuple-element.11), calls=%async_computation | async-start | bytes 524288 | tf_op jit(solution)/shard_map/all_to_all | solution.py:170
  23.0 14.2 %collective-permute-start.3 = (bf16[768,128]{1,0:T(8,128)(2,1)S(1)}, bf16[768,128]{1,0:T(8,128)(2,1)S(1)}, u32[]{:S(2)}, u32[]{:S(2)}) collective-permute-start(bf16[768,128]{1,0:T(8,128)(2,1)S(1)} %constant_dynamic-update-slice_fusion), channel_id=1, source_target_pairs={{16,432},{32,128},{80,496},{96,192},{144,48},{160,256},{208,112},{... | collective-permute-start | bytes 589832 | tf_op jit(solution)/shard_map/ppermute | solution.py:160
  27.7 9.5 %collective-permute-start.2 = (bf16[768,128]{1,0:T(8,128)(2,1)S(1)}, bf16[768,128]{1,0:T(8,128)(2,1)S(1)}, u32[]{:S(2)}, u32[]{:S(2)}) collective-permute-start(bf16[768,128]{1,0:T(8,128)(2,1)S(1)} %constant_dynamic-update-slice_fusion), channel_id=1, source_target_pairs={{0,128},{16,400},{32,160},{48,432},{64,192},{80,464},{96,224},{112... | collective-permute-start | bytes 589832 | tf_op jit(solution)/shard_map/ppermute | solution.py:160
  30.6 10.3 %collective-permute-start.4 = (bf16[1152,128]{1,0:T(8,128)(2,1)S(1)}, bf16[1152,128]{1,0:T(8,128)(2,1)S(1)}, u32[]{:S(2)}, u32[]{:S(2)}) collective-permute-start(bf16[1152,128]{1,0:T(8,128)(2,1)S(1)} %pad_maximum_fusion), channel_id=1, source_target_pairs={{0,32},{16,48},{32,0},{48,16},{64,96},{80,112},{96,64},{112,80},{1... | collective-permute-start | bytes 884744 | tf_op jit(solution)/shard_map/ppermute | solution.py:156
  41.0 5.1 %collective-permute-start.5 = (bf16[3712,128]{1,0:T(8,128)(2,1)S(1)}, bf16[3712,128]{1,0:T(8,128)(2,1)S(1)}, u32[]{:S(2)}, u32[]{:S(2)}) collective-permute-start(bf16[3712,128]{1,0:T(8,128)(2,1)S(1)} %constant_dynamic-update-slice_fusion.2.ours), channel_id=1, source_target_pairs={{0,16},{16,0},{32,48},{48,32},{64,80},{80,64},{96,112},{112,96},{1... | collective-permute-start | bytes 2850824 | tf_op jit(solution)/shard_map/ppermute | solution.py:156
  49.2 47.0 %all-to-all-start.1 = ((bf16[16,384,128]{2,1,0:T(8,128)(2,1)}), bf16[16,384,128]{2,1,0:T(8,128)(2,1)S(1)}, u32[]{:S(2)}, u32[]{:S(2)}) async-start(bf16[16,384,128]{2,1,0:T(8,128)(2,1)} %get-tuple-element.12), calls=%async_computation.1 | async-start | bytes 3145728 | tf_op jit(solution)/shard_map/all_to_all | solution.py:204
  58.2 5.0 %collective-permute-start.6 = (f32[128,128]{1,0:T(8,128)S(1)}, f32[128,128]{1,0:T(8,128)S(1)}, u32[]{:S(2)}, u32[]{:S(2)}) collective-permute-start(f32[128,128]{1,0:T(8,128)S(1)} %get-tuple-element.13), channel_id=1, source_target_pairs={{0,64},{16,80},{32,96},{48,112},{64,0},{80,16},{96,32},{112,48},{1... | collective-permute-start | bytes 196616 | tf_op jit(solution)/shard_map/ppermute | solution.py:181
  63.2 6.2 %collective-permute-start.7 = (f32[128,128]{1,0:T(8,128)S(1)}, f32[128,128]{1,0:T(8,128)S(1)}, u32[]{:S(2)}, u32[]{:S(2)}) collective-permute-start(f32[128,128]{1,0:T(8,128)S(1)} %add.15), channel_id=1, source_target_pairs={{0,128},{16,144},{32,160},{48,176},{64,192},{80,208},{96,224},{112... | collective-permute-start | bytes 196616 | tf_op jit(solution)/shard_map/ppermute | solution.py:181
  69.4 9.2 %collective-permute-start.8 = (f32[128,128]{1,0:T(8,128)S(1)}, f32[128,128]{1,0:T(8,128)S(1)}, u32[]{:S(2)}, u32[]{:S(2)}) collective-permute-start(f32[128,128]{1,0:T(8,128)S(1)} %add.16), channel_id=1, source_target_pairs={{0,256},{16,272},{32,288},{48,304},{64,320},{80,336},{96,352},{112... | collective-permute-start | bytes 196616 | tf_op jit(solution)/shard_map/ppermute | solution.py:181
  78.6 6.8 %collective-permute-start.9 = (f32[128,128]{1,0:T(8,128)S(1)}, f32[128,128]{1,0:T(8,128)S(1)}, u32[]{:S(2)}, u32[]{:S(2)}) collective-permute-start(f32[128,128]{1,0:T(8,128)S(1)} %add.17), channel_id=1, source_target_pairs={{0,32},{16,48},{32,0},{48,16},{64,96},{80,112},{96,64},{112,80},{1... | collective-permute-start | bytes 196616 | tf_op jit(solution)/shard_map/ppermute | solution.py:181
  85.5 7.2 %collective-permute-start.10 = (f32[128,128]{1,0:T(8,128)S(1)}, f32[128,128]{1,0:T(8,128)S(1)}, u32[]{:S(2)}, u32[]{:S(2)}) collective-permute-start(f32[128,128]{1,0:T(8,128)S(1)} %add.18), channel_id=1, source_target_pairs={{0,8},{1,9},{2,10},{3,11},{4,12},{5,13},{6,14},{7,15},{8,0},{9,1},... | collective-permute-start | bytes 196616 | tf_op jit(solution)/shard_map/ppermute | solution.py:181

commit v16 on v15

--- a/solution.py
+++ b/solution.py
@@ -202,9 +202,15 @@
     )(places, targets, tile_values, adjoint, beside, received, other)
 
     got = lax.all_to_all(sends, "col", 0, 0)
-    for bit in [PLANE << k for k in range((row_count // PLANE - 1).bit_length())] + [2]:
+    planes = row_count // PLANE
+    for bit in [PLANE << k for k in range((planes - 1).bit_length() - 1)]:
         wsum = wsum + partner(wsum, "row", bit)
-    wsum = wsum + partner(wsum, "col", half)
+    mirrored = [(i, (planes - 1 - i // PLANE) * PLANE + i % PLANE) for i in range(row_count)]
+    wsum = wsum + lax.ppermute(wsum, "row", mirrored)
+    wsum = wsum + partner(wsum, "row", 2)
+    spots = [(r, c) for r in range(row_count) for c in range(col_count)]
+    facing = [(r * col_count + c, (r ^ 2) * col_count + (c + half) % col_count) for r, c in spots]
+    wsum = wsum + lax.ppermute(wsum, ("row", "col"), facing)
     scale = 1.0 / float(nodes * row_count * col_count) ** 0.5
     node_grad, weight_grad = pl.pallas_call(
         functools.partial(finish_kernel, scale),

time: 98.7 us -> 98.7 us (level)
  starting transfers between devices: 58.7 us -> 55.3 us
  waiting for transfers between devices: 29.9 us -> 33.2 us
    ppermute x5 -> x3, starting transfers between devices: 18.6 us -> 8.45 us  [partner(): lax.ppermute(value, axis, [(i, i ^ bit) for i in range(lax.axis_size(axis...]
    ppermute x5 -> x3, waiting for transfers between devices: 15.8 us -> 8.62 us  [partner(): lax.ppermute(value, axis, [(i, i ^ bit) for i in range(lax.axis_size(axis...]
    ppermute x0 -> x2, waiting for transfers between devices: none -> 6.87 us  [the longest x1 4.22 us: on_device(): wsum = wsum + lax.ppermute(wsum, 'row', mirrored)]
    ppermute x0 -> x2, starting transfers between devices: none -> 6.82 us  [the longest x1 4.53 us: on_device(): wsum = wsum + lax.ppermute(wsum, ('row', 'col'), facing)]
    all_to_all x1, waiting for transfers between devices: 3.57 us -> 7.2 us  [on_device(): got = lax.all_to_all(sends, 'col', 0, 0)]
where the time goes in v16:
time: 98.7 us; the launch traced here: 97.1 us
  starting transfers between devices  55.3 us (56%)
  waiting for transfers between devices  33.2 us (34%)
  Pallas kernels  6.54 us (7%)
  local copies, waits for them, and re-layouts  1.06 us (1%)
    ppermute x3, starting transfers between devices, swap(): return lax.ppermute(value, 'row', [(i, i ^ bit) for i in range(row_count)])  13.7 us
    ppermute x3, starting transfers between devices, to_plane(): lax.ppermute(value, 'row', [pair for pair in pairs if pair[0] % PLANE in...  9.47 us
    all_to_all x1, starting transfers between devices, on_device(): got = lax.all_to_all(sends, 'col', 0, 0)  8.93 us
    ppermute x3, waiting for transfers between devices, partner(): lax.ppermute(value, axis, [(i, i ^ bit) for i in range(lax.axis_size(axis...  8.62 us
    ppermute x3, starting transfers between devices, partner(): lax.ppermute(value, axis, [(i, i ^ bit) for i in range(lax.axis_size(axis...  8.45 us
    all_to_all x1, starting transfers between devices, on_device(): wz = lax.all_to_all(wpart, 'col', 0, 0, axis_index_groups=groups)  7.98 us
    all_to_all x1, waiting for transfers between devices, on_device(): got = lax.all_to_all(sends, 'col', 0, 0)  7.2 us
    ppermute x3, waiting for transfers between devices, swap(): return lax.ppermute(value, 'row', [(i, i ^ bit) for i in range(row_count)])  5.93 us
  transfers between devices with their start and end apart: 13, of which 10 were waited for; matrix products, arithmetic and copies ran while one was open for 1% of the time, Pallas kernels for 0%

profile of v16, /device:TPU:1, one launch (start us, length us, event | category | flops | bytes accessed | tf_op | source)
XLA Modules:
  0.0 97.1 jit_solution(4638776325085664996)
XLA Ops:
  0.6 2.5 %adjoint.1 = (bf16[384,128]{1,0:T(8,128)(2,1)}, bf16[8,128,128]{2,1,0:T(8,128)(2,1)}, s32[1,32]{1,0:T(1,128)}, s32[1,32]{1,0:T(1,128)}) custom-call(s32[3,128]{1,0:T(4,128)} %bitcast.3, bf16[384,128]{1,0:T(8,128)(2,1)} %cot_in.1, bf16[384,128]{1,0:T(8,128)(2,1)} %pre_in.1, bf16[384,128]{1,0:T(8,128)(2,1)} %agg_in.1, bf16[128,128]{1,0:T(8,128)(2,1)} %w_in.1, ...), custom_call_target="tpu_custom_call" | custom-call | tf_op jit(solution)/shard_map/adjoint/pallas_call | solution.py:136
  3.1 8.8 %collective-permute-start = (bf16[384,128]{1,0:T(8,128)(2,1)}, bf16[384,128]{1,0:T(8,128)(2,1)S(1)}, u32[]{:S(2)}, u32[]{:S(2)}) collective-permute-start(bf16[384,128]{1,0:T(8,128)(2,1)} %get-tuple-element.10.own), channel_id=1, source_target_pairs={{0,16},{16,0},{32,48},{48,32},{64,80},{80,64},{96,112},{112,96},{1... | collective-permute-start | bytes 294920 | tf_op jit(solution)/shard_map/ppermute | solution.py:156
  11.9 0.9 constant_dynamic-update-slice_fusion.1
  12.8 0.2 collective-permute-done.beside
  13.1 1.9 %collective-permute-start.1 = (bf16[768,128]{1,0:T(8,128)(2,1)S(1)}, bf16[768,128]{1,0:T(8,128)(2,1)S(1)}, u32[]{:S(2)}, u32[]{:S(2)}) collective-permute-start(bf16[768,128]{1,0:T(8,128)(2,1)S(1)} %constant_dynamic-update-slice_fusion), channel_id=1, source_target_pairs={{0,64},{16,464},{32,96},{48,496},{64,128},{80,16},{96,160},{112,48... | collective-permute-start | bytes 589832 | tf_op jit(solution)/shard_map/ppermute | solution.py:160
  15.0 0.0 copy-start
  15.0 0.0 copy-start.1
  15.0 0.0 copy-start.2
  15.0 0.0 copy-start.3
  15.0 8.0 %all-to-all-start = ((bf16[8,128,128]{2,1,0:T(8,128)(2,1)}), bf16[8,128,128]{2,1,0:T(8,128)(2,1)S(1)}, u32[]{:S(2)}, u32[]{:S(2)}) async-start(bf16[8,128,128]{2,1,0:T(8,128)(2,1)} %get-tuple-element.11), calls=%async_computation | async-start | bytes 524288 | tf_op jit(solution)/shard_map/all_to_all | solution.py:170
  23.0 4.7 %collective-permute-start.3 = (bf16[768,128]{1,0:T(8,128)(2,1)S(1)}, bf16[768,128]{1,0:T(8,128)(2,1)S(1)}, u32[]{:S(2)}, u32[]{:S(2)}) collective-permute-start(bf16[768,128]{1,0:T(8,128)(2,1)S(1)} %constant_dynamic-update-slice_fusion), channel_id=1, source_target_pairs={{16,432},{32,128},{80,496},{96,192},{144,48},{160,256},{208,112},{... | collective-permute-start | bytes 589832 | tf_op jit(solution)/shard_map/ppermute | solution.py:160
  27.7 2.9 %collective-permute-start.2 = (bf16[768,128]{1,0:T(8,128)(2,1)S(1)}, bf16[768,128]{1,0:T(8,128)(2,1)S(1)}, u32[]{:S(2)}, u32[]{:S(2)}) collective-permute-start(bf16[768,128]{1,0:T(8,128)(2,1)S(1)} %constant_dynamic-update-slice_fusion), channel_id=1, source_target_pairs={{0,128},{16,400},{32,160},{48,432},{64,192},{80,464},{96,224},{112... | collective-permute-start | bytes 589832 | tf_op jit(solution)/shard_map/ppermute | solution.py:160
  30.6 0.0 collective-permute-done.1
  30.6 1.9 %collective-permute-start.4 = (bf16[1152,128]{1,0:T(8,128)(2,1)S(1)}, bf16[1152,128]{1,0:T(8,128)(2,1)S(1)}, u32[]{:S(2)}, u32[]{:S(2)}) collective-permute-start(bf16[1152,128]{1,0:T(8,128)(2,1)S(1)} %pad_maximum_fusion), channel_id=1, source_target_pairs={{0,32},{16,48},{32,0},{48,16},{64,96},{80,112},{96,64},{112,80},{1... | collective-permute-start | bytes 884744 | tf_op jit(solution)/shard_map/ppermute | solution.py:156
  32.6 4.6 %collective-permute-done.2 = bf16[768,128]{1,0:T(8,128)(2,1)S(1)} collective-permute-done((bf16[768,128]{1,0:T(8,128)(2,1)S(1)}, bf16[768,128]{1,0:T(8,128)(2,1)S(1)}, u32[]{:S(2)}, u32[]{:S(2)}) %collective-permute-start.2) | collective-permute-done | bytes 196640 | tf_op jit(solution)/shard_map/ppermute | solution.py:160
  37.2 0.0 collective-permute-done.3
  37.3 0.0 all-to-all-done.parts_ref
  37.3 3.6 %collective-permute-done.4 = bf16[1152,128]{1,0:T(8,128)(2,1)S(1)} collective-permute-done((bf16[1152,128]{1,0:T(8,128)(2,1)S(1)}, bf16[1152,128]{1,0:T(8,128)(2,1)S(1)}, u32[]{:S(2)}, u32[]{:S(2)}) %collective-permute-start.4) | collective-permute-done | bytes 294944 | tf_op jit(solution)/shard_map/ppermute | solution.py:156
  41.0 3.0 %collective-permute-start.5 = (bf16[3712,128]{1,0:T(8,128)(2,1)S(1)}, bf16[3712,128]{1,0:T(8,128)(2,1)S(1)}, u32[]{:S(2)}, u32[]{:S(2)}) collective-permute-start(bf16[3712,128]{1,0:T(8,128)(2,1)S(1)} %constant_dynamic-update-slice_fusion.2.ours), channel_id=1, source_target_pairs={{0,16},{16,0},{32,48},{48,32},{64,80},{80,64},{96,112},{112,96},{1... | collective-permute-start | bytes 2850824 | tf_op jit(solution)/shard_map/ppermute | solution.py:156
  43.9 2.1 %collective-permute-done.5.theirs = bf16[3712,128]{1,0:T(8,128)(2,1)S(1)} collective-permute-done((bf16[3712,128]{1,0:T(8,128)(2,1)S(1)}, bf16[3712,128]{1,0:T(8,128)(2,1)S(1)}, u32[]{:S(2)}, u32[]{:S(2)}) %collective-permute-start.5) | collective-permute-done | bytes 950304 | tf_op jit(solution)/shard_map/ppermute | solution.py:156
  46.1 0.0 copy-done
  46.1 0.0 copy-done.1
  46.1 0.0 copy-done.2
  46.1 0.0 copy-done.3
  46.1 3.1 %tiles.1 = (bf16[16,384,128]{2,1,0:T(8,128)(2,1)}, f32[128,128]{1,0:T(8,128)S(1)}) custom-call(s32[1,32]{1,0:T(1,128)S(1)} %copy-done.2, s32[1,32]{1,0:T(1,128)S(1)} %copy-done.3, bf16[32,128,128]{2,1,0:T(8,128)(2,1)S(1)} %copy-done, bf16[384,128]{1,0:T(8,128)(2,1)S(1)} %copy-done.1, bf16[384,128]{1,0:T(8,128)(2,1)S(1)} %collective-permute-done.beside, ...), custom_call_target="tpu_custom_call" | custom-call | flops 134217728 | bytes 6291456 | tf_op jit(solution)/shard_map/tiles/pallas_call | solution.py:186
  49.2 8.9 %all-to-all-start.1 = ((bf16[16,384,128]{2,1,0:T(8,128)(2,1)}), bf16[16,384,128]{2,1,0:T(8,128)(2,1)S(1)}, u32[]{:S(2)}, u32[]{:S(2)}) async-start(bf16[16,384,128]{2,1,0:T(8,128)(2,1)} %get-tuple-element.12), calls=%async_computation.1 | async-start | bytes 3145728 | tf_op jit(solution)/shard_map/all_to_all | solution.py:204
  58.2 3.2 %collective-permute-start.6 = (f32[128,128]{1,0:T(8,128)S(1)}, f32[128,128]{1,0:T(8,128)S(1)}, u32[]{:S(2)}, u32[]{:S(2)}) collective-permute-start(f32[128,128]{1,0:T(8,128)S(1)} %get-tuple-element.13), channel_id=1, source_target_pairs={{0,64},{16,80},{32,96},{48,112},{64,0},{80,16},{96,32},{112,48},{1... | collective-permute-start | bytes 196616 | tf_op jit(solution)/shard_map/ppermute | solution.py:181
  61.4 1.8 %collective-permute-done.6 = f32[128,128]{1,0:T(8,128)S(1)} collective-permute-done((f32[128,128]{1,0:T(8,128)S(1)}, f32[128,128]{1,0:T(8,128)S(1)}, u32[]{:S(2)}, u32[]{:S(2)}) %collective-permute-start.6) | collective-permute-done | bytes 65568 | tf_op jit(solution)/shard_map/ppermute | solution.py:181
  63.2 3.3 %collective-permute-start.7 = (f32[128,128]{1,0:T(8,128)S(1)}, f32[128,128]{1,0:T(8,128)S(1)}, u32[]{:S(2)}, u32[]{:S(2)}) collective-permute-start(f32[128,128]{1,0:T(8,128)S(1)} %add.15), channel_id=1, source_target_pairs={{0,128},{16,144},{32,160},{48,176},{64,192},{80,208},{96,224},{112... | collective-permute-start | bytes 196616 | tf_op jit(solution)/shard_map/ppermute | solution.py:181
  66.5 2.9 %collective-permute-done.7 = f32[128,128]{1,0:T(8,128)S(1)} collective-permute-done((f32[128,128]{1,0:T(8,128)S(1)}, f32[128,128]{1,0:T(8,128)S(1)}, u32[]{:S(2)}, u32[]{:S(2)}) %collective-permute-start.7) | collective-permute-done | bytes 65568 | tf_op jit(solution)/shard_map/ppermute | solution.py:181
  69.4 2.3 %collective-permute-start.8 = (f32[128,128]{1,0:T(8,128)S(1)}, f32[128,128]{1,0:T(8,128)S(1)}, u32[]{:S(2)}, u32[]{:S(2)}) collective-permute-start(f32[128,128]{1,0:T(8,128)S(1)} %add.16), channel_id=1, source_target_pairs={{0,448},{16,464},{32,480},{48,496},{64,384},{80,400},{96,416},{112... | collective-permute-start | bytes 196616 | tf_op jit(solution)/shard_map/ppermute | solution.py:209
  71.7 4.2 %collective-permute-done.8 = f32[128,128]{1,0:T(8,128)S(1)} collective-permute-done((f32[128,128]{1,0:T(8,128)S(1)}, f32[128,128]{1,0:T(8,128)S(1)}, u32[]{:S(2)}, u32[]{:S(2)}) %collective-permute-start.8) | collective-permute-done | bytes 65568 | tf_op jit(solution)/shard_map/ppermute | solution.py:209
  75.9 1.9 %collective-permute-start.9 = (f32[128,128]{1,0:T(8,128)S(1)}, f32[128,128]{1,0:T(8,128)S(1)}, u32[]{:S(2)}, u32[]{:S(2)}) collective-permute-start(f32[128,128]{1,0:T(8,128)S(1)} %add.17), channel_id=1, source_target_pairs={{0,32},{16,48},{32,0},{48,16},{64,96},{80,112},{96,64},{112,80},{1... | collective-permute-start | bytes 196616 | tf_op jit(solution)/shard_map/ppermute | solution.py:181
  77.8 3.9 %collective-permute-done.9 = f32[128,128]{1,0:T(8,128)S(1)} collective-permute-done((f32[128,128]{1,0:T(8,128)S(1)}, f32[128,128]{1,0:T(8,128)S(1)}, u32[]{:S(2)}, u32[]{:S(2)}) %collective-permute-start.9) | collective-permute-done | bytes 65568 | tf_op jit(solution)/shard_map/ppermute | solution.py:181
  81.8 4.5 %collective-permute-start.10 = (f32[128,128]{1,0:T(8,128)S(1)}, f32[128,128]{1,0:T(8,128)S(1)}, u32[]{:S(2)}, u32[]{:S(2)}) collective-permute-start(f32[128,128]{1,0:T(8,128)S(1)} %add.18), channel_id=1, source_target_pairs={{0,40},{1,41},{2,42},{3,43},{4,44},{5,45},{6,46},{7,47},{8,32},{9,... | collective-permute-start | bytes 196616 | tf_op jit(solution)/shard_map/ppermute | solution.py:213
  86.4 2.7 %collective-permute-done.10 = f32[128,128]{1,0:T(8,128)S(1)} collective-permute-done((f32[128,128]{1,0:T(8,128)S(1)}, f32[128,128]{1,0:T(8,128)S(1)}, u32[]{:S(2)}, u32[]{:S(2)}) %collective-permute-start.10) | collective-permute-done | bytes 65568 | tf_op jit(solution)/shard_map/ppermute | solution.py:213
  89.0 7.2 %all-to-all-done.1.got_ref = bf16[16,384,128]{2,1,0:T(8,128)(2,1)S(1)} async-done(((bf16[16,384,128]{2,1,0:T(8,128)(2,1)}), bf16[16,384,128]{2,1,0:T(8,128)(2,1)S(1)}, u32[]{:S(2)}, u32[]{:S(2)}) %all-to-all-start.1) | async-done | bytes 1572896 | tf_op jit(solution)/shard_map/all_to_all | solution.py:204
  96.2 0.9 finish.1
  (13 shorter events, 0.2 us)
Async XLA Ops:
  3.1 9.9 %collective-permute-start = (bf16[384,128]{1,0:T(8,128)(2,1)}, bf16[384,128]{1,0:T(8,128)(2,1)S(1)}, u32[]{:S(2)}, u32[]{:S(2)}) collective-permute-start(bf16[384,128]{1,0:T(8,128)(2,1)} %get-tuple-element.10.own), channel_id=1, source_target_pairs={{0,16},{16,0},{32,48},{48,32},{64,80},{80,64},{96,112},{112,96},{1... | collective-permute-start | bytes 294920 | tf_op jit(solution)/shard_map/ppermute | solution.py:156
  13.1 17.5 %collective-permute-start.1 = (bf16[768,128]{1,0:T(8,128)(2,1)S(1)}, bf16[768,128]{1,0:T(8,128)(2,1)S(1)}, u32[]{:S(2)}, u32[]{:S(2)}) collective-permute-start(bf16[768,128]{1,0:T(8,128)(2,1)S(1)} %constant_dynamic-update-slice_fusion), channel_id=1, source_target_pairs={{0,64},{16,464},{32,96},{48,496},{64,128},{80,16},{96,160},{112,48... | collective-permute-start | bytes 589832 | tf_op jit(solution)/shard_map/ppermute | solution.py:160
  15.0 31.1 %copy-start = (bf16[32,128,128]{2,1,0:T(8,128)(2,1)S(1)}, bf16[32,128,128]{2,1,0:T(8,128)(2,1)}, u32[]{:S(2)}) copy-start(bf16[32,128,128]{2,1,0:T(8,128)(2,1)} %tiles_ref.1) | copy-start | bytes 3145732
  15.0 31.0 %copy-start.1 = (bf16[384,128]{1,0:T(8,128)(2,1)S(1)}, bf16[384,128]{1,0:T(8,128)(2,1)}, u32[]{:S(2)}) copy-start(bf16[384,128]{1,0:T(8,128)(2,1)} %get-tuple-element.10.own) | copy-start | bytes 294916
  15.0 31.0 %copy-start.2 = (s32[1,32]{1,0:T(1,128)S(1)}, s32[1,32]{1,0:T(1,128)}, u32[]{:S(2)}) copy-start(s32[1,32]{1,0:T(1,128)} %get-tuple-element.8.from_ref) | copy-start | bytes 388
  15.0 31.0 %copy-start.3 = (s32[1,32]{1,0:T(1,128)S(1)}, s32[1,32]{1,0:T(1,128)}, u32[]{:S(2)}) copy-start(s32[1,32]{1,0:T(1,128)} %get-tuple-element.9.to_ref) | copy-start | bytes 388
  15.0 22.2 %all-to-all-start = ((bf16[8,128,128]{2,1,0:T(8,128)(2,1)}), bf16[8,128,128]{2,1,0:T(8,128)(2,1)S(1)}, u32[]{:S(2)}, u32[]{:S(2)}) async-start(bf16[8,128,128]{2,1,0:T(8,128)(2,1)} %get-tuple-element.11), calls=%async_computation | async-start | bytes 524288 | tf_op jit(solution)/shard_map/all_to_all | solution.py:170
  23.0 14.2 %collective-permute-start.3 = (bf16[768,128]{1,0:T(8,128)(2,1)S(1)}, bf16[768,128]{1,0:T(8,128)(2,1)S(1)}, u32[]{:S(2)}, u32[]{:S(2)}) collective-permute-start(bf16[768,128]{1,0:T(8,128)(2,1)S(1)} %constant_dynamic-update-slice_fusion), channel_id=1, source_target_pairs={{16,432},{32,128},{80,496},{96,192},{144,48},{160,256},{208,112},{... | collective-permute-start | bytes 589832 | tf_op jit(solution)/shard_map/ppermute | solution.py:160
  27.7 9.5 %collective-permute-start.2 = (bf16[768,128]{1,0:T(8,128)(2,1)S(1)}, bf16[768,128]{1,0:T(8,128)(2,1)S(1)}, u32[]{:S(2)}, u32[]{:S(2)}) collective-permute-start(bf16[768,128]{1,0:T(8,128)(2,1)S(1)} %constant_dynamic-update-slice_fusion), channel_id=1, source_target_pairs={{0,128},{16,400},{32,160},{48,432},{64,192},{80,464},{96,224},{112... | collective-permute-start | bytes 589832 | tf_op jit(solution)/shard_map/ppermute | solution.py:160
  30.6 10.3 %collective-permute-start.4 = (bf16[1152,128]{1,0:T(8,128)(2,1)S(1)}, bf16[1152,128]{1,0:T(8,128)(2,1)S(1)}, u32[]{:S(2)}, u32[]{:S(2)}) collective-permute-start(bf16[1152,128]{1,0:T(8,128)(2,1)S(1)} %pad_maximum_fusion), channel_id=1, source_target_pairs={{0,32},{16,48},{32,0},{48,16},{64,96},{80,112},{96,64},{112,80},{1... | collective-permute-start | bytes 884744 | tf_op jit(solution)/shard_map/ppermute | solution.py:156
  41.0 5.1 %collective-permute-start.5 = (bf16[3712,128]{1,0:T(8,128)(2,1)S(1)}, bf16[3712,128]{1,0:T(8,128)(2,1)S(1)}, u32[]{:S(2)}, u32[]{:S(2)}) collective-permute-start(bf16[3712,128]{1,0:T(8,128)(2,1)S(1)} %constant_dynamic-update-slice_fusion.2.ours), channel_id=1, source_target_pairs={{0,16},{16,0},{32,48},{48,32},{64,80},{80,64},{96,112},{112,96},{1... | collective-permute-start | bytes 2850824 | tf_op jit(solution)/shard_map/ppermute | solution.py:156
  49.2 47.0 %all-to-all-start.1 = ((bf16[16,384,128]{2,1,0:T(8,128)(2,1)}), bf16[16,384,128]{2,1,0:T(8,128)(2,1)S(1)}, u32[]{:S(2)}, u32[]{:S(2)}) async-start(bf16[16,384,128]{2,1,0:T(8,128)(2,1)} %get-tuple-element.12), calls=%async_computation.1 | async-start | bytes 3145728 | tf_op jit(solution)/shard_map/all_to_all | solution.py:204
  58.2 5.0 %collective-permute-start.6 = (f32[128,128]{1,0:T(8,128)S(1)}, f32[128,128]{1,0:T(8,128)S(1)}, u32[]{:S(2)}, u32[]{:S(2)}) collective-permute-start(f32[128,128]{1,0:T(8,128)S(1)} %get-tuple-element.13), channel_id=1, source_target_pairs={{0,64},{16,80},{32,96},{48,112},{64,0},{80,16},{96,32},{112,48},{1... | collective-permute-start | bytes 196616 | tf_op jit(solution)/shard_map/ppermute | solution.py:181
  63.2 6.2 %collective-permute-start.7 = (f32[128,128]{1,0:T(8,128)S(1)}, f32[128,128]{1,0:T(8,128)S(1)}, u32[]{:S(2)}, u32[]{:S(2)}) collective-permute-start(f32[128,128]{1,0:T(8,128)S(1)} %add.15), channel_id=1, source_target_pairs={{0,128},{16,144},{32,160},{48,176},{64,192},{80,208},{96,224},{112... | collective-permute-start | bytes 196616 | tf_op jit(solution)/shard_map/ppermute | solution.py:181
  69.4 6.5 %collective-permute-start.8 = (f32[128,128]{1,0:T(8,128)S(1)}, f32[128,128]{1,0:T(8,128)S(1)}, u32[]{:S(2)}, u32[]{:S(2)}) collective-permute-start(f32[128,128]{1,0:T(8,128)S(1)} %add.16), channel_id=1, source_target_pairs={{0,448},{16,464},{32,480},{48,496},{64,384},{80,400},{96,416},{112... | collective-permute-start | bytes 196616 | tf_op jit(solution)/shard_map/ppermute | solution.py:209
  75.9 5.9 %collective-permute-start.9 = (f32[128,128]{1,0:T(8,128)S(1)}, f32[128,128]{1,0:T(8,128)S(1)}, u32[]{:S(2)}, u32[]{:S(2)}) collective-permute-start(f32[128,128]{1,0:T(8,128)S(1)} %add.17), channel_id=1, source_target_pairs={{0,32},{16,48},{32,0},{48,16},{64,96},{80,112},{96,64},{112,80},{1... | collective-permute-start | bytes 196616 | tf_op jit(solution)/shard_map/ppermute | solution.py:181
  81.8 7.2 %collective-permute-start.10 = (f32[128,128]{1,0:T(8,128)S(1)}, f32[128,128]{1,0:T(8,128)S(1)}, u32[]{:S(2)}, u32[]{:S(2)}) collective-permute-start(f32[128,128]{1,0:T(8,128)S(1)} %add.18), channel_id=1, source_target_pairs={{0,40},{1,41},{2,42},{3,43},{4,44},{5,45},{6,46},{7,47},{8,32},{9,... | collective-permute-start | bytes 196616 | tf_op jit(solution)/shard_map/ppermute | solution.py:213

commit v17 on v16

--- a/solution.py
+++ b/solution.py
@@ -27,8 +27,8 @@
     below = gap > planes // 2
     steps = jnp.where(below, planes - gap, gap)
     receiver = jnp.where(gap == 0, 1 - core, jnp.where(below, 0, 1))
-    first = jnp.where(steps == 2, jnp.where(same_chip, 2, 4), jnp.where(same_chip, 0, 7))
-    place = jnp.where(gap == 0, 6, first + jnp.where(core == receiver, 0, 1))
+    first = jnp.where(steps == 2, jnp.where(same_chip, 7, 5), jnp.where(same_chip, 0, 3))
+    place = jnp.where(gap == 0, 2, first + jnp.where(core == receiver, 0, 1))
     slot = 2 + place + jnp.where(receiver == lax.rem(row, 2), 0, 9)
     slot = jnp.where((gap == 0) & same_chip, jnp.where(same_core, 0, 1), slot)
     return slot * blocks + lax.rem(block, blocks)
@@ -180,7 +180,7 @@
     def partner(value, axis, bit):
         return lax.ppermute(value, axis, [(i, i ^ bit) for i in range(lax.axis_size(axis))])
 
-    received = jnp.concatenate([near, far, across_far, across, halves])
+    received = jnp.concatenate([near, across, across_far, far, halves])
     other = swap(received, 1)
 
     sends, wsum = pl.pallas_call(

time: 98.7 us -> 103 us (1.044)
  the two profiles are of different devices: /device:TPU:1 before, /device:TPU:8 now
where the time goes in v17:
time: 103 us; the launch traced here: 102 us
  starting transfers between devices  50.5 us (49%)
  waiting for transfers between devices  40.7 us (40%)
  Pallas kernels  6.54 us (6%)
  local copies, waits for them, and re-layouts  3.26 us (3%)
    ppermute x3, waiting for transfers between devices, partner(): lax.ppermute(value, axis, [(i, i ^ bit) for i in range(lax.axis_size(axis...  13.6 us
    ppermute x3, waiting for transfers between devices, to_plane(): lax.ppermute(value, 'row', [pair for pair in pairs if pair[0] % PLANE in...  10.8 us
    ppermute x3, starting transfers between devices, to_plane(): lax.ppermute(value, 'row', [pair for pair in pairs if pair[0] % PLANE in...  10.5 us
    all_to_all x1, starting transfers between devices, on_device(): wz = lax.all_to_all(wpart, 'col', 0, 0, axis_index_groups=groups)  10.5 us
    all_to_all x1, starting transfers between devices, on_device(): got = lax.all_to_all(sends, 'col', 0, 0)  9.2 us
    ppermute x3, starting transfers between devices, swap(): return lax.ppermute(value, 'row', [(i, i ^ bit) for i in range(row_count)])  7.24 us
    ppermute x1, waiting for transfers between devices, on_device(): wsum = wsum + lax.ppermute(wsum, 'row', mirrored)  6.25 us
    ppermute x3, starting transfers between devices, partner(): lax.ppermute(value, axis, [(i, i ^ bit) for i in range(lax.axis_size(axis...  5.8 us
  transfers between devices with their start and end apart: 13, of which 9 were waited for; matrix products, arithmetic and copies ran while one was open for 3% of the time, Pallas kernels for 0%

profile of v17, /device:TPU:8, one launch (start us, length us, event | category | flops | bytes accessed | tf_op | source)
XLA Modules:
  0.0 101.9 jit_solution(2793304415129880042)
XLA Ops:
  0.6 2.5 %adjoint.1 = (bf16[384,128]{1,0:T(8,128)(2,1)}, bf16[8,128,128]{2,1,0:T(8,128)(2,1)}, s32[1,32]{1,0:T(1,128)}, s32[1,32]{1,0:T(1,128)}) custom-call(s32[3,128]{1,0:T(4,128)} %bitcast.3, bf16[384,128]{1,0:T(8,128)(2,1)} %cot_in.1, bf16[384,128]{1,0:T(8,128)(2,1)} %pre_in.1, bf16[384,128]{1,0:T(8,128)(2,1)} %agg_in.1, bf16[128,128]{1,0:T(8,128)(2,1)} %w_in.1, ...), custom_call_target="tpu_custom_call" | custom-call | tf_op jit(solution)/shard_map/adjoint/pallas_call | solution.py:136
  3.1 1.9 %collective-permute-start = (bf16[384,128]{1,0:T(8,128)(2,1)}, bf16[384,128]{1,0:T(8,128)(2,1)S(1)}, u32[]{:S(2)}, u32[]{:S(2)}) collective-permute-start(bf16[384,128]{1,0:T(8,128)(2,1)} %get-tuple-element.10.own), channel_id=1, source_target_pairs={{0,16},{16,0},{32,48},{48,32},{64,80},{80,64},{96,112},{112,96},{1... | collective-permute-start | bytes 294920 | tf_op jit(solution)/shard_map/ppermute | solution.py:156
  5.1 1.5 %constant_dynamic-update-slice_fusion.1 = bf16[768,128]{1,0:T(8,128)(2,1)} fusion(bf16[384,128]{1,0:T(8,128)(2,1)} %get-tuple-element.10.own), kind=kLoop, calls=%fused_computation.2 | loop fusion | bytes 196608
  6.6 0.0 collective-permute-done.beside
  6.6 0.6 constant_dynamic-update-slice_fusion
  7.2 3.5 %collective-permute-start.1 = (bf16[768,128]{1,0:T(8,128)(2,1)}, bf16[768,128]{1,0:T(8,128)(2,1)S(1)}, u32[]{:S(2)}, u32[]{:S(2)}) collective-permute-start(bf16[768,128]{1,0:T(8,128)(2,1)} %constant_dynamic-update-slice_fusion), channel_id=1, source_target_pairs={{0,64},{16,464},{32,96},{48,496},{64,128},{80,16},{96,160},{112,48... | collective-permute-start | bytes 589832 | tf_op jit(solution)/shard_map/ppermute | solution.py:160
  10.7 0.0 copy-start
  10.7 0.0 copy-start.1
  10.7 0.0 copy-start.2
  10.8 0.0 copy-start.3
  10.8 10.5 %all-to-all-start = ((bf16[8,128,128]{2,1,0:T(8,128)(2,1)}), bf16[8,128,128]{2,1,0:T(8,128)(2,1)S(1)}, u32[]{:S(2)}, u32[]{:S(2)}) async-start(bf16[8,128,128]{2,1,0:T(8,128)(2,1)} %get-tuple-element.11), calls=%async_computation | async-start | bytes 524288 | tf_op jit(solution)/shard_map/all_to_all | solution.py:170
  21.2 0.0 collective-permute-done.1
  21.3 3.4 %collective-permute-start.2 = (bf16[1152,128]{1,0:T(8,128)(2,1)S(1)}, bf16[1152,128]{1,0:T(8,128)(2,1)S(1)}, u32[]{:S(2)}, u32[]{:S(2)}) collective-permute-start(bf16[1152,128]{1,0:T(8,128)(2,1)S(1)} %pad_maximum_fusion), channel_id=1, source_target_pairs={{0,32},{16,48},{32,0},{48,16},{64,96},{80,112},{96,64},{112,80},{1... | collective-permute-start | bytes 884744 | tf_op jit(solution)/shard_map/ppermute | solution.py:156
  24.7 5.7 %collective-permute-start.4 = (bf16[768,128]{1,0:T(8,128)(2,1)}, bf16[768,128]{1,0:T(8,128)(2,1)S(1)}, u32[]{:S(2)}, u32[]{:S(2)}) collective-permute-start(bf16[768,128]{1,0:T(8,128)(2,1)} %constant_dynamic-update-slice_fusion), channel_id=1, source_target_pairs={{0,128},{16,400},{32,160},{48,432},{64,192},{80,464},{96,224},{112... | collective-permute-start | bytes 589832 | tf_op jit(solution)/shard_map/ppermute | solution.py:160
  30.4 1.3 %collective-permute-start.3 = (bf16[768,128]{1,0:T(8,128)(2,1)}, bf16[768,128]{1,0:T(8,128)(2,1)}, u32[]{:S(2)}, u32[]{:S(2)}) collective-permute-start(bf16[768,128]{1,0:T(8,128)(2,1)} %constant_dynamic-update-slice_fusion), channel_id=1, source_target_pairs={{16,432},{32,128},{80,496},{96,192},{144,48},{160,256},{208,112},{... | collective-permute-start | bytes 589832 | tf_op jit(solution)/shard_map/ppermute | solution.py:160
  31.7 0.7 all-to-all-done.parts_ref
  32.4 0.0 collective-permute-done.2
  32.5 10.8 %collective-permute-done.3 = bf16[768,128]{1,0:T(8,128)(2,1)} collective-permute-done((bf16[768,128]{1,0:T(8,128)(2,1)}, bf16[768,128]{1,0:T(8,128)(2,1)}, u32[]{:S(2)}, u32[]{:S(2)}) %collective-permute-start.3) | collective-permute-done | bytes 196640 | tf_op jit(solution)/shard_map/ppermute | solution.py:160
  43.2 1.0 constant_dynamic-update-slice_fusion.4
  44.2 0.0 collective-permute-done.4
  44.3 1.9 %collective-permute-start.5 = (bf16[3712,128]{1,0:T(8,128)(2,1)S(1)}, bf16[3712,128]{1,0:T(8,128)(2,1)S(1)}, u32[]{:S(2)}, u32[]{:S(2)}) collective-permute-start(bf16[3712,128]{1,0:T(8,128)(2,1)S(1)} %constant_dynamic-update-slice_fusion.2.ours), channel_id=1, source_target_pairs={{0,16},{16,0},{32,48},{48,32},{64,80},{80,64},{96,112},{112,96},{1... | collective-permute-start | bytes 2850824 | tf_op jit(solution)/shard_map/ppermute | solution.py:156
  46.2 2.5 %collective-permute-done.5.theirs = bf16[3712,128]{1,0:T(8,128)(2,1)S(1)} collective-permute-done((bf16[3712,128]{1,0:T(8,128)(2,1)S(1)}, bf16[3712,128]{1,0:T(8,128)(2,1)S(1)}, u32[]{:S(2)}, u32[]{:S(2)}) %collective-permute-start.5) | collective-permute-done | bytes 950304 | tf_op jit(solution)/shard_map/ppermute | solution.py:156
  48.7 0.0 copy-done
  48.7 0.0 copy-done.1
  48.7 0.0 copy-done.2
  48.7 0.0 copy-done.3
  48.7 3.1 %tiles.1 = (bf16[16,384,128]{2,1,0:T(8,128)(2,1)}, f32[128,128]{1,0:T(8,128)S(1)}) custom-call(s32[1,32]{1,0:T(1,128)S(1)} %copy-done.2, s32[1,32]{1,0:T(1,128)S(1)} %copy-done.3, bf16[32,128,128]{2,1,0:T(8,128)(2,1)S(1)} %copy-done, bf16[384,128]{1,0:T(8,128)(2,1)S(1)} %copy-done.1, bf16[384,128]{1,0:T(8,128)(2,1)S(1)} %collective-permute-done.beside, ...), custom_call_target="tpu_custom_call" | custom-call | flops 134217728 | bytes 6291456 | tf_op jit(solution)/shard_map/tiles/pallas_call | solution.py:186
  51.9 9.2 %all-to-all-start.1 = ((bf16[16,384,128]{2,1,0:T(8,128)(2,1)}), bf16[16,384,128]{2,1,0:T(8,128)(2,1)S(1)}, u32[]{:S(2)}, u32[]{:S(2)}) async-start(bf16[16,384,128]{2,1,0:T(8,128)(2,1)} %get-tuple-element.12), calls=%async_computation.1 | async-start | bytes 3145728 | tf_op jit(solution)/shard_map/all_to_all | solution.py:204
  61.1 1.9 %collective-permute-start.6 = (f32[128,128]{1,0:T(8,128)S(1)}, f32[128,128]{1,0:T(8,128)S(1)}, u32[]{:S(2)}, u32[]{:S(2)}) collective-permute-start(f32[128,128]{1,0:T(8,128)S(1)} %get-tuple-element.13), channel_id=1, source_target_pairs={{0,64},{16,80},{32,96},{48,112},{64,0},{80,16},{96,32},{112,48},{1... | collective-permute-start | bytes 196616 | tf_op jit(solution)/shard_map/ppermute | solution.py:181
  63.0 4.2 %collective-permute-done.6 = f32[128,128]{1,0:T(8,128)S(1)} collective-permute-done((f32[128,128]{1,0:T(8,128)S(1)}, f32[128,128]{1,0:T(8,128)S(1)}, u32[]{:S(2)}, u32[]{:S(2)}) %collective-permute-start.6) | collective-permute-done | bytes 65568 | tf_op jit(solution)/shard_map/ppermute | solution.py:181
  67.2 2.0 %collective-permute-start.7 = (f32[128,128]{1,0:T(8,128)S(1)}, f32[128,128]{1,0:T(8,128)S(1)}, u32[]{:S(2)}, u32[]{:S(2)}) collective-permute-start(f32[128,128]{1,0:T(8,128)S(1)} %add.15), channel_id=1, source_target_pairs={{0,128},{16,144},{32,160},{48,176},{64,192},{80,208},{96,224},{112... | collective-permute-start | bytes 196616 | tf_op jit(solution)/shard_map/ppermute | solution.py:181
  69.2 5.1 %collective-permute-done.7 = f32[128,128]{1,0:T(8,128)S(1)} collective-permute-done((f32[128,128]{1,0:T(8,128)S(1)}, f32[128,128]{1,0:T(8,128)S(1)}, u32[]{:S(2)}, u32[]{:S(2)}) %collective-permute-start.7) | collective-permute-done | bytes 65568 | tf_op jit(solution)/shard_map/ppermute | solution.py:181
  74.3 2.9 %collective-permute-start.8 = (f32[128,128]{1,0:T(8,128)S(1)}, f32[128,128]{1,0:T(8,128)S(1)}, u32[]{:S(2)}, u32[]{:S(2)}) collective-permute-start(f32[128,128]{1,0:T(8,128)S(1)} %add.16), channel_id=1, source_target_pairs={{0,448},{16,464},{32,480},{48,496},{64,384},{80,400},{96,416},{112... | collective-permute-start | bytes 196616 | tf_op jit(solution)/shard_map/ppermute | solution.py:209
  77.2 6.2 %collective-permute-done.8 = f32[128,128]{1,0:T(8,128)S(1)} collective-permute-done((f32[128,128]{1,0:T(8,128)S(1)}, f32[128,128]{1,0:T(8,128)S(1)}, u32[]{:S(2)}, u32[]{:S(2)}) %collective-permute-start.8) | collective-permute-done | bytes 65568 | tf_op jit(solution)/shard_map/ppermute | solution.py:209
  83.5 1.9 %collective-permute-start.9 = (f32[128,128]{1,0:T(8,128)S(1)}, f32[128,128]{1,0:T(8,128)S(1)}, u32[]{:S(2)}, u32[]{:S(2)}) collective-permute-start(f32[128,128]{1,0:T(8,128)S(1)} %add.17), channel_id=1, source_target_pairs={{0,32},{16,48},{32,0},{48,16},{64,96},{80,112},{96,64},{112,80},{1... | collective-permute-start | bytes 196616 | tf_op jit(solution)/shard_map/ppermute | solution.py:181
  85.4 4.3 %collective-permute-done.9 = f32[128,128]{1,0:T(8,128)S(1)} collective-permute-done((f32[128,128]{1,0:T(8,128)S(1)}, f32[128,128]{1,0:T(8,128)S(1)}, u32[]{:S(2)}, u32[]{:S(2)}) %collective-permute-start.9) | collective-permute-done | bytes 65568 | tf_op jit(solution)/shard_map/ppermute | solution.py:181
  89.7 4.4 %collective-permute-start.10 = (f32[128,128]{1,0:T(8,128)S(1)}, f32[128,128]{1,0:T(8,128)S(1)}, u32[]{:S(2)}, u32[]{:S(2)}) collective-permute-start(f32[128,128]{1,0:T(8,128)S(1)} %add.18), channel_id=1, source_target_pairs={{0,40},{1,41},{2,42},{3,43},{4,44},{5,45},{6,46},{7,47},{8,32},{9,... | collective-permute-start | bytes 196616 | tf_op jit(solution)/shard_map/ppermute | solution.py:213
  94.2 3.1 %collective-permute-done.10 = f32[128,128]{1,0:T(8,128)S(1)} collective-permute-done((f32[128,128]{1,0:T(8,128)S(1)}, f32[128,128]{1,0:T(8,128)S(1)}, u32[]{:S(2)}, u32[]{:S(2)}) %collective-permute-start.10) | collective-permute-done | bytes 65568 | tf_op jit(solution)/shard_map/ppermute | solution.py:213
  97.2 3.8 %all-to-all-done.1.got_ref = bf16[16,384,128]{2,1,0:T(8,128)(2,1)S(1)} async-done(((bf16[16,384,128]{2,1,0:T(8,128)(2,1)}), bf16[16,384,128]{2,1,0:T(8,128)(2,1)S(1)}, u32[]{:S(2)}, u32[]{:S(2)}) %all-to-all-start.1) | async-done | bytes 1572896 | tf_op jit(solution)/shard_map/all_to_all | solution.py:204
  101.0 0.9 finish.1
  (11 shorter events, 0.2 us)
Async XLA Ops:
  3.1 3.5 %collective-permute-start = (bf16[384,128]{1,0:T(8,128)(2,1)}, bf16[384,128]{1,0:T(8,128)(2,1)S(1)}, u32[]{:S(2)}, u32[]{:S(2)}) collective-permute-start(bf16[384,128]{1,0:T(8,128)(2,1)} %get-tuple-element.10.own), channel_id=1, source_target_pairs={{0,16},{16,0},{32,48},{48,32},{64,80},{80,64},{96,112},{112,96},{1... | collective-permute-start | bytes 294920 | tf_op jit(solution)/shard_map/ppermute | solution.py:156
  7.2 14.0 %collective-permute-start.1 = (bf16[768,128]{1,0:T(8,128)(2,1)}, bf16[768,128]{1,0:T(8,128)(2,1)S(1)}, u32[]{:S(2)}, u32[]{:S(2)}) collective-permute-start(bf16[768,128]{1,0:T(8,128)(2,1)} %constant_dynamic-update-slice_fusion), channel_id=1, source_target_pairs={{0,64},{16,464},{32,96},{48,496},{64,128},{80,16},{96,160},{112,48... | collective-permute-start | bytes 589832 | tf_op jit(solution)/shard_map/ppermute | solution.py:160
  10.7 38.0 %copy-start = (bf16[32,128,128]{2,1,0:T(8,128)(2,1)S(1)}, bf16[32,128,128]{2,1,0:T(8,128)(2,1)}, u32[]{:S(2)}) copy-start(bf16[32,128,128]{2,1,0:T(8,128)(2,1)} %tiles_ref.1) | copy-start | bytes 3145732
  10.7 38.0 %copy-start.1 = (bf16[384,128]{1,0:T(8,128)(2,1)S(1)}, bf16[384,128]{1,0:T(8,128)(2,1)}, u32[]{:S(2)}) copy-start(bf16[384,128]{1,0:T(8,128)(2,1)} %get-tuple-element.10.own) | copy-start | bytes 294916
  10.7 37.9 %copy-start.2 = (s32[1,32]{1,0:T(1,128)S(1)}, s32[1,32]{1,0:T(1,128)}, u32[]{:S(2)}) copy-start(s32[1,32]{1,0:T(1,128)} %get-tuple-element.8.from_ref) | copy-start | bytes 388
  10.8 37.9 %copy-start.3 = (s32[1,32]{1,0:T(1,128)S(1)}, s32[1,32]{1,0:T(1,128)}, u32[]{:S(2)}) copy-start(s32[1,32]{1,0:T(1,128)} %get-tuple-element.9.to_ref) | copy-start | bytes 388
  10.8 21.6 %all-to-all-start = ((bf16[8,128,128]{2,1,0:T(8,128)(2,1)}), bf16[8,128,128]{2,1,0:T(8,128)(2,1)S(1)}, u32[]{:S(2)}, u32[]{:S(2)}) async-start(bf16[8,128,128]{2,1,0:T(8,128)(2,1)} %get-tuple-element.11), calls=%async_computation | async-start | bytes 524288 | tf_op jit(solution)/shard_map/all_to_all | solution.py:170
  21.3 11.1 %collective-permute-start.2 = (bf16[1152,128]{1,0:T(8,128)(2,1)S(1)}, bf16[1152,128]{1,0:T(8,128)(2,1)S(1)}, u32[]{:S(2)}, u32[]{:S(2)}) collective-permute-start(bf16[1152,128]{1,0:T(8,128)(2,1)S(1)} %pad_maximum_fusion), channel_id=1, source_target_pairs={{0,32},{16,48},{32,0},{48,16},{64,96},{80,112},{96,64},{112,80},{1... | collective-permute-start | bytes 884744 | tf_op jit(solution)/shard_map/ppermute | solution.py:156
  24.7 19.5 %collective-permute-start.4 = (bf16[768,128]{1,0:T(8,128)(2,1)}, bf16[768,128]{1,0:T(8,128)(2,1)S(1)}, u32[]{:S(2)}, u32[]{:S(2)}) collective-permute-start(bf16[768,128]{1,0:T(8,128)(2,1)} %constant_dynamic-update-slice_fusion), channel_id=1, source_target_pairs={{0,128},{16,400},{32,160},{48,432},{64,192},{80,464},{96,224},{112... | collective-permute-start | bytes 589832 | tf_op jit(solution)/shard_map/ppermute | solution.py:160
  30.4 12.9 %collective-permute-start.3 = (bf16[768,128]{1,0:T(8,128)(2,1)}, bf16[768,128]{1,0:T(8,128)(2,1)}, u32[]{:S(2)}, u32[]{:S(2)}) collective-permute-start(bf16[768,128]{1,0:T(8,128)(2,1)} %constant_dynamic-update-slice_fusion), channel_id=1, source_target_pairs={{16,432},{32,128},{80,496},{96,192},{144,48},{160,256},{208,112},{... | collective-permute-start | bytes 589832 | tf_op jit(solution)/shard_map/ppermute | solution.py:160
  44.3 4.4 %collective-permute-start.5 = (bf16[3712,128]{1,0:T(8,128)(2,1)S(1)}, bf16[3712,128]{1,0:T(8,128)(2,1)S(1)}, u32[]{:S(2)}, u32[]{:S(2)}) collective-permute-start(bf16[3712,128]{1,0:T(8,128)(2,1)S(1)} %constant_dynamic-update-slice_fusion.2.ours), channel_id=1, source_target_pairs={{0,16},{16,0},{32,48},{48,32},{64,80},{80,64},{96,112},{112,96},{1... | collective-permute-start | bytes 2850824 | tf_op jit(solution)/shard_map/ppermute | solution.py:156
  51.9 49.1 %all-to-all-start.1 = ((bf16[16,384,128]{2,1,0:T(8,128)(2,1)}), bf16[16,384,128]{2,1,0:T(8,128)(2,1)S(1)}, u32[]{:S(2)}, u32[]{:S(2)}) async-start(bf16[16,384,128]{2,1,0:T(8,128)(2,1)} %get-tuple-element.12), calls=%async_computation.1 | async-start | bytes 3145728 | tf_op jit(solution)/shard_map/all_to_all | solution.py:204
  61.1 6.2 %collective-permute-start.6 = (f32[128,128]{1,0:T(8,128)S(1)}, f32[128,128]{1,0:T(8,128)S(1)}, u32[]{:S(2)}, u32[]{:S(2)}) collective-permute-start(f32[128,128]{1,0:T(8,128)S(1)} %get-tuple-element.13), channel_id=1, source_target_pairs={{0,64},{16,80},{32,96},{48,112},{64,0},{80,16},{96,32},{112,48},{1... | collective-permute-start | bytes 196616 | tf_op jit(solution)/shard_map/ppermute | solution.py:181
  67.2 7.1 %collective-permute-start.7 = (f32[128,128]{1,0:T(8,128)S(1)}, f32[128,128]{1,0:T(8,128)S(1)}, u32[]{:S(2)}, u32[]{:S(2)}) collective-permute-start(f32[128,128]{1,0:T(8,128)S(1)} %add.15), channel_id=1, source_target_pairs={{0,128},{16,144},{32,160},{48,176},{64,192},{80,208},{96,224},{112... | collective-permute-start | bytes 196616 | tf_op jit(solution)/shard_map/ppermute | solution.py:181
  74.3 9.2 %collective-permute-start.8 = (f32[128,128]{1,0:T(8,128)S(1)}, f32[128,128]{1,0:T(8,128)S(1)}, u32[]{:S(2)}, u32[]{:S(2)}) collective-permute-start(f32[128,128]{1,0:T(8,128)S(1)} %add.16), channel_id=1, source_target_pairs={{0,448},{16,464},{32,480},{48,496},{64,384},{80,400},{96,416},{112... | collective-permute-start | bytes 196616 | tf_op jit(solution)/shard_map/ppermute | solution.py:209
  83.5 6.2 %collective-permute-start.9 = (f32[128,128]{1,0:T(8,128)S(1)}, f32[128,128]{1,0:T(8,128)S(1)}, u32[]{:S(2)}, u32[]{:S(2)}) collective-permute-start(f32[128,128]{1,0:T(8,128)S(1)} %add.17), channel_id=1, source_target_pairs={{0,32},{16,48},{32,0},{48,16},{64,96},{80,112},{96,64},{112,80},{1... | collective-permute-start | bytes 196616 | tf_op jit(solution)/shard_map/ppermute | solution.py:181
  89.7 7.5 %collective-permute-start.10 = (f32[128,128]{1,0:T(8,128)S(1)}, f32[128,128]{1,0:T(8,128)S(1)}, u32[]{:S(2)}, u32[]{:S(2)}) collective-permute-start(f32[128,128]{1,0:T(8,128)S(1)} %add.18), channel_id=1, source_target_pairs={{0,40},{1,41},{2,42},{3,43},{4,44},{5,45},{6,46},{7,47},{8,32},{9,... | collective-permute-start | bytes 196616 | tf_op jit(solution)/shard_map/ppermute | solution.py:213

commit v18 on v16

--- a/solution.py
+++ b/solution.py
@@ -27,7 +27,7 @@
     below = gap > planes // 2
     steps = jnp.where(below, planes - gap, gap)
     receiver = jnp.where(gap == 0, 1 - core, jnp.where(below, 0, 1))
-    first = jnp.where(steps == 2, jnp.where(same_chip, 2, 4), jnp.where(same_chip, 0, 7))
+    first = jnp.where(steps == 2, jnp.where(same_chip, 4, 2), jnp.where(same_chip, 0, 7))
     place = jnp.where(gap == 0, 6, first + jnp.where(core == receiver, 0, 1))
     slot = 2 + place + jnp.where(receiver == lax.rem(row, 2), 0, 9)
     slot = jnp.where((gap == 0) & same_chip, jnp.where(same_core, 0, 1), slot)
@@ -180,7 +180,7 @@
     def partner(value, axis, bit):
         return lax.ppermute(value, axis, [(i, i ^ bit) for i in range(lax.axis_size(axis))])
 
-    received = jnp.concatenate([near, far, across_far, across, halves])
+    received = jnp.concatenate([near, across_far, far, across, halves])
     other = swap(received, 1)
 
     sends, wsum = pl.pallas_call(

time: 98.7 us -> 101 us (1.023)
  waiting for transfers between devices: 33.2 us -> 34.5 us
    ppermute x3, waiting for transfers between devices: 5.93 us -> 9.51 us  [swap(): return lax.ppermute(value, 'row', [(i, i ^ bit) for i in range(row_count)])]
    ppermute x3, waiting for transfers between devices: 4.61 us -> 3.23 us  [to_plane(): lax.ppermute(value, 'row', [pair for pair in pairs if pair[0] % PLANE in...]
where the time goes in v18:
time: 101 us; the launch traced here: 99.2 us
  starting transfers between devices  56.1 us (56%)
  waiting for transfers between devices  34.5 us (34%)
  Pallas kernels  6.54 us (6%)
  local copies, waits for them, and re-layouts  1.06 us (1%)
    ppermute x3, starting transfers between devices, swap(): return lax.ppermute(value, 'row', [(i, i ^ bit) for i in range(row_count)])  13.1 us
    ppermute x3, waiting for transfers between devices, swap(): return lax.ppermute(value, 'row', [(i, i ^ bit) for i in range(row_count)])  9.51 us
    ppermute x3, starting transfers between devices, to_plane(): lax.ppermute(value, 'row', [pair for pair in pairs if pair[0] % PLANE in...  9.47 us
    all_to_all x1, starting transfers between devices, on_device(): got = lax.all_to_all(sends, 'col', 0, 0)  9.31 us
    ppermute x3, waiting for transfers between devices, partner(): lax.ppermute(value, axis, [(i, i ^ bit) for i in range(lax.axis_size(axis...  8.52 us
    ppermute x3, starting transfers between devices, partner(): lax.ppermute(value, axis, [(i, i ^ bit) for i in range(lax.axis_size(axis...  8.51 us
    all_to_all x1, starting transfers between devices, on_device(): wz = lax.all_to_all(wpart, 'col', 0, 0, axis_index_groups=groups)  7.98 us
    all_to_all x1, waiting for transfers between devices, on_device(): got = lax.all_to_all(sends, 'col', 0, 0)  7.17 us
  transfers between devices with their start and end apart: 13, of which 10 were waited for; matrix products, arithmetic and copies ran while one was open for 1% of the time, Pallas kernels for 0%

profile of v18, /device:TPU:1, one launch (start us, length us, event | category | flops | bytes accessed | tf_op | source)
XLA Modules:
  0.0 99.2 jit_solution(665036173078711931)
XLA Ops:
  0.6 2.5 %adjoint.1 = (bf16[384,128]{1,0:T(8,128)(2,1)}, bf16[8,128,128]{2,1,0:T(8,128)(2,1)}, s32[1,32]{1,0:T(1,128)}, s32[1,32]{1,0:T(1,128)}) custom-call(s32[3,128]{1,0:T(4,128)} %bitcast.3, bf16[384,128]{1,0:T(8,128)(2,1)} %cot_in.1, bf16[384,128]{1,0:T(8,128)(2,1)} %pre_in.1, bf16[384,128]{1,0:T(8,128)(2,1)} %agg_in.1, bf16[128,128]{1,0:T(8,128)(2,1)} %w_in.1, ...), custom_call_target="tpu_custom_call" | custom-call | tf_op jit(solution)/shard_map/adjoint/pallas_call | solution.py:136
  3.1 8.8 %collective-permute-start = (bf16[384,128]{1,0:T(8,128)(2,1)}, bf16[384,128]{1,0:T(8,128)(2,1)S(1)}, u32[]{:S(2)}, u32[]{:S(2)}) collective-permute-start(bf16[384,128]{1,0:T(8,128)(2,1)} %get-tuple-element.10.own), channel_id=1, source_target_pairs={{0,16},{16,0},{32,48},{48,32},{64,80},{80,64},{96,112},{112,96},{1... | collective-permute-start | bytes 294920 | tf_op jit(solution)/shard_map/ppermute | solution.py:156
  11.9 0.9 constant_dynamic-update-slice_fusion.1
  12.8 0.2 collective-permute-done.beside
  13.1 1.9 %collective-permute-start.1 = (bf16[768,128]{1,0:T(8,128)(2,1)S(1)}, bf16[768,128]{1,0:T(8,128)(2,1)S(1)}, u32[]{:S(2)}, u32[]{:S(2)}) collective-permute-start(bf16[768,128]{1,0:T(8,128)(2,1)S(1)} %constant_dynamic-update-slice_fusion), channel_id=1, source_target_pairs={{0,64},{16,464},{32,96},{48,496},{64,128},{80,16},{96,160},{112,48... | collective-permute-start | bytes 589832 | tf_op jit(solution)/shard_map/ppermute | solution.py:160
  15.0 0.0 copy-start
  15.0 0.0 copy-start.1
  15.0 0.0 copy-start.2
  15.0 0.0 copy-start.3
  15.0 8.0 %all-to-all-start = ((bf16[8,128,128]{2,1,0:T(8,128)(2,1)}), bf16[8,128,128]{2,1,0:T(8,128)(2,1)S(1)}, u32[]{:S(2)}, u32[]{:S(2)}) async-start(bf16[8,128,128]{2,1,0:T(8,128)(2,1)} %get-tuple-element.11), calls=%async_computation | async-start | bytes 524288 | tf_op jit(solution)/shard_map/all_to_all | solution.py:170
  23.0 3.7 %collective-permute-start.3 = (bf16[768,128]{1,0:T(8,128)(2,1)S(1)}, bf16[768,128]{1,0:T(8,128)(2,1)S(1)}, u32[]{:S(2)}, u32[]{:S(2)}) collective-permute-start(bf16[768,128]{1,0:T(8,128)(2,1)S(1)} %constant_dynamic-update-slice_fusion), channel_id=1, source_target_pairs={{0,128},{16,400},{32,160},{48,432},{64,192},{80,464},{96,224},{112... | collective-permute-start | bytes 589832 | tf_op jit(solution)/shard_map/ppermute | solution.py:160
  26.8 3.8 %collective-permute-start.2 = (bf16[768,128]{1,0:T(8,128)(2,1)S(1)}, bf16[768,128]{1,0:T(8,128)(2,1)S(1)}, u32[]{:S(2)}, u32[]{:S(2)}) collective-permute-start(bf16[768,128]{1,0:T(8,128)(2,1)S(1)} %constant_dynamic-update-slice_fusion), channel_id=1, source_target_pairs={{16,432},{32,128},{80,496},{96,192},{144,48},{160,256},{208,112},{... | collective-permute-start | bytes 589832 | tf_op jit(solution)/shard_map/ppermute | solution.py:160
  30.6 0.0 collective-permute-done.1
  30.6 1.9 %collective-permute-start.4 = (bf16[1152,128]{1,0:T(8,128)(2,1)S(1)}, bf16[1152,128]{1,0:T(8,128)(2,1)S(1)}, u32[]{:S(2)}, u32[]{:S(2)}) collective-permute-start(bf16[1152,128]{1,0:T(8,128)(2,1)S(1)} %pad_maximum_fusion), channel_id=1, source_target_pairs={{0,32},{16,48},{32,0},{48,16},{64,96},{80,112},{96,64},{112,80},{1... | collective-permute-start | bytes 884744 | tf_op jit(solution)/shard_map/ppermute | solution.py:156
  32.6 3.2 %collective-permute-done.2 = bf16[768,128]{1,0:T(8,128)(2,1)S(1)} collective-permute-done((bf16[768,128]{1,0:T(8,128)(2,1)S(1)}, bf16[768,128]{1,0:T(8,128)(2,1)S(1)}, u32[]{:S(2)}, u32[]{:S(2)}) %collective-permute-start.2) | collective-permute-done | bytes 196640 | tf_op jit(solution)/shard_map/ppermute | solution.py:160
  35.8 0.0 collective-permute-done.3
  35.9 0.0 all-to-all-done.parts_ref
  36.0 7.2 %collective-permute-done.4 = bf16[1152,128]{1,0:T(8,128)(2,1)S(1)} collective-permute-done((bf16[1152,128]{1,0:T(8,128)(2,1)S(1)}, bf16[1152,128]{1,0:T(8,128)(2,1)S(1)}, u32[]{:S(2)}, u32[]{:S(2)}) %collective-permute-start.4) | collective-permute-done | bytes 294944 | tf_op jit(solution)/shard_map/ppermute | solution.py:156
  43.2 2.4 %collective-permute-start.5 = (bf16[3712,128]{1,0:T(8,128)(2,1)S(1)}, bf16[3712,128]{1,0:T(8,128)(2,1)S(1)}, u32[]{:S(2)}, u32[]{:S(2)}) collective-permute-start(bf16[3712,128]{1,0:T(8,128)(2,1)S(1)} %constant_dynamic-update-slice_fusion.2.ours), channel_id=1, source_target_pairs={{0,16},{16,0},{32,48},{48,32},{64,80},{80,64},{96,112},{112,96},{1... | collective-permute-start | bytes 2850824 | tf_op jit(solution)/shard_map/ppermute | solution.py:156
  45.6 2.1 %collective-permute-done.5.theirs = bf16[3712,128]{1,0:T(8,128)(2,1)S(1)} collective-permute-done((bf16[3712,128]{1,0:T(8,128)(2,1)S(1)}, bf16[3712,128]{1,0:T(8,128)(2,1)S(1)}, u32[]{:S(2)}, u32[]{:S(2)}) %collective-permute-start.5) | collective-permute-done | bytes 950304 | tf_op jit(solution)/shard_map/ppermute | solution.py:156
  47.7 0.0 copy-done
  47.7 0.0 copy-done.1
  47.7 0.0 copy-done.2
  47.7 0.0 copy-done.3
  47.7 3.1 %tiles.1 = (bf16[16,384,128]{2,1,0:T(8,128)(2,1)}, f32[128,128]{1,0:T(8,128)S(1)}) custom-call(s32[1,32]{1,0:T(1,128)S(1)} %copy-done.2, s32[1,32]{1,0:T(1,128)S(1)} %copy-done.3, bf16[32,128,128]{2,1,0:T(8,128)(2,1)S(1)} %copy-done, bf16[384,128]{1,0:T(8,128)(2,1)S(1)} %copy-done.1, bf16[384,128]{1,0:T(8,128)(2,1)S(1)} %collective-permute-done.beside, ...), custom_call_target="tpu_custom_call" | custom-call | flops 134217728 | bytes 6291456 | tf_op jit(solution)/shard_map/tiles/pallas_call | solution.py:186
  50.9 9.3 %all-to-all-start.1 = ((bf16[16,384,128]{2,1,0:T(8,128)(2,1)}), bf16[16,384,128]{2,1,0:T(8,128)(2,1)S(1)}, u32[]{:S(2)}, u32[]{:S(2)}) async-start(bf16[16,384,128]{2,1,0:T(8,128)(2,1)} %get-tuple-element.12), calls=%async_computation.1 | async-start | bytes 3145728 | tf_op jit(solution)/shard_map/all_to_all | solution.py:204
  60.2 3.2 %collective-permute-start.6 = (f32[128,128]{1,0:T(8,128)S(1)}, f32[128,128]{1,0:T(8,128)S(1)}, u32[]{:S(2)}, u32[]{:S(2)}) collective-permute-start(f32[128,128]{1,0:T(8,128)S(1)} %get-tuple-element.13), channel_id=1, source_target_pairs={{0,64},{16,80},{32,96},{48,112},{64,0},{80,16},{96,32},{112,48},{1... | collective-permute-start | bytes 196616 | tf_op jit(solution)/shard_map/ppermute | solution.py:181
  63.5 1.8 %collective-permute-done.6 = f32[128,128]{1,0:T(8,128)S(1)} collective-permute-done((f32[128,128]{1,0:T(8,128)S(1)}, f32[128,128]{1,0:T(8,128)S(1)}, u32[]{:S(2)}, u32[]{:S(2)}) %collective-permute-start.6) | collective-permute-done | bytes 65568 | tf_op jit(solution)/shard_map/ppermute | solution.py:181
  65.2 3.4 %collective-permute-start.7 = (f32[128,128]{1,0:T(8,128)S(1)}, f32[128,128]{1,0:T(8,128)S(1)}, u32[]{:S(2)}, u32[]{:S(2)}) collective-permute-start(f32[128,128]{1,0:T(8,128)S(1)} %add.15), channel_id=1, source_target_pairs={{0,128},{16,144},{32,160},{48,176},{64,192},{80,208},{96,224},{112... | collective-permute-start | bytes 196616 | tf_op jit(solution)/shard_map/ppermute | solution.py:181
  68.6 2.8 %collective-permute-done.7 = f32[128,128]{1,0:T(8,128)S(1)} collective-permute-done((f32[128,128]{1,0:T(8,128)S(1)}, f32[128,128]{1,0:T(8,128)S(1)}, u32[]{:S(2)}, u32[]{:S(2)}) %collective-permute-start.7) | collective-permute-done | bytes 65568 | tf_op jit(solution)/shard_map/ppermute | solution.py:181
  71.5 2.7 %collective-permute-start.8 = (f32[128,128]{1,0:T(8,128)S(1)}, f32[128,128]{1,0:T(8,128)S(1)}, u32[]{:S(2)}, u32[]{:S(2)}) collective-permute-start(f32[128,128]{1,0:T(8,128)S(1)} %add.16), channel_id=1, source_target_pairs={{0,448},{16,464},{32,480},{48,496},{64,384},{80,400},{96,416},{112... | collective-permute-start | bytes 196616 | tf_op jit(solution)/shard_map/ppermute | solution.py:209
  74.2 3.8 %collective-permute-done.8 = f32[128,128]{1,0:T(8,128)S(1)} collective-permute-done((f32[128,128]{1,0:T(8,128)S(1)}, f32[128,128]{1,0:T(8,128)S(1)}, u32[]{:S(2)}, u32[]{:S(2)}) %collective-permute-start.8) | collective-permute-done | bytes 65568 | tf_op jit(solution)/shard_map/ppermute | solution.py:209
  78.0 1.9 %collective-permute-start.9 = (f32[128,128]{1,0:T(8,128)S(1)}, f32[128,128]{1,0:T(8,128)S(1)}, u32[]{:S(2)}, u32[]{:S(2)}) collective-permute-start(f32[128,128]{1,0:T(8,128)S(1)} %add.17), channel_id=1, source_target_pairs={{0,32},{16,48},{32,0},{48,16},{64,96},{80,112},{96,64},{112,80},{1... | collective-permute-start | bytes 196616 | tf_op jit(solution)/shard_map/ppermute | solution.py:181
  79.9 3.9 %collective-permute-done.9 = f32[128,128]{1,0:T(8,128)S(1)} collective-permute-done((f32[128,128]{1,0:T(8,128)S(1)}, f32[128,128]{1,0:T(8,128)S(1)}, u32[]{:S(2)}, u32[]{:S(2)}) %collective-permute-start.9) | collective-permute-done | bytes 65568 | tf_op jit(solution)/shard_map/ppermute | solution.py:181
  83.8 5.0 %collective-permute-start.10 = (f32[128,128]{1,0:T(8,128)S(1)}, f32[128,128]{1,0:T(8,128)S(1)}, u32[]{:S(2)}, u32[]{:S(2)}) collective-permute-start(f32[128,128]{1,0:T(8,128)S(1)} %add.18), channel_id=1, source_target_pairs={{0,40},{1,41},{2,42},{3,43},{4,44},{5,45},{6,46},{7,47},{8,32},{9,... | collective-permute-start | bytes 196616 | tf_op jit(solution)/shard_map/ppermute | solution.py:213
  88.9 2.3 %collective-permute-done.10 = f32[128,128]{1,0:T(8,128)S(1)} collective-permute-done((f32[128,128]{1,0:T(8,128)S(1)}, f32[128,128]{1,0:T(8,128)S(1)}, u32[]{:S(2)}, u32[]{:S(2)}) %collective-permute-start.10) | collective-permute-done | bytes 65568 | tf_op jit(solution)/shard_map/ppermute | solution.py:213
  91.2 7.2 %all-to-all-done.1.got_ref = bf16[16,384,128]{2,1,0:T(8,128)(2,1)S(1)} async-done(((bf16[16,384,128]{2,1,0:T(8,128)(2,1)}), bf16[16,384,128]{2,1,0:T(8,128)(2,1)S(1)}, u32[]{:S(2)}, u32[]{:S(2)}) %all-to-all-start.1) | async-done | bytes 1572896 | tf_op jit(solution)/shard_map/all_to_all | solution.py:204
  98.3 0.9 finish.1
  (13 shorter events, 0.2 us)
Async XLA Ops:
  3.1 9.9 %collective-permute-start = (bf16[384,128]{1,0:T(8,128)(2,1)}, bf16[384,128]{1,0:T(8,128)(2,1)S(1)}, u32[]{:S(2)}, u32[]{:S(2)}) collective-permute-start(bf16[384,128]{1,0:T(8,128)(2,1)} %get-tuple-element.10.own), channel_id=1, source_target_pairs={{0,16},{16,0},{32,48},{48,32},{64,80},{80,64},{96,112},{112,96},{1... | collective-permute-start | bytes 294920 | tf_op jit(solution)/shard_map/ppermute | solution.py:156
  13.1 17.5 %collective-permute-start.1 = (bf16[768,128]{1,0:T(8,128)(2,1)S(1)}, bf16[768,128]{1,0:T(8,128)(2,1)S(1)}, u32[]{:S(2)}, u32[]{:S(2)}) collective-permute-start(bf16[768,128]{1,0:T(8,128)(2,1)S(1)} %constant_dynamic-update-slice_fusion), channel_id=1, source_target_pairs={{0,64},{16,464},{32,96},{48,496},{64,128},{80,16},{96,160},{112,48... | collective-permute-start | bytes 589832 | tf_op jit(solution)/shard_map/ppermute | solution.py:160
  15.0 32.7 %copy-start = (bf16[32,128,128]{2,1,0:T(8,128)(2,1)S(1)}, bf16[32,128,128]{2,1,0:T(8,128)(2,1)}, u32[]{:S(2)}) copy-start(bf16[32,128,128]{2,1,0:T(8,128)(2,1)} %tiles_ref.1) | copy-start | bytes 3145732
  15.0 32.7 %copy-start.1 = (bf16[384,128]{1,0:T(8,128)(2,1)S(1)}, bf16[384,128]{1,0:T(8,128)(2,1)}, u32[]{:S(2)}) copy-start(bf16[384,128]{1,0:T(8,128)(2,1)} %get-tuple-element.10.own) | copy-start | bytes 294916
  15.0 32.7 %copy-start.2 = (s32[1,32]{1,0:T(1,128)S(1)}, s32[1,32]{1,0:T(1,128)}, u32[]{:S(2)}) copy-start(s32[1,32]{1,0:T(1,128)} %get-tuple-element.8.from_ref) | copy-start | bytes 388
  15.0 32.7 %copy-start.3 = (s32[1,32]{1,0:T(1,128)S(1)}, s32[1,32]{1,0:T(1,128)}, u32[]{:S(2)}) copy-start(s32[1,32]{1,0:T(1,128)} %get-tuple-element.9.to_ref) | copy-start | bytes 388
  15.0 20.8 %all-to-all-start = ((bf16[8,128,128]{2,1,0:T(8,128)(2,1)}), bf16[8,128,128]{2,1,0:T(8,128)(2,1)S(1)}, u32[]{:S(2)}, u32[]{:S(2)}) async-start(bf16[8,128,128]{2,1,0:T(8,128)(2,1)} %get-tuple-element.11), calls=%async_computation | async-start | bytes 524288 | tf_op jit(solution)/shard_map/all_to_all | solution.py:170
  23.0 12.8 %collective-permute-start.3 = (bf16[768,128]{1,0:T(8,128)(2,1)S(1)}, bf16[768,128]{1,0:T(8,128)(2,1)S(1)}, u32[]{:S(2)}, u32[]{:S(2)}) collective-permute-start(bf16[768,128]{1,0:T(8,128)(2,1)S(1)} %constant_dynamic-update-slice_fusion), channel_id=1, source_target_pairs={{0,128},{16,400},{32,160},{48,432},{64,192},{80,464},{96,224},{112... | collective-permute-start | bytes 589832 | tf_op jit(solution)/shard_map/ppermute | solution.py:160
  26.8 9.0 %collective-permute-start.2 = (bf16[768,128]{1,0:T(8,128)(2,1)S(1)}, bf16[768,128]{1,0:T(8,128)(2,1)S(1)}, u32[]{:S(2)}, u32[]{:S(2)}) collective-permute-start(bf16[768,128]{1,0:T(8,128)(2,1)S(1)} %constant_dynamic-update-slice_fusion), channel_id=1, source_target_pairs={{16,432},{32,128},{80,496},{96,192},{144,48},{160,256},{208,112},{... | collective-permute-start | bytes 589832 | tf_op jit(solution)/shard_map/ppermute | solution.py:160
  30.6 12.5 %collective-permute-start.4 = (bf16[1152,128]{1,0:T(8,128)(2,1)S(1)}, bf16[1152,128]{1,0:T(8,128)(2,1)S(1)}, u32[]{:S(2)}, u32[]{:S(2)}) collective-permute-start(bf16[1152,128]{1,0:T(8,128)(2,1)S(1)} %pad_maximum_fusion), channel_id=1, source_target_pairs={{0,32},{16,48},{32,0},{48,16},{64,96},{80,112},{96,64},{112,80},{1... | collective-permute-start | bytes 884744 | tf_op jit(solution)/shard_map/ppermute | solution.py:156
  43.2 4.6 %collective-permute-start.5 = (bf16[3712,128]{1,0:T(8,128)(2,1)S(1)}, bf16[3712,128]{1,0:T(8,128)(2,1)S(1)}, u32[]{:S(2)}, u32[]{:S(2)}) collective-permute-start(bf16[3712,128]{1,0:T(8,128)(2,1)S(1)} %constant_dynamic-update-slice_fusion.2.ours), channel_id=1, source_target_pairs={{0,16},{16,0},{32,48},{48,32},{64,80},{80,64},{96,112},{112,96},{1... | collective-permute-start | bytes 2850824 | tf_op jit(solution)/shard_map/ppermute | solution.py:156
  50.9 47.4 %all-to-all-start.1 = ((bf16[16,384,128]{2,1,0:T(8,128)(2,1)}), bf16[16,384,128]{2,1,0:T(8,128)(2,1)S(1)}, u32[]{:S(2)}, u32[]{:S(2)}) async-start(bf16[16,384,128]{2,1,0:T(8,128)(2,1)} %get-tuple-element.12), calls=%async_computation.1 | async-start | bytes 3145728 | tf_op jit(solution)/shard_map/all_to_all | solution.py:204
  60.2 5.0 %collective-permute-start.6 = (f32[128,128]{1,0:T(8,128)S(1)}, f32[128,128]{1,0:T(8,128)S(1)}, u32[]{:S(2)}, u32[]{:S(2)}) collective-permute-start(f32[128,128]{1,0:T(8,128)S(1)} %get-tuple-element.13), channel_id=1, source_target_pairs={{0,64},{16,80},{32,96},{48,112},{64,0},{80,16},{96,32},{112,48},{1... | collective-permute-start | bytes 196616 | tf_op jit(solution)/shard_map/ppermute | solution.py:181
  65.2 6.2 %collective-permute-start.7 = (f32[128,128]{1,0:T(8,128)S(1)}, f32[128,128]{1,0:T(8,128)S(1)}, u32[]{:S(2)}, u32[]{:S(2)}) collective-permute-start(f32[128,128]{1,0:T(8,128)S(1)} %add.15), channel_id=1, source_target_pairs={{0,128},{16,144},{32,160},{48,176},{64,192},{80,208},{96,224},{112... | collective-permute-start | bytes 196616 | tf_op jit(solution)/shard_map/ppermute | solution.py:181
  71.5 6.5 %collective-permute-start.8 = (f32[128,128]{1,0:T(8,128)S(1)}, f32[128,128]{1,0:T(8,128)S(1)}, u32[]{:S(2)}, u32[]{:S(2)}) collective-permute-start(f32[128,128]{1,0:T(8,128)S(1)} %add.16), channel_id=1, source_target_pairs={{0,448},{16,464},{32,480},{48,496},{64,384},{80,400},{96,416},{112... | collective-permute-start | bytes 196616 | tf_op jit(solution)/shard_map/ppermute | solution.py:209
  78.0 5.8 %collective-permute-start.9 = (f32[128,128]{1,0:T(8,128)S(1)}, f32[128,128]{1,0:T(8,128)S(1)}, u32[]{:S(2)}, u32[]{:S(2)}) collective-permute-start(f32[128,128]{1,0:T(8,128)S(1)} %add.17), channel_id=1, source_target_pairs={{0,32},{16,48},{32,0},{48,16},{64,96},{80,112},{96,64},{112,80},{1... | collective-permute-start | bytes 196616 | tf_op jit(solution)/shard_map/ppermute | solution.py:181
  83.8 7.3 %collective-permute-start.10 = (f32[128,128]{1,0:T(8,128)S(1)}, f32[128,128]{1,0:T(8,128)S(1)}, u32[]{:S(2)}, u32[]{:S(2)}) collective-permute-start(f32[128,128]{1,0:T(8,128)S(1)} %add.18), channel_id=1, source_target_pairs={{0,40},{1,41},{2,42},{3,43},{4,44},{5,45},{6,46},{7,47},{8,32},{9,... | collective-permute-start | bytes 196616 | tf_op jit(solution)/shard_map/ppermute | solution.py:213
